TPU v7x, 32 devices: a whole 2x2x4 slice. The times are simulated.
32 devices in a mesh: freq: 4 (over y, x), rtile: 4 (over z), rep: 2 (over core).
Axes of the slice: x: 2, y: 2, z: 4, core: 2. Of those that a mesh axis runs over, the one named last changes fastest.
Arguments:
- model: bfloat16 [4, 512, 32, 1024], P('rtile', 'freq'), may hold values from -0.1796875 to 0.1796875
- green_left: bfloat16 [2, 12, 8, 8, 48, 256], P(None, 'freq', 'rep', 'rtile'), may hold values from -0.21875 to 0.21875
- green_right: bfloat16 [2, 12, 8, 8, 48, 256], P(None, 'freq', 'rep', 'rtile'), may hold values from -0.25 to 0.25
- ranks: int32 [12, 8, 8], P('freq', 'rep', 'rtile'), may hold values from 8 to 48
- data: float32 [2, 384, 2048], P(None, ('freq', 'rtile'), 'rep'), may hold values from -3 to 3
Outputs:
- residual: float32 [2, 384, 2048], P(None, ('freq', 'rtile'), 'rep')
- gradient: bfloat16 [4, 512, 32, 1024], P('rtile', ('freq', 'rep'))
All inputs are finite; a program needn't handle non-finite values.
Results may differ from a plain program's by a relative error of at most 0.014.
Values may be sent and summed in bfloat16 or wider, within the bound.
No kernel may reach another device: no remote copies, remote signals or barrier semaphores. Data moves between devices by JAX's collectives and lax.ppermute only.
A program may use at most 64 MiB of HBM per device.

v0:
```python
import math

import jax
import jax.numpy as jnp
from jax import lax
from jax.sharding import PartitionSpec as P


def tables(count, length):
    freq_bins = 1 + jnp.arange(count, dtype=jnp.int32)
    samples = jnp.arange(length, dtype=jnp.int32)
    phases = (samples[:, None] * freq_bins[None, :] % length).astype(jnp.float32) * (
        2.0 * math.pi / length
    )
    return (jnp.cos(phases).astype(jnp.bfloat16), (-jnp.sin(phases)).astype(jnp.bfloat16))


def product(form, first, second):
    return jnp.einsum(form, first, second, preferred_element_type=jnp.float32)


def shards(model, green_left, green_right, ranks, data):
    freq_count = lax.axis_size("freq")
    freq_local = ranks.shape[0]
    freq_total = freq_local * freq_count
    length = model.shape[-1]
    rhs_count = model.shape[2]
    rank_size = green_left.shape[4]
    tile_size = green_left.shape[5]
    row_tiles = green_left.shape[2]
    col_tiles = green_left.shape[3]
    cosine, sine_neg = tables(freq_total, length)
    own_traces = model[0]
    spectrum = jnp.stack(
        [product("mrt,tq->qmr", own_traces, cosine), product("mrt,tq->qmr", own_traces, sine_neg)]
    ).astype(jnp.bfloat16)
    spectrum = lax.all_to_all(spectrum, "freq", split_axis=1, concat_axis=2, tiled=True)
    spectrum = spectrum.reshape(2, freq_local, col_tiles, tile_size, rhs_count)
    rank_mask = (jnp.arange(rank_size, dtype=jnp.int32) < ranks[..., None]).astype(jnp.float32)[
        ..., None
    ]
    proj_re = product("fijkn,fjnr->fijkr", green_right[0], spectrum[0]) + product(
        "fijkn,fjnr->fijkr", green_right[1], spectrum[1]
    )
    proj_im = product("fijkn,fjnr->fijkr", green_right[0], spectrum[1]) - product(
        "fijkn,fjnr->fijkr", green_right[1], spectrum[0]
    )
    proj_re = (proj_re * rank_mask).astype(jnp.bfloat16)
    proj_im = (proj_im * rank_mask).astype(jnp.bfloat16)
    out_re = product("fijks,fijkr->fris", green_left[0], proj_re) - product(
        "fijks,fijkr->fris", green_left[1], proj_im
    )
    out_im = product("fijks,fijkr->fris", green_left[0], proj_im) + product(
        "fijks,fijkr->fris", green_left[1], proj_re
    )
    pair_count = freq_local * rhs_count
    predicted = jnp.stack([out_re, out_im]).reshape(2, pair_count, row_tiles * tile_size)
    own_sums = lax.psum_scatter(predicted, "rtile", scatter_dimension=1, tiled=True)
    residual = own_sums - data
    misfit_low = lax.all_gather(residual.astype(jnp.bfloat16), "rtile", axis=1, tiled=True)
    misfit_low = misfit_low.reshape(2, freq_local, rhs_count, row_tiles, tile_size)
    back_re = product("fijks,fris->fijkr", green_left[0], misfit_low[0]) + product(
        "fijks,fris->fijkr", green_left[1], misfit_low[1]
    )
    back_im = product("fijks,fris->fijkr", green_left[0], misfit_low[1]) - product(
        "fijks,fris->fijkr", green_left[1], misfit_low[0]
    )
    back_re = (back_re * rank_mask).astype(jnp.bfloat16)
    back_im = (back_im * rank_mask).astype(jnp.bfloat16)
    grad_re = product("fijkn,fijkr->fjnr", green_right[0], back_re) - product(
        "fijkn,fijkr->fjnr", green_right[1], back_im
    )
    grad_im = product("fijkn,fijkr->fjnr", green_right[0], back_im) + product(
        "fijkn,fijkr->fjnr", green_right[1], back_re
    )
    partial_grad = jnp.stack([grad_re, grad_im]).reshape(
        2, freq_local, col_tiles * tile_size, rhs_count
    )
    arrived = lax.all_to_all(partial_grad, ("freq", "rep"), split_axis=2, concat_axis=1, tiled=True)
    group_size = arrived.shape[2]
    arrived = arrived.reshape(2, freq_count, 2, freq_local, group_size, rhs_count)
    grad_spec = (
        jnp.sum(arrived, axis=2).reshape(2, freq_total, group_size, rhs_count).astype(jnp.bfloat16)
    )
    gradient = product("qmr,tq->mrt", grad_spec[0], cosine) + product(
        "qmr,tq->mrt", grad_spec[1], sine_neg
    )
    return (residual, gradient.astype(jnp.bfloat16)[None])


def solution(mesh):
    return jax.shard_map(
        shards,
        mesh=mesh,
        in_specs=(
            P("rtile", "freq", None, None),
            P(None, "freq", "rep", "rtile", None, None),
            P(None, "freq", "rep", "rtile", None, None),
            P("freq", "rep", "rtile"),
            P(None, ("freq", "rtile"), "rep"),
        ),
        out_specs=(P(None, ("freq", "rtile"), "rep"), P("rtile", ("freq", "rep"), None, None)),
        check_vma=False,
    )
```

profile of v0, /device:TPU:0, one launch (start us, length us, event | category | flops | bytes accessed | tf_op | source)
XLA Modules:
  0.0 125.9 jit_solution(13473869220474865711)
XLA Ops:
  7.2 0.0 copy-start.4
  7.2 12.5 %fusion.31 = bf16[1,12,128,32]{2,1,3,0:T(8,128)(2,1)S(1)} fusion(bf16[128,32,1024]{2,1,0:T(8,128)(2,1)} %bitcast.154, s32[12]{0:T(128)S(1)} %iota_add_fusion), kind=kOutput, calls=%fused_computation.40 | convolution fusion | flops 100909056 | bytes 8486960 | tf_op jit(solution)/shard_map/mrt,tq->qmr/dot_general | solution.py:19
  19.7 0.0 copy-done.4
  19.7 9.2 %fusion.34 = bf16[1,12,128,32]{2,1,3,0:T(8,128)(2,1)S(1)} fusion(bf16[128,32,1024]{2,1,0:T(8,128)(2,1)S(1)} %bitcast.155, s32[12]{0:T(128)S(1)} %iota_add_fusion), kind=kOutput, calls=%fused_computation.41 | convolution fusion | flops 100896768 | bytes 8486960 | tf_op jit(solution)/shard_map/mrt,tq->qmr/dot_general | solution.py:19
  28.9 0.0 copy-start.1
  29.0 0.7 copy.87
  29.7 5.2 %all-to-all-start = ((bf16[2,12,128,32]{2,3,0,1:T(8,128)(2,1)}), bf16[2,12,128,32]{2,3,0,1:T(8,128)(2,1)S(1)}, u32[]{:S(2)}, u32[]{:S(2)}) async-start(bf16[2,12,128,32]{2,3,0,1:T(8,128)(2,1)} %copy.87), calls=%async_computation | async-start | bytes 393216 | tf_op jit(solution)/shard_map/all_to_all | solution.py:37
  34.9 0.0 copy-start.3
  34.9 0.0 reduce-scatter.2.cloned.1.call-start
  34.9 0.0 copy-done.1
  34.9 0.1 fusion.104
  35.0 0.6 copy-done.3
  35.5 0.1 fusion.86
  35.6 4.4 %all-to-all-done = bf16[2,12,128,32]{2,3,0,1:T(8,128)(2,1)S(1)} async-done(((bf16[2,12,128,32]{2,3,0,1:T(8,128)(2,1)}), bf16[2,12,128,32]{2,3,0,1:T(8,128)(2,1)S(1)}, u32[]{:S(2)}, u32[]{:S(2)}) %all-to-all-start) | async-done | bytes 196640 | tf_op jit(solution)/shard_map/all_to_all | solution.py:37
  40.1 0.1 copy.92
  40.2 0.1 squeeze.25
  40.2 0.1 copy.89
  40.3 0.1 squeeze.23
  40.4 0.4 fusion.47
  40.8 0.5 fusion.48
  41.3 0.5 fusion.17
  41.7 0.5 fusion.18
  42.2 0.4 copy-done
  42.5 0.3 convolution_bitcast_fusion
  42.8 1.0 convolution_bitcast_fusion.2
  43.8 0.3 fusion.14
  44.1 0.3 copy.102
  44.4 0.2 stack.34
  44.6 1.3 %fusion.12 = f32[3,32,4,256]{3,1,2,0:T(8,128)S(1)} fusion(f32[3,4,32,256]{3,2,1,0:T(8,128)} %convolution_bitcast_fusion.2, bf16[2,3,4,2,48,256]{5,4,3,2,1,0:T(8,128)(2,1)S(1)} %copy-done, bf16[3,4,2,48,32]{3,4,1,2,0:T(8,128)(2,1)S(1)} %fusion.18), kind=kOutput, calls=%fused_computation.21 | convolution fusion | flops 18972672 | bytes 1572864 | tf_op jit(solution)/shard_map/fijks,fijkr->fris/dot_general | solution.py:19
  45.9 0.3 copy.99
  46.1 1.0 stack.33
  47.1 2.0 %pad_maximum_fusion = f32[2,96,1024]{2,1,0:T(8,128)} fusion(f32[1,96,1024]{2,1,0:T(8,128)S(1)} %stack.34, f32[1,96,1024]{2,1,0:T(8,128)} %stack.33), kind=kLoop, calls=%fused_computation.42 | loop fusion | flops 196608 | bytes 1572864 | tf_op jit(solution)/shard_map/stack | solution.py:57
  49.1 0.0 reduce-scatter.2.cloned.1.call-update
  49.1 23.3 %reduce-scatter.2.cloned.1.call-done = f32[2,24,1024]{2,1,0:T(8,128)} async-done(((f32[2,96,1024]{2,1,0:T(8,128)}), f32[2,24,1024]{2,1,0:T(8,128)}) %reduce-scatter.2.cloned.1.call-update) | async-done | bytes 196624 | tf_op jit(solution)/shard_map/reduce_scatter | solution.py:58
  72.4 0.0 copy-done.2
  72.4 1.6 %fusion.103 = (bf16[2,24,1024]{2,1,0:T(8,128)(2,1)S(1)}, f32[2,24,1024]{2,1,0:T(8,128)}) fusion(f32[2,24,1024]{2,1,0:T(8,128)} %reduce-scatter.2.cloned.1.call-done, f32[2,24,1024]{2,1,0:T(8,128)S(1)} %copy-done.2), kind=kLoop, calls=%fused_computation.116 | loop fusion | flops 98304 | bytes 688128 | tf_op jit(solution)/shard_map/convert_element_type | solution.py:60
  74.1 15.2 %all_gather.3 = bf16[2,96,1024]{2,1,0:T(8,128)(2,1)S(1)} all-gather(bf16[2,24,1024]{2,1,0:T(8,128)(2,1)S(1)} %get-tuple-element.2), channel_id=1, replica_groups=mesh['freq'=4,'rtile'=4,'rep'=2] {'rtile'}, dimensions={1}, use_global_device_ids=true | all-gather | bytes 491520 | tf_op jit(solution)/shard_map/all_gather | solution.py:60
  89.3 0.1 squeeze.57
  89.4 0.1 squeeze.56
  89.5 0.4 fusion.43
  90.0 0.4 fusion.41
  90.4 0.5 fusion.20
  90.9 0.4 fusion.19
  91.3 0.2 convolution_bitcast_fusion.6
  91.6 0.3 convolution_bitcast_fusion.4
  91.9 0.3 fusion.28
  92.1 0.3 fusion.30
  92.4 0.2 copy.113
  92.6 0.2 stack.37
  92.7 0.2 copy.110
  92.9 0.2 stack.36
  93.1 1.1 copy.114
  94.2 1.5 %reshape.63 = f32[8,1,12288]{2,1,0:T(1,128)S(1)} reshape(f32[512,3,2,32]{3,2,1,0:T(2,128)S(1)} %bitcast.142) | data formatting | bytes 786432
  95.7 11.8 %all_to_all.30 = f32[8,1,12288]{2,1,0:T(1,128)S(1)} all-to-all(f32[8,1,12288]{2,1,0:T(1,128)S(1)} %reshape.63), channel_id=1, replica_groups=mesh['freq'=4,'rtile'=4,'rep'=2] {'freq','rep'}, dimensions={0} | all-to-all | bytes 786432 | tf_op jit(solution)/shard_map/all_to_all | solution.py:79
  107.5 0.5 broadcast.33
  108.1 1.6 %reduce.1 = f32[8,12288]{1,0:T(8,128)S(1)} reduce(f32[8,1,12288]{2,1,0:T(1,128)S(1)} %all_to_all.30, f32[]{:T(128)} %broadcast.33), dimensions={1}, to_apply=%all_to_all.25.reduce_sub_computation | reduce | bytes 786436 | tf_op jit(solution)/shard_map/all_to_all | solution.py:79
  109.6 1.3 %reshape.64 = f32[512,3,2,32]{3,2,1,0:T(2,128)S(1)} reshape(f32[8,12288]{1,0:T(8,128)S(1)} %reduce.1) | data formatting | bytes 786432
  111.0 1.5 %reduce = bf16[2,4,3,64,32]{4,0,2,3,1:T(2,128)(2,1)S(1)} reduce(f32[2,4,2,3,64,32]{5,0,3,4,2,1:T(2,128)S(1)} %bitcast.141, f32[]{:T(128)} %constant.20.clone.1), dimensions={2}, to_apply=%region_1.2 | reduce | flops 49152 | bytes 491524
  112.5 0.8 copy.152
  113.3 0.1 fusion.106
  113.4 0.3 copy.117
  113.7 0.3 copy.119
  114.0 1.5 %fusion.83 = f32[64,32,1024]{2,1,0:T(8,128)S(1)} fusion(bf16[12,64,32]{2,0,1:T(8,128)(2,1)S(1)} %copy.117, s32[12]{0:T(128)S(1)} %iota_add_fusion), kind=kOutput, calls=%fused_computation.96 | convolution fusion | flops 50515968 | bytes 8437808 | tf_op jit(solution)/shard_map/qmr,tq->mrt/dot_general | solution.py:19
  115.5 3.6 %fusion.4 = bf16[1,64,32,1024]{3,2,1,0:T(8,128)(2,1)} fusion(f32[64,32,1024]{2,1,0:T(8,128)S(1)} %fusion.83, bf16[12,64,32]{2,0,1:T(8,128)(2,1)S(1)} %copy.119, s32[12]{0:T(128)S(1)} %iota_add_fusion), kind=kOutput, calls=%fused_computation.5 | convolution fusion | flops 54722560 | bytes 12632112 | tf_op jit(solution)/shard_map/qmr,tq->mrt/dot_general | solution.py:19
  (11 shorter events, 0.2 us)
Async XLA Ops:
  7.2 12.6 %copy-start.4 = (bf16[1,128,32,1024]{3,2,1,0:T(8,128)(2,1)S(1)}, bf16[1,128,32,1024]{3,2,1,0:T(8,128)(2,1)}, u32[]{:S(2)}) copy-start(bf16[1,128,32,1024]{3,2,1,0:T(8,128)(2,1)} %param.5) | copy-start | bytes 25165828
  28.9 6.0 %copy-start.1 = (bf16[2,3,4,2,48,256]{5,4,3,2,1,0:T(8,128)(2,1)S(1)}, bf16[2,3,4,2,48,256]{5,4,3,2,1,0:T(8,128)(2,1)}, u32[]{:S(2)}) copy-start(bf16[2,3,4,2,48,256]{5,4,3,2,1,0:T(8,128)(2,1)} %param.7) | copy-start | bytes 3538948
  29.7 10.4 %all-to-all-start = ((bf16[2,12,128,32]{2,3,0,1:T(8,128)(2,1)}), bf16[2,12,128,32]{2,3,0,1:T(8,128)(2,1)S(1)}, u32[]{:S(2)}, u32[]{:S(2)}) async-start(bf16[2,12,128,32]{2,3,0,1:T(8,128)(2,1)} %copy.87), calls=%async_computation | async-start | bytes 393216 | tf_op jit(solution)/shard_map/all_to_all | solution.py:37
  34.9 0.7 copy-start.3
  34.9 37.6 %reduce-scatter.2.cloned.1.call-start = ((), (), s32[]{:S(2)}) async-start(), calls=%async_computation.3 | async-start | bytes 983040 | tf_op jit(solution)/shard_map/reduce_scatter | solution.py:58
  41.3 1.3 %copy-start = (bf16[2,3,4,2,48,256]{5,4,3,2,1,0:T(8,128)(2,1)S(1)}, bf16[2,3,4,2,48,256]{5,4,3,2,1,0:T(8,128)(2,1)}, u32[]{:S(2)}) copy-start(bf16[2,3,4,2,48,256]{5,4,3,2,1,0:T(8,128)(2,1)} %param.6) | copy-start | bytes 3538948
  47.1 25.4 %copy-start.2 = (f32[2,24,1024]{2,1,0:T(8,128)S(1)}, f32[2,24,1024]{2,1,0:T(8,128)}, u32[]{:S(2)}) copy-start(f32[2,24,1024]{2,1,0:T(8,128)} %param.9) | copy-start | bytes 589828
Sparse Core Ops, SparseCore 0:
  49.2 23.1 reduce-scatter.1
where the time goes:
time: 126 us
  matrix products  34.3 us (27%)
  waiting for transfers between devices  27.8 us (22%)
  blocking collectives  27 us (21%)
  between operations  14.4 us (11%)
  local copies, waits for them, and re-layouts  10.5 us (8%)
  other arithmetic  6.86 us (5%)
  starting transfers between devices  5.17 us (4%)
    dot_general x20, matrix products, product(): return jnp.einsum(form, first, second, preferred_element_type=jnp.float32)  34.3 us
    reduce_scatter x1, waiting for transfers between devices, shards(): lax.psum_scatter(predicted, 'rtile', scatter_dimension=1, tiled=True)  23.3 us
    all_gather x1, blocking collectives, shards(): lax.all_gather(residual.astype(jnp.bfloat16), 'rtile', axis=1, tiled=True)  15.2 us
    all_to_all x1, blocking collectives, shards(): lax.all_to_all(partial_grad, ('freq', 'rep'), split_axis=2, concat_axis=1...  11.8 us
    all_to_all x1, starting transfers between devices, shards(): lax.all_to_all(spectrum, 'freq', split_axis=1, concat_axis=2, tiled=True)  5.16 us
    all_to_all x1, waiting for transfers between devices, shards(): lax.all_to_all(spectrum, 'freq', split_axis=1, concat_axis=2, tiled=True)  4.44 us
    unnamed x12, local copies, waits for them, and re-layouts  3.82 us
  transfers between devices with their start and end apart: 2, of which 2 were waited for; matrix products, arithmetic and copies ran while one was open for 0% of the time, Pallas kernels for 0%

commit v1 on v0

v1 whole, which is shorter than its diff:
```python
import functools
import math

import jax
import jax.numpy as jnp
import numpy as np
from jax import lax
from jax.experimental import pallas as pl
from jax.experimental.pallas import tpu as pltpu
from jax.sharding import PartitionSpec as P

LANES = 128
VMEM_LIMIT = 48 * 1024 * 1024


def tables(count, length):
    freq_bins = 1 + np.arange(count, dtype=np.int32)
    samples = np.arange(length, dtype=np.int32)
    phases = (freq_bins[:, None] * samples[None, :] % length).astype(np.float32)
    phases = phases * np.float32(2.0 * math.pi / length)
    rows = np.concatenate([np.cos(phases), -np.sin(phases)])
    return jnp.asarray(rows.astype(jnp.bfloat16))


def dot(first, second, first_dim, second_dim):
    return lax.dot_general(
        first,
        second,
        (((first_dim,), (second_dim,)), ((), ())),
        preferred_element_type=jnp.float32,
    )


def turned(pair):
    half = pair.shape[1] // 2
    return jnp.concatenate([-pair[:, half:], pair[:, :half]], axis=1)


def spectrum_kernel(table_ref, model_ref, out_ref, rows_ref):
    step = pl.program_id(0)
    high, part, rhs, length = model_ref.shape
    dests, freqs, _, low, lanes = out_ref.shape
    table = table_ref[...]
    bins = table.shape[0]
    for start in range(0, part, 2):
        width = min(2, part - start)
        block = jnp.concatenate(
            [model_ref[:, start + at].reshape(high * rhs, length) for at in range(width)]
        )
        sums = dot(table, block, 1, 1)
        for at in range(width):
            rows = pl.ds((step * part + start + at) * bins, bins)
            rows_ref[rows, :] = sums[:, at * lanes : (at + 1) * lanes]

    @pl.when(step == pl.num_programs(0) - 1)
    def _():
        for dest in range(dests):
            for f in range(freqs):
                for c in range(2):
                    q = c * dests * freqs + dest * freqs + f
                    picked = rows_ref[pl.ds(q, low, stride=bins), :]
                    out_ref[dest, f, c] = picked.astype(out_ref.dtype)


def spectrum_of(model, table, dests, freqs):
    traces, rhs, length = model.shape
    high = LANES // rhs
    low = traces // high
    steps = 4 if low % 4 == 0 else 1
    bins = table.shape[0]
    return pl.pallas_call(
        spectrum_kernel,
        grid=(steps,),
        in_specs=[
            pl.BlockSpec((bins, length), lambda s: (0, 0)),
            pl.BlockSpec((high, low // steps, rhs, length), lambda s: (0, s, 0, 0)),
        ],
        out_specs=pl.BlockSpec((dests, freqs, 2, low, LANES), lambda s: (0, 0, 0, 0, 0)),
        out_shape=jax.ShapeDtypeStruct((dests, freqs, 2, low, LANES), jnp.bfloat16),
        scratch_shapes=[pltpu.VMEM((low * bins, LANES), jnp.float32)],
        compiler_params=pltpu.CompilerParams(vmem_limit_bytes=VMEM_LIMIT),
        name="spectrum",
    )(table, model.reshape(high, low, rhs, length))


def masked(product, ranks_ref, places, size):
    row = lax.broadcasted_iota(jnp.int32, (size, product.shape[1]), 0)
    kept = [
        jnp.where(row < ranks_ref[place], product[at * size : (at + 1) * size], 0.0)
        for at, place in enumerate(places)
    ]
    return [part.astype(jnp.bfloat16) for part in kept]


def predict_kernel(ranks_ref, spec_ref, right_ref, left_ref, out_ref, sum_ref):
    groups, freqs, _, low, lanes = spec_ref.shape
    _, _, row_tiles, col_tiles, size, tile = left_ref.shape
    parts, _, pairs, _ = out_ref.shape
    rhs = parts * pairs // freqs
    high = lanes // rhs
    per_tile = groups // col_tiles
    for f in range(freqs):
        projected = []
        for j in range(col_tiles):
            halves = []
            for c in range(2):
                blocks = []
                for g in range(j * per_tile, (j + 1) * per_tile):
                    got = spec_ref[g, f, c].astype(jnp.float32)
                    blocks += [got[:, h * rhs : (h + 1) * rhs] for h in range(high)]
                halves.append(jnp.concatenate(blocks))
            first = jnp.concatenate(halves, axis=1).astype(jnp.bfloat16)
            second = jnp.concatenate([halves[1], -halves[0]], axis=1).astype(jnp.bfloat16)
            right = [right_ref[c, f, :, j].reshape(row_tiles * size, tile) for c in range(2)]
            product = dot(right[0], first, 1, 0) + dot(right[1], second, 1, 0)
            places = [(f, i, j) for i in range(row_tiles)]
            projected.append(masked(product, ranks_ref, places, size))
        for i in range(row_tiles):
            straight = [projected[j][i] for j in range(col_tiles)]
            factors = jnp.concatenate(straight + [turned(part) for part in straight])
            left = left_ref[:, f, i].reshape(2 * col_tiles * size, tile)
            predicted = dot(factors, left, 0, 0)
            for c in range(2):
                sum_ref[c, f * rhs : (f + 1) * rhs, i * tile : (i + 1) * tile] = predicted[
                    c * rhs : (c + 1) * rhs
                ]
    for part in range(parts):
        for c in range(2):
            out_ref[part, c] = sum_ref[c, part * pairs : (part + 1) * pairs].astype(out_ref.dtype)


def predict(ranks, spectrum, green_right, green_left, parts):
    freqs, row_tiles = ranks.shape[:2]
    tile = green_left.shape[5]
    rhs = LANES * spectrum.shape[0] * spectrum.shape[3] // (green_left.shape[3] * tile)
    pairs = freqs * rhs
    sources = row_tiles * tile
    return pl.pallas_call(
        predict_kernel,
        in_specs=[pl.BlockSpec(memory_space=pltpu.SMEM)]
        + [pl.BlockSpec(memory_space=pltpu.VMEM)] * 3,
        out_specs=pl.BlockSpec(memory_space=pltpu.VMEM),
        out_shape=jax.ShapeDtypeStruct((parts, 2, pairs // parts, sources), jnp.bfloat16),
        scratch_shapes=[pltpu.VMEM((2, pairs, sources), jnp.float32)],
        compiler_params=pltpu.CompilerParams(vmem_limit_bytes=VMEM_LIMIT),
        name="predict",
    )(ranks, spectrum, green_right, green_left)


def back_kernel(ranks_ref, misfit_ref, right_ref, left_ref, out_ref, misfit_all_ref):
    parts, _, pairs, _ = misfit_ref.shape
    _, freqs, row_tiles, col_tiles, size, tile = left_ref.shape
    dests, _, _, low, lanes = out_ref.shape
    rhs = parts * pairs // freqs
    high = lanes // rhs
    per_tile = dests // col_tiles
    for part in range(parts):
        for c in range(2):
            misfit_all_ref[c, part * pairs : (part + 1) * pairs] = misfit_ref[part, c].astype(
                jnp.float32
            )
    for f in range(freqs):
        back = []
        for i in range(row_tiles):
            rows = [
                misfit_all_ref[c, f * rhs : (f + 1) * rhs, i * tile : (i + 1) * tile]
                for c in range(2)
            ]
            first = jnp.concatenate(rows).astype(jnp.bfloat16)
            second = jnp.concatenate([rows[1], -rows[0]]).astype(jnp.bfloat16)
            left = [left_ref[c, f, i].reshape(col_tiles * size, tile) for c in range(2)]
            product = dot(left[0], first, 1, 1) + dot(left[1], second, 1, 1)
            places = [(f, i, j) for j in range(col_tiles)]
            back.append(masked(product, ranks_ref, places, size))
        for j in range(col_tiles):
            straight = [back[i][j] for i in range(row_tiles)]
            factors = jnp.concatenate(straight + [turned(part) for part in straight])
            right = jnp.concatenate(
                [right_ref[c, f, :, j].reshape(row_tiles * size, tile) for c in range(2)]
            )
            grad = dot(factors, right, 0, 0).T
            for at in range(per_tile):
                rows = at * high * low
                for c in range(2):
                    blocks = [
                        grad[rows + h * low : rows + (h + 1) * low, c * rhs : (c + 1) * rhs]
                        for h in range(high)
                    ]
                    out_ref[j * per_tile + at, f, c] = jnp.concatenate(blocks, axis=1).astype(
                        out_ref.dtype
                    )


def back_project(ranks, misfit, green_right, green_left, dests):
    freqs = ranks.shape[0]
    parts, _, pairs, _ = misfit.shape
    rhs = parts * pairs // freqs
    low = green_left.shape[3] * green_left.shape[5] * rhs // (dests * LANES)
    return pl.pallas_call(
        back_kernel,
        in_specs=[pl.BlockSpec(memory_space=pltpu.SMEM)]
        + [pl.BlockSpec(memory_space=pltpu.VMEM)] * 3,
        out_specs=pl.BlockSpec(memory_space=pltpu.VMEM),
        out_shape=jax.ShapeDtypeStruct((dests, freqs, 2, low, LANES), jnp.bfloat16),
        scratch_shapes=[pltpu.VMEM((2, parts * pairs, misfit.shape[3]), jnp.float32)],
        compiler_params=pltpu.CompilerParams(vmem_limit_bytes=VMEM_LIMIT),
        name="back_project",
    )(ranks, misfit, green_right, green_left)


def gradient_kernel(table_ref, parts_ref, out_ref, rows_ref):
    step = pl.program_id(0)
    groups, reps, freqs, _, low, lanes = parts_ref.shape
    high, part, rhs, length = out_ref.shape
    bins = table_ref.shape[0]

    @pl.when(step == 0)
    def _():
        for g in range(groups):
            for f in range(freqs):
                for c in range(2):
                    total = parts_ref[g, 0, f, c].astype(jnp.float32)
                    for rep in range(1, reps):
                        total = total + parts_ref[g, rep, f, c].astype(jnp.float32)
                    rows_ref[pl.ds(c * groups * freqs + g * freqs + f, low, stride=bins), :] = total

    table = table_ref[...]
    for at in range(part):
        coefficients = rows_ref[pl.ds((step * part + at) * bins, bins), :].astype(jnp.bfloat16)
        traces = dot(coefficients, table, 0, 0).astype(out_ref.dtype)
        out_ref[:, at] = traces.reshape(high, rhs, length)


def gradient_of(parts, table, rhs):
    groups, reps, freqs, _, low, lanes = parts.shape
    bins, length = table.shape
    high = lanes // rhs
    steps = 4 if low % 4 == 0 else 1
    out = pl.pallas_call(
        gradient_kernel,
        grid=(steps,),
        in_specs=[
            pl.BlockSpec((bins, length), lambda s: (0, 0)),
            pl.BlockSpec(parts.shape, lambda s: (0,) * 6),
        ],
        out_specs=pl.BlockSpec((high, low // steps, rhs, length), lambda s: (0, s, 0, 0)),
        out_shape=jax.ShapeDtypeStruct((high, low, rhs, length), jnp.bfloat16),
        scratch_shapes=[pltpu.VMEM((low * bins, lanes), jnp.float32)],
        compiler_params=pltpu.CompilerParams(vmem_limit_bytes=VMEM_LIMIT),
        name="gradient",
    )(table, parts)
    return out.reshape(1, high * low, rhs, length)


def shards(model, green_left, green_right, ranks, data):
    freq_count = lax.axis_size("freq")
    tile_count = lax.axis_size("rtile")
    rep_count = lax.axis_size("rep")
    freq_local = ranks.shape[0]
    rhs_count = model.shape[2]
    table = tables(freq_local * freq_count, model.shape[3])
    spectrum = spectrum_of(model[0], table, freq_count, freq_local)
    spectrum = lax.all_to_all(spectrum, "freq", split_axis=0, concat_axis=0, tiled=True)
    predicted = predict(ranks, spectrum, green_right, green_left, tile_count)
    arrived = lax.all_to_all(predicted, "rtile", split_axis=0, concat_axis=0, tiled=True)
    residual = jnp.sum(arrived.astype(jnp.float32), axis=0) - data
    misfit = lax.all_gather(residual.astype(jnp.bfloat16), "rtile", axis=0)
    partial = back_project(ranks, misfit, green_right, green_left, freq_count * rep_count)
    arrived = lax.all_to_all(partial, ("freq", "rep"), split_axis=0, concat_axis=0, tiled=True)
    arrived = arrived.reshape((freq_count, rep_count) + arrived.shape[1:])
    return (residual, gradient_of(arrived, table, rhs_count))


def solution(mesh):
    return jax.shard_map(
        shards,
        mesh=mesh,
        in_specs=(
            P("rtile", "freq", None, None),
            P(None, "freq", "rep", "rtile", None, None),
            P(None, "freq", "rep", "rtile", None, None),
            P("freq", "rep", "rtile"),
            P(None, ("freq", "rtile"), "rep"),
        ),
        out_specs=(P(None, ("freq", "rtile"), "rep"), P("rtile", ("freq", "rep"), None, None)),
        check_vma=False,
    )
```

time: 126 us -> 65.9 us (0.52)
  matrix products: 34.3 us -> 0 us
  waiting for transfers between devices: 27.8 us -> 5.09 us
  Pallas kernels: 0 us -> 14.3 us
  between operations: 14.4 us -> 0.67 us
  blocking collectives: 27 us -> 38.6 us
  local copies, waits for them, and re-layouts: 10.5 us -> 0.92 us
  other arithmetic: 6.86 us -> 0.76 us
    dot_general x20 -> x0, matrix products: 34.3 us -> none  [product(): return jnp.einsum(form, first, second, preferred_element_type=jnp.float32)]
    reduce_scatter x1 -> x0, waiting for transfers between devices: 23.3 us -> none  [shards(): lax.psum_scatter(predicted, 'rtile', scatter_dimension=1, tiled=True)]
    pallas_call x0 -> x4, Pallas kernels: none -> 14.3 us  [the longest x1 6.42 us: spectrum_of(): pl.pallas_call(spectrum_kernel, grid=(steps,), in_specs=[pl.BlockSpec((bi...]
    all_to_all x1 -> x2, blocking collectives: 11.8 us -> 23.6 us  [the longest x1 14.9 us: shards(): lax.all_to_all(predicted, 'rtile', split_axis=0, concat_axis=0, tiled=True)]
    another operation x6 -> x0, local copies, waits for them, and re-layouts: 3.3 us -> none  [the longest x3 1.41 us: shards(): jnp.stack([grad_re, grad_im])]
    unnamed x12 -> x13, local copies, waits for them, and re-layouts: 3.82 us -> 0.92 us
    another operation x3 -> x0, other arithmetic: 2.06 us -> none  [the longest x1 1.99 us: shards(): jnp.stack([out_re, out_im]).reshape(2, pair_count, row_tiles * tile_size)]
    all_to_all x1 -> x0, other arithmetic: 1.57 us -> none  [shards(): lax.all_to_all(partial_grad, ('freq', 'rep'), split_axis=2, concat_axis=1...]
  transfers between devices with their start and end apart: 2 -> 1, of which waited for: 2 -> 1; matrix products, arithmetic and copies ran while one was open for 0% -> 0% of each run, Pallas kernels for 0% -> 0%
where the time goes in v1:
time: 65.9 us; the launch traced here: 65.6 us
  blocking collectives  38.6 us (59%)
  Pallas kernels  14.3 us (22%)
  starting transfers between devices  5.29 us (8%)
  waiting for transfers between devices  5.09 us (8%)
  local copies, waits for them, and re-layouts  0.92 us (1%)
  other arithmetic  0.76 us (1%)
  between operations  0.67 us (1%)
    all_gather x1, blocking collectives, shards(): misfit = lax.all_gather(residual.astype(jnp.bfloat16), 'rtile', axis=0)  15 us
    all_to_all x1, blocking collectives, shards(): lax.all_to_all(predicted, 'rtile', split_axis=0, concat_axis=0, tiled=True)  14.9 us
    all_to_all x1, blocking collectives, shards(): lax.all_to_all(partial, ('freq', 'rep'), split_axis=0, concat_axis=0, til...  8.65 us
    pallas_call x1, Pallas kernels, spectrum_of(): pl.pallas_call(spectrum_kernel, grid=(steps,), in_specs=[pl.BlockSpec((bi...  6.42 us
    all_to_all x1, starting transfers between devices, shards(): lax.all_to_all(spectrum, 'freq', split_axis=0, concat_axis=0, tiled=True)  5.29 us
    all_to_all x1, waiting for transfers between devices, shards(): lax.all_to_all(spectrum, 'freq', split_axis=0, concat_axis=0, tiled=True)  5.09 us
    pallas_call x1, Pallas kernels, gradient_of(): pl.pallas_call(gradient_kernel, grid=(steps,), in_specs=[pl.BlockSpec((bi...  3.36 us
    pallas_call x1, Pallas kernels, predict(): pl.pallas_call(predict_kernel, in_specs=[pl.BlockSpec(memory_space=pltpu....  2.28 us
  transfers between devices with their start and end apart: 1, of which 1 were waited for; matrix products, arithmetic and copies ran while one was open for 0% of the time, Pallas kernels for 0%

profile of v1, /device:TPU:0, one launch (start us, length us, event | category | flops | bytes accessed | tf_op | source)
XLA Modules:
  0.0 65.6 jit_solution(4600584414229522285)
XLA Ops:
  0.6 0.0 copy-start.2
  0.6 0.8 %copy-done.2 = bf16[24,1024]{1,0:T(8,128)(2,1)S(1)} copy-done((bf16[24,1024]{1,0:T(8,128)(2,1)S(1)}, bf16[24,1024]{1,0:T(8,128)(2,1)}, u32[]{:S(2)}) %copy-start.2) | copy-done | bytes 49176
  1.4 0.0 copy-start.5
  1.4 0.0 copy-start
  1.4 0.0 copy-start.1
  1.4 6.4 %spectrum.1 = bf16[4,3,2,32,128]{4,3,2,1,0:T(8,128)(2,1)} custom-call(bf16[24,1024]{1,0:T(8,128)(2,1)S(1)} %copy-done.2, bf16[4,32,32,1024]{3,2,1,0:T(8,128)(2,1)} %bitcast.6), custom_call_target="tpu_custom_call" | custom-call | tf_op jit(solution)/shard_map/spectrum/pallas_call | solution.py:71
  7.9 0.0 copy-start.4
  7.9 5.3 %all-to-all-start = ((bf16[4,3,2,32,128]{4,3,2,1,0:T(8,128)(2,1)}), bf16[4,3,2,32,128]{4,3,2,1,0:T(8,128)(2,1)S(1)}, u32[]{:S(2)}, u32[]{:S(2)}) async-start(bf16[4,3,2,32,128]{4,3,2,1,0:T(8,128)(2,1)} %spectrum.1), calls=%async_computation | async-start | bytes 393216 | tf_op jit(solution)/shard_map/all_to_all | solution.py:263
  13.2 0.0 copy-done.5
  13.2 0.1 copy.10.ranks_ref
  13.3 0.0 copy-start.3
  13.3 5.1 %all-to-all-done.spec_ref = bf16[4,3,2,32,128]{4,3,2,1,0:T(8,128)(2,1)S(1)} async-done(((bf16[4,3,2,32,128]{4,3,2,1,0:T(8,128)(2,1)}), bf16[4,3,2,32,128]{4,3,2,1,0:T(8,128)(2,1)S(1)}, u32[]{:S(2)}, u32[]{:S(2)}) %all-to-all-start) | async-done | bytes 196640 | tf_op jit(solution)/shard_map/all_to_all | solution.py:263
  18.4 0.0 copy-done
  18.4 0.0 copy-done.1
  18.4 2.3 %predict.1 = bf16[4,2,24,1024]{3,2,1,0:T(8,128)(2,1)S(1)} custom-call(s32[3,4,2]{2,1,0:T(4,128)S(1)} %copy.10.ranks_ref, bf16[4,3,2,32,128]{4,3,2,1,0:T(8,128)(2,1)S(1)} %all-to-all-done.spec_ref, bf16[2,3,4,2,48,256]{5,4,3,2,1,0:T(8,128)(2,1)S(1)} %copy-done, bf16[2,3,4,2,48,256]{5,4,3,2,1,0:T(8,128)(2,1)S(1)} %copy-done.1), custom_call_target="tpu_custom_call" | custom-call | tf_op jit(solution)/shard_map/predict/pallas_call | solution.py:138
  20.6 14.9 %all_to_all.15 = bf16[4,2,24,1024]{3,2,1,0:T(8,128)(2,1)S(1)} all-to-all(bf16[4,2,24,1024]{3,2,1,0:T(8,128)(2,1)S(1)} %predict.1), channel_id=1, replica_groups=mesh['freq'=4,'rtile'=4,'rep'=2] {'rtile'}, dimensions={0} | all-to-all | bytes 786432 | tf_op jit(solution)/shard_map/all_to_all | solution.py:265
  35.6 0.1 convert_reduce_fusion
  35.6 0.0 copy-done.4
  35.6 0.7 %fusion = (bf16[2,24,1024]{2,1,0:T(8,128)(2,1)S(1)}, f32[2,24,1024]{2,1,0:T(8,128)}) fusion(f32[2,24,1024]{2,1,0:T(8,128)S(1)} %convert_reduce_fusion, f32[2,24,1024]{2,1,0:T(8,128)S(1)} %copy-done.4), kind=kLoop, calls=%fused_computation.1 | loop fusion | flops 98304 | bytes 688128 | tf_op jit(solution)/shard_map/convert_element_type | solution.py:267
  36.3 15.0 %all-gather = bf16[8,24,1024]{2,1,0:T(8,128)(2,1)S(1)} all-gather(bf16[2,24,1024]{2,1,0:T(8,128)(2,1)S(1)} %get-tuple-element.2), channel_id=2, replica_groups=mesh['freq'=4,'rtile'=4,'rep'=2] {'rtile'}, dimensions={0}, use_global_device_ids=true | all-gather | bytes 491520 | tf_op jit(solution)/shard_map/all_gather | solution.py:267
  51.3 2.2 %back_project.1 = bf16[8,3,2,16,128]{4,3,2,1,0:T(8,128)(2,1)S(1)} custom-call(s32[3,4,2]{2,1,0:T(4,128)S(1)} %copy.10.ranks_ref, bf16[4,2,24,1024]{3,2,1,0:T(8,128)(2,1)S(1)} %bitcast.4, bf16[2,3,4,2,48,256]{5,4,3,2,1,0:T(8,128)(2,1)S(1)} %copy-done, bf16[2,3,4,2,48,256]{5,4,3,2,1,0:T(8,128)(2,1)S(1)} %copy-done.1), custom_call_target="tpu_custom_call" | custom-call | tf_op jit(solution)/shard_map/back_project/pallas_call | solution.py:199
  53.6 8.6 %all_to_all.16 = bf16[8,3,2,16,128]{4,3,2,1,0:T(8,128)(2,1)S(1)} all-to-all(bf16[8,3,2,16,128]{4,3,2,1,0:T(8,128)(2,1)S(1)} %back_project.1), channel_id=1, replica_groups=mesh['freq'=4,'rtile'=4,'rep'=2] {'freq','rep'}, dimensions={0} | all-to-all | bytes 393216 | tf_op jit(solution)/shard_map/all_to_all | solution.py:269
  62.2 0.0 copy-done.3
  62.2 3.4 %gradient.1 = bf16[4,16,32,1024]{3,2,1,0:T(8,128)(2,1)} custom-call(bf16[24,1024]{1,0:T(8,128)(2,1)S(1)} %copy-done.3, bf16[4,2,3,2,16,128]{5,4,3,2,1,0:T(8,128)(2,1)S(1)} %bitcast.5), custom_call_target="tpu_custom_call" | custom-call | tf_op jit(solution)/shard_map/gradient/pallas_call | solution.py:239
Async XLA Ops:
  0.6 0.8 %copy-start.2 = (bf16[24,1024]{1,0:T(8,128)(2,1)S(1)}, bf16[24,1024]{1,0:T(8,128)(2,1)}, u32[]{:S(2)}) copy-start(bf16[24,1024]{1,0:T(8,128)(2,1)} %constant.4.clone.table_ref) | copy-start | bytes 147460
  1.4 11.7 %copy-start.5 = (s32[3,4,2]{1,2,0:T(2,128)S(1)}, s32[3,4,2]{1,2,0:T(2,128)}, u32[]{:S(2)}) copy-start(s32[3,4,2]{1,2,0:T(2,128)} %param.9) | copy-start | bytes 292
  1.4 16.9 %copy-start = (bf16[2,3,4,2,48,256]{5,4,3,2,1,0:T(8,128)(2,1)S(1)}, bf16[2,3,4,2,48,256]{5,4,3,2,1,0:T(8,128)(2,1)}, u32[]{:S(2)}) copy-start(bf16[2,3,4,2,48,256]{5,4,3,2,1,0:T(8,128)(2,1)} %right_ref.3) | copy-start | bytes 3538948
  1.4 16.9 %copy-start.1 = (bf16[2,3,4,2,48,256]{5,4,3,2,1,0:T(8,128)(2,1)S(1)}, bf16[2,3,4,2,48,256]{5,4,3,2,1,0:T(8,128)(2,1)}, u32[]{:S(2)}) copy-start(bf16[2,3,4,2,48,256]{5,4,3,2,1,0:T(8,128)(2,1)} %left_ref.3) | copy-start | bytes 3538948
  7.9 27.8 %copy-start.4 = (f32[2,24,1024]{2,1,0:T(8,128)S(1)}, f32[2,24,1024]{2,1,0:T(8,128)}, u32[]{:S(2)}) copy-start(f32[2,24,1024]{2,1,0:T(8,128)} %param.10) | copy-start | bytes 589828
  7.9 10.5 %all-to-all-start = ((bf16[4,3,2,32,128]{4,3,2,1,0:T(8,128)(2,1)}), bf16[4,3,2,32,128]{4,3,2,1,0:T(8,128)(2,1)S(1)}, u32[]{:S(2)}, u32[]{:S(2)}) async-start(bf16[4,3,2,32,128]{4,3,2,1,0:T(8,128)(2,1)} %spectrum.1), calls=%async_computation | async-start | bytes 393216 | tf_op jit(solution)/shard_map/all_to_all | solution.py:263
  13.3 48.9 %copy-start.3 = (bf16[24,1024]{1,0:T(8,128)(2,1)S(1)}, bf16[24,1024]{1,0:T(8,128)(2,1)}, u32[]{:S(2)}) copy-start(bf16[24,1024]{1,0:T(8,128)(2,1)} %constant.4.clone.table_ref) | copy-start | bytes 147460

commit v2 on v1

--- a/solution.py
+++ b/solution.py
@@ -36,10 +36,29 @@
     return jnp.concatenate([-pair[:, half:], pair[:, :half]], axis=1)
 
 
-def spectrum_kernel(table_ref, model_ref, out_ref, rows_ref):
+def target(me, step, count):
+    return me ^ step if count & (count - 1) == 0 else lax.rem(me + step, count)
+
+
+def origin(me, step, count):
+    return me ^ step if count & (count - 1) == 0 else lax.rem(me + count - step, count)
+
+
+def exchange(blocks, axis):
+    count = len(blocks)
+    arrived = [blocks[0]]
+    for step in range(1, count):
+        pairs = [(me, me ^ step if count & (count - 1) == 0 else (me + step) % count) for me in range(count)]
+        arrived.append(lax.ppermute(blocks[step], axis, pairs))
+    return arrived
+
+
+def spectrum_kernel(table_ref, model_ref, *refs):
+    out_refs, rows_ref = refs[:-1], refs[-1]
     step = pl.program_id(0)
     high, part, rhs, length = model_ref.shape
-    dests, freqs, _, low, lanes = out_ref.shape
+    dests = len(out_refs)
+    freqs, _, low, lanes = out_refs[0].shape
     table = table_ref[...]
     bins = table.shape[0]
     for start in range(0, part, 2):
@@ -54,12 +73,14 @@
 
     @pl.when(step == pl.num_programs(0) - 1)
     def _():
-        for dest in range(dests):
+        me = lax.axis_index("freq")
+        for at, out_ref in enumerate(out_refs):
+            dest = target(me, at, dests)
             for f in range(freqs):
                 for c in range(2):
                     q = c * dests * freqs + dest * freqs + f
                     picked = rows_ref[pl.ds(q, low, stride=bins), :]
-                    out_ref[dest, f, c] = picked.astype(out_ref.dtype)
+                    out_ref[f, c] = picked.astype(out_ref.dtype)
 
 
 def spectrum_of(model, table, dests, freqs):
@@ -75,8 +96,8 @@
             pl.BlockSpec((bins, length), lambda s: (0, 0)),
             pl.BlockSpec((high, low // steps, rhs, length), lambda s: (0, s, 0, 0)),
         ],
-        out_specs=pl.BlockSpec((dests, freqs, 2, low, LANES), lambda s: (0, 0, 0, 0, 0)),
-        out_shape=jax.ShapeDtypeStruct((dests, freqs, 2, low, LANES), jnp.bfloat16),
+        out_specs=[pl.BlockSpec((freqs, 2, low, LANES), lambda s: (0, 0, 0, 0))] * dests,
+        out_shape=[jax.ShapeDtypeStruct((freqs, 2, low, LANES), jnp.bfloat16)] * dests,
         scratch_shapes=[pltpu.VMEM((low * bins, LANES), jnp.float32)],
         compiler_params=pltpu.CompilerParams(vmem_limit_bytes=VMEM_LIMIT),
         name="spectrum",
@@ -92,10 +113,25 @@
     return [part.astype(jnp.bfloat16) for part in kept]
 
 
-def predict_kernel(ranks_ref, spec_ref, right_ref, left_ref, out_ref, sum_ref):
-    groups, freqs, _, low, lanes = spec_ref.shape
+def spans(first, count, size):
+    found = []
+    at = first
+    while at < first + count:
+        length = min(size - at % size, first + count - at)
+        found.append((at // size, at % size, length))
+        at += length
+    return found
+
+
+def predict_kernel(groups, parts, ranks_ref, right_ref, left_ref, *refs):
+    arrived_refs, out_refs = refs[:groups], refs[groups : groups + parts]
+    spec_ref, sum_ref = refs[groups + parts :]
+    _, freqs, _, low, lanes = spec_ref.shape
     _, _, row_tiles, col_tiles, size, tile = left_ref.shape
-    parts, _, pairs, _ = out_ref.shape
+    _, pairs, _ = out_refs[0].shape
+    me = lax.axis_index("freq")
+    for at, arrived_ref in enumerate(arrived_refs):
+        spec_ref[origin(me, at, groups)] = arrived_ref[...]
     rhs = parts * pairs // freqs
     high = lanes // rhs
     per_tile = groups // col_tiles
@@ -121,49 +157,62 @@
             left = left_ref[:, f, i].reshape(2 * col_tiles * size, tile)
             predicted = dot(factors, left, 0, 0)
             for c in range(2):
-                sum_ref[c, f * rhs : (f + 1) * rhs, i * tile : (i + 1) * tile] = predicted[
-                    c * rhs : (c + 1) * rhs
-                ]
-    for part in range(parts):
-        for c in range(2):
-            out_ref[part, c] = sum_ref[c, part * pairs : (part + 1) * pairs].astype(out_ref.dtype)
+                row = c * rhs
+                for part, start, length in spans(f * rhs, rhs, pairs):
+                    sum_ref[part, c, start : start + length, i * tile : (i + 1) * tile] = predicted[
+                        row : row + length
+                    ]
+                    row += length
+    me = lax.axis_index("rtile")
+    for at, out_ref in enumerate(out_refs):
+        out_ref[...] = sum_ref[target(me, at, parts)].astype(out_ref.dtype)
 
 
 def predict(ranks, spectrum, green_right, green_left, parts):
     freqs, row_tiles = ranks.shape[:2]
     tile = green_left.shape[5]
-    rhs = LANES * spectrum.shape[0] * spectrum.shape[3] // (green_left.shape[3] * tile)
+    groups = len(spectrum)
+    low = spectrum[0].shape[2]
+    rhs = LANES * groups * low // (green_left.shape[3] * tile)
     pairs = freqs * rhs
     sources = row_tiles * tile
     return pl.pallas_call(
-        predict_kernel,
+        functools.partial(predict_kernel, groups, parts),
         in_specs=[pl.BlockSpec(memory_space=pltpu.SMEM)]
-        + [pl.BlockSpec(memory_space=pltpu.VMEM)] * 3,
-        out_specs=pl.BlockSpec(memory_space=pltpu.VMEM),
-        out_shape=jax.ShapeDtypeStruct((parts, 2, pairs // parts, sources), jnp.bfloat16),
-        scratch_shapes=[pltpu.VMEM((2, pairs, sources), jnp.float32)],
+        + [pl.BlockSpec(memory_space=pltpu.VMEM)] * (2 + groups),
+        out_specs=[pl.BlockSpec(memory_space=pltpu.VMEM)] * parts,
+        out_shape=[jax.ShapeDtypeStruct((2, pairs // parts, sources), jnp.bfloat16)] * parts,
+        scratch_shapes=[
+            pltpu.VMEM((groups,) + spectrum[0].shape, jnp.bfloat16),
+            pltpu.VMEM((parts, 2, pairs // parts, sources), jnp.float32),
+        ],
         compiler_params=pltpu.CompilerParams(vmem_limit_bytes=VMEM_LIMIT),
         name="predict",
-    )(ranks, spectrum, green_right, green_left)
-
-
-def back_kernel(ranks_ref, misfit_ref, right_ref, left_ref, out_ref, misfit_all_ref):
-    parts, _, pairs, _ = misfit_ref.shape
+    )(ranks, green_right, green_left, *spectrum)
+
+
+def back_kernel(parts, dests, ranks_ref, right_ref, left_ref, *refs):
+    misfit_refs, out_refs = refs[:parts], refs[parts : parts + dests]
+    misfit_all_ref, grad_ref = refs[parts + dests :]
+    _, pairs, _ = misfit_refs[0].shape
     _, freqs, row_tiles, col_tiles, size, tile = left_ref.shape
-    dests, _, _, low, lanes = out_ref.shape
+    _, _, low, lanes = out_refs[0].shape
     rhs = parts * pairs // freqs
     high = lanes // rhs
     per_tile = dests // col_tiles
-    for part in range(parts):
-        for c in range(2):
-            misfit_all_ref[c, part * pairs : (part + 1) * pairs] = misfit_ref[part, c].astype(
-                jnp.float32
-            )
+    me = lax.axis_index("rtile")
+    for at, misfit_ref in enumerate(misfit_refs):
+        misfit_all_ref[origin(me, at, parts)] = misfit_ref[...].astype(jnp.float32)
     for f in range(freqs):
         back = []
         for i in range(row_tiles):
             rows = [
-                misfit_all_ref[c, f * rhs : (f + 1) * rhs, i * tile : (i + 1) * tile]
+                jnp.concatenate(
+                    [
+                        misfit_all_ref[part, c, start : start + length, i * tile : (i + 1) * tile]
+                        for part, start, length in spans(f * rhs, rhs, pairs)
+                    ]
+                )
                 for c in range(2)
             ]
             first = jnp.concatenate(rows).astype(jnp.bfloat16)
@@ -186,42 +235,53 @@
                         grad[rows + h * low : rows + (h + 1) * low, c * rhs : (c + 1) * rhs]
                         for h in range(high)
                     ]
-                    out_ref[j * per_tile + at, f, c] = jnp.concatenate(blocks, axis=1).astype(
-                        out_ref.dtype
+                    grad_ref[j * per_tile + at, f, c] = jnp.concatenate(blocks, axis=1).astype(
+                        grad_ref.dtype
                     )
+    me = lax.axis_index(("freq", "rep"))
+    for at, out_ref in enumerate(out_refs):
+        out_ref[...] = grad_ref[target(me, at, dests)]
 
 
 def back_project(ranks, misfit, green_right, green_left, dests):
     freqs = ranks.shape[0]
-    parts, _, pairs, _ = misfit.shape
+    parts = len(misfit)
+    _, pairs, sources = misfit[0].shape
     rhs = parts * pairs // freqs
     low = green_left.shape[3] * green_left.shape[5] * rhs // (dests * LANES)
     return pl.pallas_call(
-        back_kernel,
+        functools.partial(back_kernel, parts, dests),
         in_specs=[pl.BlockSpec(memory_space=pltpu.SMEM)]
-        + [pl.BlockSpec(memory_space=pltpu.VMEM)] * 3,
-        out_specs=pl.BlockSpec(memory_space=pltpu.VMEM),
-        out_shape=jax.ShapeDtypeStruct((dests, freqs, 2, low, LANES), jnp.bfloat16),
-        scratch_shapes=[pltpu.VMEM((2, parts * pairs, misfit.shape[3]), jnp.float32)],
+        + [pl.BlockSpec(memory_space=pltpu.VMEM)] * (2 + parts),
+        out_specs=[pl.BlockSpec(memory_space=pltpu.VMEM)] * dests,
+        out_shape=[jax.ShapeDtypeStruct((freqs, 2, low, LANES), jnp.bfloat16)] * dests,
+        scratch_shapes=[
+            pltpu.VMEM((parts, 2, pairs, sources), jnp.float32),
+            pltpu.VMEM((dests, freqs, 2, low, LANES), jnp.bfloat16),
+        ],
         compiler_params=pltpu.CompilerParams(vmem_limit_bytes=VMEM_LIMIT),
         name="back_project",
-    )(ranks, misfit, green_right, green_left)
-
-
-def gradient_kernel(table_ref, parts_ref, out_ref, rows_ref):
+    )(ranks, green_right, green_left, *misfit)
+
+
+def gradient_kernel(reps, table_ref, *refs):
+    part_refs, out_ref, rows_ref = refs[:-2], refs[-2], refs[-1]
     step = pl.program_id(0)
-    groups, reps, freqs, _, low, lanes = parts_ref.shape
+    groups = len(part_refs) // reps
+    freqs, _, low, lanes = part_refs[0].shape
     high, part, rhs, length = out_ref.shape
     bins = table_ref.shape[0]
 
     @pl.when(step == 0)
     def _():
-        for g in range(groups):
+        me = lax.axis_index("freq")
+        for at in range(groups):
+            g = origin(me, at, groups)
             for f in range(freqs):
                 for c in range(2):
-                    total = parts_ref[g, 0, f, c].astype(jnp.float32)
+                    total = part_refs[at * reps][f, c].astype(jnp.float32)
                     for rep in range(1, reps):
-                        total = total + parts_ref[g, rep, f, c].astype(jnp.float32)
+                        total = total + part_refs[at * reps + rep][f, c].astype(jnp.float32)
                     rows_ref[pl.ds(c * groups * freqs + g * freqs + f, low, stride=bins), :] = total
 
     table = table_ref[...]
@@ -231,24 +291,24 @@
         out_ref[:, at] = traces.reshape(high, rhs, length)
 
 
-def gradient_of(parts, table, rhs):
-    groups, reps, freqs, _, low, lanes = parts.shape
+def gradient_of(parts, table, rhs, reps):
+    freqs, _, low, lanes = parts[0].shape
     bins, length = table.shape
     high = lanes // rhs
     steps = 4 if low % 4 == 0 else 1
     out = pl.pallas_call(
-        gradient_kernel,
+        functools.partial(gradient_kernel, reps),
         grid=(steps,),
         in_specs=[
             pl.BlockSpec((bins, length), lambda s: (0, 0)),
-            pl.BlockSpec(parts.shape, lambda s: (0,) * 6),
-        ],
+        ]
+        + [pl.BlockSpec(parts[0].shape, lambda s: (0, 0, 0, 0))] * len(parts),
         out_specs=pl.BlockSpec((high, low // steps, rhs, length), lambda s: (0, s, 0, 0)),
         out_shape=jax.ShapeDtypeStruct((high, low, rhs, length), jnp.bfloat16),
         scratch_shapes=[pltpu.VMEM((low * bins, lanes), jnp.float32)],
         compiler_params=pltpu.CompilerParams(vmem_limit_bytes=VMEM_LIMIT),
         name="gradient",
-    )(table, parts)
+    )(table, *parts)
     return out.reshape(1, high * low, rhs, length)
 
 
@@ -260,15 +320,14 @@
     rhs_count = model.shape[2]
     table = tables(freq_local * freq_count, model.shape[3])
     spectrum = spectrum_of(model[0], table, freq_count, freq_local)
-    spectrum = lax.all_to_all(spectrum, "freq", split_axis=0, concat_axis=0, tiled=True)
+    spectrum = exchange(spectrum, "freq")
     predicted = predict(ranks, spectrum, green_right, green_left, tile_count)
-    arrived = lax.all_to_all(predicted, "rtile", split_axis=0, concat_axis=0, tiled=True)
-    residual = jnp.sum(arrived.astype(jnp.float32), axis=0) - data
-    misfit = lax.all_gather(residual.astype(jnp.bfloat16), "rtile", axis=0)
+    arrived = exchange(predicted, "rtile")
+    residual = sum(block.astype(jnp.float32) for block in arrived) - data
+    misfit = exchange([residual.astype(jnp.bfloat16)] * tile_count, "rtile")
     partial = back_project(ranks, misfit, green_right, green_left, freq_count * rep_count)
-    arrived = lax.all_to_all(partial, ("freq", "rep"), split_axis=0, concat_axis=0, tiled=True)
-    arrived = arrived.reshape((freq_count, rep_count) + arrived.shape[1:])
-    return (residual, gradient_of(arrived, table, rhs_count))
+    arrived = exchange(partial, ("freq", "rep"))
+    return (residual, gradient_of(arrived, table, rhs_count, rep_count))
 
 
 def solution(mesh):

time: 65.9 us -> 54.5 us (0.83)
  blocking collectives: 38.6 us -> 0 us
  starting transfers between devices: 5.29 us -> 19.7 us
  waiting for transfers between devices: 5.09 us -> 18.5 us
    all_to_all x2 -> x0, blocking collectives: 23.6 us -> none  [the longest x1 14.9 us: shards(): lax.all_to_all(predicted, 'rtile', split_axis=0, concat_axis=0, tiled=True)]
    ppermute x0 -> x16, starting transfers between devices: none -> 19.7 us  [exchange(): arrived.append(lax.ppermute(blocks[step], axis, pairs))]
    ppermute x0 -> x16, waiting for transfers between devices: none -> 18.5 us  [exchange(): arrived.append(lax.ppermute(blocks[step], axis, pairs))]
    all_gather x1 -> x0, blocking collectives: 15 us -> none  [shards(): misfit = lax.all_gather(residual.astype(jnp.bfloat16), 'rtile', axis=0)]
    all_to_all x1 -> x0, starting transfers between devices: 5.29 us -> none  [shards(): lax.all_to_all(spectrum, 'freq', split_axis=0, concat_axis=0, tiled=True)]
    all_to_all x1 -> x0, waiting for transfers between devices: 5.09 us -> none  [shards(): lax.all_to_all(spectrum, 'freq', split_axis=0, concat_axis=0, tiled=True)]
  transfers between devices with their start and end apart: 1 -> 16, of which waited for: 1 -> 10; matrix products, arithmetic and copies ran while one was open for 0% -> 0% of each run, Pallas kernels for 0% -> 0%
where the time goes in v2:
time: 54.5 us; the launch traced here: 54.3 us
  starting transfers between devices  19.7 us (36%)
  waiting for transfers between devices  18.5 us (34%)
  Pallas kernels  13.8 us (25%)
  local copies, waits for them, and re-layouts  0.92 us (2%)
  other arithmetic  0.74 us (1%)
  between operations  0.71 us (1%)
    ppermute x16, starting transfers between devices, exchange(): arrived.append(lax.ppermute(blocks[step], axis, pairs))  19.7 us
    ppermute x16, waiting for transfers between devices, exchange(): arrived.append(lax.ppermute(blocks[step], axis, pairs))  18.5 us
    pallas_call x1, Pallas kernels, spectrum_of(): pl.pallas_call(spectrum_kernel, grid=(steps,), in_specs=[pl.BlockSpec((bi...  5.76 us
    pallas_call x1, Pallas kernels, gradient_of(): pl.pallas_call(functools.partial(gradient_kernel, reps), grid=(steps,), i...  3.37 us
    pallas_call x1, Pallas kernels, predict(): pl.pallas_call(functools.partial(predict_kernel, groups, parts), in_specs...  2.37 us
    pallas_call x1, Pallas kernels, back_project(): pl.pallas_call(functools.partial(back_kernel, parts, dests), in_specs=[pl...  2.28 us
  transfers between devices with their start and end apart: 16, of which 10 were waited for; matrix products, arithmetic and copies ran while one was open for 0% of the time, Pallas kernels for 0%

profile of v2, /device:TPU:0, one launch (start us, length us, event | category | flops | bytes accessed | tf_op | source)
XLA Modules:
  0.0 54.3 jit_solution(8073572676913296194)
XLA Ops:
  0.6 0.0 copy-start.2
  0.6 0.8 %copy-done.2 = bf16[24,1024]{1,0:T(8,128)(2,1)S(1)} copy-done((bf16[24,1024]{1,0:T(8,128)(2,1)S(1)}, bf16[24,1024]{1,0:T(8,128)(2,1)}, u32[]{:S(2)}) %copy-start.2) | copy-done | bytes 49176
  1.4 0.0 copy-start.5
  1.4 0.0 copy-start
  1.4 0.0 copy-start.1
  1.4 0.0 copy-start.4
  1.4 5.8 %spectrum.1 = (bf16[3,2,32,128]{3,2,1,0:T(8,128)(2,1)S(1)}, bf16[3,2,32,128]{3,2,1,0:T(8,128)(2,1)S(1)}, bf16[3,2,32,128]{3,2,1,0:T(8,128)(2,1)S(1)}, bf16[3,2,32,128]{3,2,1,0:T(8,128)(2,1)S(1)}) custom-call(bf16[24,1024]{1,0:T(8,128)(2,1)S(1)} %copy-done.2, bf16[4,32,32,1024]{3,2,1,0:T(8,128)(2,1)} %bitcast.2), custom_call_target="tpu_custom_call" | custom-call | tf_op jit(solution)/shard_map/spectrum/pallas_call | solution.py:92
  7.2 0.0 copy-start.3
  7.2 3.0 %collective-permute-start = (bf16[3,2,32,128]{3,2,1,0:T(8,128)(2,1)S(1)}, bf16[3,2,32,128]{3,2,1,0:T(8,128)(2,1)S(1)}, u32[]{:S(2)}, u32[]{:S(2)}) collective-permute-start(bf16[3,2,32,128]{3,2,1,0:T(8,128)(2,1)S(1)} %get-tuple-element.19), channel_id=1, source_target_pairs={{0,8},{8,0},{16,24},{24,16},{1,9},{9,1},{17,25},{25,17},{2,10},{10... | collective-permute-start | bytes 147464 | tf_op jit(solution)/shard_map/ppermute | solution.py:52
  10.2 1.5 %collective-permute-start.1 = (bf16[3,2,32,128]{3,2,1,0:T(8,128)(2,1)S(1)}, bf16[3,2,32,128]{3,2,1,0:T(8,128)(2,1)S(1)}, u32[]{:S(2)}, u32[]{:S(2)}) collective-permute-start(bf16[3,2,32,128]{3,2,1,0:T(8,128)(2,1)S(1)} %get-tuple-element.20), channel_id=1, source_target_pairs={{0,16},{8,24},{16,0},{24,8},{1,17},{9,25},{17,1},{25,9},{2,18},{10... | collective-permute-start | bytes 147464 | tf_op jit(solution)/shard_map/ppermute | solution.py:52
  11.8 0.0 collective-permute-start.2
  11.8 0.0 copy-done.5
  11.8 0.1 copy.8.ranks_ref
  11.9 0.4 collective-permute-done.refs_1_
  12.3 2.0 %collective-permute-done.1.refs_2_ = bf16[3,2,32,128]{3,2,1,0:T(8,128)(2,1)S(1)} collective-permute-done((bf16[3,2,32,128]{3,2,1,0:T(8,128)(2,1)S(1)}, bf16[3,2,32,128]{3,2,1,0:T(8,128)(2,1)S(1)}, u32[]{:S(2)}, u32[]{:S(2)}) %collective-permute-start.1) | collective-permute-done | bytes 49184 | tf_op jit(solution)/shard_map/ppermute | solution.py:52
  14.3 2.4 %collective-permute-done.2.refs_3_ = bf16[3,2,32,128]{3,2,1,0:T(8,128)(2,1)S(1)} collective-permute-done((bf16[3,2,32,128]{3,2,1,0:T(8,128)(2,1)S(1)}, bf16[3,2,32,128]{3,2,1,0:T(8,128)(2,1)S(1)}, u32[]{:S(2)}, u32[]{:S(2)}) %collective-permute-start.2) | collective-permute-done | bytes 49184 | tf_op jit(solution)/shard_map/ppermute | solution.py:52
  16.7 0.0 copy-done
  16.7 0.0 copy-done.1
  16.7 2.4 %predict.1 = (bf16[2,24,1024]{2,1,0:T(8,128)(2,1)S(1)}, bf16[2,24,1024]{2,1,0:T(8,128)(2,1)S(1)}, bf16[2,24,1024]{2,1,0:T(8,128)(2,1)S(1)}, bf16[2,24,1024]{2,1,0:T(8,128)(2,1)S(1)}) custom-call(s32[3,4,2]{2,1,0:T(4,128)S(1)} %copy.8.ranks_ref, bf16[2,3,4,2,48,256]{5,4,3,2,1,0:T(8,128)(2,1)S(1)} %copy-done, bf16[2,3,4,2,48,256]{5,4,3,2,1,0:T(8,128)(2,1)S(1)} %copy-done.1, ...), custom_call_target="tpu_custom_call" | custom-call | tf_op jit(solution)/shard_map/predict/pallas_call | solution.py:179
  19.1 1.6 %collective-permute-start.3 = (bf16[2,24,1024]{2,1,0:T(8,128)(2,1)S(1)}, bf16[2,24,1024]{2,1,0:T(8,128)(2,1)S(1)}, u32[]{:S(2)}, u32[]{:S(2)}) collective-permute-start(bf16[2,24,1024]{2,1,0:T(8,128)(2,1)S(1)} %get-tuple-element.23), channel_id=1, source_target_pairs={{0,2},{2,0},{4,6},{6,4},{1,3},{3,1},{5,7},{7,5},{8,10},{10,8},{12,... | collective-permute-start | bytes 294920 | tf_op jit(solution)/shard_map/ppermute | solution.py:52
  20.8 2.6 %collective-permute-start.4 = (bf16[2,24,1024]{2,1,0:T(8,128)(2,1)S(1)}, bf16[2,24,1024]{2,1,0:T(8,128)(2,1)S(1)}, u32[]{:S(2)}, u32[]{:S(2)}) collective-permute-start(bf16[2,24,1024]{2,1,0:T(8,128)(2,1)S(1)} %get-tuple-element.24), channel_id=1, source_target_pairs={{0,4},{2,6},{4,0},{6,2},{1,5},{3,7},{5,1},{7,3},{8,12},{10,14},{12... | collective-permute-start | bytes 294920 | tf_op jit(solution)/shard_map/ppermute | solution.py:52
  23.4 0.2 collective-permute-start.5
  23.6 0.6 %collective-permute-done.3 = bf16[2,24,1024]{2,1,0:T(8,128)(2,1)S(1)} collective-permute-done((bf16[2,24,1024]{2,1,0:T(8,128)(2,1)S(1)}, bf16[2,24,1024]{2,1,0:T(8,128)(2,1)S(1)}, u32[]{:S(2)}, u32[]{:S(2)}) %collective-permute-start.3) | collective-permute-done | bytes 98336 | tf_op jit(solution)/shard_map/ppermute | solution.py:52
  24.1 4.3 %collective-permute-done.4 = bf16[2,24,1024]{2,1,0:T(8,128)(2,1)S(1)} collective-permute-done((bf16[2,24,1024]{2,1,0:T(8,128)(2,1)S(1)}, bf16[2,24,1024]{2,1,0:T(8,128)(2,1)S(1)}, u32[]{:S(2)}, u32[]{:S(2)}) %collective-permute-start.4) | collective-permute-done | bytes 98336 | tf_op jit(solution)/shard_map/ppermute | solution.py:52
  28.4 1.5 %collective-permute-done.5 = bf16[2,24,1024]{2,1,0:T(8,128)(2,1)S(1)} collective-permute-done((bf16[2,24,1024]{2,1,0:T(8,128)(2,1)S(1)}, bf16[2,24,1024]{2,1,0:T(8,128)(2,1)S(1)}, u32[]{:S(2)}, u32[]{:S(2)}) %collective-permute-start.5) | collective-permute-done | bytes 98336 | tf_op jit(solution)/shard_map/ppermute | solution.py:52
  29.9 0.0 copy-done.4
  29.9 0.7 %fusion = (bf16[2,24,1024]{2,1,0:T(8,128)(2,1)S(1)}, f32[2,24,1024]{2,1,0:T(8,128)}) fusion(f32[2,24,1024]{2,1,0:T(8,128)S(1)} %copy-done.4, bf16[2,24,1024]{2,1,0:T(8,128)(2,1)S(1)} %collective-permute-done.5, bf16[2,24,1024]{2,1,0:T(8,128)(2,1)S(1)} %collective-permute-done.4, bf16[2,24,1024]{2,1,0:T(8,128)(2,1)S(1)} %collective-permute-done.3, ...), kind=kLoop, calls=%fused_computation.1 | loop fusion | flops 442368 | bytes 884736 | tf_op jit(solution)/shard_map/convert_element_type | solution.py:327
  30.6 2.1 %collective-permute-start.8 = (bf16[2,24,1024]{2,1,0:T(8,128)(2,1)S(1)}, bf16[2,24,1024]{2,1,0:T(8,128)(2,1)S(1)}, u32[]{:S(2)}, u32[]{:S(2)}) collective-permute-start(bf16[2,24,1024]{2,1,0:T(8,128)(2,1)S(1)} %get-tuple-element.34.refs_0_), channel_id=1, source_target_pairs={{0,6},{2,4},{4,2},{6,0},{1,7},{3,5},{5,3},{7,1},{8,14},{10,12},{12... | collective-permute-start | bytes 294920 | tf_op jit(solution)/shard_map/ppermute | solution.py:52
  32.7 0.6 %collective-permute-start.7 = (bf16[2,24,1024]{2,1,0:T(8,128)(2,1)S(1)}, bf16[2,24,1024]{2,1,0:T(8,128)(2,1)S(1)}, u32[]{:S(2)}, u32[]{:S(2)}) collective-permute-start(bf16[2,24,1024]{2,1,0:T(8,128)(2,1)S(1)} %get-tuple-element.34.refs_0_), channel_id=1, source_target_pairs={{0,4},{2,6},{4,0},{6,2},{1,5},{3,7},{5,1},{7,3},{8,12},{10,14},{12... | collective-permute-start | bytes 294920 | tf_op jit(solution)/shard_map/ppermute | solution.py:52
  33.3 1.7 %collective-permute-start.6 = (bf16[2,24,1024]{2,1,0:T(8,128)(2,1)S(1)}, bf16[2,24,1024]{2,1,0:T(8,128)(2,1)S(1)}, u32[]{:S(2)}, u32[]{:S(2)}) collective-permute-start(bf16[2,24,1024]{2,1,0:T(8,128)(2,1)S(1)} %get-tuple-element.34.refs_0_), channel_id=1, source_target_pairs={{0,2},{2,0},{4,6},{6,4},{1,3},{3,1},{5,7},{7,5},{8,10},{10,8},{12,... | collective-permute-start | bytes 294920 | tf_op jit(solution)/shard_map/ppermute | solution.py:52
  35.0 2.3 %collective-permute-done.8.refs_3_ = bf16[2,24,1024]{2,1,0:T(8,128)(2,1)S(1)} collective-permute-done((bf16[2,24,1024]{2,1,0:T(8,128)(2,1)S(1)}, bf16[2,24,1024]{2,1,0:T(8,128)(2,1)S(1)}, u32[]{:S(2)}, u32[]{:S(2)}) %collective-permute-start.8) | collective-permute-done | bytes 98336 | tf_op jit(solution)/shard_map/ppermute | solution.py:52
  37.3 2.7 %collective-permute-done.7.refs_2_ = bf16[2,24,1024]{2,1,0:T(8,128)(2,1)S(1)} collective-permute-done((bf16[2,24,1024]{2,1,0:T(8,128)(2,1)S(1)}, bf16[2,24,1024]{2,1,0:T(8,128)(2,1)S(1)}, u32[]{:S(2)}, u32[]{:S(2)}) %collective-permute-start.7) | collective-permute-done | bytes 98336 | tf_op jit(solution)/shard_map/ppermute | solution.py:52
  40.0 0.0 collective-permute-done.6.refs_1_
  40.0 2.3 %back_project.1 = (bf16[3,2,16,128]{3,2,1,0:T(8,128)(2,1)S(1)}, bf16[3,2,16,128]{3,2,1,0:T(8,128)(2,1)S(1)}, bf16[3,2,16,128]{3,2,1,0:T(8,128)(2,1)S(1)}, bf16[3...) custom-call(s32[3,4,2]{2,1,0:T(4,128)S(1)} %copy.8.ranks_ref, ...), custom_call_target="tpu_custom_call" | custom-call | tf_op jit(solution)/shard_map/back_project/pallas_call | solution.py:252
  42.3 0.1 collective-permute-start.9
  42.4 0.9 %collective-permute-start.10 = (bf16[3,2,16,128]{3,2,1,0:T(8,128)(2,1)S(1)}, bf16[3,2,16,128]{3,2,1,0:T(8,128)(2,1)S(1)}, u32[]{:S(2)}, u32[]{:S(2)}) collective-permute-start(bf16[3,2,16,128]{3,2,1,0:T(8,128)(2,1)S(1)} %get-tuple-element.28), channel_id=1, source_target_pairs={{0,8},{1,9},{8,0},{9,1},{16,24},{17,25},{24,16},{25,17},{2,10},{3,... | collective-permute-start | bytes 73736 | tf_op jit(solution)/shard_map/ppermute | solution.py:52
  43.3 1.0 %collective-permute-start.11 = (bf16[3,2,16,128]{3,2,1,0:T(8,128)(2,1)S(1)}, bf16[3,2,16,128]{3,2,1,0:T(8,128)(2,1)S(1)}, u32[]{:S(2)}, u32[]{:S(2)}) collective-permute-start(bf16[3,2,16,128]{3,2,1,0:T(8,128)(2,1)S(1)} %get-tuple-element.29), channel_id=1, source_target_pairs={{0,9},{1,8},{8,1},{9,0},{16,25},{17,24},{24,17},{25,16},{2,11},{3,... | collective-permute-start | bytes 73736 | tf_op jit(solution)/shard_map/ppermute | solution.py:52
  44.2 0.5 %collective-permute-start.12 = (bf16[3,2,16,128]{3,2,1,0:T(8,128)(2,1)S(1)}, bf16[3,2,16,128]{3,2,1,0:T(8,128)(2,1)S(1)}, u32[]{:S(2)}, u32[]{:S(2)}) collective-permute-start(bf16[3,2,16,128]{3,2,1,0:T(8,128)(2,1)S(1)} %get-tuple-element.30), channel_id=1, source_target_pairs={{0,16},{1,17},{8,24},{9,25},{16,0},{17,1},{24,8},{25,9},{2,18},{3,... | collective-permute-start | bytes 73736 | tf_op jit(solution)/shard_map/ppermute | solution.py:52
  44.8 1.1 %collective-permute-start.13 = (bf16[3,2,16,128]{3,2,1,0:T(8,128)(2,1)S(1)}, bf16[3,2,16,128]{3,2,1,0:T(8,128)(2,1)S(1)}, u32[]{:S(2)}, u32[]{:S(2)}) collective-permute-start(bf16[3,2,16,128]{3,2,1,0:T(8,128)(2,1)S(1)} %get-tuple-element.31), channel_id=1, source_target_pairs={{0,17},{1,16},{8,25},{9,24},{16,1},{17,0},{24,9},{25,8},{2,19},{3,... | collective-permute-start | bytes 73736 | tf_op jit(solution)/shard_map/ppermute | solution.py:52
  45.9 0.0 collective-permute-done.9.refs_1_
  45.9 0.8 %collective-permute-start.14 = (bf16[3,2,16,128]{3,2,1,0:T(8,128)(2,1)S(1)}, bf16[3,2,16,128]{3,2,1,0:T(8,128)(2,1)S(1)}, u32[]{:S(2)}, u32[]{:S(2)}) collective-permute-start(bf16[3,2,16,128]{3,2,1,0:T(8,128)(2,1)S(1)} %get-tuple-element.32), channel_id=1, source_target_pairs={{0,24},{1,25},{8,16},{9,17},{16,8},{17,9},{24,0},{25,1},{2,26},{3,... | collective-permute-start | bytes 73736 | tf_op jit(solution)/shard_map/ppermute | solution.py:52
  46.8 0.0 collective-permute-done.10.refs_2_
  46.8 1.8 %collective-permute-start.15 = (bf16[3,2,16,128]{3,2,1,0:T(8,128)(2,1)S(1)}, bf16[3,2,16,128]{3,2,1,0:T(8,128)(2,1)S(1)}, u32[]{:S(2)}, u32[]{:S(2)}) collective-permute-start(bf16[3,2,16,128]{3,2,1,0:T(8,128)(2,1)S(1)} %get-tuple-element.33), channel_id=1, source_target_pairs={{0,25},{1,24},{8,17},{9,16},{16,9},{17,8},{24,1},{25,0},{2,27},{3,... | collective-permute-start | bytes 73736 | tf_op jit(solution)/shard_map/ppermute | solution.py:52
  48.6 0.0 collective-permute-done.11.refs_3_
  48.7 0.0 collective-permute-done.12.refs_4_
  48.7 0.0 collective-permute-done.13.refs_5_
  48.7 2.0 %collective-permute-done.14.refs_6_ = bf16[3,2,16,128]{3,2,1,0:T(8,128)(2,1)S(1)} collective-permute-done((bf16[3,2,16,128]{3,2,1,0:T(8,128)(2,1)S(1)}, bf16[3,2,16,128]{3,2,1,0:T(8,128)(2,1)S(1)}, u32[]{:S(2)}, u32[]{:S(2)}) %collective-permute-start.14) | collective-permute-done | bytes 24608 | tf_op jit(solution)/shard_map/ppermute | solution.py:52
  50.7 0.3 collective-permute-done.15.refs_7_
  51.0 0.0 copy-done.3
  51.0 3.4 %gradient.1 = bf16[4,16,32,1024]{3,2,1,0:T(8,128)(2,1)} custom-call(bf16[24,1024]{1,0:T(8,128)(2,1)S(1)} %copy-done.3, bf16[3,2,16,128]{3,2,1,0:T(8,128)(2,1)S(1)} %get-tuple-element.26.refs_0_, bf16[3,2,16,128]{3,2,1,0:T(8,128)(2,1)S(1)} %collective-permute-done.9.refs_1_, bf16[3,2,16,128]{3,2,1,0:T(8,128)(2,1)S(1)} %collective-permute-done.10.refs_2_, ...), custom_call_target="tpu_custom_call" | custom-call | tf_op jit(solution)/shard_map/gradient/pallas_call | solution.py:299
Async XLA Ops:
  0.6 0.8 %copy-start.2 = (bf16[24,1024]{1,0:T(8,128)(2,1)S(1)}, bf16[24,1024]{1,0:T(8,128)(2,1)}, u32[]{:S(2)}) copy-start(bf16[24,1024]{1,0:T(8,128)(2,1)} %constant.2.clone.table_ref) | copy-start | bytes 147460
  1.4 10.3 %copy-start.5 = (s32[3,4,2]{1,2,0:T(2,128)S(1)}, s32[3,4,2]{1,2,0:T(2,128)}, u32[]{:S(2)}) copy-start(s32[3,4,2]{1,2,0:T(2,128)} %param.9) | copy-start | bytes 292
  1.4 15.3 %copy-start = (bf16[2,3,4,2,48,256]{5,4,3,2,1,0:T(8,128)(2,1)S(1)}, bf16[2,3,4,2,48,256]{5,4,3,2,1,0:T(8,128)(2,1)}, u32[]{:S(2)}) copy-start(bf16[2,3,4,2,48,256]{5,4,3,2,1,0:T(8,128)(2,1)} %right_ref.3) | copy-start | bytes 3538948
  1.4 15.3 %copy-start.1 = (bf16[2,3,4,2,48,256]{5,4,3,2,1,0:T(8,128)(2,1)S(1)}, bf16[2,3,4,2,48,256]{5,4,3,2,1,0:T(8,128)(2,1)}, u32[]{:S(2)}) copy-start(bf16[2,3,4,2,48,256]{5,4,3,2,1,0:T(8,128)(2,1)} %left_ref.3) | copy-start | bytes 3538948
  1.4 28.5 %copy-start.4 = (f32[2,24,1024]{2,1,0:T(8,128)S(1)}, f32[2,24,1024]{2,1,0:T(8,128)}, u32[]{:S(2)}) copy-start(f32[2,24,1024]{2,1,0:T(8,128)} %param.10) | copy-start | bytes 589828
  7.2 43.7 %copy-start.3 = (bf16[24,1024]{1,0:T(8,128)(2,1)S(1)}, bf16[24,1024]{1,0:T(8,128)(2,1)}, u32[]{:S(2)}) copy-start(bf16[24,1024]{1,0:T(8,128)(2,1)} %constant.2.clone.table_ref) | copy-start | bytes 147460
  7.2 5.1 %collective-permute-start = (bf16[3,2,32,128]{3,2,1,0:T(8,128)(2,1)S(1)}, bf16[3,2,32,128]{3,2,1,0:T(8,128)(2,1)S(1)}, u32[]{:S(2)}, u32[]{:S(2)}) collective-permute-start(bf16[3,2,32,128]{3,2,1,0:T(8,128)(2,1)S(1)} %get-tuple-element.19), channel_id=1, source_target_pairs={{0,8},{8,0},{16,24},{24,16},{1,9},{9,1},{17,25},{25,17},{2,10},{10... | collective-permute-start | bytes 147464 | tf_op jit(solution)/shard_map/ppermute | solution.py:52
  10.2 4.1 %collective-permute-start.1 = (bf16[3,2,32,128]{3,2,1,0:T(8,128)(2,1)S(1)}, bf16[3,2,32,128]{3,2,1,0:T(8,128)(2,1)S(1)}, u32[]{:S(2)}, u32[]{:S(2)}) collective-permute-start(bf16[3,2,32,128]{3,2,1,0:T(8,128)(2,1)S(1)} %get-tuple-element.20), channel_id=1, source_target_pairs={{0,16},{8,24},{16,0},{24,8},{1,17},{9,25},{17,1},{25,9},{2,18},{10... | collective-permute-start | bytes 147464 | tf_op jit(solution)/shard_map/ppermute | solution.py:52
  11.8 5.0 %collective-permute-start.2 = (bf16[3,2,32,128]{3,2,1,0:T(8,128)(2,1)S(1)}, bf16[3,2,32,128]{3,2,1,0:T(8,128)(2,1)S(1)}, u32[]{:S(2)}, u32[]{:S(2)}) collective-permute-start(bf16[3,2,32,128]{3,2,1,0:T(8,128)(2,1)S(1)} %get-tuple-element.21), channel_id=1, source_target_pairs={{0,24},{8,16},{16,8},{24,0},{1,25},{9,17},{17,9},{25,1},{2,26},{10... | collective-permute-start | bytes 147464 | tf_op jit(solution)/shard_map/ppermute | solution.py:52
  19.1 5.0 %collective-permute-start.3 = (bf16[2,24,1024]{2,1,0:T(8,128)(2,1)S(1)}, bf16[2,24,1024]{2,1,0:T(8,128)(2,1)S(1)}, u32[]{:S(2)}, u32[]{:S(2)}) collective-permute-start(bf16[2,24,1024]{2,1,0:T(8,128)(2,1)S(1)} %get-tuple-element.23), channel_id=1, source_target_pairs={{0,2},{2,0},{4,6},{6,4},{1,3},{3,1},{5,7},{7,5},{8,10},{10,8},{12,... | collective-permute-start | bytes 294920 | tf_op jit(solution)/shard_map/ppermute | solution.py:52
  20.8 7.7 %collective-permute-start.4 = (bf16[2,24,1024]{2,1,0:T(8,128)(2,1)S(1)}, bf16[2,24,1024]{2,1,0:T(8,128)(2,1)S(1)}, u32[]{:S(2)}, u32[]{:S(2)}) collective-permute-start(bf16[2,24,1024]{2,1,0:T(8,128)(2,1)S(1)} %get-tuple-element.24), channel_id=1, source_target_pairs={{0,4},{2,6},{4,0},{6,2},{1,5},{3,7},{5,1},{7,3},{8,12},{10,14},{12... | collective-permute-start | bytes 294920 | tf_op jit(solution)/shard_map/ppermute | solution.py:52
  23.4 6.5 %collective-permute-start.5 = (bf16[2,24,1024]{2,1,0:T(8,128)(2,1)S(1)}, bf16[2,24,1024]{2,1,0:T(8,128)(2,1)S(1)}, u32[]{:S(2)}, u32[]{:S(2)}) collective-permute-start(bf16[2,24,1024]{2,1,0:T(8,128)(2,1)S(1)} %get-tuple-element.25), channel_id=1, source_target_pairs={{0,6},{2,4},{4,2},{6,0},{1,7},{3,5},{5,3},{7,1},{8,14},{10,12},{12... | collective-permute-start | bytes 294920 | tf_op jit(solution)/shard_map/ppermute | solution.py:52
  30.6 6.7 %collective-permute-start.8 = (bf16[2,24,1024]{2,1,0:T(8,128)(2,1)S(1)}, bf16[2,24,1024]{2,1,0:T(8,128)(2,1)S(1)}, u32[]{:S(2)}, u32[]{:S(2)}) collective-permute-start(bf16[2,24,1024]{2,1,0:T(8,128)(2,1)S(1)} %get-tuple-element.34.refs_0_), channel_id=1, source_target_pairs={{0,6},{2,4},{4,2},{6,0},{1,7},{3,5},{5,3},{7,1},{8,14},{10,12},{12... | collective-permute-start | bytes 294920 | tf_op jit(solution)/shard_map/ppermute | solution.py:52
  32.7 7.3 %collective-permute-start.7 = (bf16[2,24,1024]{2,1,0:T(8,128)(2,1)S(1)}, bf16[2,24,1024]{2,1,0:T(8,128)(2,1)S(1)}, u32[]{:S(2)}, u32[]{:S(2)}) collective-permute-start(bf16[2,24,1024]{2,1,0:T(8,128)(2,1)S(1)} %get-tuple-element.34.refs_0_), channel_id=1, source_target_pairs={{0,4},{2,6},{4,0},{6,2},{1,5},{3,7},{5,1},{7,3},{8,12},{10,14},{12... | collective-permute-start | bytes 294920 | tf_op jit(solution)/shard_map/ppermute | solution.py:52
  33.3 6.7 %collective-permute-start.6 = (bf16[2,24,1024]{2,1,0:T(8,128)(2,1)S(1)}, bf16[2,24,1024]{2,1,0:T(8,128)(2,1)S(1)}, u32[]{:S(2)}, u32[]{:S(2)}) collective-permute-start(bf16[2,24,1024]{2,1,0:T(8,128)(2,1)S(1)} %get-tuple-element.34.refs_0_), channel_id=1, source_target_pairs={{0,2},{2,0},{4,6},{6,4},{1,3},{3,1},{5,7},{7,5},{8,10},{10,8},{12,... | collective-permute-start | bytes 294920 | tf_op jit(solution)/shard_map/ppermute | solution.py:52
  42.3 3.6 %collective-permute-start.9 = (bf16[3,2,16,128]{3,2,1,0:T(8,128)(2,1)S(1)}, bf16[3,2,16,128]{3,2,1,0:T(8,128)(2,1)S(1)}, u32[]{:S(2)}, u32[]{:S(2)}) collective-permute-start(bf16[3,2,16,128]{3,2,1,0:T(8,128)(2,1)S(1)} %get-tuple-element.27), channel_id=1, source_target_pairs={{0,1},{1,0},{8,9},{9,8},{16,17},{17,16},{24,25},{25,24},{2,3},{3,2... | collective-permute-start | bytes 73736 | tf_op jit(solution)/shard_map/ppermute | solution.py:52
  42.4 4.4 %collective-permute-start.10 = (bf16[3,2,16,128]{3,2,1,0:T(8,128)(2,1)S(1)}, bf16[3,2,16,128]{3,2,1,0:T(8,128)(2,1)S(1)}, u32[]{:S(2)}, u32[]{:S(2)}) collective-permute-start(bf16[3,2,16,128]{3,2,1,0:T(8,128)(2,1)S(1)} %get-tuple-element.28), channel_id=1, source_target_pairs={{0,8},{1,9},{8,0},{9,1},{16,24},{17,25},{24,16},{25,17},{2,10},{3,... | collective-permute-start | bytes 73736 | tf_op jit(solution)/shard_map/ppermute | solution.py:52
  43.3 5.4 %collective-permute-start.11 = (bf16[3,2,16,128]{3,2,1,0:T(8,128)(2,1)S(1)}, bf16[3,2,16,128]{3,2,1,0:T(8,128)(2,1)S(1)}, u32[]{:S(2)}, u32[]{:S(2)}) collective-permute-start(bf16[3,2,16,128]{3,2,1,0:T(8,128)(2,1)S(1)} %get-tuple-element.29), channel_id=1, source_target_pairs={{0,9},{1,8},{8,1},{9,0},{16,25},{17,24},{24,17},{25,16},{2,11},{3,... | collective-permute-start | bytes 73736 | tf_op jit(solution)/shard_map/ppermute | solution.py:52
  44.2 4.4 %collective-permute-start.12 = (bf16[3,2,16,128]{3,2,1,0:T(8,128)(2,1)S(1)}, bf16[3,2,16,128]{3,2,1,0:T(8,128)(2,1)S(1)}, u32[]{:S(2)}, u32[]{:S(2)}) collective-permute-start(bf16[3,2,16,128]{3,2,1,0:T(8,128)(2,1)S(1)} %get-tuple-element.30), channel_id=1, source_target_pairs={{0,16},{1,17},{8,24},{9,25},{16,0},{17,1},{24,8},{25,9},{2,18},{3,... | collective-permute-start | bytes 73736 | tf_op jit(solution)/shard_map/ppermute | solution.py:52
  44.8 3.9 %collective-permute-start.13 = (bf16[3,2,16,128]{3,2,1,0:T(8,128)(2,1)S(1)}, bf16[3,2,16,128]{3,2,1,0:T(8,128)(2,1)S(1)}, u32[]{:S(2)}, u32[]{:S(2)}) collective-permute-start(bf16[3,2,16,128]{3,2,1,0:T(8,128)(2,1)S(1)} %get-tuple-element.31), channel_id=1, source_target_pairs={{0,17},{1,16},{8,25},{9,24},{16,1},{17,0},{24,9},{25,8},{2,19},{3,... | collective-permute-start | bytes 73736 | tf_op jit(solution)/shard_map/ppermute | solution.py:52
  45.9 4.7 %collective-permute-start.14 = (bf16[3,2,16,128]{3,2,1,0:T(8,128)(2,1)S(1)}, bf16[3,2,16,128]{3,2,1,0:T(8,128)(2,1)S(1)}, u32[]{:S(2)}, u32[]{:S(2)}) collective-permute-start(bf16[3,2,16,128]{3,2,1,0:T(8,128)(2,1)S(1)} %get-tuple-element.32), channel_id=1, source_target_pairs={{0,24},{1,25},{8,16},{9,17},{16,8},{17,9},{24,0},{25,1},{2,26},{3,... | collective-permute-start | bytes 73736 | tf_op jit(solution)/shard_map/ppermute | solution.py:52
  46.8 4.2 %collective-permute-start.15 = (bf16[3,2,16,128]{3,2,1,0:T(8,128)(2,1)S(1)}, bf16[3,2,16,128]{3,2,1,0:T(8,128)(2,1)S(1)}, u32[]{:S(2)}, u32[]{:S(2)}) collective-permute-start(bf16[3,2,16,128]{3,2,1,0:T(8,128)(2,1)S(1)} %get-tuple-element.33), channel_id=1, source_target_pairs={{0,25},{1,24},{8,17},{9,16},{16,9},{17,8},{24,1},{25,0},{2,27},{3,... | collective-permute-start | bytes 73736 | tf_op jit(solution)/shard_map/ppermute | solution.py:52

commit v3 on v2

--- a/solution.py
+++ b/solution.py
@@ -19,7 +19,12 @@
     phases = (freq_bins[:, None] * samples[None, :] % length).astype(np.float32)
     phases = phases * np.float32(2.0 * math.pi / length)
     rows = np.concatenate([np.cos(phases), -np.sin(phases)])
-    return jnp.asarray(rows.astype(jnp.bfloat16))
+    return rows.astype(jnp.bfloat16)
+
+
+def wide_table(table):
+    bins = table.shape[0]
+    return np.pad(table.T, ((0, 0), (0, -bins % LANES)))
 
 
 def dot(first, second, first_dim, second_dim):
@@ -53,55 +58,62 @@
     return arrived
 
 
-def spectrum_kernel(table_ref, model_ref, *refs):
-    out_refs, rows_ref = refs[:-1], refs[-1]
-    step = pl.program_id(0)
-    high, part, rhs, length = model_ref.shape
+def spectrum_kernel(table_hbm, model_hbm, *refs):
+    out_refs = refs[:-5]
+    table_ref, model_ref, rows_ref, table_sem, model_sems = refs[-5:]
+    high, low, rhs, length = model_ref.shape
     dests = len(out_refs)
-    freqs, _, low, lanes = out_refs[0].shape
+    freqs = out_refs[0].shape[0]
+    bins = 2 * dests * freqs
+    chunks = model_sems.shape[0]
+    part = low // chunks
+    own = model_hbm.at[lax.axis_index("rep")]
+    table_copy = pltpu.make_async_copy(table_hbm, table_ref, table_sem)
+    table_copy.start()
+    copies = []
+    for at in range(chunks):
+        rows = pl.ds(at * part, part)
+        copies.append(
+            pltpu.make_async_copy(own.at[:, rows], model_ref.at[:, rows], model_sems.at[at])
+        )
+        copies[-1].start()
+    table_copy.wait()
     table = table_ref[...]
-    bins = table.shape[0]
-    for start in range(0, part, 2):
-        width = min(2, part - start)
-        block = jnp.concatenate(
-            [model_ref[:, start + at].reshape(high * rhs, length) for at in range(width)]
-        )
-        sums = dot(table, block, 1, 1)
-        for at in range(width):
-            rows = pl.ds((step * part + start + at) * bins, bins)
-            rows_ref[rows, :] = sums[:, at * lanes : (at + 1) * lanes]
-
-    @pl.when(step == pl.num_programs(0) - 1)
-    def _():
-        me = lax.axis_index("freq")
-        for at, out_ref in enumerate(out_refs):
-            dest = target(me, at, dests)
-            for f in range(freqs):
-                for c in range(2):
-                    q = c * dests * freqs + dest * freqs + f
-                    picked = rows_ref[pl.ds(q, low, stride=bins), :]
-                    out_ref[f, c] = picked.astype(out_ref.dtype)
-
-
-def spectrum_of(model, table, dests, freqs):
+    for at in range(chunks):
+        copies[at].wait()
+        for row in range(at * part, (at + 1) * part):
+            block = model_ref[:, row].reshape(high * rhs, length)
+            rows_ref[row * bins : (row + 1) * bins] = dot(block, table, 1, 0).T[:bins]
+    me = lax.axis_index("freq")
+    for at, out_ref in enumerate(out_refs):
+        dest = target(me, at, dests)
+        for f in range(freqs):
+            for c in range(2):
+                q = c * dests * freqs + dest * freqs + f
+                out_ref[f, c] = rows_ref[pl.ds(q, low, stride=bins), :].astype(out_ref.dtype)
+
+
+def spectrum_of(model, table, dests, freqs, reps):
     traces, rhs, length = model.shape
     high = LANES // rhs
-    low = traces // high
-    steps = 4 if low % 4 == 0 else 1
-    bins = table.shape[0]
+    low = traces // (reps * high)
+    chunks = math.gcd(low, 8)
+    bins = 2 * dests * freqs
     return pl.pallas_call(
         spectrum_kernel,
-        grid=(steps,),
-        in_specs=[
-            pl.BlockSpec((bins, length), lambda s: (0, 0)),
-            pl.BlockSpec((high, low // steps, rhs, length), lambda s: (0, s, 0, 0)),
+        in_specs=[pl.BlockSpec(memory_space=pltpu.HBM)] * 2,
+        out_specs=[pl.BlockSpec(memory_space=pltpu.VMEM)] * dests,
+        out_shape=[jax.ShapeDtypeStruct((freqs, 2, low, LANES), jnp.bfloat16)] * dests,
+        scratch_shapes=[
+            pltpu.VMEM(table.shape, table.dtype),
+            pltpu.VMEM((high, low, rhs, length), model.dtype),
+            pltpu.VMEM((low * bins, LANES), jnp.float32),
+            pltpu.SemaphoreType.DMA,
+            pltpu.SemaphoreType.DMA((chunks,)),
         ],
-        out_specs=[pl.BlockSpec((freqs, 2, low, LANES), lambda s: (0, 0, 0, 0))] * dests,
-        out_shape=[jax.ShapeDtypeStruct((freqs, 2, low, LANES), jnp.bfloat16)] * dests,
-        scratch_shapes=[pltpu.VMEM((low * bins, LANES), jnp.float32)],
         compiler_params=pltpu.CompilerParams(vmem_limit_bytes=VMEM_LIMIT),
         name="spectrum",
-    )(table, model.reshape(high, low, rhs, length))
+    )(table, model.reshape(reps, high, low, rhs, length))
 
 
 def masked(product, ranks_ref, places, size):
@@ -129,7 +141,7 @@
     _, freqs, _, low, lanes = spec_ref.shape
     _, _, row_tiles, col_tiles, size, tile = left_ref.shape
     _, pairs, _ = out_refs[0].shape
-    me = lax.axis_index("freq")
+    me = lax.axis_index(("freq", "rep"))
     for at, arrived_ref in enumerate(arrived_refs):
         spec_ref[origin(me, at, groups)] = arrived_ref[...]
     rhs = parts * pairs // freqs
@@ -264,48 +276,62 @@
     )(ranks, green_right, green_left, *misfit)
 
 
-def gradient_kernel(reps, table_ref, *refs):
-    part_refs, out_ref, rows_ref = refs[:-2], refs[-2], refs[-1]
-    step = pl.program_id(0)
+def gradient_kernel(reps, table_hbm, *refs):
+    part_refs = refs[:-6]
+    out_hbm, table_ref, out_ref, rows_ref, table_sem, out_sems = refs[-6:]
     groups = len(part_refs) // reps
     freqs, _, low, lanes = part_refs[0].shape
-    high, part, rhs, length = out_ref.shape
+    high, _, rhs, length = out_ref.shape
     bins = table_ref.shape[0]
-
-    @pl.when(step == 0)
-    def _():
-        me = lax.axis_index("freq")
-        for at in range(groups):
-            g = origin(me, at, groups)
-            for f in range(freqs):
-                for c in range(2):
-                    total = part_refs[at * reps][f, c].astype(jnp.float32)
-                    for rep in range(1, reps):
-                        total = total + part_refs[at * reps + rep][f, c].astype(jnp.float32)
-                    rows_ref[pl.ds(c * groups * freqs + g * freqs + f, low, stride=bins), :] = total
-
+    chunks = out_sems.shape[0]
+    part = low // chunks
+    table_copy = pltpu.make_async_copy(table_hbm, table_ref, table_sem)
+    table_copy.start()
+    me = lax.axis_index("freq")
+    for at in range(groups):
+        g = origin(me, at, groups)
+        for f in range(freqs):
+            for c in range(2):
+                total = part_refs[at * reps][f, c].astype(jnp.float32)
+                for rep in range(1, reps):
+                    total = total + part_refs[at * reps + rep][f, c].astype(jnp.float32)
+                rows_ref[pl.ds(c * groups * freqs + g * freqs + f, low, stride=bins), :] = total
+    table_copy.wait()
     table = table_ref[...]
-    for at in range(part):
-        coefficients = rows_ref[pl.ds((step * part + at) * bins, bins), :].astype(jnp.bfloat16)
-        traces = dot(coefficients, table, 0, 0).astype(out_ref.dtype)
-        out_ref[:, at] = traces.reshape(high, rhs, length)
+    copies = []
+    for at in range(chunks):
+        for row in range(at * part, (at + 1) * part):
+            coefficients = rows_ref[row * bins : (row + 1) * bins].astype(jnp.bfloat16)
+            traces = dot(coefficients, table, 0, 0).astype(out_ref.dtype)
+            out_ref[:, row] = traces.reshape(high, rhs, length)
+        rows = pl.ds(at * part, part)
+        copies.append(
+            pltpu.make_async_copy(out_ref.at[:, rows], out_hbm.at[:, rows], out_sems.at[at])
+        )
+        copies[-1].start()
+    for copy in copies:
+        copy.wait()
 
 
 def gradient_of(parts, table, rhs, reps):
     freqs, _, low, lanes = parts[0].shape
     bins, length = table.shape
     high = lanes // rhs
-    steps = 4 if low % 4 == 0 else 1
+    chunks = math.gcd(low, 8)
+    shape = (high, low, rhs, length)
     out = pl.pallas_call(
         functools.partial(gradient_kernel, reps),
-        grid=(steps,),
-        in_specs=[
-            pl.BlockSpec((bins, length), lambda s: (0, 0)),
-        ]
-        + [pl.BlockSpec(parts[0].shape, lambda s: (0, 0, 0, 0))] * len(parts),
-        out_specs=pl.BlockSpec((high, low // steps, rhs, length), lambda s: (0, s, 0, 0)),
-        out_shape=jax.ShapeDtypeStruct((high, low, rhs, length), jnp.bfloat16),
-        scratch_shapes=[pltpu.VMEM((low * bins, lanes), jnp.float32)],
+        in_specs=[pl.BlockSpec(memory_space=pltpu.HBM)]
+        + [pl.BlockSpec(memory_space=pltpu.VMEM)] * len(parts),
+        out_specs=pl.BlockSpec(memory_space=pltpu.HBM),
+        out_shape=jax.ShapeDtypeStruct(shape, jnp.bfloat16),
+        scratch_shapes=[
+            pltpu.VMEM(table.shape, table.dtype),
+            pltpu.VMEM(shape, jnp.bfloat16),
+            pltpu.VMEM((low * bins, lanes), jnp.float32),
+            pltpu.SemaphoreType.DMA,
+            pltpu.SemaphoreType.DMA((chunks,)),
+        ],
         compiler_params=pltpu.CompilerParams(vmem_limit_bytes=VMEM_LIMIT),
         name="gradient",
     )(table, *parts)
@@ -319,8 +345,8 @@
     freq_local = ranks.shape[0]
     rhs_count = model.shape[2]
     table = tables(freq_local * freq_count, model.shape[3])
-    spectrum = spectrum_of(model[0], table, freq_count, freq_local)
-    spectrum = exchange(spectrum, "freq")
+    spectrum = spectrum_of(model[0], wide_table(table), freq_count, freq_local, rep_count)
+    spectrum = exchange([block for block in spectrum for _ in range(rep_count)], ("freq", "rep"))
     predicted = predict(ranks, spectrum, green_right, green_left, tile_count)
     arrived = exchange(predicted, "rtile")
     residual = sum(block.astype(jnp.float32) for block in arrived) - data

time: 54.5 us -> 56.3 us (1.033)
  starting transfers between devices: 19.7 us -> 23 us
  Pallas kernels: 13.8 us -> 11.1 us
  waiting for transfers between devices: 18.5 us -> 19.5 us
    ppermute x16 -> x20, starting transfers between devices: 19.7 us -> 23 us  [exchange(): arrived.append(lax.ppermute(blocks[step], axis, pairs))]
    pallas_call x2, Pallas kernels: 9.13 us -> 6.44 us  [the longest x1 3.96 us: spectrum_of(): pl.pallas_call(spectrum_kernel, in_specs=[pl.BlockSpec(memory_space=pltpu...]
    ppermute x16 -> x20, waiting for transfers between devices: 18.5 us -> 19.5 us  [exchange(): arrived.append(lax.ppermute(blocks[step], axis, pairs))]
  transfers between devices with their start and end apart: 16 -> 20, of which waited for: 10 -> 9; matrix products, arithmetic and copies ran while one was open for 0% -> 0% of each run, Pallas kernels for 0% -> 0%
where the time goes in v3:
time: 56.3 us; the launch traced here: 56.1 us
  starting transfers between devices  23 us (41%)
  waiting for transfers between devices  19.5 us (35%)
  Pallas kernels  11.1 us (20%)
  local copies, waits for them, and re-layouts  1.07 us (2%)
  other arithmetic  0.74 us (1%)
  between operations  0.71 us (1%)
    ppermute x20, starting transfers between devices, exchange(): arrived.append(lax.ppermute(blocks[step], axis, pairs))  23 us
    ppermute x20, waiting for transfers between devices, exchange(): arrived.append(lax.ppermute(blocks[step], axis, pairs))  19.5 us
    pallas_call x1, Pallas kernels, spectrum_of(): pl.pallas_call(spectrum_kernel, in_specs=[pl.BlockSpec(memory_space=pltpu...  3.96 us
    pallas_call x1, Pallas kernels, gradient_of(): pl.pallas_call(functools.partial(gradient_kernel, reps), in_specs=[pl.Blo...  2.48 us
    pallas_call x1, Pallas kernels, predict(): pl.pallas_call(functools.partial(predict_kernel, groups, parts), in_specs...  2.38 us
    pallas_call x1, Pallas kernels, back_project(): pl.pallas_call(functools.partial(back_kernel, parts, dests), in_specs=[pl...  2.28 us
  transfers between devices with their start and end apart: 20, of which 9 were waited for; matrix products, arithmetic and copies ran while one was open for 0% of the time, Pallas kernels for 0%

profile of v3, /device:TPU:0, one launch (start us, length us, event | category | flops | bytes accessed | tf_op | source)
XLA Modules:
  0.0 56.1 jit_solution(2612035701024993105)
XLA Ops:
  0.6 0.0 copy-start.2
  0.6 0.9 %copy-done.2 = bf16[1024,128]{1,0:T(8,128)(2,1)S(1)} copy-done((bf16[1024,128]{1,0:T(8,128)(2,1)S(1)}, bf16[1024,128]{1,0:T(8,128)(2,1)}, u32[]{:S(2)}) %copy-start.2) | copy-done | bytes 262168
  1.6 0.0 copy-start.5
  1.6 0.0 copy-start
  1.6 0.0 copy-start.1
  1.6 0.0 copy-start.4
  1.6 4.0 %spectrum.1 = (bf16[3,2,16,128]{3,2,1,0:T(8,128)(2,1)S(1)}, bf16[3,2,16,128]{3,2,1,0:T(8,128)(2,1)S(1)}, bf16[3,2,16,128]{3,2,1,0:T(8,128)(2,1)S(1)}, bf16[3,2,16,128]{3,2,1,0:T(8,128)(2,1)S(1)}) custom-call(bf16[1024,128]{1,0:T(8,128)(2,1)S(1)} %copy-done.2, bf16[2,4,16,32,1024]{4,3,2,1,0:T(8,128)(2,1)} %bitcast.2), custom_call_target="tpu_custom_call" | custom-call | tf_op jit(solution)/shard_map/spectrum/pallas_call | solution.py:102
  5.6 0.0 copy-start.3
  5.6 0.5 collective-permute-start
  6.1 2.6 %collective-permute-start.2 = (bf16[3,2,16,128]{3,2,1,0:T(8,128)(2,1)S(1)}, bf16[3,2,16,128]{3,2,1,0:T(8,128)(2,1)S(1)}, u32[]{:S(2)}, u32[]{:S(2)}) collective-permute-start(bf16[3,2,16,128]{3,2,1,0:T(8,128)(2,1)S(1)} %get-tuple-element.19), channel_id=1, source_target_pairs={{0,9},{1,8},{8,1},{9,0},{16,25},{17,24},{24,17},{25,16},{2,11},{3,... | collective-permute-start | bytes 73736 | tf_op jit(solution)/shard_map/ppermute | solution.py:57
  8.7 0.0 collective-permute-start.1
  8.8 1.4 %collective-permute-start.4 = (bf16[3,2,16,128]{3,2,1,0:T(8,128)(2,1)S(1)}, bf16[3,2,16,128]{3,2,1,0:T(8,128)(2,1)S(1)}, u32[]{:S(2)}, u32[]{:S(2)}) collective-permute-start(bf16[3,2,16,128]{3,2,1,0:T(8,128)(2,1)S(1)} %get-tuple-element.20), channel_id=1, source_target_pairs={{0,17},{1,16},{8,25},{9,24},{16,1},{17,0},{24,9},{25,8},{2,19},{3,... | collective-permute-start | bytes 73736 | tf_op jit(solution)/shard_map/ppermute | solution.py:57
  10.2 0.6 %collective-permute-start.3 = (bf16[3,2,16,128]{3,2,1,0:T(8,128)(2,1)S(1)}, bf16[3,2,16,128]{3,2,1,0:T(8,128)(2,1)S(1)}, u32[]{:S(2)}, u32[]{:S(2)}) collective-permute-start(bf16[3,2,16,128]{3,2,1,0:T(8,128)(2,1)S(1)} %get-tuple-element.20), channel_id=1, source_target_pairs={{0,16},{1,17},{8,24},{9,25},{16,0},{17,1},{24,8},{25,9},{2,18},{3,... | collective-permute-start | bytes 73736 | tf_op jit(solution)/shard_map/ppermute | solution.py:57
  10.8 0.0 collective-permute-done.refs_1_
  10.8 2.4 %collective-permute-start.6 = (bf16[3,2,16,128]{3,2,1,0:T(8,128)(2,1)S(1)}, bf16[3,2,16,128]{3,2,1,0:T(8,128)(2,1)S(1)}, u32[]{:S(2)}, u32[]{:S(2)}) collective-permute-start(bf16[3,2,16,128]{3,2,1,0:T(8,128)(2,1)S(1)} %get-tuple-element.21), channel_id=1, source_target_pairs={{0,25},{1,24},{8,17},{9,16},{16,9},{17,8},{24,1},{25,0},{2,27},{3,... | collective-permute-start | bytes 73736 | tf_op jit(solution)/shard_map/ppermute | solution.py:57
  13.2 0.0 collective-permute-done.2.refs_3_
  13.2 0.3 collective-permute-start.5
  13.4 0.0 copy-done.5
  13.4 0.1 copy.9.ranks_ref
  13.5 0.0 collective-permute-done.1.refs_2_
  13.5 0.0 collective-permute-done.4.refs_5_
  13.5 0.5 collective-permute-done.3.refs_4_
  14.0 1.0 %collective-permute-done.6.refs_7_ = bf16[3,2,16,128]{3,2,1,0:T(8,128)(2,1)S(1)} collective-permute-done((bf16[3,2,16,128]{3,2,1,0:T(8,128)(2,1)S(1)}, bf16[3,2,16,128]{3,2,1,0:T(8,128)(2,1)S(1)}, u32[]{:S(2)}, u32[]{:S(2)}) %collective-permute-start.6) | collective-permute-done | bytes 24608 | tf_op jit(solution)/shard_map/ppermute | solution.py:57
  15.0 2.9 %collective-permute-done.5.refs_6_ = bf16[3,2,16,128]{3,2,1,0:T(8,128)(2,1)S(1)} collective-permute-done((bf16[3,2,16,128]{3,2,1,0:T(8,128)(2,1)S(1)}, bf16[3,2,16,128]{3,2,1,0:T(8,128)(2,1)S(1)}, u32[]{:S(2)}, u32[]{:S(2)}) %collective-permute-start.5) | collective-permute-done | bytes 24608 | tf_op jit(solution)/shard_map/ppermute | solution.py:57
  17.9 0.0 copy-done
  17.9 0.0 copy-done.1
  17.9 2.4 %predict.1 = (bf16[2,24,1024]{2,1,0:T(8,128)(2,1)S(1)}, bf16[2,24,1024]{2,1,0:T(8,128)(2,1)S(1)}, bf16[2,24,1024]{2,1,0:T(8,128)(2,1)S(1)}, bf16[2,24,1024]{2,1,0:T(8,128)(2,1)S(1)}) custom-call(s32[3,4,2]{2,1,0:T(4,128)S(1)} %copy.9.ranks_ref, bf16[2,3,4,2,48,256]{5,4,3,2,1,0:T(8,128)(2,1)S(1)} %copy-done, bf16[2,3,4,2,48,256]{5,4,3,2,1,0:T(8,128)(2,1)S(1)} %copy-done.1, ...), custom_call_target="tpu_custom_call" | custom-call | tf_op jit(solution)/shard_map/predict/pallas_call | solution.py:191
  20.3 1.7 %collective-permute-start.7 = (bf16[2,24,1024]{2,1,0:T(8,128)(2,1)S(1)}, bf16[2,24,1024]{2,1,0:T(8,128)(2,1)S(1)}, u32[]{:S(2)}, u32[]{:S(2)}) collective-permute-start(bf16[2,24,1024]{2,1,0:T(8,128)(2,1)S(1)} %get-tuple-element.23), channel_id=1, source_target_pairs={{0,2},{2,0},{4,6},{6,4},{1,3},{3,1},{5,7},{7,5},{8,10},{10,8},{12,... | collective-permute-start | bytes 294920 | tf_op jit(solution)/shard_map/ppermute | solution.py:57
  21.9 2.6 %collective-permute-start.8 = (bf16[2,24,1024]{2,1,0:T(8,128)(2,1)S(1)}, bf16[2,24,1024]{2,1,0:T(8,128)(2,1)S(1)}, u32[]{:S(2)}, u32[]{:S(2)}) collective-permute-start(bf16[2,24,1024]{2,1,0:T(8,128)(2,1)S(1)} %get-tuple-element.24), channel_id=1, source_target_pairs={{0,4},{2,6},{4,0},{6,2},{1,5},{3,7},{5,1},{7,3},{8,12},{10,14},{12... | collective-permute-start | bytes 294920 | tf_op jit(solution)/shard_map/ppermute | solution.py:57
  24.5 0.2 collective-permute-start.9
  24.7 1.2 %collective-permute-done.7 = bf16[2,24,1024]{2,1,0:T(8,128)(2,1)S(1)} collective-permute-done((bf16[2,24,1024]{2,1,0:T(8,128)(2,1)S(1)}, bf16[2,24,1024]{2,1,0:T(8,128)(2,1)S(1)}, u32[]{:S(2)}, u32[]{:S(2)}) %collective-permute-start.7) | collective-permute-done | bytes 98336 | tf_op jit(solution)/shard_map/ppermute | solution.py:57
  25.9 5.5 %collective-permute-done.8 = bf16[2,24,1024]{2,1,0:T(8,128)(2,1)S(1)} collective-permute-done((bf16[2,24,1024]{2,1,0:T(8,128)(2,1)S(1)}, bf16[2,24,1024]{2,1,0:T(8,128)(2,1)S(1)}, u32[]{:S(2)}, u32[]{:S(2)}) %collective-permute-start.8) | collective-permute-done | bytes 98336 | tf_op jit(solution)/shard_map/ppermute | solution.py:57
  31.4 0.0 collective-permute-done.9
  31.4 0.0 copy-done.4
  31.4 0.7 %fusion = (bf16[2,24,1024]{2,1,0:T(8,128)(2,1)S(1)}, f32[2,24,1024]{2,1,0:T(8,128)}) fusion(f32[2,24,1024]{2,1,0:T(8,128)S(1)} %copy-done.4, bf16[2,24,1024]{2,1,0:T(8,128)(2,1)S(1)} %collective-permute-done.9, bf16[2,24,1024]{2,1,0:T(8,128)(2,1)S(1)} %collective-permute-done.8, bf16[2,24,1024]{2,1,0:T(8,128)(2,1)S(1)} %collective-permute-done.7, ...), kind=kLoop, calls=%fused_computation.1 | loop fusion | flops 442368 | bytes 884736 | tf_op jit(solution)/shard_map/convert_element_type | solution.py:353
  32.2 2.5 %collective-permute-start.12 = (bf16[2,24,1024]{2,1,0:T(8,128)(2,1)S(1)}, bf16[2,24,1024]{2,1,0:T(8,128)(2,1)S(1)}, u32[]{:S(2)}, u32[]{:S(2)}) collective-permute-start(bf16[2,24,1024]{2,1,0:T(8,128)(2,1)S(1)} %get-tuple-element.34.refs_0_), channel_id=1, source_target_pairs={{0,6},{2,4},{4,2},{6,0},{1,7},{3,5},{5,3},{7,1},{8,14},{10,12},{12... | collective-permute-start | bytes 294920 | tf_op jit(solution)/shard_map/ppermute | solution.py:57
  34.7 0.6 %collective-permute-start.11 = (bf16[2,24,1024]{2,1,0:T(8,128)(2,1)S(1)}, bf16[2,24,1024]{2,1,0:T(8,128)(2,1)S(1)}, u32[]{:S(2)}, u32[]{:S(2)}) collective-permute-start(bf16[2,24,1024]{2,1,0:T(8,128)(2,1)S(1)} %get-tuple-element.34.refs_0_), channel_id=1, source_target_pairs={{0,4},{2,6},{4,0},{6,2},{1,5},{3,7},{5,1},{7,3},{8,12},{10,14},{12... | collective-permute-start | bytes 294920 | tf_op jit(solution)/shard_map/ppermute | solution.py:57
  35.3 1.3 %collective-permute-start.10 = (bf16[2,24,1024]{2,1,0:T(8,128)(2,1)S(1)}, bf16[2,24,1024]{2,1,0:T(8,128)(2,1)S(1)}, u32[]{:S(2)}, u32[]{:S(2)}) collective-permute-start(bf16[2,24,1024]{2,1,0:T(8,128)(2,1)S(1)} %get-tuple-element.34.refs_0_), channel_id=1, source_target_pairs={{0,2},{2,0},{4,6},{6,4},{1,3},{3,1},{5,7},{7,5},{8,10},{10,8},{12,... | collective-permute-start | bytes 294920 | tf_op jit(solution)/shard_map/ppermute | solution.py:57
  36.6 2.8 %collective-permute-done.12.refs_3_ = bf16[2,24,1024]{2,1,0:T(8,128)(2,1)S(1)} collective-permute-done((bf16[2,24,1024]{2,1,0:T(8,128)(2,1)S(1)}, bf16[2,24,1024]{2,1,0:T(8,128)(2,1)S(1)}, u32[]{:S(2)}, u32[]{:S(2)}) %collective-permute-start.12) | collective-permute-done | bytes 98336 | tf_op jit(solution)/shard_map/ppermute | solution.py:57
  39.4 3.3 %collective-permute-done.11.refs_2_ = bf16[2,24,1024]{2,1,0:T(8,128)(2,1)S(1)} collective-permute-done((bf16[2,24,1024]{2,1,0:T(8,128)(2,1)S(1)}, bf16[2,24,1024]{2,1,0:T(8,128)(2,1)S(1)}, u32[]{:S(2)}, u32[]{:S(2)}) %collective-permute-start.11) | collective-permute-done | bytes 98336 | tf_op jit(solution)/shard_map/ppermute | solution.py:57
  42.7 0.0 collective-permute-done.10.refs_1_
  42.7 2.3 %back_project.1 = (bf16[3,2,16,128]{3,2,1,0:T(8,128)(2,1)S(1)}, bf16[3,2,16,128]{3,2,1,0:T(8,128)(2,1)S(1)}, bf16[3,2,16,128]{3,2,1,0:T(8,128)(2,1)S(1)}, bf16[3...) custom-call(s32[3,4,2]{2,1,0:T(4,128)S(1)} %copy.9.ranks_ref, ...), custom_call_target="tpu_custom_call" | custom-call | tf_op jit(solution)/shard_map/back_project/pallas_call | solution.py:264
  45.0 0.1 collective-permute-start.13
  45.1 0.6 %collective-permute-start.14 = (bf16[3,2,16,128]{3,2,1,0:T(8,128)(2,1)S(1)}, bf16[3,2,16,128]{3,2,1,0:T(8,128)(2,1)S(1)}, u32[]{:S(2)}, u32[]{:S(2)}) collective-permute-start(bf16[3,2,16,128]{3,2,1,0:T(8,128)(2,1)S(1)} %get-tuple-element.28), channel_id=1, source_target_pairs={{0,8},{1,9},{8,0},{9,1},{16,24},{17,25},{24,16},{25,17},{2,10},{3,... | collective-permute-start | bytes 73736 | tf_op jit(solution)/shard_map/ppermute | solution.py:57
  45.7 1.3 %collective-permute-start.15 = (bf16[3,2,16,128]{3,2,1,0:T(8,128)(2,1)S(1)}, bf16[3,2,16,128]{3,2,1,0:T(8,128)(2,1)S(1)}, u32[]{:S(2)}, u32[]{:S(2)}) collective-permute-start(bf16[3,2,16,128]{3,2,1,0:T(8,128)(2,1)S(1)} %get-tuple-element.29), channel_id=1, source_target_pairs={{0,9},{1,8},{8,1},{9,0},{16,25},{17,24},{24,17},{25,16},{2,11},{3,... | collective-permute-start | bytes 73736 | tf_op jit(solution)/shard_map/ppermute | solution.py:57
  46.9 0.6 %collective-permute-start.16 = (bf16[3,2,16,128]{3,2,1,0:T(8,128)(2,1)S(1)}, bf16[3,2,16,128]{3,2,1,0:T(8,128)(2,1)S(1)}, u32[]{:S(2)}, u32[]{:S(2)}) collective-permute-start(bf16[3,2,16,128]{3,2,1,0:T(8,128)(2,1)S(1)} %get-tuple-element.30), channel_id=1, source_target_pairs={{0,16},{1,17},{8,24},{9,25},{16,0},{17,1},{24,8},{25,9},{2,18},{3,... | collective-permute-start | bytes 73736 | tf_op jit(solution)/shard_map/ppermute | solution.py:57
  47.5 1.1 %collective-permute-start.17 = (bf16[3,2,16,128]{3,2,1,0:T(8,128)(2,1)S(1)}, bf16[3,2,16,128]{3,2,1,0:T(8,128)(2,1)S(1)}, u32[]{:S(2)}, u32[]{:S(2)}) collective-permute-start(bf16[3,2,16,128]{3,2,1,0:T(8,128)(2,1)S(1)} %get-tuple-element.31), channel_id=1, source_target_pairs={{0,17},{1,16},{8,25},{9,24},{16,1},{17,0},{24,9},{25,8},{2,19},{3,... | collective-permute-start | bytes 73736 | tf_op jit(solution)/shard_map/ppermute | solution.py:57
  48.6 0.0 collective-permute-done.13.refs_1_
  48.6 0.9 %collective-permute-start.18 = (bf16[3,2,16,128]{3,2,1,0:T(8,128)(2,1)S(1)}, bf16[3,2,16,128]{3,2,1,0:T(8,128)(2,1)S(1)}, u32[]{:S(2)}, u32[]{:S(2)}) collective-permute-start(bf16[3,2,16,128]{3,2,1,0:T(8,128)(2,1)S(1)} %get-tuple-element.32), channel_id=1, source_target_pairs={{0,24},{1,25},{8,16},{9,17},{16,8},{17,9},{24,0},{25,1},{2,26},{3,... | collective-permute-start | bytes 73736 | tf_op jit(solution)/shard_map/ppermute | solution.py:57
  49.5 0.0 collective-permute-done.14.refs_2_
  49.5 1.8 %collective-permute-start.19 = (bf16[3,2,16,128]{3,2,1,0:T(8,128)(2,1)S(1)}, bf16[3,2,16,128]{3,2,1,0:T(8,128)(2,1)S(1)}, u32[]{:S(2)}, u32[]{:S(2)}) collective-permute-start(bf16[3,2,16,128]{3,2,1,0:T(8,128)(2,1)S(1)} %get-tuple-element.33), channel_id=1, source_target_pairs={{0,25},{1,24},{8,17},{9,16},{16,9},{17,8},{24,1},{25,0},{2,27},{3,... | collective-permute-start | bytes 73736 | tf_op jit(solution)/shard_map/ppermute | solution.py:57
  51.3 0.0 collective-permute-done.15.refs_3_
  51.3 0.0 collective-permute-done.16.refs_4_
  51.3 0.0 collective-permute-done.17.refs_5_
  51.3 2.0 %collective-permute-done.18.refs_6_ = bf16[3,2,16,128]{3,2,1,0:T(8,128)(2,1)S(1)} collective-permute-done((bf16[3,2,16,128]{3,2,1,0:T(8,128)(2,1)S(1)}, bf16[3,2,16,128]{3,2,1,0:T(8,128)(2,1)S(1)}, u32[]{:S(2)}, u32[]{:S(2)}) %collective-permute-start.18) | collective-permute-done | bytes 24608 | tf_op jit(solution)/shard_map/ppermute | solution.py:57
  53.3 0.3 collective-permute-done.19.refs_7_
  53.6 0.0 copy-done.3
  53.6 2.5 %gradient.1 = bf16[4,16,32,1024]{3,2,1,0:T(8,128)(2,1)} custom-call(bf16[24,1024]{1,0:T(8,128)(2,1)S(1)} %copy-done.3, bf16[3,2,16,128]{3,2,1,0:T(8,128)(2,1)S(1)} %get-tuple-element.26.refs_0_, bf16[3,2,16,128]{3,2,1,0:T(8,128)(2,1)S(1)} %collective-permute-done.13.refs_1_, bf16[3,2,16,128]{3,2,1,0:T(8,128)(2,1)S(1)} %collective-permute-done.14.refs_2_, ...), custom_call_target="tpu_custom_call" | custom-call | tf_op jit(solution)/shard_map/gradient/pallas_call | solution.py:322
Async XLA Ops:
  0.6 1.0 %copy-start.2 = (bf16[1024,128]{1,0:T(8,128)(2,1)S(1)}, bf16[1024,128]{1,0:T(8,128)(2,1)}, u32[]{:S(2)}) copy-start(bf16[1024,128]{1,0:T(8,128)(2,1)} %constant.4.clone.table_hbm) | copy-start | bytes 786436
  1.6 11.8 %copy-start.5 = (s32[3,4,2]{1,2,0:T(2,128)S(1)}, s32[3,4,2]{1,2,0:T(2,128)}, u32[]{:S(2)}) copy-start(s32[3,4,2]{1,2,0:T(2,128)} %param.10) | copy-start | bytes 292
  1.6 16.3 %copy-start = (bf16[2,3,4,2,48,256]{5,4,3,2,1,0:T(8,128)(2,1)S(1)}, bf16[2,3,4,2,48,256]{5,4,3,2,1,0:T(8,128)(2,1)}, u32[]{:S(2)}) copy-start(bf16[2,3,4,2,48,256]{5,4,3,2,1,0:T(8,128)(2,1)} %right_ref.3) | copy-start | bytes 3538948
  1.6 16.3 %copy-start.1 = (bf16[2,3,4,2,48,256]{5,4,3,2,1,0:T(8,128)(2,1)S(1)}, bf16[2,3,4,2,48,256]{5,4,3,2,1,0:T(8,128)(2,1)}, u32[]{:S(2)}) copy-start(bf16[2,3,4,2,48,256]{5,4,3,2,1,0:T(8,128)(2,1)} %left_ref.3) | copy-start | bytes 3538948
  1.6 29.8 %copy-start.4 = (f32[2,24,1024]{2,1,0:T(8,128)S(1)}, f32[2,24,1024]{2,1,0:T(8,128)}, u32[]{:S(2)}) copy-start(f32[2,24,1024]{2,1,0:T(8,128)} %param.11) | copy-start | bytes 589828
  5.6 48.1 %copy-start.3 = (bf16[24,1024]{1,0:T(8,128)(2,1)S(1)}, bf16[24,1024]{1,0:T(8,128)(2,1)}, u32[]{:S(2)}) copy-start(bf16[24,1024]{1,0:T(8,128)(2,1)} %constant.5.clone.table_hbm) | copy-start | bytes 147460
  5.6 5.2 %collective-permute-start = (bf16[3,2,16,128]{3,2,1,0:T(8,128)(2,1)S(1)}, bf16[3,2,16,128]{3,2,1,0:T(8,128)(2,1)S(1)}, u32[]{:S(2)}, u32[]{:S(2)}) collective-permute-start(bf16[3,2,16,128]{3,2,1,0:T(8,128)(2,1)S(1)} %get-tuple-element.18.refs_0_), channel_id=1, source_target_pairs={{0,1},{1,0},{8,9},{9,8},{16,17},{17,16},{24,25},{25,24},{2,3},{3,2... | collective-permute-start | bytes 73736 | tf_op jit(solution)/shard_map/ppermute | solution.py:57
  6.1 7.1 %collective-permute-start.2 = (bf16[3,2,16,128]{3,2,1,0:T(8,128)(2,1)S(1)}, bf16[3,2,16,128]{3,2,1,0:T(8,128)(2,1)S(1)}, u32[]{:S(2)}, u32[]{:S(2)}) collective-permute-start(bf16[3,2,16,128]{3,2,1,0:T(8,128)(2,1)S(1)} %get-tuple-element.19), channel_id=1, source_target_pairs={{0,9},{1,8},{8,1},{9,0},{16,25},{17,24},{24,17},{25,16},{2,11},{3,... | collective-permute-start | bytes 73736 | tf_op jit(solution)/shard_map/ppermute | solution.py:57
  8.7 4.8 %collective-permute-start.1 = (bf16[3,2,16,128]{3,2,1,0:T(8,128)(2,1)S(1)}, bf16[3,2,16,128]{3,2,1,0:T(8,128)(2,1)S(1)}, u32[]{:S(2)}, u32[]{:S(2)}) collective-permute-start(bf16[3,2,16,128]{3,2,1,0:T(8,128)(2,1)S(1)} %get-tuple-element.19), channel_id=1, source_target_pairs={{0,8},{1,9},{8,0},{9,1},{16,24},{17,25},{24,16},{25,17},{2,10},{3,... | collective-permute-start | bytes 73736 | tf_op jit(solution)/shard_map/ppermute | solution.py:57
  8.8 4.8 %collective-permute-start.4 = (bf16[3,2,16,128]{3,2,1,0:T(8,128)(2,1)S(1)}, bf16[3,2,16,128]{3,2,1,0:T(8,128)(2,1)S(1)}, u32[]{:S(2)}, u32[]{:S(2)}) collective-permute-start(bf16[3,2,16,128]{3,2,1,0:T(8,128)(2,1)S(1)} %get-tuple-element.20), channel_id=1, source_target_pairs={{0,17},{1,16},{8,25},{9,24},{16,1},{17,0},{24,9},{25,8},{2,19},{3,... | collective-permute-start | bytes 73736 | tf_op jit(solution)/shard_map/ppermute | solution.py:57
  10.2 3.8 %collective-permute-start.3 = (bf16[3,2,16,128]{3,2,1,0:T(8,128)(2,1)S(1)}, bf16[3,2,16,128]{3,2,1,0:T(8,128)(2,1)S(1)}, u32[]{:S(2)}, u32[]{:S(2)}) collective-permute-start(bf16[3,2,16,128]{3,2,1,0:T(8,128)(2,1)S(1)} %get-tuple-element.20), channel_id=1, source_target_pairs={{0,16},{1,17},{8,24},{9,25},{16,0},{17,1},{24,8},{25,9},{2,18},{3,... | collective-permute-start | bytes 73736 | tf_op jit(solution)/shard_map/ppermute | solution.py:57
  10.8 4.2 %collective-permute-start.6 = (bf16[3,2,16,128]{3,2,1,0:T(8,128)(2,1)S(1)}, bf16[3,2,16,128]{3,2,1,0:T(8,128)(2,1)S(1)}, u32[]{:S(2)}, u32[]{:S(2)}) collective-permute-start(bf16[3,2,16,128]{3,2,1,0:T(8,128)(2,1)S(1)} %get-tuple-element.21), channel_id=1, source_target_pairs={{0,25},{1,24},{8,17},{9,16},{16,9},{17,8},{24,1},{25,0},{2,27},{3,... | collective-permute-start | bytes 73736 | tf_op jit(solution)/shard_map/ppermute | solution.py:57
  13.2 4.7 %collective-permute-start.5 = (bf16[3,2,16,128]{3,2,1,0:T(8,128)(2,1)S(1)}, bf16[3,2,16,128]{3,2,1,0:T(8,128)(2,1)S(1)}, u32[]{:S(2)}, u32[]{:S(2)}) collective-permute-start(bf16[3,2,16,128]{3,2,1,0:T(8,128)(2,1)S(1)} %get-tuple-element.21), channel_id=1, source_target_pairs={{0,24},{1,25},{8,16},{9,17},{16,8},{17,9},{24,0},{25,1},{2,26},{3,... | collective-permute-start | bytes 73736 | tf_op jit(solution)/shard_map/ppermute | solution.py:57
  20.3 5.7 %collective-permute-start.7 = (bf16[2,24,1024]{2,1,0:T(8,128)(2,1)S(1)}, bf16[2,24,1024]{2,1,0:T(8,128)(2,1)S(1)}, u32[]{:S(2)}, u32[]{:S(2)}) collective-permute-start(bf16[2,24,1024]{2,1,0:T(8,128)(2,1)S(1)} %get-tuple-element.23), channel_id=1, source_target_pairs={{0,2},{2,0},{4,6},{6,4},{1,3},{3,1},{5,7},{7,5},{8,10},{10,8},{12,... | collective-permute-start | bytes 294920 | tf_op jit(solution)/shard_map/ppermute | solution.py:57
  21.9 9.5 %collective-permute-start.8 = (bf16[2,24,1024]{2,1,0:T(8,128)(2,1)S(1)}, bf16[2,24,1024]{2,1,0:T(8,128)(2,1)S(1)}, u32[]{:S(2)}, u32[]{:S(2)}) collective-permute-start(bf16[2,24,1024]{2,1,0:T(8,128)(2,1)S(1)} %get-tuple-element.24), channel_id=1, source_target_pairs={{0,4},{2,6},{4,0},{6,2},{1,5},{3,7},{5,1},{7,3},{8,12},{10,14},{12... | collective-permute-start | bytes 294920 | tf_op jit(solution)/shard_map/ppermute | solution.py:57
  24.5 6.9 %collective-permute-start.9 = (bf16[2,24,1024]{2,1,0:T(8,128)(2,1)S(1)}, bf16[2,24,1024]{2,1,0:T(8,128)(2,1)S(1)}, u32[]{:S(2)}, u32[]{:S(2)}) collective-permute-start(bf16[2,24,1024]{2,1,0:T(8,128)(2,1)S(1)} %get-tuple-element.25), channel_id=1, source_target_pairs={{0,6},{2,4},{4,2},{6,0},{1,7},{3,5},{5,3},{7,1},{8,14},{10,12},{12... | collective-permute-start | bytes 294920 | tf_op jit(solution)/shard_map/ppermute | solution.py:57
  32.2 7.2 %collective-permute-start.12 = (bf16[2,24,1024]{2,1,0:T(8,128)(2,1)S(1)}, bf16[2,24,1024]{2,1,0:T(8,128)(2,1)S(1)}, u32[]{:S(2)}, u32[]{:S(2)}) collective-permute-start(bf16[2,24,1024]{2,1,0:T(8,128)(2,1)S(1)} %get-tuple-element.34.refs_0_), channel_id=1, source_target_pairs={{0,6},{2,4},{4,2},{6,0},{1,7},{3,5},{5,3},{7,1},{8,14},{10,12},{12... | collective-permute-start | bytes 294920 | tf_op jit(solution)/shard_map/ppermute | solution.py:57
  34.7 8.0 %collective-permute-start.11 = (bf16[2,24,1024]{2,1,0:T(8,128)(2,1)S(1)}, bf16[2,24,1024]{2,1,0:T(8,128)(2,1)S(1)}, u32[]{:S(2)}, u32[]{:S(2)}) collective-permute-start(bf16[2,24,1024]{2,1,0:T(8,128)(2,1)S(1)} %get-tuple-element.34.refs_0_), channel_id=1, source_target_pairs={{0,4},{2,6},{4,0},{6,2},{1,5},{3,7},{5,1},{7,3},{8,12},{10,14},{12... | collective-permute-start | bytes 294920 | tf_op jit(solution)/shard_map/ppermute | solution.py:57
  35.3 7.4 %collective-permute-start.10 = (bf16[2,24,1024]{2,1,0:T(8,128)(2,1)S(1)}, bf16[2,24,1024]{2,1,0:T(8,128)(2,1)S(1)}, u32[]{:S(2)}, u32[]{:S(2)}) collective-permute-start(bf16[2,24,1024]{2,1,0:T(8,128)(2,1)S(1)} %get-tuple-element.34.refs_0_), channel_id=1, source_target_pairs={{0,2},{2,0},{4,6},{6,4},{1,3},{3,1},{5,7},{7,5},{8,10},{10,8},{12,... | collective-permute-start | bytes 294920 | tf_op jit(solution)/shard_map/ppermute | solution.py:57
  45.0 3.6 %collective-permute-start.13 = (bf16[3,2,16,128]{3,2,1,0:T(8,128)(2,1)S(1)}, bf16[3,2,16,128]{3,2,1,0:T(8,128)(2,1)S(1)}, u32[]{:S(2)}, u32[]{:S(2)}) collective-permute-start(bf16[3,2,16,128]{3,2,1,0:T(8,128)(2,1)S(1)} %get-tuple-element.27), channel_id=1, source_target_pairs={{0,1},{1,0},{8,9},{9,8},{16,17},{17,16},{24,25},{25,24},{2,3},{3,2... | collective-permute-start | bytes 73736 | tf_op jit(solution)/shard_map/ppermute | solution.py:57
  45.1 4.4 %collective-permute-start.14 = (bf16[3,2,16,128]{3,2,1,0:T(8,128)(2,1)S(1)}, bf16[3,2,16,128]{3,2,1,0:T(8,128)(2,1)S(1)}, u32[]{:S(2)}, u32[]{:S(2)}) collective-permute-start(bf16[3,2,16,128]{3,2,1,0:T(8,128)(2,1)S(1)} %get-tuple-element.28), channel_id=1, source_target_pairs={{0,8},{1,9},{8,0},{9,1},{16,24},{17,25},{24,16},{25,17},{2,10},{3,... | collective-permute-start | bytes 73736 | tf_op jit(solution)/shard_map/ppermute | solution.py:57
  45.7 5.7 %collective-permute-start.15 = (bf16[3,2,16,128]{3,2,1,0:T(8,128)(2,1)S(1)}, bf16[3,2,16,128]{3,2,1,0:T(8,128)(2,1)S(1)}, u32[]{:S(2)}, u32[]{:S(2)}) collective-permute-start(bf16[3,2,16,128]{3,2,1,0:T(8,128)(2,1)S(1)} %get-tuple-element.29), channel_id=1, source_target_pairs={{0,9},{1,8},{8,1},{9,0},{16,25},{17,24},{24,17},{25,16},{2,11},{3,... | collective-permute-start | bytes 73736 | tf_op jit(solution)/shard_map/ppermute | solution.py:57
  46.9 4.4 %collective-permute-start.16 = (bf16[3,2,16,128]{3,2,1,0:T(8,128)(2,1)S(1)}, bf16[3,2,16,128]{3,2,1,0:T(8,128)(2,1)S(1)}, u32[]{:S(2)}, u32[]{:S(2)}) collective-permute-start(bf16[3,2,16,128]{3,2,1,0:T(8,128)(2,1)S(1)} %get-tuple-element.30), channel_id=1, source_target_pairs={{0,16},{1,17},{8,24},{9,25},{16,0},{17,1},{24,8},{25,9},{2,18},{3,... | collective-permute-start | bytes 73736 | tf_op jit(solution)/shard_map/ppermute | solution.py:57
  47.5 3.8 %collective-permute-start.17 = (bf16[3,2,16,128]{3,2,1,0:T(8,128)(2,1)S(1)}, bf16[3,2,16,128]{3,2,1,0:T(8,128)(2,1)S(1)}, u32[]{:S(2)}, u32[]{:S(2)}) collective-permute-start(bf16[3,2,16,128]{3,2,1,0:T(8,128)(2,1)S(1)} %get-tuple-element.31), channel_id=1, source_target_pairs={{0,17},{1,16},{8,25},{9,24},{16,1},{17,0},{24,9},{25,8},{2,19},{3,... | collective-permute-start | bytes 73736 | tf_op jit(solution)/shard_map/ppermute | solution.py:57
  48.6 4.7 %collective-permute-start.18 = (bf16[3,2,16,128]{3,2,1,0:T(8,128)(2,1)S(1)}, bf16[3,2,16,128]{3,2,1,0:T(8,128)(2,1)S(1)}, u32[]{:S(2)}, u32[]{:S(2)}) collective-permute-start(bf16[3,2,16,128]{3,2,1,0:T(8,128)(2,1)S(1)} %get-tuple-element.32), channel_id=1, source_target_pairs={{0,24},{1,25},{8,16},{9,17},{16,8},{17,9},{24,0},{25,1},{2,26},{3,... | collective-permute-start | bytes 73736 | tf_op jit(solution)/shard_map/ppermute | solution.py:57
  49.5 4.2 %collective-permute-start.19 = (bf16[3,2,16,128]{3,2,1,0:T(8,128)(2,1)S(1)}, bf16[3,2,16,128]{3,2,1,0:T(8,128)(2,1)S(1)}, u32[]{:S(2)}, u32[]{:S(2)}) collective-permute-start(bf16[3,2,16,128]{3,2,1,0:T(8,128)(2,1)S(1)} %get-tuple-element.33), channel_id=1, source_target_pairs={{0,25},{1,24},{8,17},{9,16},{16,9},{17,8},{24,1},{25,0},{2,27},{3,... | collective-permute-start | bytes 73736 | tf_op jit(solution)/shard_map/ppermute | solution.py:57

commit v4 on v3

--- a/solution.py
+++ b/solution.py
@@ -3,7 +3,6 @@
 
 import jax
 import jax.numpy as jnp
-import numpy as np
 from jax import lax
 from jax.experimental import pallas as pl
 from jax.experimental.pallas import tpu as pltpu
@@ -13,18 +12,25 @@
 VMEM_LIMIT = 48 * 1024 * 1024
 
 
-def tables(count, length):
-    freq_bins = 1 + np.arange(count, dtype=np.int32)
-    samples = np.arange(length, dtype=np.int32)
-    phases = (freq_bins[:, None] * samples[None, :] % length).astype(np.float32)
-    phases = phases * np.float32(2.0 * math.pi / length)
-    rows = np.concatenate([np.cos(phases), -np.sin(phases)])
-    return rows.astype(jnp.bfloat16)
-
-
-def wide_table(table):
-    bins = table.shape[0]
-    return np.pad(table.T, ((0, 0), (0, -bins % LANES)))
+def tables(rows, bins, length):
+    row = lax.broadcasted_iota(jnp.int32, (rows, length), 0)
+    sample = lax.broadcasted_iota(jnp.int32, (rows, length), 1)
+    is_sine = row >= bins // 2
+    freq_bin = jnp.where(is_sine, row - bins // 2, row) + 1
+    phase = lax.rem(freq_bin * sample, length) + jnp.where(is_sine, length // 4, 0)
+    quarter = lax.div(phase + length // 8, length // 4)
+    angle = (phase - quarter * (length // 4)).astype(jnp.float32) * (2.0 * math.pi / length)
+    square = angle * angle
+    even = 1.0
+    odd = 1.0
+    for order in (8, 6, 4, 2):
+        even = 1.0 - square * even * (1.0 / (order * (order - 1)))
+        odd = 1.0 - square * odd * (1.0 / (order * (order + 1)))
+    odd = odd * angle
+    quarter = quarter & 3
+    value = jnp.where((quarter & 1) == 0, even, odd)
+    value = jnp.where((quarter == 1) | (quarter == 2), -value, value)
+    return jnp.where(row < bins, value, 0.0).astype(jnp.bfloat16)
 
 
 def dot(first, second, first_dim, second_dim):
@@ -58,32 +64,36 @@
     return arrived
 
 
-def spectrum_kernel(table_hbm, model_hbm, *refs):
-    out_refs = refs[:-5]
-    table_ref, model_ref, rows_ref, table_sem, model_sems = refs[-5:]
+def spectrum_kernel(model_hbm, table_out_ref, *refs):
+    out_refs = refs[:-3]
+    model_ref, rows_ref, model_sems = refs[-3:]
     high, low, rhs, length = model_ref.shape
     dests = len(out_refs)
     freqs = out_refs[0].shape[0]
     bins = 2 * dests * freqs
     chunks = model_sems.shape[0]
     part = low // chunks
-    own = model_hbm.at[lax.axis_index("rep")]
-    table_copy = pltpu.make_async_copy(table_hbm, table_ref, table_sem)
-    table_copy.start()
     copies = []
     for at in range(chunks):
         rows = pl.ds(at * part, part)
         copies.append(
-            pltpu.make_async_copy(own.at[:, rows], model_ref.at[:, rows], model_sems.at[at])
+            pltpu.make_async_copy(
+                model_hbm.at[:, rows], model_ref.at[:, rows], model_sems.at[at]
+            )
         )
         copies[-1].start()
-    table_copy.wait()
-    table = table_ref[...]
+    table = tables(LANES, bins, length)
+    table_out_ref[...] = table[:bins]
     for at in range(chunks):
         copies[at].wait()
-        for row in range(at * part, (at + 1) * part):
-            block = model_ref[:, row].reshape(high * rhs, length)
-            rows_ref[row * bins : (row + 1) * bins] = dot(block, table, 1, 0).T[:bins]
+        block = model_ref[:, at * part : (at + 1) * part].reshape(high * part * rhs, length)
+        sums = dot(block, table, 1, 1)
+        for row in range(part):
+            mine = jnp.concatenate(
+                [sums[(h * part + row) * rhs : (h * part + row + 1) * rhs] for h in range(high)]
+            )
+            place = (at * part + row) * bins
+            rows_ref[place : place + bins] = mine.T[:bins]
     me = lax.axis_index("freq")
     for at, out_ref in enumerate(out_refs):
         dest = target(me, at, dests)
@@ -93,27 +103,27 @@
                 out_ref[f, c] = rows_ref[pl.ds(q, low, stride=bins), :].astype(out_ref.dtype)
 
 
-def spectrum_of(model, table, dests, freqs, reps):
+def spectrum_of(model, dests, freqs):
     traces, rhs, length = model.shape
     high = LANES // rhs
-    low = traces // (reps * high)
-    chunks = math.gcd(low, 8)
+    low = traces // high
+    chunks = math.gcd(low, 4)
     bins = 2 * dests * freqs
-    return pl.pallas_call(
+    table, *blocks = pl.pallas_call(
         spectrum_kernel,
-        in_specs=[pl.BlockSpec(memory_space=pltpu.HBM)] * 2,
-        out_specs=[pl.BlockSpec(memory_space=pltpu.VMEM)] * dests,
-        out_shape=[jax.ShapeDtypeStruct((freqs, 2, low, LANES), jnp.bfloat16)] * dests,
+        in_specs=[pl.BlockSpec(memory_space=pltpu.HBM)],
+        out_specs=[pl.BlockSpec(memory_space=pltpu.VMEM)] * (1 + dests),
+        out_shape=[jax.ShapeDtypeStruct((bins, length), jnp.bfloat16)]
+        + [jax.ShapeDtypeStruct((freqs, 2, low, LANES), jnp.bfloat16)] * dests,
         scratch_shapes=[
-            pltpu.VMEM(table.shape, table.dtype),
             pltpu.VMEM((high, low, rhs, length), model.dtype),
             pltpu.VMEM((low * bins, LANES), jnp.float32),
-            pltpu.SemaphoreType.DMA,
             pltpu.SemaphoreType.DMA((chunks,)),
         ],
         compiler_params=pltpu.CompilerParams(vmem_limit_bytes=VMEM_LIMIT),
         name="spectrum",
-    )(table, model.reshape(reps, high, low, rhs, length))
+    )(model.reshape(high, low, rhs, length))
+    return table, blocks
 
 
 def masked(product, ranks_ref, places, size):
@@ -141,7 +151,7 @@
     _, freqs, _, low, lanes = spec_ref.shape
     _, _, row_tiles, col_tiles, size, tile = left_ref.shape
     _, pairs, _ = out_refs[0].shape
-    me = lax.axis_index(("freq", "rep"))
+    me = lax.axis_index("freq")
     for at, arrived_ref in enumerate(arrived_refs):
         spec_ref[origin(me, at, groups)] = arrived_ref[...]
     rhs = parts * pairs // freqs
@@ -203,12 +213,13 @@
     )(ranks, green_right, green_left, *spectrum)
 
 
-def back_kernel(parts, dests, ranks_ref, right_ref, left_ref, *refs):
-    misfit_refs, out_refs = refs[:parts], refs[parts : parts + dests]
-    misfit_all_ref, grad_ref = refs[parts + dests :]
+def back_kernel(parts, groups, reps, ranks_ref, right_ref, left_ref, *refs):
+    misfit_refs, out_refs = refs[:parts], refs[parts : parts + reps]
+    misfit_all_ref, grad_ref = refs[parts + reps :]
+    dests = groups * reps
     _, pairs, _ = misfit_refs[0].shape
     _, freqs, row_tiles, col_tiles, size, tile = left_ref.shape
-    _, _, low, lanes = out_refs[0].shape
+    _, _, _, low, lanes = out_refs[0].shape
     rhs = parts * pairs // freqs
     high = lanes // rhs
     per_tile = dests // col_tiles
@@ -250,23 +261,26 @@
                     grad_ref[j * per_tile + at, f, c] = jnp.concatenate(blocks, axis=1).astype(
                         grad_ref.dtype
                     )
-    me = lax.axis_index(("freq", "rep"))
+    me, own = lax.axis_index("freq"), lax.axis_index("rep")
     for at, out_ref in enumerate(out_refs):
-        out_ref[...] = grad_ref[target(me, at, dests)]
-
-
-def back_project(ranks, misfit, green_right, green_left, dests):
+        rep = target(own, at, reps)
+        for step in range(groups):
+            out_ref[step] = grad_ref[target(me, step, groups) * reps + rep]
+
+
+def back_project(ranks, misfit, green_right, green_left, groups, reps):
+    dests = groups * reps
     freqs = ranks.shape[0]
     parts = len(misfit)
     _, pairs, sources = misfit[0].shape
     rhs = parts * pairs // freqs
     low = green_left.shape[3] * green_left.shape[5] * rhs // (dests * LANES)
     return pl.pallas_call(
-        functools.partial(back_kernel, parts, dests),
+        functools.partial(back_kernel, parts, groups, reps),
         in_specs=[pl.BlockSpec(memory_space=pltpu.SMEM)]
         + [pl.BlockSpec(memory_space=pltpu.VMEM)] * (2 + parts),
-        out_specs=[pl.BlockSpec(memory_space=pltpu.VMEM)] * dests,
-        out_shape=[jax.ShapeDtypeStruct((freqs, 2, low, LANES), jnp.bfloat16)] * dests,
+        out_specs=[pl.BlockSpec(memory_space=pltpu.VMEM)] * reps,
+        out_shape=[jax.ShapeDtypeStruct((groups, freqs, 2, low, LANES), jnp.bfloat16)] * reps,
         scratch_shapes=[
             pltpu.VMEM((parts, 2, pairs, sources), jnp.float32),
             pltpu.VMEM((dests, freqs, 2, low, LANES), jnp.bfloat16),
@@ -276,34 +290,53 @@
     )(ranks, green_right, green_left, *misfit)
 
 
-def gradient_kernel(reps, table_hbm, *refs):
-    part_refs = refs[:-6]
-    out_hbm, table_ref, out_ref, rows_ref, table_sem, out_sems = refs[-6:]
-    groups = len(part_refs) // reps
+def gather_kernel(reps, *refs):
+    part_refs, out_refs = refs[:reps], refs[reps:]
+    for step, out_ref in enumerate(out_refs):
+        total = sum(part_ref[step].astype(jnp.float32) for part_ref in part_refs)
+        out_ref[...] = total.astype(out_ref.dtype)
+
+
+def gather(parts):
+    shape = parts[0].shape
+    return pl.pallas_call(
+        functools.partial(gather_kernel, len(parts)),
+        in_specs=[pl.BlockSpec(memory_space=pltpu.VMEM)] * len(parts),
+        out_specs=[pl.BlockSpec(memory_space=pltpu.VMEM)] * shape[0],
+        out_shape=[jax.ShapeDtypeStruct(shape[1:], jnp.bfloat16)] * shape[0],
+        compiler_params=pltpu.CompilerParams(vmem_limit_bytes=VMEM_LIMIT),
+        name="gather",
+    )(*parts)
+
+
+def gradient_kernel(table_ref, *refs):
+    part_refs = refs[:-4]
+    out_hbm, out_ref, rows_ref, out_sems = refs[-4:]
+    groups = len(part_refs)
     freqs, _, low, lanes = part_refs[0].shape
     high, _, rhs, length = out_ref.shape
     bins = table_ref.shape[0]
     chunks = out_sems.shape[0]
     part = low // chunks
-    table_copy = pltpu.make_async_copy(table_hbm, table_ref, table_sem)
-    table_copy.start()
     me = lax.axis_index("freq")
-    for at in range(groups):
+    for at, part_ref in enumerate(part_refs):
         g = origin(me, at, groups)
         for f in range(freqs):
             for c in range(2):
-                total = part_refs[at * reps][f, c].astype(jnp.float32)
-                for rep in range(1, reps):
-                    total = total + part_refs[at * reps + rep][f, c].astype(jnp.float32)
-                rows_ref[pl.ds(c * groups * freqs + g * freqs + f, low, stride=bins), :] = total
-    table_copy.wait()
+                rows = pl.ds(c * groups * freqs + g * freqs + f, low, stride=bins)
+                rows_ref[rows, :] = part_ref[f, c].astype(jnp.float32)
     table = table_ref[...]
     copies = []
     for at in range(chunks):
-        for row in range(at * part, (at + 1) * part):
-            coefficients = rows_ref[row * bins : (row + 1) * bins].astype(jnp.bfloat16)
-            traces = dot(coefficients, table, 0, 0).astype(out_ref.dtype)
-            out_ref[:, row] = traces.reshape(high, rhs, length)
+        coefficients = jnp.concatenate(
+            [rows_ref[row * bins : (row + 1) * bins] for row in range(at * part, (at + 1) * part)],
+            axis=1,
+        ).astype(jnp.bfloat16)
+        traces = dot(coefficients, table, 0, 0).astype(out_ref.dtype)
+        for row in range(part):
+            out_ref[:, at * part + row] = traces[row * lanes : (row + 1) * lanes].reshape(
+                high, rhs, length
+            )
         rows = pl.ds(at * part, part)
         copies.append(
             pltpu.make_async_copy(out_ref.at[:, rows], out_hbm.at[:, rows], out_sems.at[at])
@@ -313,23 +346,20 @@
         copy.wait()
 
 
-def gradient_of(parts, table, rhs, reps):
+def gradient_of(parts, table, rhs):
     freqs, _, low, lanes = parts[0].shape
     bins, length = table.shape
     high = lanes // rhs
-    chunks = math.gcd(low, 8)
+    chunks = math.gcd(low, 4)
     shape = (high, low, rhs, length)
     out = pl.pallas_call(
-        functools.partial(gradient_kernel, reps),
-        in_specs=[pl.BlockSpec(memory_space=pltpu.HBM)]
-        + [pl.BlockSpec(memory_space=pltpu.VMEM)] * len(parts),
+        gradient_kernel,
+        in_specs=[pl.BlockSpec(memory_space=pltpu.VMEM)] * (1 + len(parts)),
         out_specs=pl.BlockSpec(memory_space=pltpu.HBM),
         out_shape=jax.ShapeDtypeStruct(shape, jnp.bfloat16),
         scratch_shapes=[
-            pltpu.VMEM(table.shape, table.dtype),
             pltpu.VMEM(shape, jnp.bfloat16),
             pltpu.VMEM((low * bins, lanes), jnp.float32),
-            pltpu.SemaphoreType.DMA,
             pltpu.SemaphoreType.DMA((chunks,)),
         ],
         compiler_params=pltpu.CompilerParams(vmem_limit_bytes=VMEM_LIMIT),
@@ -344,16 +374,15 @@
     rep_count = lax.axis_size("rep")
     freq_local = ranks.shape[0]
     rhs_count = model.shape[2]
-    table = tables(freq_local * freq_count, model.shape[3])
-    spectrum = spectrum_of(model[0], wide_table(table), freq_count, freq_local, rep_count)
-    spectrum = exchange([block for block in spectrum for _ in range(rep_count)], ("freq", "rep"))
+    table, spectrum = spectrum_of(model[0], freq_count, freq_local)
+    spectrum = exchange(spectrum, "freq")
     predicted = predict(ranks, spectrum, green_right, green_left, tile_count)
     arrived = exchange(predicted, "rtile")
     residual = sum(block.astype(jnp.float32) for block in arrived) - data
     misfit = exchange([residual.astype(jnp.bfloat16)] * tile_count, "rtile")
-    partial = back_project(ranks, misfit, green_right, green_left, freq_count * rep_count)
-    arrived = exchange(partial, ("freq", "rep"))
-    return (residual, gradient_of(arrived, table, rhs_count, rep_count))
+    partial = back_project(ranks, misfit, green_right, green_left, freq_count, rep_count)
+    arrived = exchange(gather(exchange(partial, "rep")), "freq")
+    return (residual, gradient_of(arrived, table, rhs_count))
 
 
 def solution(mesh):

time: 56.3 us -> 53.1 us (0.943)
  starting transfers between devices: 23 us -> 17 us
  Pallas kernels: 11.1 us -> 14.2 us
  local copies, waits for them, and re-layouts: 1.07 us -> 0.12 us
  waiting for transfers between devices: 19.5 us -> 20.1 us
    ppermute x20 -> x13, starting transfers between devices: 23 us -> 17 us  [exchange(): arrived.append(lax.ppermute(blocks[step], axis, pairs))]
    pallas_call x1, Pallas kernels: 3.96 us -> 7.02 us  [spectrum_of(): pl.pallas_call(spectrum_kernel, in_specs=[pl.BlockSpec(memory_space=pltpu...]
    unnamed x13 -> x9, local copies, waits for them, and re-layouts: 1.07 us -> 0.12 us
    ppermute x20 -> x13, waiting for transfers between devices: 19.5 us -> 20.1 us  [exchange(): arrived.append(lax.ppermute(blocks[step], axis, pairs))]
    pallas_call x2 -> x3, Pallas kernels: 4.76 us -> 4.84 us  [the longest x1 2.53 us: gradient_of(): pl.pallas_call(gradient_kernel, in_specs=[pl.BlockSpec(memory_space=pltpu...]
  transfers between devices with their start and end apart: 20 -> 13, of which waited for: 9 -> 12; matrix products, arithmetic and copies ran while one was open for 0% -> 0% of each run, Pallas kernels for 0% -> 0%
where the time goes in v4:
time: 53.1 us; the launch traced here: 52.9 us
  waiting for transfers between devices  20.1 us (38%)
  starting transfers between devices  17 us (32%)
  Pallas kernels  14.2 us (27%)
  other arithmetic  0.74 us (1%)
  between operations  0.71 us (1%)
    ppermute x13, waiting for transfers between devices, exchange(): arrived.append(lax.ppermute(blocks[step], axis, pairs))  20.1 us
    ppermute x13, starting transfers between devices, exchange(): arrived.append(lax.ppermute(blocks[step], axis, pairs))  17 us
    pallas_call x1, Pallas kernels, spectrum_of(): pl.pallas_call(spectrum_kernel, in_specs=[pl.BlockSpec(memory_space=pltpu...  7.02 us
    pallas_call x1, Pallas kernels, gradient_of(): pl.pallas_call(gradient_kernel, in_specs=[pl.BlockSpec(memory_space=pltpu...  2.53 us
    pallas_call x1, Pallas kernels, predict(): pl.pallas_call(functools.partial(predict_kernel, groups, parts), in_specs...  2.37 us
    pallas_call x1, Pallas kernels, back_project(): pl.pallas_call(functools.partial(back_kernel, parts, groups, reps), in_sp...  2.28 us
  transfers between devices with their start and end apart: 13, of which 12 were waited for; matrix products, arithmetic and copies ran while one was open for 0% of the time, Pallas kernels for 0%

profile of v4, /device:TPU:0, one launch (start us, length us, event | category | flops | bytes accessed | tf_op | source)
XLA Modules:
  0.0 52.9 jit_solution(16815588679613653438)
XLA Ops:
  0.6 0.0 copy-start.3
  0.6 0.0 copy-start
  0.7 0.0 copy-start.1
  0.7 0.0 copy-start.2
  0.7 7.0 %spectrum.1 = (bf16[24,1024]{1,0:T(8,128)(2,1)S(1)}, bf16[3,2,32,128]{3,2,1,0:T(8,128)(2,1)S(1)}, bf16[3,2,32,128]{3,2,1,0:T(8,128)(2,1)S(1)}, bf16[3,2,32,128]{...) custom-call(bf16[4,32,32,1024]{3,2,1,0:T(8,128)(2,1)} %bitcast.2), custom_call_target="tpu_custom_call" | custom-call | tf_op jit(solution)/shard_map/spectrum/pallas_call | solution.py:112
  7.7 3.0 %collective-permute-start = (bf16[3,2,32,128]{3,2,1,0:T(8,128)(2,1)S(1)}, bf16[3,2,32,128]{3,2,1,0:T(8,128)(2,1)S(1)}, u32[]{:S(2)}, u32[]{:S(2)}) collective-permute-start(bf16[3,2,32,128]{3,2,1,0:T(8,128)(2,1)S(1)} %get-tuple-element.18), channel_id=1, source_target_pairs={{0,8},{8,0},{16,24},{24,16},{1,9},{9,1},{17,25},{25,17},{2,10},{10... | collective-permute-start | bytes 147464 | tf_op jit(solution)/shard_map/ppermute | solution.py:63
  10.7 1.5 %collective-permute-start.1 = (bf16[3,2,32,128]{3,2,1,0:T(8,128)(2,1)S(1)}, bf16[3,2,32,128]{3,2,1,0:T(8,128)(2,1)S(1)}, u32[]{:S(2)}, u32[]{:S(2)}) collective-permute-start(bf16[3,2,32,128]{3,2,1,0:T(8,128)(2,1)S(1)} %get-tuple-element.19), channel_id=1, source_target_pairs={{0,16},{8,24},{16,0},{24,8},{1,17},{9,25},{17,1},{25,9},{2,18},{10... | collective-permute-start | bytes 147464 | tf_op jit(solution)/shard_map/ppermute | solution.py:63
  12.2 0.0 collective-permute-start.2
  12.2 0.0 copy-done.3
  12.2 0.1 copy.7.ranks_ref
  12.3 0.4 collective-permute-done.refs_1_
  12.8 2.0 %collective-permute-done.1.refs_2_ = bf16[3,2,32,128]{3,2,1,0:T(8,128)(2,1)S(1)} collective-permute-done((bf16[3,2,32,128]{3,2,1,0:T(8,128)(2,1)S(1)}, bf16[3,2,32,128]{3,2,1,0:T(8,128)(2,1)S(1)}, u32[]{:S(2)}, u32[]{:S(2)}) %collective-permute-start.1) | collective-permute-done | bytes 49184 | tf_op jit(solution)/shard_map/ppermute | solution.py:63
  14.8 2.4 %collective-permute-done.2.refs_3_ = bf16[3,2,32,128]{3,2,1,0:T(8,128)(2,1)S(1)} collective-permute-done((bf16[3,2,32,128]{3,2,1,0:T(8,128)(2,1)S(1)}, bf16[3,2,32,128]{3,2,1,0:T(8,128)(2,1)S(1)}, u32[]{:S(2)}, u32[]{:S(2)}) %collective-permute-start.2) | collective-permute-done | bytes 49184 | tf_op jit(solution)/shard_map/ppermute | solution.py:63
  17.2 0.0 copy-done
  17.2 0.0 copy-done.1
  17.2 2.4 %predict.1 = (bf16[2,24,1024]{2,1,0:T(8,128)(2,1)S(1)}, bf16[2,24,1024]{2,1,0:T(8,128)(2,1)S(1)}, bf16[2,24,1024]{2,1,0:T(8,128)(2,1)S(1)}, bf16[2,24,1024]{2,1,0:T(8,128)(2,1)S(1)}) custom-call(s32[3,4,2]{2,1,0:T(4,128)S(1)} %copy.7.ranks_ref, bf16[2,3,4,2,48,256]{5,4,3,2,1,0:T(8,128)(2,1)S(1)} %copy-done, bf16[2,3,4,2,48,256]{5,4,3,2,1,0:T(8,128)(2,1)S(1)} %copy-done.1, ...), custom_call_target="tpu_custom_call" | custom-call | tf_op jit(solution)/shard_map/predict/pallas_call | solution.py:201
  19.6 1.6 %collective-permute-start.3 = (bf16[2,24,1024]{2,1,0:T(8,128)(2,1)S(1)}, bf16[2,24,1024]{2,1,0:T(8,128)(2,1)S(1)}, u32[]{:S(2)}, u32[]{:S(2)}) collective-permute-start(bf16[2,24,1024]{2,1,0:T(8,128)(2,1)S(1)} %get-tuple-element.22), channel_id=1, source_target_pairs={{0,2},{2,0},{4,6},{6,4},{1,3},{3,1},{5,7},{7,5},{8,10},{10,8},{12,... | collective-permute-start | bytes 294920 | tf_op jit(solution)/shard_map/ppermute | solution.py:63
  21.2 2.6 %collective-permute-start.4 = (bf16[2,24,1024]{2,1,0:T(8,128)(2,1)S(1)}, bf16[2,24,1024]{2,1,0:T(8,128)(2,1)S(1)}, u32[]{:S(2)}, u32[]{:S(2)}) collective-permute-start(bf16[2,24,1024]{2,1,0:T(8,128)(2,1)S(1)} %get-tuple-element.23), channel_id=1, source_target_pairs={{0,4},{2,6},{4,0},{6,2},{1,5},{3,7},{5,1},{7,3},{8,12},{10,14},{12... | collective-permute-start | bytes 294920 | tf_op jit(solution)/shard_map/ppermute | solution.py:63
  23.9 0.2 collective-permute-start.5
  24.1 0.6 %collective-permute-done.3 = bf16[2,24,1024]{2,1,0:T(8,128)(2,1)S(1)} collective-permute-done((bf16[2,24,1024]{2,1,0:T(8,128)(2,1)S(1)}, bf16[2,24,1024]{2,1,0:T(8,128)(2,1)S(1)}, u32[]{:S(2)}, u32[]{:S(2)}) %collective-permute-start.3) | collective-permute-done | bytes 98336 | tf_op jit(solution)/shard_map/ppermute | solution.py:63
  24.6 4.3 %collective-permute-done.4 = bf16[2,24,1024]{2,1,0:T(8,128)(2,1)S(1)} collective-permute-done((bf16[2,24,1024]{2,1,0:T(8,128)(2,1)S(1)}, bf16[2,24,1024]{2,1,0:T(8,128)(2,1)S(1)}, u32[]{:S(2)}, u32[]{:S(2)}) %collective-permute-start.4) | collective-permute-done | bytes 98336 | tf_op jit(solution)/shard_map/ppermute | solution.py:63
  28.9 1.5 %collective-permute-done.5 = bf16[2,24,1024]{2,1,0:T(8,128)(2,1)S(1)} collective-permute-done((bf16[2,24,1024]{2,1,0:T(8,128)(2,1)S(1)}, bf16[2,24,1024]{2,1,0:T(8,128)(2,1)S(1)}, u32[]{:S(2)}, u32[]{:S(2)}) %collective-permute-start.5) | collective-permute-done | bytes 98336 | tf_op jit(solution)/shard_map/ppermute | solution.py:63
  30.4 0.0 copy-done.2
  30.4 0.7 %fusion = (bf16[2,24,1024]{2,1,0:T(8,128)(2,1)S(1)}, f32[2,24,1024]{2,1,0:T(8,128)}) fusion(f32[2,24,1024]{2,1,0:T(8,128)S(1)} %copy-done.2, bf16[2,24,1024]{2,1,0:T(8,128)(2,1)S(1)} %collective-permute-done.5, bf16[2,24,1024]{2,1,0:T(8,128)(2,1)S(1)} %collective-permute-done.4, bf16[2,24,1024]{2,1,0:T(8,128)(2,1)S(1)} %collective-permute-done.3, ...), kind=kLoop, calls=%fused_computation.1 | loop fusion | flops 442368 | bytes 884736 | tf_op jit(solution)/shard_map/convert_element_type | solution.py:382
  31.1 2.1 %collective-permute-start.8 = (bf16[2,24,1024]{2,1,0:T(8,128)(2,1)S(1)}, bf16[2,24,1024]{2,1,0:T(8,128)(2,1)S(1)}, u32[]{:S(2)}, u32[]{:S(2)}) collective-permute-start(bf16[2,24,1024]{2,1,0:T(8,128)(2,1)S(1)} %get-tuple-element.32.refs_0_), channel_id=1, source_target_pairs={{0,6},{2,4},{4,2},{6,0},{1,7},{3,5},{5,3},{7,1},{8,14},{10,12},{12... | collective-permute-start | bytes 294920 | tf_op jit(solution)/shard_map/ppermute | solution.py:63
  33.2 0.6 %collective-permute-start.7 = (bf16[2,24,1024]{2,1,0:T(8,128)(2,1)S(1)}, bf16[2,24,1024]{2,1,0:T(8,128)(2,1)S(1)}, u32[]{:S(2)}, u32[]{:S(2)}) collective-permute-start(bf16[2,24,1024]{2,1,0:T(8,128)(2,1)S(1)} %get-tuple-element.32.refs_0_), channel_id=1, source_target_pairs={{0,4},{2,6},{4,0},{6,2},{1,5},{3,7},{5,1},{7,3},{8,12},{10,14},{12... | collective-permute-start | bytes 294920 | tf_op jit(solution)/shard_map/ppermute | solution.py:63
  33.8 1.7 %collective-permute-start.6 = (bf16[2,24,1024]{2,1,0:T(8,128)(2,1)S(1)}, bf16[2,24,1024]{2,1,0:T(8,128)(2,1)S(1)}, u32[]{:S(2)}, u32[]{:S(2)}) collective-permute-start(bf16[2,24,1024]{2,1,0:T(8,128)(2,1)S(1)} %get-tuple-element.32.refs_0_), channel_id=1, source_target_pairs={{0,2},{2,0},{4,6},{6,4},{1,3},{3,1},{5,7},{7,5},{8,10},{10,8},{12,... | collective-permute-start | bytes 294920 | tf_op jit(solution)/shard_map/ppermute | solution.py:63
  35.5 2.3 %collective-permute-done.8.refs_3_ = bf16[2,24,1024]{2,1,0:T(8,128)(2,1)S(1)} collective-permute-done((bf16[2,24,1024]{2,1,0:T(8,128)(2,1)S(1)}, bf16[2,24,1024]{2,1,0:T(8,128)(2,1)S(1)}, u32[]{:S(2)}, u32[]{:S(2)}) %collective-permute-start.8) | collective-permute-done | bytes 98336 | tf_op jit(solution)/shard_map/ppermute | solution.py:63
  37.8 2.7 %collective-permute-done.7.refs_2_ = bf16[2,24,1024]{2,1,0:T(8,128)(2,1)S(1)} collective-permute-done((bf16[2,24,1024]{2,1,0:T(8,128)(2,1)S(1)}, bf16[2,24,1024]{2,1,0:T(8,128)(2,1)S(1)}, u32[]{:S(2)}, u32[]{:S(2)}) %collective-permute-start.7) | collective-permute-done | bytes 98336 | tf_op jit(solution)/shard_map/ppermute | solution.py:63
  40.5 0.0 collective-permute-done.6.refs_1_
  40.5 2.3 %back_project.1 = (bf16[4,3,2,16,128]{4,3,2,1,0:T(8,128)(2,1)S(1)}, bf16[4,3,2,16,128]{4,3,2,1,0:T(8,128)(2,1)S(1)}) custom-call(s32[3,4,2]{2,1,0:T(4,128)S(1)} %copy.7.ranks_ref, bf16[2,3,4,2,48,256]{5,4,3,2,1,0:T(8,128)(2,1)S(1)} %copy-done, bf16[2,3,4,2,48,256]{5,4,3,2,1,0:T(8,128)(2,1)S(1)} %copy-done.1, ...), custom_call_target="tpu_custom_call" | custom-call | tf_op jit(solution)/shard_map/back_project/pallas_call | solution.py:278
  42.8 0.1 collective-permute-start.9
  42.9 1.3 %collective-permute-done.9.refs_1_ = bf16[4,3,2,16,128]{4,3,2,1,0:T(8,128)(2,1)S(1)} collective-permute-done((bf16[4,3,2,16,128]{4,3,2,1,0:T(8,128)(2,1)S(1)}, bf16[4,3,2,16,128]{4,3,2,1,0:T(8,128)(2,1)S(1)}, u32[]{:S(2)}, u32[]{:S(2)}) %collective-permute-start.9) | collective-permute-done | bytes 98336 | tf_op jit(solution)/shard_map/ppermute | solution.py:63
  44.2 0.9 %collective-permute-start.10 = (bf16[3,2,16,128]{3,2,1,0:T(8,128)(2,1)S(1)}, bf16[3,2,16,128]{3,2,1,0:T(8,128)(2,1)S(1)}, u32[]{:S(2)}, u32[]{:S(2)}) collective-permute-start(bf16[3,2,16,128]{3,2,1,0:T(8,128)(2,1)S(1)} %get-tuple-element.29), channel_id=1, source_target_pairs={{0,8},{8,0},{16,24},{24,16},{1,9},{9,1},{17,25},{25,17},{2,10},{10... | collective-permute-start | bytes 73736 | tf_op jit(solution)/shard_map/ppermute | solution.py:63
  45.0 0.6 %collective-permute-start.11 = (bf16[3,2,16,128]{3,2,1,0:T(8,128)(2,1)S(1)}, bf16[3,2,16,128]{3,2,1,0:T(8,128)(2,1)S(1)}, u32[]{:S(2)}, u32[]{:S(2)}) collective-permute-start(bf16[3,2,16,128]{3,2,1,0:T(8,128)(2,1)S(1)} %get-tuple-element.30), channel_id=1, source_target_pairs={{0,16},{8,24},{16,0},{24,8},{1,17},{9,25},{17,1},{25,9},{2,18},{10... | collective-permute-start | bytes 73736 | tf_op jit(solution)/shard_map/ppermute | solution.py:63
  45.6 2.1 %collective-permute-start.12 = (bf16[3,2,16,128]{3,2,1,0:T(8,128)(2,1)S(1)}, bf16[3,2,16,128]{3,2,1,0:T(8,128)(2,1)S(1)}, u32[]{:S(2)}, u32[]{:S(2)}) collective-permute-start(bf16[3,2,16,128]{3,2,1,0:T(8,128)(2,1)S(1)} %get-tuple-element.31), channel_id=1, source_target_pairs={{0,24},{8,16},{16,8},{24,0},{1,25},{9,17},{17,9},{25,1},{2,26},{10... | collective-permute-start | bytes 73736 | tf_op jit(solution)/shard_map/ppermute | solution.py:63
  47.7 0.3 collective-permute-done.10.refs_1_
  48.1 1.1 %collective-permute-done.11.refs_2_ = bf16[3,2,16,128]{3,2,1,0:T(8,128)(2,1)S(1)} collective-permute-done((bf16[3,2,16,128]{3,2,1,0:T(8,128)(2,1)S(1)}, bf16[3,2,16,128]{3,2,1,0:T(8,128)(2,1)S(1)}, u32[]{:S(2)}, u32[]{:S(2)}) %collective-permute-start.11) | collective-permute-done | bytes 24608 | tf_op jit(solution)/shard_map/ppermute | solution.py:63
  49.1 1.2 %collective-permute-done.12.refs_3_ = bf16[3,2,16,128]{3,2,1,0:T(8,128)(2,1)S(1)} collective-permute-done((bf16[3,2,16,128]{3,2,1,0:T(8,128)(2,1)S(1)}, bf16[3,2,16,128]{3,2,1,0:T(8,128)(2,1)S(1)}, u32[]{:S(2)}, u32[]{:S(2)}) %collective-permute-start.12) | collective-permute-done | bytes 24608 | tf_op jit(solution)/shard_map/ppermute | solution.py:63
  50.4 2.5 %gradient.1 = bf16[4,16,32,1024]{3,2,1,0:T(8,128)(2,1)} custom-call(bf16[24,1024]{1,0:T(8,128)(2,1)S(1)} %get-tuple-element.25.table_ref, bf16[3,2,16,128]{3,2,1,0:T(8,128)(2,1)S(1)} %get-tuple-element.28.refs_0_, bf16[3,2,16,128]{3,2,1,0:T(8,128)(2,1)S(1)} %collective-permute-done.10.refs_1_, bf16[3,2,16,128]{3,2,1,0:T(8,128)(2,1)S(1)} %collective-permute-done.11.refs_2_, ...), custom_call_target="tpu_custom_call" | custom-call | tf_op jit(solution)/shard_map/gradient/pallas_call | solution.py:355
  (1 shorter events, 0.0 us)
Async XLA Ops:
  0.6 11.6 %copy-start.3 = (s32[3,4,2]{1,2,0:T(2,128)S(1)}, s32[3,4,2]{1,2,0:T(2,128)}, u32[]{:S(2)}) copy-start(s32[3,4,2]{1,2,0:T(2,128)} %param.8) | copy-start | bytes 292
  0.6 16.6 %copy-start = (bf16[2,3,4,2,48,256]{5,4,3,2,1,0:T(8,128)(2,1)S(1)}, bf16[2,3,4,2,48,256]{5,4,3,2,1,0:T(8,128)(2,1)}, u32[]{:S(2)}) copy-start(bf16[2,3,4,2,48,256]{5,4,3,2,1,0:T(8,128)(2,1)} %right_ref.3) | copy-start | bytes 3538948
  0.7 16.6 %copy-start.1 = (bf16[2,3,4,2,48,256]{5,4,3,2,1,0:T(8,128)(2,1)S(1)}, bf16[2,3,4,2,48,256]{5,4,3,2,1,0:T(8,128)(2,1)}, u32[]{:S(2)}) copy-start(bf16[2,3,4,2,48,256]{5,4,3,2,1,0:T(8,128)(2,1)} %left_ref.3) | copy-start | bytes 3538948
  0.7 29.7 %copy-start.2 = (f32[2,24,1024]{2,1,0:T(8,128)S(1)}, f32[2,24,1024]{2,1,0:T(8,128)}, u32[]{:S(2)}) copy-start(f32[2,24,1024]{2,1,0:T(8,128)} %param.9) | copy-start | bytes 589828
  7.7 5.1 %collective-permute-start = (bf16[3,2,32,128]{3,2,1,0:T(8,128)(2,1)S(1)}, bf16[3,2,32,128]{3,2,1,0:T(8,128)(2,1)S(1)}, u32[]{:S(2)}, u32[]{:S(2)}) collective-permute-start(bf16[3,2,32,128]{3,2,1,0:T(8,128)(2,1)S(1)} %get-tuple-element.18), channel_id=1, source_target_pairs={{0,8},{8,0},{16,24},{24,16},{1,9},{9,1},{17,25},{25,17},{2,10},{10... | collective-permute-start | bytes 147464 | tf_op jit(solution)/shard_map/ppermute | solution.py:63
  10.7 4.1 %collective-permute-start.1 = (bf16[3,2,32,128]{3,2,1,0:T(8,128)(2,1)S(1)}, bf16[3,2,32,128]{3,2,1,0:T(8,128)(2,1)S(1)}, u32[]{:S(2)}, u32[]{:S(2)}) collective-permute-start(bf16[3,2,32,128]{3,2,1,0:T(8,128)(2,1)S(1)} %get-tuple-element.19), channel_id=1, source_target_pairs={{0,16},{8,24},{16,0},{24,8},{1,17},{9,25},{17,1},{25,9},{2,18},{10... | collective-permute-start | bytes 147464 | tf_op jit(solution)/shard_map/ppermute | solution.py:63
  12.2 5.0 %collective-permute-start.2 = (bf16[3,2,32,128]{3,2,1,0:T(8,128)(2,1)S(1)}, bf16[3,2,32,128]{3,2,1,0:T(8,128)(2,1)S(1)}, u32[]{:S(2)}, u32[]{:S(2)}) collective-permute-start(bf16[3,2,32,128]{3,2,1,0:T(8,128)(2,1)S(1)} %get-tuple-element.20), channel_id=1, source_target_pairs={{0,24},{8,16},{16,8},{24,0},{1,25},{9,17},{17,9},{25,1},{2,26},{10... | collective-permute-start | bytes 147464 | tf_op jit(solution)/shard_map/ppermute | solution.py:63
  19.6 5.0 %collective-permute-start.3 = (bf16[2,24,1024]{2,1,0:T(8,128)(2,1)S(1)}, bf16[2,24,1024]{2,1,0:T(8,128)(2,1)S(1)}, u32[]{:S(2)}, u32[]{:S(2)}) collective-permute-start(bf16[2,24,1024]{2,1,0:T(8,128)(2,1)S(1)} %get-tuple-element.22), channel_id=1, source_target_pairs={{0,2},{2,0},{4,6},{6,4},{1,3},{3,1},{5,7},{7,5},{8,10},{10,8},{12,... | collective-permute-start | bytes 294920 | tf_op jit(solution)/shard_map/ppermute | solution.py:63
  21.2 7.7 %collective-permute-start.4 = (bf16[2,24,1024]{2,1,0:T(8,128)(2,1)S(1)}, bf16[2,24,1024]{2,1,0:T(8,128)(2,1)S(1)}, u32[]{:S(2)}, u32[]{:S(2)}) collective-permute-start(bf16[2,24,1024]{2,1,0:T(8,128)(2,1)S(1)} %get-tuple-element.23), channel_id=1, source_target_pairs={{0,4},{2,6},{4,0},{6,2},{1,5},{3,7},{5,1},{7,3},{8,12},{10,14},{12... | collective-permute-start | bytes 294920 | tf_op jit(solution)/shard_map/ppermute | solution.py:63
  23.9 6.5 %collective-permute-start.5 = (bf16[2,24,1024]{2,1,0:T(8,128)(2,1)S(1)}, bf16[2,24,1024]{2,1,0:T(8,128)(2,1)S(1)}, u32[]{:S(2)}, u32[]{:S(2)}) collective-permute-start(bf16[2,24,1024]{2,1,0:T(8,128)(2,1)S(1)} %get-tuple-element.24), channel_id=1, source_target_pairs={{0,6},{2,4},{4,2},{6,0},{1,7},{3,5},{5,3},{7,1},{8,14},{10,12},{12... | collective-permute-start | bytes 294920 | tf_op jit(solution)/shard_map/ppermute | solution.py:63
  31.1 6.7 %collective-permute-start.8 = (bf16[2,24,1024]{2,1,0:T(8,128)(2,1)S(1)}, bf16[2,24,1024]{2,1,0:T(8,128)(2,1)S(1)}, u32[]{:S(2)}, u32[]{:S(2)}) collective-permute-start(bf16[2,24,1024]{2,1,0:T(8,128)(2,1)S(1)} %get-tuple-element.32.refs_0_), channel_id=1, source_target_pairs={{0,6},{2,4},{4,2},{6,0},{1,7},{3,5},{5,3},{7,1},{8,14},{10,12},{12... | collective-permute-start | bytes 294920 | tf_op jit(solution)/shard_map/ppermute | solution.py:63
  33.2 7.3 %collective-permute-start.7 = (bf16[2,24,1024]{2,1,0:T(8,128)(2,1)S(1)}, bf16[2,24,1024]{2,1,0:T(8,128)(2,1)S(1)}, u32[]{:S(2)}, u32[]{:S(2)}) collective-permute-start(bf16[2,24,1024]{2,1,0:T(8,128)(2,1)S(1)} %get-tuple-element.32.refs_0_), channel_id=1, source_target_pairs={{0,4},{2,6},{4,0},{6,2},{1,5},{3,7},{5,1},{7,3},{8,12},{10,14},{12... | collective-permute-start | bytes 294920 | tf_op jit(solution)/shard_map/ppermute | solution.py:63
  33.8 6.7 %collective-permute-start.6 = (bf16[2,24,1024]{2,1,0:T(8,128)(2,1)S(1)}, bf16[2,24,1024]{2,1,0:T(8,128)(2,1)S(1)}, u32[]{:S(2)}, u32[]{:S(2)}) collective-permute-start(bf16[2,24,1024]{2,1,0:T(8,128)(2,1)S(1)} %get-tuple-element.32.refs_0_), channel_id=1, source_target_pairs={{0,2},{2,0},{4,6},{6,4},{1,3},{3,1},{5,7},{7,5},{8,10},{10,8},{12,... | collective-permute-start | bytes 294920 | tf_op jit(solution)/shard_map/ppermute | solution.py:63
  42.8 1.4 %collective-permute-start.9 = (bf16[4,3,2,16,128]{4,3,2,1,0:T(8,128)(2,1)S(1)}, bf16[4,3,2,16,128]{4,3,2,1,0:T(8,128)(2,1)S(1)}, u32[]{:S(2)}, u32[]{:S(2)}) collective-permute-start(bf16[4,3,2,16,128]{4,3,2,1,0:T(8,128)(2,1)S(1)} %get-tuple-element.27), channel_id=1, source_target_pairs={{0,1},{1,0},{2,3},{3,2},{4,5},{5,4},{6,7},{7,6},{8,9},{9,8},{10,11... | collective-permute-start | bytes 294920 | tf_op jit(solution)/shard_map/ppermute | solution.py:63
  44.2 3.9 %collective-permute-start.10 = (bf16[3,2,16,128]{3,2,1,0:T(8,128)(2,1)S(1)}, bf16[3,2,16,128]{3,2,1,0:T(8,128)(2,1)S(1)}, u32[]{:S(2)}, u32[]{:S(2)}) collective-permute-start(bf16[3,2,16,128]{3,2,1,0:T(8,128)(2,1)S(1)} %get-tuple-element.29), channel_id=1, source_target_pairs={{0,8},{8,0},{16,24},{24,16},{1,9},{9,1},{17,25},{25,17},{2,10},{10... | collective-permute-start | bytes 73736 | tf_op jit(solution)/shard_map/ppermute | solution.py:63
  45.0 4.1 %collective-permute-start.11 = (bf16[3,2,16,128]{3,2,1,0:T(8,128)(2,1)S(1)}, bf16[3,2,16,128]{3,2,1,0:T(8,128)(2,1)S(1)}, u32[]{:S(2)}, u32[]{:S(2)}) collective-permute-start(bf16[3,2,16,128]{3,2,1,0:T(8,128)(2,1)S(1)} %get-tuple-element.30), channel_id=1, source_target_pairs={{0,16},{8,24},{16,0},{24,8},{1,17},{9,25},{17,1},{25,9},{2,18},{10... | collective-permute-start | bytes 73736 | tf_op jit(solution)/shard_map/ppermute | solution.py:63
  45.6 4.7 %collective-permute-start.12 = (bf16[3,2,16,128]{3,2,1,0:T(8,128)(2,1)S(1)}, bf16[3,2,16,128]{3,2,1,0:T(8,128)(2,1)S(1)}, u32[]{:S(2)}, u32[]{:S(2)}) collective-permute-start(bf16[3,2,16,128]{3,2,1,0:T(8,128)(2,1)S(1)} %get-tuple-element.31), channel_id=1, source_target_pairs={{0,24},{8,16},{16,8},{24,0},{1,25},{9,17},{17,9},{25,1},{2,26},{10... | collective-permute-start | bytes 73736 | tf_op jit(solution)/shard_map/ppermute | solution.py:63

commit v5 on v4

--- a/solution.py
+++ b/solution.py
@@ -12,9 +12,9 @@
 VMEM_LIMIT = 48 * 1024 * 1024
 
 
-def tables(rows, bins, length):
-    row = lax.broadcasted_iota(jnp.int32, (rows, length), 0)
-    sample = lax.broadcasted_iota(jnp.int32, (rows, length), 1)
+def tables(bins, length):
+    row = lax.broadcasted_iota(jnp.int32, (bins, length), 0)
+    sample = lax.broadcasted_iota(jnp.int32, (bins, length), 1)
     is_sine = row >= bins // 2
     freq_bin = jnp.where(is_sine, row - bins // 2, row) + 1
     phase = lax.rem(freq_bin * sample, length) + jnp.where(is_sine, length // 4, 0)
@@ -29,8 +29,7 @@
     odd = odd * angle
     quarter = quarter & 3
     value = jnp.where((quarter & 1) == 0, even, odd)
-    value = jnp.where((quarter == 1) | (quarter == 2), -value, value)
-    return jnp.where(row < bins, value, 0.0).astype(jnp.bfloat16)
+    return jnp.where((quarter == 1) | (quarter == 2), -value, value).astype(jnp.bfloat16)
 
 
 def dot(first, second, first_dim, second_dim):
@@ -73,17 +72,16 @@
     bins = 2 * dests * freqs
     chunks = model_sems.shape[0]
     part = low // chunks
+    own = model_hbm.at[lax.axis_index("rep")]
     copies = []
     for at in range(chunks):
         rows = pl.ds(at * part, part)
         copies.append(
-            pltpu.make_async_copy(
-                model_hbm.at[:, rows], model_ref.at[:, rows], model_sems.at[at]
-            )
+            pltpu.make_async_copy(own.at[:, rows], model_ref.at[:, rows], model_sems.at[at])
         )
         copies[-1].start()
-    table = tables(LANES, bins, length)
-    table_out_ref[...] = table[:bins]
+    table = tables(bins, length)
+    table_out_ref[...] = table
     for at in range(chunks):
         copies[at].wait()
         block = model_ref[:, at * part : (at + 1) * part].reshape(high * part * rhs, length)
@@ -93,7 +91,7 @@
                 [sums[(h * part + row) * rhs : (h * part + row + 1) * rhs] for h in range(high)]
             )
             place = (at * part + row) * bins
-            rows_ref[place : place + bins] = mine.T[:bins]
+            rows_ref[place : place + bins] = mine.T
     me = lax.axis_index("freq")
     for at, out_ref in enumerate(out_refs):
         dest = target(me, at, dests)
@@ -103,10 +101,10 @@
                 out_ref[f, c] = rows_ref[pl.ds(q, low, stride=bins), :].astype(out_ref.dtype)
 
 
-def spectrum_of(model, dests, freqs):
+def spectrum_of(model, dests, freqs, reps):
     traces, rhs, length = model.shape
     high = LANES // rhs
-    low = traces // high
+    low = traces // (reps * high)
     chunks = math.gcd(low, 4)
     bins = 2 * dests * freqs
     table, *blocks = pl.pallas_call(
@@ -122,8 +120,35 @@
         ],
         compiler_params=pltpu.CompilerParams(vmem_limit_bytes=VMEM_LIMIT),
         name="spectrum",
-    )(model.reshape(high, low, rhs, length))
+    )(model.reshape(reps, high, low, rhs, length))
     return table, blocks
+
+
+def pack_kernel(*refs):
+    block_refs, out_ref = refs[:-1], refs[-1]
+    me = lax.axis_index("freq")
+    for at, block_ref in enumerate(block_refs):
+        out_ref[origin(me, at, len(block_refs))] = block_ref[...]
+
+
+def pack(blocks):
+    shape = (len(blocks),) + blocks[0].shape
+    return pl.pallas_call(
+        pack_kernel,
+        in_specs=[pl.BlockSpec(memory_space=pltpu.VMEM)] * len(blocks),
+        out_specs=pl.BlockSpec(memory_space=pltpu.VMEM),
+        out_shape=jax.ShapeDtypeStruct(shape, blocks[0].dtype),
+        compiler_params=pltpu.CompilerParams(vmem_limit_bytes=VMEM_LIMIT),
+        name="pack",
+    )(*blocks)
+
+
+def tile_cost(count, size, tile, rhs):
+    return pl.CostEstimate(
+        flops=count * 2 * 8 * size * tile * rhs,
+        bytes_accessed=count * 2 * 4 * size * tile,
+        transcendentals=0,
+    )
 
 
 def masked(product, ranks_ref, places, size):
@@ -145,15 +170,17 @@
     return found
 
 
-def predict_kernel(groups, parts, ranks_ref, right_ref, left_ref, *refs):
-    arrived_refs, out_refs = refs[:groups], refs[groups : groups + parts]
-    spec_ref, sum_ref = refs[groups + parts :]
-    _, freqs, _, low, lanes = spec_ref.shape
-    _, _, row_tiles, col_tiles, size, tile = left_ref.shape
+def predict_kernel(reps, parts, tiles, ranks_ref, right_ref, left_ref, *refs):
+    arrived_refs, out_refs = refs[:reps], refs[reps : reps + parts]
+    spec_ref, sum_ref = refs[reps + parts :]
+    _, groups, freqs, _, low, lanes = spec_ref.shape
+    col_tiles, size, tile = left_ref.shape[3:]
+    first, last = tiles
+    row_tiles = last - first
     _, pairs, _ = out_refs[0].shape
-    me = lax.axis_index("freq")
+    own = lax.axis_index("rep")
     for at, arrived_ref in enumerate(arrived_refs):
-        spec_ref[origin(me, at, groups)] = arrived_ref[...]
+        spec_ref[origin(own, at, reps)] = arrived_ref[...]
     rhs = parts * pairs // freqs
     high = lanes // rhs
     per_tile = groups // col_tiles
@@ -164,19 +191,22 @@
             for c in range(2):
                 blocks = []
                 for g in range(j * per_tile, (j + 1) * per_tile):
-                    got = spec_ref[g, f, c].astype(jnp.float32)
-                    blocks += [got[:, h * rhs : (h + 1) * rhs] for h in range(high)]
+                    for rep in range(reps):
+                        got = spec_ref[rep, g, f, c].astype(jnp.float32)
+                        blocks += [got[:, h * rhs : (h + 1) * rhs] for h in range(high)]
                 halves.append(jnp.concatenate(blocks))
-            first = jnp.concatenate(halves, axis=1).astype(jnp.bfloat16)
-            second = jnp.concatenate([halves[1], -halves[0]], axis=1).astype(jnp.bfloat16)
-            right = [right_ref[c, f, :, j].reshape(row_tiles * size, tile) for c in range(2)]
-            product = dot(right[0], first, 1, 0) + dot(right[1], second, 1, 0)
-            places = [(f, i, j) for i in range(row_tiles)]
+            straight = jnp.concatenate(halves, axis=1).astype(jnp.bfloat16)
+            crossed = jnp.concatenate([halves[1], -halves[0]], axis=1).astype(jnp.bfloat16)
+            right = [
+                right_ref[c, f, first:last, j].reshape(row_tiles * size, tile) for c in range(2)
+            ]
+            product = dot(right[0], straight, 1, 0) + dot(right[1], crossed, 1, 0)
+            places = [(f, i, j) for i in range(first, last)]
             projected.append(masked(product, ranks_ref, places, size))
         for i in range(row_tiles):
             straight = [projected[j][i] for j in range(col_tiles)]
             factors = jnp.concatenate(straight + [turned(part) for part in straight])
-            left = left_ref[:, f, i].reshape(2 * col_tiles * size, tile)
+            left = left_ref[:, f, first + i].reshape(2 * col_tiles * size, tile)
             predicted = dot(factors, left, 0, 0)
             for c in range(2):
                 row = c * rhs
@@ -190,45 +220,77 @@
         out_ref[...] = sum_ref[target(me, at, parts)].astype(out_ref.dtype)
 
 
-def predict(ranks, spectrum, green_right, green_left, parts):
-    freqs, row_tiles = ranks.shape[:2]
-    tile = green_left.shape[5]
-    groups = len(spectrum)
-    low = spectrum[0].shape[2]
-    rhs = LANES * groups * low // (green_left.shape[3] * tile)
+def predict(ranks, spectrum, green_right, green_left, parts, tiles):
+    freqs = ranks.shape[0]
+    row_tiles = tiles[1] - tiles[0]
+    col_tiles, size, tile = green_left.shape[3:]
+    reps = len(spectrum)
+    groups, _, _, low, _ = spectrum[0].shape
+    rhs = LANES * reps * groups * low // (col_tiles * tile)
     pairs = freqs * rhs
     sources = row_tiles * tile
     return pl.pallas_call(
-        functools.partial(predict_kernel, groups, parts),
+        functools.partial(predict_kernel, reps, parts, tiles),
         in_specs=[pl.BlockSpec(memory_space=pltpu.SMEM)]
-        + [pl.BlockSpec(memory_space=pltpu.VMEM)] * (2 + groups),
+        + [pl.BlockSpec(memory_space=pltpu.VMEM)] * (2 + reps),
         out_specs=[pl.BlockSpec(memory_space=pltpu.VMEM)] * parts,
         out_shape=[jax.ShapeDtypeStruct((2, pairs // parts, sources), jnp.bfloat16)] * parts,
         scratch_shapes=[
-            pltpu.VMEM((groups,) + spectrum[0].shape, jnp.bfloat16),
+            pltpu.VMEM((reps,) + spectrum[0].shape, jnp.bfloat16),
             pltpu.VMEM((parts, 2, pairs // parts, sources), jnp.float32),
         ],
         compiler_params=pltpu.CompilerParams(vmem_limit_bytes=VMEM_LIMIT),
+        cost_estimate=tile_cost(freqs * row_tiles * col_tiles, size, tile, rhs),
         name="predict",
     )(ranks, green_right, green_left, *spectrum)
 
 
-def back_kernel(parts, groups, reps, ranks_ref, right_ref, left_ref, *refs):
-    misfit_refs, out_refs = refs[:parts], refs[parts : parts + reps]
-    misfit_all_ref, grad_ref = refs[parts + reps :]
+def residual_kernel(column, data_ref, *refs):
+    block_refs, (misfit_ref, residual_ref) = refs[:-2], refs[-2:]
+    observed = data_ref[:, :, column : column + residual_ref.shape[2]]
+    residual = sum(block_ref[...].astype(jnp.float32) for block_ref in block_refs) - observed
+    residual_ref[...] = residual
+    misfit_ref[...] = residual.astype(misfit_ref.dtype)
+
+
+def residual_of(blocks, data, column):
+    shape = blocks[0].shape
+    return pl.pallas_call(
+        functools.partial(residual_kernel, column),
+        in_specs=[pl.BlockSpec(memory_space=pltpu.VMEM)] * (1 + len(blocks)),
+        out_specs=[pl.BlockSpec(memory_space=pltpu.VMEM)] * 2,
+        out_shape=[
+            jax.ShapeDtypeStruct(shape, jnp.bfloat16),
+            jax.ShapeDtypeStruct(shape, jnp.float32),
+        ],
+        compiler_params=pltpu.CompilerParams(vmem_limit_bytes=VMEM_LIMIT),
+        name="residual",
+    )(data, *blocks)
+
+
+def back_kernel(parts, groups, reps, tiles, ranks_ref, right_ref, left_ref, *refs):
+    first, last = tiles
+    _, freqs, row_tiles, col_tiles, size, tile = left_ref.shape
+    carried, final = first > 0, last == row_tiles
+    misfit_refs, refs = refs[:parts], refs[parts:]
+    if carried:
+        carried_ref, refs = refs[0], refs[1:]
     dests = groups * reps
     _, pairs, _ = misfit_refs[0].shape
-    _, freqs, row_tiles, col_tiles, size, tile = left_ref.shape
-    _, _, _, low, lanes = out_refs[0].shape
     rhs = parts * pairs // freqs
-    high = lanes // rhs
-    per_tile = dests // col_tiles
+    if final:
+        out_refs, (misfit_all_ref, grad_ref) = refs[:reps], refs[reps:]
+        _, _, _, low, lanes = out_refs[0].shape
+        high = lanes // rhs
+        per_tile = dests // col_tiles
+    else:
+        carry_ref, misfit_all_ref = refs
     me = lax.axis_index("rtile")
     for at, misfit_ref in enumerate(misfit_refs):
         misfit_all_ref[origin(me, at, parts)] = misfit_ref[...].astype(jnp.float32)
     for f in range(freqs):
         back = []
-        for i in range(row_tiles):
+        for i in range(last - first):
             rows = [
                 jnp.concatenate(
                     [
@@ -238,19 +300,28 @@
                 )
                 for c in range(2)
             ]
-            first = jnp.concatenate(rows).astype(jnp.bfloat16)
-            second = jnp.concatenate([rows[1], -rows[0]]).astype(jnp.bfloat16)
-            left = [left_ref[c, f, i].reshape(col_tiles * size, tile) for c in range(2)]
-            product = dot(left[0], first, 1, 1) + dot(left[1], second, 1, 1)
-            places = [(f, i, j) for j in range(col_tiles)]
+            straight = jnp.concatenate(rows).astype(jnp.bfloat16)
+            crossed = jnp.concatenate([rows[1], -rows[0]]).astype(jnp.bfloat16)
+            left = [left_ref[c, f, first + i].reshape(col_tiles * size, tile) for c in range(2)]
+            product = dot(left[0], straight, 1, 1) + dot(left[1], crossed, 1, 1)
+            places = [(f, first + i, j) for j in range(col_tiles)]
             back.append(masked(product, ranks_ref, places, size))
         for j in range(col_tiles):
-            straight = [back[i][j] for i in range(row_tiles)]
+            straight = [part[j] for part in back]
             factors = jnp.concatenate(straight + [turned(part) for part in straight])
             right = jnp.concatenate(
-                [right_ref[c, f, :, j].reshape(row_tiles * size, tile) for c in range(2)]
+                [
+                    right_ref[c, f, first:last, j].reshape((last - first) * size, tile)
+                    for c in range(2)
+                ]
             )
-            grad = dot(factors, right, 0, 0).T
+            grad = dot(factors, right, 0, 0)
+            if carried:
+                grad = grad + carried_ref[f, j]
+            if not final:
+                carry_ref[f, j] = grad
+                continue
+            grad = grad.T
             for at in range(per_tile):
                 rows = at * high * low
                 for c in range(2):
@@ -261,6 +332,8 @@
                     grad_ref[j * per_tile + at, f, c] = jnp.concatenate(blocks, axis=1).astype(
                         grad_ref.dtype
                     )
+    if not final:
+        return
     me, own = lax.axis_index("freq"), lax.axis_index("rep")
     for at, out_ref in enumerate(out_refs):
         rep = target(own, at, reps)
@@ -268,26 +341,32 @@
             out_ref[step] = grad_ref[target(me, step, groups) * reps + rep]
 
 
-def back_project(ranks, misfit, green_right, green_left, groups, reps):
-    dests = groups * reps
+def back_project(ranks, misfit, green_right, green_left, groups, reps, tiles, carried):
     freqs = ranks.shape[0]
     parts = len(misfit)
     _, pairs, sources = misfit[0].shape
+    row_tiles, col_tiles, size, tile = green_left.shape[2:]
     rhs = parts * pairs // freqs
-    low = green_left.shape[3] * green_left.shape[5] * rhs // (dests * LANES)
+    final = tiles[1] == row_tiles
+    scratch = [pltpu.VMEM((parts, 2, pairs, sources), jnp.float32)]
+    if final:
+        low = col_tiles * tile * rhs // (groups * reps * LANES)
+        block = (freqs, 2, low, LANES)
+        out_shape = [jax.ShapeDtypeStruct((groups,) + block, jnp.bfloat16)] * reps
+        scratch.append(pltpu.VMEM((groups * reps,) + block, jnp.bfloat16))
+    else:
+        out_shape = [jax.ShapeDtypeStruct((freqs, col_tiles, 2 * rhs, tile), jnp.float32)]
     return pl.pallas_call(
-        functools.partial(back_kernel, parts, groups, reps),
+        functools.partial(back_kernel, parts, groups, reps, tiles),
         in_specs=[pl.BlockSpec(memory_space=pltpu.SMEM)]
-        + [pl.BlockSpec(memory_space=pltpu.VMEM)] * (2 + parts),
-        out_specs=[pl.BlockSpec(memory_space=pltpu.VMEM)] * reps,
-        out_shape=[jax.ShapeDtypeStruct((groups, freqs, 2, low, LANES), jnp.bfloat16)] * reps,
-        scratch_shapes=[
-            pltpu.VMEM((parts, 2, pairs, sources), jnp.float32),
-            pltpu.VMEM((dests, freqs, 2, low, LANES), jnp.bfloat16),
-        ],
-        compiler_params=pltpu.CompilerParams(vmem_limit_bytes=VMEM_LIMIT),
+        + [pl.BlockSpec(memory_space=pltpu.VMEM)] * (2 + parts + len(carried)),
+        out_specs=[pl.BlockSpec(memory_space=pltpu.VMEM)] * len(out_shape),
+        out_shape=out_shape,
+        scratch_shapes=scratch,
+        compiler_params=pltpu.CompilerParams(vmem_limit_bytes=VMEM_LIMIT),
+        cost_estimate=tile_cost(freqs * (tiles[1] - tiles[0]) * col_tiles, size, tile, rhs),
         name="back_project",
-    )(ranks, green_right, green_left, *misfit)
+    )(ranks, green_right, green_left, *misfit, *carried)
 
 
 def gather_kernel(reps, *refs):
@@ -374,15 +453,27 @@
     rep_count = lax.axis_size("rep")
     freq_local = ranks.shape[0]
     rhs_count = model.shape[2]
-    table, spectrum = spectrum_of(model[0], freq_count, freq_local)
-    spectrum = exchange(spectrum, "freq")
-    predicted = predict(ranks, spectrum, green_right, green_left, tile_count)
-    arrived = exchange(predicted, "rtile")
-    residual = sum(block.astype(jnp.float32) for block in arrived) - data
-    misfit = exchange([residual.astype(jnp.bfloat16)] * tile_count, "rtile")
-    partial = back_project(ranks, misfit, green_right, green_left, freq_count, rep_count)
+    table, spectrum = spectrum_of(model[0], freq_count, freq_local, rep_count)
+    spectrum = pack(exchange(spectrum, "freq"))
+    spectrum = exchange([spectrum] * rep_count, "rep")
+    row_tiles, _, _, tile = green_left.shape[2:]
+    halves = [(0, row_tiles // 2), (row_tiles // 2, row_tiles)]
+    predicted = [
+        predict(ranks, spectrum, green_right, green_left, tile_count, tiles) for tiles in halves
+    ]
+    arrived = [exchange(blocks, "rtile") for blocks in predicted]
+    pairs = [
+        residual_of(blocks, data, first * tile) for blocks, (first, _) in zip(arrived, halves)
+    ]
+    misfit = [exchange([half] * tile_count, "rtile") for half, _ in pairs]
+    residual = [half for _, half in pairs]
+    partial = []
+    for blocks, tiles in zip(misfit, halves):
+        partial = back_project(
+            ranks, blocks, green_right, green_left, freq_count, rep_count, tiles, partial
+        )
     arrived = exchange(gather(exchange(partial, "rep")), "freq")
-    return (residual, gradient_of(arrived, table, rhs_count))
+    return (jnp.concatenate(residual, axis=2), gradient_of(arrived, table, rhs_count))
 
 
 def solution(mesh):

time: 53.1 us -> 53.7 us (1.011)
  starting transfers between devices: 17 us -> 26.1 us
  waiting for transfers between devices: 20.1 us -> 11.2 us
    ppermute x13 -> x20, starting transfers between devices: 17 us -> 26.1 us  [exchange(): arrived.append(lax.ppermute(blocks[step], axis, pairs))]
    ppermute x13 -> x20, waiting for transfers between devices: 20.1 us -> 11.2 us  [exchange(): arrived.append(lax.ppermute(blocks[step], axis, pairs))]
    pallas_call x2 -> x7, Pallas kernels: 4.65 us -> 7.81 us  [the longest x2 3.9 us: predict(): pl.pallas_call(functools.partial(predict_kernel, reps, parts, tiles), in_...]
    pallas_call x1, Pallas kernels: 7.02 us -> 4.33 us  [spectrum_of(): pl.pallas_call(spectrum_kernel, in_specs=[pl.BlockSpec(memory_space=pltpu...]
    convert_element_type x1 -> x0, other arithmetic: 0.74 us -> none  [shards(): misfit = exchange([residual.astype(jnp.bfloat16)] * tile_count, 'rtile')]
    concatenate x0 -> x1, other arithmetic: none -> 0.69 us  [shards(): jnp.concatenate(residual, axis=2)]
  transfers between devices with their start and end apart: 13 -> 20, of which waited for: 12 -> 9; matrix products, arithmetic and copies ran while one was open for 0% -> 1% of each run, Pallas kernels for 0% -> 7%
where the time goes in v5:
time: 53.7 us; the launch traced here: 53.6 us
  starting transfers between devices  26.1 us (49%)
  Pallas kernels  14.7 us (27%)
  waiting for transfers between devices  11.2 us (21%)
  between operations  0.77 us (1%)
  other arithmetic  0.69 us (1%)
    ppermute x20, starting transfers between devices, exchange(): arrived.append(lax.ppermute(blocks[step], axis, pairs))  26.1 us
    ppermute x20, waiting for transfers between devices, exchange(): arrived.append(lax.ppermute(blocks[step], axis, pairs))  11.2 us
    pallas_call x1, Pallas kernels, spectrum_of(): pl.pallas_call(spectrum_kernel, in_specs=[pl.BlockSpec(memory_space=pltpu...  4.33 us
    pallas_call x2, Pallas kernels, predict(): pl.pallas_call(functools.partial(predict_kernel, reps, parts, tiles), in_...  3.9 us
    pallas_call x2, Pallas kernels, back_project(): pl.pallas_call(functools.partial(back_kernel, parts, groups, reps, tiles)...  3.83 us
    pallas_call x1, Pallas kernels, gradient_of(): pl.pallas_call(gradient_kernel, in_specs=[pl.BlockSpec(memory_space=pltpu...  2.54 us
  transfers between devices with their start and end apart: 20, of which 9 were waited for; matrix products, arithmetic and copies ran while one was open for 1% of the time, Pallas kernels for 7%

profile of v5, /device:TPU:0, one launch (start us, length us, event | category | flops | bytes accessed | tf_op | source)
XLA Modules:
  0.0 53.6 jit_solution(5295550605349455112)
XLA Ops:
  0.6 0.0 copy-start.3
  0.6 0.0 copy-start
  0.7 0.0 copy-start.1
  0.7 4.3 %spectrum.1 = (bf16[24,1024]{1,0:T(8,128)(2,1)S(1)}, bf16[3,2,16,128]{3,2,1,0:T(8,128)(2,1)S(1)}, bf16[3,2,16,128]{3,2,1,0:T(8,128)(2,1)S(1)}, bf16[3,2,16,128]{...) custom-call(bf16[2,4,16,32,1024]{4,3,2,1,0:T(8,128)(2,1)} %bitcast.2), custom_call_target="tpu_custom_call" | custom-call | tf_op jit(solution)/shard_map/spectrum/pallas_call | solution.py:110
  5.0 0.0 copy-start.2
  5.0 3.0 %collective-permute-start = (bf16[3,2,16,128]{3,2,1,0:T(8,128)(2,1)S(1)}, bf16[3,2,16,128]{3,2,1,0:T(8,128)(2,1)S(1)}, u32[]{:S(2)}, u32[]{:S(2)}) collective-permute-start(bf16[3,2,16,128]{3,2,1,0:T(8,128)(2,1)S(1)} %get-tuple-element.26), channel_id=1, source_target_pairs={{0,8},{8,0},{16,24},{24,16},{1,9},{9,1},{17,25},{25,17},{2,10},{10... | collective-permute-start | bytes 73736 | tf_op jit(solution)/shard_map/ppermute | solution.py:62
  8.0 1.5 %collective-permute-start.1 = (bf16[3,2,16,128]{3,2,1,0:T(8,128)(2,1)S(1)}, bf16[3,2,16,128]{3,2,1,0:T(8,128)(2,1)S(1)}, u32[]{:S(2)}, u32[]{:S(2)}) collective-permute-start(bf16[3,2,16,128]{3,2,1,0:T(8,128)(2,1)S(1)} %get-tuple-element.27), channel_id=1, source_target_pairs={{0,16},{8,24},{16,0},{24,8},{1,17},{9,25},{17,1},{25,9},{2,18},{10... | collective-permute-start | bytes 73736 | tf_op jit(solution)/shard_map/ppermute | solution.py:62
  9.5 0.0 collective-permute-start.2
  9.6 0.3 collective-permute-done.refs_1_
  9.8 2.0 %collective-permute-done.1.refs_2_ = bf16[3,2,16,128]{3,2,1,0:T(8,128)(2,1)S(1)} collective-permute-done((bf16[3,2,16,128]{3,2,1,0:T(8,128)(2,1)S(1)}, bf16[3,2,16,128]{3,2,1,0:T(8,128)(2,1)S(1)}, u32[]{:S(2)}, u32[]{:S(2)}) %collective-permute-start.1) | collective-permute-done | bytes 24608 | tf_op jit(solution)/shard_map/ppermute | solution.py:62
  11.8 2.4 %collective-permute-done.2.refs_3_ = bf16[3,2,16,128]{3,2,1,0:T(8,128)(2,1)S(1)} collective-permute-done((bf16[3,2,16,128]{3,2,1,0:T(8,128)(2,1)S(1)}, bf16[3,2,16,128]{3,2,1,0:T(8,128)(2,1)S(1)}, u32[]{:S(2)}, u32[]{:S(2)}) %collective-permute-start.2) | collective-permute-done | bytes 24608 | tf_op jit(solution)/shard_map/ppermute | solution.py:62
  14.3 0.1 collective-permute-start.3
  14.4 0.0 copy-done.3
  14.4 0.1 copy.7.ranks_ref
  14.5 1.2 %collective-permute-done.3.refs_1_ = bf16[4,3,2,16,128]{4,3,2,1,0:T(8,128)(2,1)S(1)} collective-permute-done((bf16[4,3,2,16,128]{4,3,2,1,0:T(8,128)(2,1)S(1)}, bf16[4,3,2,16,128]{4,3,2,1,0:T(8,128)(2,1)S(1)}, u32[]{:S(2)}, u32[]{:S(2)}) %collective-permute-start.3) | collective-permute-done | bytes 98336 | tf_op jit(solution)/shard_map/ppermute | solution.py:62
  15.6 0.0 copy-done
  15.6 0.0 copy-done.1
  15.7 2.0 %predict.2 = (bf16[2,24,512]{2,1,0:T(8,128)(2,1)S(1)}, bf16[2,24,512]{2,1,0:T(8,128)(2,1)S(1)}, bf16[2,24,512]{2,1,0:T(8,128)(2,1)S(1)}, bf16[2,24,512]{2,1,0:T(8,128)(2,1)S(1)}) custom-call(s32[3,4,2]{2,1,0:T(4,128)S(1)} %copy.7.ranks_ref, bf16[2,3,4,2,48,256]{5,4,3,2,1,0:T(8,128)(2,1)S(1)} %copy-done, bf16[2,3,4,2,48,256]{5,4,3,2,1,0:T(8,128)(2,1)S(1)} %copy-done.1, ...), custom_call_target="tpu_custom_call" | custom-call | flops 75497472 | bytes 1179648 | tf_op jit(solution)/shard_map/predict/pallas_call | solution.py:232
  17.6 1.6 %collective-permute-start.4 = (bf16[2,24,512]{2,1,0:T(8,128)(2,1)S(1)}, bf16[2,24,512]{2,1,0:T(8,128)(2,1)S(1)}, u32[]{:S(2)}, u32[]{:S(2)}) collective-permute-start(bf16[2,24,512]{2,1,0:T(8,128)(2,1)S(1)} %get-tuple-element.30), channel_id=1, source_target_pairs={{0,2},{2,0},{4,6},{6,4},{1,3},{3,1},{5,7},{7,5},{8,10},{10,8},{12,... | collective-permute-start | bytes 147464 | tf_op jit(solution)/shard_map/ppermute | solution.py:62
  19.2 2.6 %collective-permute-start.5 = (bf16[2,24,512]{2,1,0:T(8,128)(2,1)S(1)}, bf16[2,24,512]{2,1,0:T(8,128)(2,1)S(1)}, u32[]{:S(2)}, u32[]{:S(2)}) collective-permute-start(bf16[2,24,512]{2,1,0:T(8,128)(2,1)S(1)} %get-tuple-element.31), channel_id=1, source_target_pairs={{0,4},{2,6},{4,0},{6,2},{1,5},{3,7},{5,1},{7,3},{8,12},{10,14},{12... | collective-permute-start | bytes 147464 | tf_op jit(solution)/shard_map/ppermute | solution.py:62
  21.9 0.2 collective-permute-start.6
  22.1 1.9 %predict.3 = (bf16[2,24,512]{2,1,0:T(8,128)(2,1)S(1)}, bf16[2,24,512]{2,1,0:T(8,128)(2,1)S(1)}, bf16[2,24,512]{2,1,0:T(8,128)(2,1)S(1)}, bf16[2,24,512]{2,1,0:T(8,128)(2,1)S(1)}) custom-call(s32[3,4,2]{2,1,0:T(4,128)S(1)} %copy.7.ranks_ref, bf16[2,3,4,2,48,256]{5,4,3,2,1,0:T(8,128)(2,1)S(1)} %copy-done, bf16[2,3,4,2,48,256]{5,4,3,2,1,0:T(8,128)(2,1)S(1)} %copy-done.1, ...), custom_call_target="tpu_custom_call" | custom-call | flops 75497472 | bytes 1179648 | tf_op jit(solution)/shard_map/predict/pallas_call | solution.py:232
  24.0 0.7 %collective-permute-start.7 = (bf16[2,24,512]{2,1,0:T(8,128)(2,1)S(1)}, bf16[2,24,512]{2,1,0:T(8,128)(2,1)S(1)}, u32[]{:S(2)}, u32[]{:S(2)}) collective-permute-start(bf16[2,24,512]{2,1,0:T(8,128)(2,1)S(1)} %get-tuple-element.35), channel_id=1, source_target_pairs={{0,2},{2,0},{4,6},{6,4},{1,3},{3,1},{5,7},{7,5},{8,10},{10,8},{12,... | collective-permute-start | bytes 147464 | tf_op jit(solution)/shard_map/ppermute | solution.py:62
  24.8 3.5 %collective-permute-start.8 = (bf16[2,24,512]{2,1,0:T(8,128)(2,1)S(1)}, bf16[2,24,512]{2,1,0:T(8,128)(2,1)S(1)}, u32[]{:S(2)}, u32[]{:S(2)}) collective-permute-start(bf16[2,24,512]{2,1,0:T(8,128)(2,1)S(1)} %get-tuple-element.36), channel_id=1, source_target_pairs={{0,4},{2,6},{4,0},{6,2},{1,5},{3,7},{5,1},{7,3},{8,12},{10,14},{12... | collective-permute-start | bytes 147464 | tf_op jit(solution)/shard_map/ppermute | solution.py:62
  28.3 0.0 collective-permute-done.4.refs_1_
  28.3 0.2 collective-permute-start.9
  28.5 0.0 collective-permute-done.5.refs_2_
  28.5 0.0 collective-permute-done.6.refs_3_
  28.5 0.0 copy-done.2
  28.5 3.7 %collective-permute-start.15 = (bf16[2,24,512]{2,1,0:T(8,128)(2,1)S(1)}, bf16[2,24,512]{2,1,0:T(8,128)(2,1)S(1)}, u32[]{:S(2)}, u32[]{:S(2)}) collective-permute-start(bf16[2,24,512]{2,1,0:T(8,128)(2,1)S(1)} %get-tuple-element.41.refs_0_), channel_id=1, source_target_pairs={{0,6},{2,4},{4,2},{6,0},{1,7},{3,5},{5,3},{7,1},{8,14},{10,12},{12... | collective-permute-start | bytes 147464 | tf_op jit(solution)/shard_map/ppermute | solution.py:62
  32.2 0.0 collective-permute-start.14
  32.2 0.0 collective-permute-done.7.refs_1_
  32.2 0.8 %collective-permute-start.13 = (bf16[2,24,512]{2,1,0:T(8,128)(2,1)S(1)}, bf16[2,24,512]{2,1,0:T(8,128)(2,1)S(1)}, u32[]{:S(2)}, u32[]{:S(2)}) collective-permute-start(bf16[2,24,512]{2,1,0:T(8,128)(2,1)S(1)} %get-tuple-element.41.refs_0_), channel_id=1, source_target_pairs={{0,2},{2,0},{4,6},{6,4},{1,3},{3,1},{5,7},{7,5},{8,10},{10,8},{12,... | collective-permute-start | bytes 147464 | tf_op jit(solution)/shard_map/ppermute | solution.py:62
  33.0 0.0 collective-permute-done.8.refs_2_
  33.0 1.3 %collective-permute-done.9.refs_3_ = bf16[2,24,512]{2,1,0:T(8,128)(2,1)S(1)} collective-permute-done((bf16[2,24,512]{2,1,0:T(8,128)(2,1)S(1)}, bf16[2,24,512]{2,1,0:T(8,128)(2,1)S(1)}, u32[]{:S(2)}, u32[]{:S(2)}) %collective-permute-start.9) | collective-permute-done | bytes 49184 | tf_op jit(solution)/shard_map/ppermute | solution.py:62
  34.3 2.4 %collective-permute-start.12 = (bf16[2,24,512]{2,1,0:T(8,128)(2,1)S(1)}, bf16[2,24,512]{2,1,0:T(8,128)(2,1)S(1)}, u32[]{:S(2)}, u32[]{:S(2)}) collective-permute-start(bf16[2,24,512]{2,1,0:T(8,128)(2,1)S(1)} %get-tuple-element.40.refs_0_), channel_id=1, source_target_pairs={{0,6},{2,4},{4,2},{6,0},{1,7},{3,5},{5,3},{7,1},{8,14},{10,12},{12... | collective-permute-start | bytes 147464 | tf_op jit(solution)/shard_map/ppermute | solution.py:62
  36.7 0.0 collective-permute-start.11
  36.7 0.0 collective-permute-done.15.refs_3_
  36.7 2.0 %collective-permute-start.10 = (bf16[2,24,512]{2,1,0:T(8,128)(2,1)S(1)}, bf16[2,24,512]{2,1,0:T(8,128)(2,1)S(1)}, u32[]{:S(2)}, u32[]{:S(2)}) collective-permute-start(bf16[2,24,512]{2,1,0:T(8,128)(2,1)S(1)} %get-tuple-element.40.refs_0_), channel_id=1, source_target_pairs={{0,2},{2,0},{4,6},{6,4},{1,3},{3,1},{5,7},{7,5},{8,10},{10,8},{12,... | collective-permute-start | bytes 147464 | tf_op jit(solution)/shard_map/ppermute | solution.py:62
  38.8 0.0 collective-permute-done.14.refs_2_
  38.8 0.0 collective-permute-done.13.refs_1_
  38.8 1.8 %back_project.2.refs_4_ = f32[3,2,64,256]{3,2,1,0:T(8,128)S(1)} custom-call(s32[3,4,2]{2,1,0:T(4,128)S(1)} %copy.7.ranks_ref, bf16[2,3,4,2,48,256]{5,4,3,2,1,0:T(8,128)(2,1)S(1)} %copy-done, bf16[2,3,4,2,48,256]{5,4,3,2,1,0:T(8,128)(2,1)S(1)} %copy-done.1, bf16[2,24,512]{2,1,0:T(8,128)(2,1)S(1)} %get-tuple-element.41.refs_0_, ...), custom_call_target="tpu_custom_call" | custom-call | flops 75497472 | bytes 1179648 | tf_op jit(solution)/shard_map/back_project/pallas_call | solution.py:359
  40.5 0.0 collective-permute-done.12.refs_3_
  40.5 1.2 %collective-permute-done.11.refs_2_ = bf16[2,24,512]{2,1,0:T(8,128)(2,1)S(1)} collective-permute-done((bf16[2,24,512]{2,1,0:T(8,128)(2,1)S(1)}, bf16[2,24,512]{2,1,0:T(8,128)(2,1)S(1)}, u32[]{:S(2)}, u32[]{:S(2)}) %collective-permute-start.11) | collective-permute-done | bytes 49184 | tf_op jit(solution)/shard_map/ppermute | solution.py:62
  41.7 0.0 collective-permute-done.10.refs_1_
  41.7 2.1 %back_project.3 = (bf16[4,3,2,16,128]{4,3,2,1,0:T(8,128)(2,1)S(1)}, bf16[4,3,2,16,128]{4,3,2,1,0:T(8,128)(2,1)S(1)}) custom-call(s32[3,4,2]{2,1,0:T(4,128)S(1)} %copy.7.ranks_ref, bf16[2,3,4,2,48,256]{5,4,3,2,1,0:T(8,128)(2,1)S(1)} %copy-done, bf16[2,3,4,2,48,256]{5,4,3,2,1,0:T(8,128)(2,1)S(1)} %copy-done.1, ...), custom_call_target="tpu_custom_call" | custom-call | flops 75497472 | bytes 1179648 | tf_op jit(solution)/shard_map/back_project/pallas_call | solution.py:359
  43.8 0.1 collective-permute-start.16
  43.9 1.3 %collective-permute-done.16.refs_1_ = bf16[4,3,2,16,128]{4,3,2,1,0:T(8,128)(2,1)S(1)} collective-permute-done((bf16[4,3,2,16,128]{4,3,2,1,0:T(8,128)(2,1)S(1)}, bf16[4,3,2,16,128]{4,3,2,1,0:T(8,128)(2,1)S(1)}, u32[]{:S(2)}, u32[]{:S(2)}) %collective-permute-start.16) | collective-permute-done | bytes 98336 | tf_op jit(solution)/shard_map/ppermute | solution.py:62
  45.2 0.6 %collective-permute-start.17 = (bf16[3,2,16,128]{3,2,1,0:T(8,128)(2,1)S(1)}, bf16[3,2,16,128]{3,2,1,0:T(8,128)(2,1)S(1)}, u32[]{:S(2)}, u32[]{:S(2)}) collective-permute-start(bf16[3,2,16,128]{3,2,1,0:T(8,128)(2,1)S(1)} %get-tuple-element.45), channel_id=1, source_target_pairs={{0,8},{8,0},{16,24},{24,16},{1,9},{9,1},{17,25},{25,17},{2,10},{10... | collective-permute-start | bytes 73736 | tf_op jit(solution)/shard_map/ppermute | solution.py:62
  45.8 0.5 collective-permute-start.18
  46.3 2.5 %collective-permute-start.19 = (bf16[3,2,16,128]{3,2,1,0:T(8,128)(2,1)S(1)}, bf16[3,2,16,128]{3,2,1,0:T(8,128)(2,1)S(1)}, u32[]{:S(2)}, u32[]{:S(2)}) collective-permute-start(bf16[3,2,16,128]{3,2,1,0:T(8,128)(2,1)S(1)} %get-tuple-element.47), channel_id=1, source_target_pairs={{0,24},{8,16},{16,8},{24,0},{1,25},{9,17},{17,9},{25,1},{2,26},{10... | collective-permute-start | bytes 73736 | tf_op jit(solution)/shard_map/ppermute | solution.py:62
  48.8 0.7 %pad_maximum_fusion = f32[2,24,1024]{2,1,0:T(8,128)} fusion(f32[2,24,512]{2,1,0:T(8,128)S(1)} %get-tuple-element.38, f32[2,24,512]{2,1,0:T(8,128)S(1)} %get-tuple-element.33), kind=kLoop, calls=%fused_computation | loop fusion | flops 49152 | bytes 393216 | tf_op jit(solution)/shard_map/concatenate | solution.py:476
  49.4 0.0 collective-permute-done.17.refs_1_
  49.4 0.4 collective-permute-done.18.refs_2_
  49.9 1.2 %collective-permute-done.19.refs_3_ = bf16[3,2,16,128]{3,2,1,0:T(8,128)(2,1)S(1)} collective-permute-done((bf16[3,2,16,128]{3,2,1,0:T(8,128)(2,1)S(1)}, bf16[3,2,16,128]{3,2,1,0:T(8,128)(2,1)S(1)}, u32[]{:S(2)}, u32[]{:S(2)}) %collective-permute-start.19) | collective-permute-done | bytes 24608 | tf_op jit(solution)/shard_map/ppermute | solution.py:62
  51.0 2.5 %gradient.1 = bf16[4,16,32,1024]{3,2,1,0:T(8,128)(2,1)} custom-call(bf16[24,1024]{1,0:T(8,128)(2,1)S(1)} %get-tuple-element.39.table_ref, bf16[3,2,16,128]{3,2,1,0:T(8,128)(2,1)S(1)} %get-tuple-element.44.refs_0_, bf16[3,2,16,128]{3,2,1,0:T(8,128)(2,1)S(1)} %collective-permute-done.17.refs_1_, bf16[3,2,16,128]{3,2,1,0:T(8,128)(2,1)S(1)} %collective-permute-done.18.refs_2_, ...), custom_call_target="tpu_custom_call" | custom-call | tf_op jit(solution)/shard_map/gradient/pallas_call | solution.py:434
  (4 shorter events, 0.1 us)
Async XLA Ops:
  0.6 13.7 %copy-start.3 = (s32[3,4,2]{1,2,0:T(2,128)S(1)}, s32[3,4,2]{1,2,0:T(2,128)}, u32[]{:S(2)}) copy-start(s32[3,4,2]{1,2,0:T(2,128)} %param.8) | copy-start | bytes 292
  0.6 15.0 %copy-start = (bf16[2,3,4,2,48,256]{5,4,3,2,1,0:T(8,128)(2,1)S(1)}, bf16[2,3,4,2,48,256]{5,4,3,2,1,0:T(8,128)(2,1)}, u32[]{:S(2)}) copy-start(bf16[2,3,4,2,48,256]{5,4,3,2,1,0:T(8,128)(2,1)} %right_ref.7) | copy-start | bytes 3538948
  0.7 15.0 %copy-start.1 = (bf16[2,3,4,2,48,256]{5,4,3,2,1,0:T(8,128)(2,1)S(1)}, bf16[2,3,4,2,48,256]{5,4,3,2,1,0:T(8,128)(2,1)}, u32[]{:S(2)}) copy-start(bf16[2,3,4,2,48,256]{5,4,3,2,1,0:T(8,128)(2,1)} %left_ref.7) | copy-start | bytes 3538948
  5.0 23.5 %copy-start.2 = (f32[2,24,1024]{2,1,0:T(8,128)S(1)}, f32[2,24,1024]{2,1,0:T(8,128)}, u32[]{:S(2)}) copy-start(f32[2,24,1024]{2,1,0:T(8,128)} %data_ref.3) | copy-start | bytes 589828
  5.0 4.8 %collective-permute-start = (bf16[3,2,16,128]{3,2,1,0:T(8,128)(2,1)S(1)}, bf16[3,2,16,128]{3,2,1,0:T(8,128)(2,1)S(1)}, u32[]{:S(2)}, u32[]{:S(2)}) collective-permute-start(bf16[3,2,16,128]{3,2,1,0:T(8,128)(2,1)S(1)} %get-tuple-element.26), channel_id=1, source_target_pairs={{0,8},{8,0},{16,24},{24,16},{1,9},{9,1},{17,25},{25,17},{2,10},{10... | collective-permute-start | bytes 73736 | tf_op jit(solution)/shard_map/ppermute | solution.py:62
  8.0 3.8 %collective-permute-start.1 = (bf16[3,2,16,128]{3,2,1,0:T(8,128)(2,1)S(1)}, bf16[3,2,16,128]{3,2,1,0:T(8,128)(2,1)S(1)}, u32[]{:S(2)}, u32[]{:S(2)}) collective-permute-start(bf16[3,2,16,128]{3,2,1,0:T(8,128)(2,1)S(1)} %get-tuple-element.27), channel_id=1, source_target_pairs={{0,16},{8,24},{16,0},{24,8},{1,17},{9,25},{17,1},{25,9},{2,18},{10... | collective-permute-start | bytes 73736 | tf_op jit(solution)/shard_map/ppermute | solution.py:62
  9.5 4.7 %collective-permute-start.2 = (bf16[3,2,16,128]{3,2,1,0:T(8,128)(2,1)S(1)}, bf16[3,2,16,128]{3,2,1,0:T(8,128)(2,1)S(1)}, u32[]{:S(2)}, u32[]{:S(2)}) collective-permute-start(bf16[3,2,16,128]{3,2,1,0:T(8,128)(2,1)S(1)} %get-tuple-element.28), channel_id=1, source_target_pairs={{0,24},{8,16},{16,8},{24,0},{1,25},{9,17},{17,9},{25,1},{2,26},{10... | collective-permute-start | bytes 73736 | tf_op jit(solution)/shard_map/ppermute | solution.py:62
  14.3 1.4 %collective-permute-start.3 = (bf16[4,3,2,16,128]{4,3,2,1,0:T(8,128)(2,1)S(1)}, bf16[4,3,2,16,128]{4,3,2,1,0:T(8,128)(2,1)S(1)}, u32[]{:S(2)}, u32[]{:S(2)}) collective-permute-start(bf16[4,3,2,16,128]{4,3,2,1,0:T(8,128)(2,1)S(1)} %pack.1.refs_0_), channel_id=1, source_target_pairs={{0,1},{1,0},{2,3},{3,2},{4,5},{5,4},{6,7},{7,6},{8,9},{9,8},{10,11... | collective-permute-start | bytes 294920 | tf_op jit(solution)/shard_map/ppermute | solution.py:62
  17.6 10.7 %collective-permute-start.4 = (bf16[2,24,512]{2,1,0:T(8,128)(2,1)S(1)}, bf16[2,24,512]{2,1,0:T(8,128)(2,1)S(1)}, u32[]{:S(2)}, u32[]{:S(2)}) collective-permute-start(bf16[2,24,512]{2,1,0:T(8,128)(2,1)S(1)} %get-tuple-element.30), channel_id=1, source_target_pairs={{0,2},{2,0},{4,6},{6,4},{1,3},{3,1},{5,7},{7,5},{8,10},{10,8},{12,... | collective-permute-start | bytes 147464 | tf_op jit(solution)/shard_map/ppermute | solution.py:62
  19.2 9.2 %collective-permute-start.5 = (bf16[2,24,512]{2,1,0:T(8,128)(2,1)S(1)}, bf16[2,24,512]{2,1,0:T(8,128)(2,1)S(1)}, u32[]{:S(2)}, u32[]{:S(2)}) collective-permute-start(bf16[2,24,512]{2,1,0:T(8,128)(2,1)S(1)} %get-tuple-element.31), channel_id=1, source_target_pairs={{0,4},{2,6},{4,0},{6,2},{1,5},{3,7},{5,1},{7,3},{8,12},{10,14},{12... | collective-permute-start | bytes 147464 | tf_op jit(solution)/shard_map/ppermute | solution.py:62
  21.9 6.6 %collective-permute-start.6 = (bf16[2,24,512]{2,1,0:T(8,128)(2,1)S(1)}, bf16[2,24,512]{2,1,0:T(8,128)(2,1)S(1)}, u32[]{:S(2)}, u32[]{:S(2)}) collective-permute-start(bf16[2,24,512]{2,1,0:T(8,128)(2,1)S(1)} %get-tuple-element.32), channel_id=1, source_target_pairs={{0,6},{2,4},{4,2},{6,0},{1,7},{3,5},{5,3},{7,1},{8,14},{10,12},{12... | collective-permute-start | bytes 147464 | tf_op jit(solution)/shard_map/ppermute | solution.py:62
  24.0 8.2 %collective-permute-start.7 = (bf16[2,24,512]{2,1,0:T(8,128)(2,1)S(1)}, bf16[2,24,512]{2,1,0:T(8,128)(2,1)S(1)}, u32[]{:S(2)}, u32[]{:S(2)}) collective-permute-start(bf16[2,24,512]{2,1,0:T(8,128)(2,1)S(1)} %get-tuple-element.35), channel_id=1, source_target_pairs={{0,2},{2,0},{4,6},{6,4},{1,3},{3,1},{5,7},{7,5},{8,10},{10,8},{12,... | collective-permute-start | bytes 147464 | tf_op jit(solution)/shard_map/ppermute | solution.py:62
  24.8 8.2 %collective-permute-start.8 = (bf16[2,24,512]{2,1,0:T(8,128)(2,1)S(1)}, bf16[2,24,512]{2,1,0:T(8,128)(2,1)S(1)}, u32[]{:S(2)}, u32[]{:S(2)}) collective-permute-start(bf16[2,24,512]{2,1,0:T(8,128)(2,1)S(1)} %get-tuple-element.36), channel_id=1, source_target_pairs={{0,4},{2,6},{4,0},{6,2},{1,5},{3,7},{5,1},{7,3},{8,12},{10,14},{12... | collective-permute-start | bytes 147464 | tf_op jit(solution)/shard_map/ppermute | solution.py:62
  28.3 6.0 %collective-permute-start.9 = (bf16[2,24,512]{2,1,0:T(8,128)(2,1)S(1)}, bf16[2,24,512]{2,1,0:T(8,128)(2,1)S(1)}, u32[]{:S(2)}, u32[]{:S(2)}) collective-permute-start(bf16[2,24,512]{2,1,0:T(8,128)(2,1)S(1)} %get-tuple-element.37), channel_id=1, source_target_pairs={{0,6},{2,4},{4,2},{6,0},{1,7},{3,5},{5,3},{7,1},{8,14},{10,12},{12... | collective-permute-start | bytes 147464 | tf_op jit(solution)/shard_map/ppermute | solution.py:62
  28.5 8.2 %collective-permute-start.15 = (bf16[2,24,512]{2,1,0:T(8,128)(2,1)S(1)}, bf16[2,24,512]{2,1,0:T(8,128)(2,1)S(1)}, u32[]{:S(2)}, u32[]{:S(2)}) collective-permute-start(bf16[2,24,512]{2,1,0:T(8,128)(2,1)S(1)} %get-tuple-element.41.refs_0_), channel_id=1, source_target_pairs={{0,6},{2,4},{4,2},{6,0},{1,7},{3,5},{5,3},{7,1},{8,14},{10,12},{12... | collective-permute-start | bytes 147464 | tf_op jit(solution)/shard_map/ppermute | solution.py:62
  32.2 6.5 %collective-permute-start.14 = (bf16[2,24,512]{2,1,0:T(8,128)(2,1)S(1)}, bf16[2,24,512]{2,1,0:T(8,128)(2,1)S(1)}, u32[]{:S(2)}, u32[]{:S(2)}) collective-permute-start(bf16[2,24,512]{2,1,0:T(8,128)(2,1)S(1)} %get-tuple-element.41.refs_0_), channel_id=1, source_target_pairs={{0,4},{2,6},{4,0},{6,2},{1,5},{3,7},{5,1},{7,3},{8,12},{10,14},{12... | collective-permute-start | bytes 147464 | tf_op jit(solution)/shard_map/ppermute | solution.py:62
  32.2 6.5 %collective-permute-start.13 = (bf16[2,24,512]{2,1,0:T(8,128)(2,1)S(1)}, bf16[2,24,512]{2,1,0:T(8,128)(2,1)S(1)}, u32[]{:S(2)}, u32[]{:S(2)}) collective-permute-start(bf16[2,24,512]{2,1,0:T(8,128)(2,1)S(1)} %get-tuple-element.41.refs_0_), channel_id=1, source_target_pairs={{0,2},{2,0},{4,6},{6,4},{1,3},{3,1},{5,7},{7,5},{8,10},{10,8},{12,... | collective-permute-start | bytes 147464 | tf_op jit(solution)/shard_map/ppermute | solution.py:62
  34.3 6.2 %collective-permute-start.12 = (bf16[2,24,512]{2,1,0:T(8,128)(2,1)S(1)}, bf16[2,24,512]{2,1,0:T(8,128)(2,1)S(1)}, u32[]{:S(2)}, u32[]{:S(2)}) collective-permute-start(bf16[2,24,512]{2,1,0:T(8,128)(2,1)S(1)} %get-tuple-element.40.refs_0_), channel_id=1, source_target_pairs={{0,6},{2,4},{4,2},{6,0},{1,7},{3,5},{5,3},{7,1},{8,14},{10,12},{12... | collective-permute-start | bytes 147464 | tf_op jit(solution)/shard_map/ppermute | solution.py:62
  36.7 5.0 %collective-permute-start.11 = (bf16[2,24,512]{2,1,0:T(8,128)(2,1)S(1)}, bf16[2,24,512]{2,1,0:T(8,128)(2,1)S(1)}, u32[]{:S(2)}, u32[]{:S(2)}) collective-permute-start(bf16[2,24,512]{2,1,0:T(8,128)(2,1)S(1)} %get-tuple-element.40.refs_0_), channel_id=1, source_target_pairs={{0,4},{2,6},{4,0},{6,2},{1,5},{3,7},{5,1},{7,3},{8,12},{10,14},{12... | collective-permute-start | bytes 147464 | tf_op jit(solution)/shard_map/ppermute | solution.py:62
  36.7 5.0 %collective-permute-start.10 = (bf16[2,24,512]{2,1,0:T(8,128)(2,1)S(1)}, bf16[2,24,512]{2,1,0:T(8,128)(2,1)S(1)}, u32[]{:S(2)}, u32[]{:S(2)}) collective-permute-start(bf16[2,24,512]{2,1,0:T(8,128)(2,1)S(1)} %get-tuple-element.40.refs_0_), channel_id=1, source_target_pairs={{0,2},{2,0},{4,6},{6,4},{1,3},{3,1},{5,7},{7,5},{8,10},{10,8},{12,... | collective-permute-start | bytes 147464 | tf_op jit(solution)/shard_map/ppermute | solution.py:62
  43.8 1.4 %collective-permute-start.16 = (bf16[4,3,2,16,128]{4,3,2,1,0:T(8,128)(2,1)S(1)}, bf16[4,3,2,16,128]{4,3,2,1,0:T(8,128)(2,1)S(1)}, u32[]{:S(2)}, u32[]{:S(2)}) collective-permute-start(bf16[4,3,2,16,128]{4,3,2,1,0:T(8,128)(2,1)S(1)} %get-tuple-element.43), channel_id=1, source_target_pairs={{0,1},{1,0},{2,3},{3,2},{4,5},{5,4},{6,7},{7,6},{8,9},{9,8},{10,11... | collective-permute-start | bytes 294920 | tf_op jit(solution)/shard_map/ppermute | solution.py:62
  45.2 4.2 %collective-permute-start.17 = (bf16[3,2,16,128]{3,2,1,0:T(8,128)(2,1)S(1)}, bf16[3,2,16,128]{3,2,1,0:T(8,128)(2,1)S(1)}, u32[]{:S(2)}, u32[]{:S(2)}) collective-permute-start(bf16[3,2,16,128]{3,2,1,0:T(8,128)(2,1)S(1)} %get-tuple-element.45), channel_id=1, source_target_pairs={{0,8},{8,0},{16,24},{24,16},{1,9},{9,1},{17,25},{25,17},{2,10},{10... | collective-permute-start | bytes 73736 | tf_op jit(solution)/shard_map/ppermute | solution.py:62
  45.8 4.1 %collective-permute-start.18 = (bf16[3,2,16,128]{3,2,1,0:T(8,128)(2,1)S(1)}, bf16[3,2,16,128]{3,2,1,0:T(8,128)(2,1)S(1)}, u32[]{:S(2)}, u32[]{:S(2)}) collective-permute-start(bf16[3,2,16,128]{3,2,1,0:T(8,128)(2,1)S(1)} %get-tuple-element.46), channel_id=1, source_target_pairs={{0,16},{8,24},{16,0},{24,8},{1,17},{9,25},{17,1},{25,9},{2,18},{10... | collective-permute-start | bytes 73736 | tf_op jit(solution)/shard_map/ppermute | solution.py:62
  46.3 4.7 %collective-permute-start.19 = (bf16[3,2,16,128]{3,2,1,0:T(8,128)(2,1)S(1)}, bf16[3,2,16,128]{3,2,1,0:T(8,128)(2,1)S(1)}, u32[]{:S(2)}, u32[]{:S(2)}) collective-permute-start(bf16[3,2,16,128]{3,2,1,0:T(8,128)(2,1)S(1)} %get-tuple-element.47), channel_id=1, source_target_pairs={{0,24},{8,16},{16,8},{24,0},{1,25},{9,17},{17,9},{25,1},{2,26},{10... | collective-permute-start | bytes 73736 | tf_op jit(solution)/shard_map/ppermute | solution.py:62

commit v6 on v5

--- a/solution.py
+++ b/solution.py
@@ -56,11 +56,11 @@
 
 def exchange(blocks, axis):
     count = len(blocks)
-    arrived = [blocks[0]]
-    for step in range(1, count):
+    arrived = []
+    for step in range(count - 1, 0, -1):
         pairs = [(me, me ^ step if count & (count - 1) == 0 else (me + step) % count) for me in range(count)]
         arrived.append(lax.ppermute(blocks[step], axis, pairs))
-    return arrived
+    return [blocks[0]] + arrived[::-1]
 
 
 def spectrum_kernel(model_hbm, table_out_ref, *refs):
@@ -77,13 +77,20 @@
     for at in range(chunks):
         rows = pl.ds(at * part, part)
         copies.append(
-            pltpu.make_async_copy(own.at[:, rows], model_ref.at[:, rows], model_sems.at[at])
+            [
+                pltpu.make_async_copy(
+                    own.at[h, rows], model_ref.at[h, rows], model_sems.at[at, h]
+                )
+                for h in range(high)
+            ]
         )
-        copies[-1].start()
+        for copy in copies[-1]:
+            copy.start()
     table = tables(bins, length)
     table_out_ref[...] = table
     for at in range(chunks):
-        copies[at].wait()
+        for copy in copies[at]:
+            copy.wait()
         block = model_ref[:, at * part : (at + 1) * part].reshape(high * part * rhs, length)
         sums = dot(block, table, 1, 1)
         for row in range(part):
@@ -116,7 +123,7 @@
         scratch_shapes=[
             pltpu.VMEM((high, low, rhs, length), model.dtype),
             pltpu.VMEM((low * bins, LANES), jnp.float32),
-            pltpu.SemaphoreType.DMA((chunks,)),
+            pltpu.SemaphoreType.DMA((chunks, high)),
         ],
         compiler_params=pltpu.CompilerParams(vmem_limit_bytes=VMEM_LIMIT),
         name="spectrum",
@@ -151,10 +158,11 @@
     )
 
 
-def masked(product, ranks_ref, places, size):
-    row = lax.broadcasted_iota(jnp.int32, (size, product.shape[1]), 0)
+def masked(product, limits_ref, places, size):
+    columns = product.shape[1]
+    row = lax.broadcasted_iota(jnp.int32, (size, columns), 0)
     kept = [
-        jnp.where(row < ranks_ref[place], product[at * size : (at + 1) * size], 0.0)
+        jnp.where(row < limits_ref[place][:, :columns], product[at * size : (at + 1) * size], 0.0)
         for at, place in enumerate(places)
     ]
     return [part.astype(jnp.bfloat16) for part in kept]
@@ -170,13 +178,11 @@
     return found
 
 
-def predict_kernel(reps, parts, tiles, ranks_ref, right_ref, left_ref, *refs):
+def predict_kernel(reps, parts, limits_ref, right_ref, left_ref, *refs):
     arrived_refs, out_refs = refs[:reps], refs[reps : reps + parts]
     spec_ref, sum_ref = refs[reps + parts :]
     _, groups, freqs, _, low, lanes = spec_ref.shape
-    col_tiles, size, tile = left_ref.shape[3:]
-    first, last = tiles
-    row_tiles = last - first
+    row_tiles, col_tiles, size, tile = left_ref.shape[2:]
     _, pairs, _ = out_refs[0].shape
     own = lax.axis_index("rep")
     for at, arrived_ref in enumerate(arrived_refs):
@@ -197,16 +203,14 @@
                 halves.append(jnp.concatenate(blocks))
             straight = jnp.concatenate(halves, axis=1).astype(jnp.bfloat16)
             crossed = jnp.concatenate([halves[1], -halves[0]], axis=1).astype(jnp.bfloat16)
-            right = [
-                right_ref[c, f, first:last, j].reshape(row_tiles * size, tile) for c in range(2)
-            ]
+            right = [right_ref[c, f, :, j].reshape(row_tiles * size, tile) for c in range(2)]
             product = dot(right[0], straight, 1, 0) + dot(right[1], crossed, 1, 0)
-            places = [(f, i, j) for i in range(first, last)]
-            projected.append(masked(product, ranks_ref, places, size))
+            places = [(f, i, j) for i in range(row_tiles)]
+            projected.append(masked(product, limits_ref, places, size))
         for i in range(row_tiles):
             straight = [projected[j][i] for j in range(col_tiles)]
             factors = jnp.concatenate(straight + [turned(part) for part in straight])
-            left = left_ref[:, f, first + i].reshape(2 * col_tiles * size, tile)
+            left = left_ref[:, f, i].reshape(2 * col_tiles * size, tile)
             predicted = dot(factors, left, 0, 0)
             for c in range(2):
                 row = c * rhs
@@ -220,19 +224,16 @@
         out_ref[...] = sum_ref[target(me, at, parts)].astype(out_ref.dtype)
 
 
-def predict(ranks, spectrum, green_right, green_left, parts, tiles):
-    freqs = ranks.shape[0]
-    row_tiles = tiles[1] - tiles[0]
-    col_tiles, size, tile = green_left.shape[3:]
+def predict(limits, spectrum, green_right, green_left, parts):
+    freqs, row_tiles, col_tiles, size, tile = green_left.shape[1:]
     reps = len(spectrum)
     groups, _, _, low, _ = spectrum[0].shape
     rhs = LANES * reps * groups * low // (col_tiles * tile)
     pairs = freqs * rhs
     sources = row_tiles * tile
     return pl.pallas_call(
-        functools.partial(predict_kernel, reps, parts, tiles),
-        in_specs=[pl.BlockSpec(memory_space=pltpu.SMEM)]
-        + [pl.BlockSpec(memory_space=pltpu.VMEM)] * (2 + reps),
+        functools.partial(predict_kernel, reps, parts),
+        in_specs=[pl.BlockSpec(memory_space=pltpu.VMEM)] * (3 + reps),
         out_specs=[pl.BlockSpec(memory_space=pltpu.VMEM)] * parts,
         out_shape=[jax.ShapeDtypeStruct((2, pairs // parts, sources), jnp.bfloat16)] * parts,
         scratch_shapes=[
@@ -242,21 +243,20 @@
         compiler_params=pltpu.CompilerParams(vmem_limit_bytes=VMEM_LIMIT),
         cost_estimate=tile_cost(freqs * row_tiles * col_tiles, size, tile, rhs),
         name="predict",
-    )(ranks, green_right, green_left, *spectrum)
-
-
-def residual_kernel(column, data_ref, *refs):
+    )(limits, green_right, green_left, *spectrum)
+
+
+def residual_kernel(data_ref, *refs):
     block_refs, (misfit_ref, residual_ref) = refs[:-2], refs[-2:]
-    observed = data_ref[:, :, column : column + residual_ref.shape[2]]
-    residual = sum(block_ref[...].astype(jnp.float32) for block_ref in block_refs) - observed
+    residual = sum(block_ref[...].astype(jnp.float32) for block_ref in block_refs) - data_ref[...]
     residual_ref[...] = residual
     misfit_ref[...] = residual.astype(misfit_ref.dtype)
 
 
-def residual_of(blocks, data, column):
+def residual_of(blocks, data):
     shape = blocks[0].shape
     return pl.pallas_call(
-        functools.partial(residual_kernel, column),
+        residual_kernel,
         in_specs=[pl.BlockSpec(memory_space=pltpu.VMEM)] * (1 + len(blocks)),
         out_specs=[pl.BlockSpec(memory_space=pltpu.VMEM)] * 2,
         out_shape=[
@@ -268,29 +268,21 @@
     )(data, *blocks)
 
 
-def back_kernel(parts, groups, reps, tiles, ranks_ref, right_ref, left_ref, *refs):
-    first, last = tiles
+def back_kernel(parts, groups, reps, limits_ref, right_ref, left_ref, *refs):
+    misfit_refs, out_refs = refs[:parts], refs[parts : parts + reps]
+    misfit_all_ref, grad_ref = refs[parts + reps :]
     _, freqs, row_tiles, col_tiles, size, tile = left_ref.shape
-    carried, final = first > 0, last == row_tiles
-    misfit_refs, refs = refs[:parts], refs[parts:]
-    if carried:
-        carried_ref, refs = refs[0], refs[1:]
-    dests = groups * reps
     _, pairs, _ = misfit_refs[0].shape
     rhs = parts * pairs // freqs
-    if final:
-        out_refs, (misfit_all_ref, grad_ref) = refs[:reps], refs[reps:]
-        _, _, _, low, lanes = out_refs[0].shape
-        high = lanes // rhs
-        per_tile = dests // col_tiles
-    else:
-        carry_ref, misfit_all_ref = refs
+    _, _, _, low, lanes = out_refs[0].shape
+    high = lanes // rhs
+    per_tile = groups * reps // col_tiles
     me = lax.axis_index("rtile")
     for at, misfit_ref in enumerate(misfit_refs):
         misfit_all_ref[origin(me, at, parts)] = misfit_ref[...].astype(jnp.float32)
     for f in range(freqs):
         back = []
-        for i in range(last - first):
+        for i in range(row_tiles):
             rows = [
                 jnp.concatenate(
                     [
@@ -302,26 +294,17 @@
             ]
             straight = jnp.concatenate(rows).astype(jnp.bfloat16)
             crossed = jnp.concatenate([rows[1], -rows[0]]).astype(jnp.bfloat16)
-            left = [left_ref[c, f, first + i].reshape(col_tiles * size, tile) for c in range(2)]
+            left = [left_ref[c, f, i].reshape(col_tiles * size, tile) for c in range(2)]
             product = dot(left[0], straight, 1, 1) + dot(left[1], crossed, 1, 1)
-            places = [(f, first + i, j) for j in range(col_tiles)]
-            back.append(masked(product, ranks_ref, places, size))
+            places = [(f, i, j) for j in range(col_tiles)]
+            back.append(masked(product, limits_ref, places, size))
         for j in range(col_tiles):
             straight = [part[j] for part in back]
             factors = jnp.concatenate(straight + [turned(part) for part in straight])
             right = jnp.concatenate(
-                [
-                    right_ref[c, f, first:last, j].reshape((last - first) * size, tile)
-                    for c in range(2)
-                ]
+                [right_ref[c, f, :, j].reshape(row_tiles * size, tile) for c in range(2)]
             )
-            grad = dot(factors, right, 0, 0)
-            if carried:
-                grad = grad + carried_ref[f, j]
-            if not final:
-                carry_ref[f, j] = grad
-                continue
-            grad = grad.T
+            grad = dot(factors, right, 0, 0).T
             for at in range(per_tile):
                 rows = at * high * low
                 for c in range(2):
@@ -332,8 +315,6 @@
                     grad_ref[j * per_tile + at, f, c] = jnp.concatenate(blocks, axis=1).astype(
                         grad_ref.dtype
                     )
-    if not final:
-        return
     me, own = lax.axis_index("freq"), lax.axis_index("rep")
     for at, out_ref in enumerate(out_refs):
         rep = target(own, at, reps)
@@ -341,32 +322,26 @@
             out_ref[step] = grad_ref[target(me, step, groups) * reps + rep]
 
 
-def back_project(ranks, misfit, green_right, green_left, groups, reps, tiles, carried):
-    freqs = ranks.shape[0]
+def back_project(limits, misfit, green_right, green_left, groups, reps):
     parts = len(misfit)
     _, pairs, sources = misfit[0].shape
-    row_tiles, col_tiles, size, tile = green_left.shape[2:]
+    freqs, row_tiles, col_tiles, size, tile = green_left.shape[1:]
     rhs = parts * pairs // freqs
-    final = tiles[1] == row_tiles
-    scratch = [pltpu.VMEM((parts, 2, pairs, sources), jnp.float32)]
-    if final:
-        low = col_tiles * tile * rhs // (groups * reps * LANES)
-        block = (freqs, 2, low, LANES)
-        out_shape = [jax.ShapeDtypeStruct((groups,) + block, jnp.bfloat16)] * reps
-        scratch.append(pltpu.VMEM((groups * reps,) + block, jnp.bfloat16))
-    else:
-        out_shape = [jax.ShapeDtypeStruct((freqs, col_tiles, 2 * rhs, tile), jnp.float32)]
+    low = col_tiles * tile * rhs // (groups * reps * LANES)
+    block = (freqs, 2, low, LANES)
     return pl.pallas_call(
-        functools.partial(back_kernel, parts, groups, reps, tiles),
-        in_specs=[pl.BlockSpec(memory_space=pltpu.SMEM)]
-        + [pl.BlockSpec(memory_space=pltpu.VMEM)] * (2 + parts + len(carried)),
-        out_specs=[pl.BlockSpec(memory_space=pltpu.VMEM)] * len(out_shape),
-        out_shape=out_shape,
-        scratch_shapes=scratch,
-        compiler_params=pltpu.CompilerParams(vmem_limit_bytes=VMEM_LIMIT),
-        cost_estimate=tile_cost(freqs * (tiles[1] - tiles[0]) * col_tiles, size, tile, rhs),
+        functools.partial(back_kernel, parts, groups, reps),
+        in_specs=[pl.BlockSpec(memory_space=pltpu.VMEM)] * (3 + parts),
+        out_specs=[pl.BlockSpec(memory_space=pltpu.VMEM)] * reps,
+        out_shape=[jax.ShapeDtypeStruct((groups,) + block, jnp.bfloat16)] * reps,
+        scratch_shapes=[
+            pltpu.VMEM((parts, 2, pairs, sources), jnp.float32),
+            pltpu.VMEM((groups * reps,) + block, jnp.bfloat16),
+        ],
+        compiler_params=pltpu.CompilerParams(vmem_limit_bytes=VMEM_LIMIT),
+        cost_estimate=tile_cost(freqs * row_tiles * col_tiles, size, tile, rhs),
         name="back_project",
-    )(ranks, green_right, green_left, *misfit, *carried)
+    )(limits, green_right, green_left, *misfit)
 
 
 def gather_kernel(reps, *refs):
@@ -417,10 +392,13 @@
                 high, rhs, length
             )
         rows = pl.ds(at * part, part)
-        copies.append(
-            pltpu.make_async_copy(out_ref.at[:, rows], out_hbm.at[:, rows], out_sems.at[at])
-        )
-        copies[-1].start()
+        for h in range(high):
+            copies.append(
+                pltpu.make_async_copy(
+                    out_ref.at[h, rows], out_hbm.at[h, rows], out_sems.at[at, h]
+                )
+            )
+            copies[-1].start()
     for copy in copies:
         copy.wait()
 
@@ -439,7 +417,7 @@
         scratch_shapes=[
             pltpu.VMEM(shape, jnp.bfloat16),
             pltpu.VMEM((low * bins, lanes), jnp.float32),
-            pltpu.SemaphoreType.DMA((chunks,)),
+            pltpu.SemaphoreType.DMA((chunks, high)),
         ],
         compiler_params=pltpu.CompilerParams(vmem_limit_bytes=VMEM_LIMIT),
         name="gradient",
@@ -456,24 +434,13 @@
     table, spectrum = spectrum_of(model[0], freq_count, freq_local, rep_count)
     spectrum = pack(exchange(spectrum, "freq"))
     spectrum = exchange([spectrum] * rep_count, "rep")
-    row_tiles, _, _, tile = green_left.shape[2:]
-    halves = [(0, row_tiles // 2), (row_tiles // 2, row_tiles)]
-    predicted = [
-        predict(ranks, spectrum, green_right, green_left, tile_count, tiles) for tiles in halves
-    ]
-    arrived = [exchange(blocks, "rtile") for blocks in predicted]
-    pairs = [
-        residual_of(blocks, data, first * tile) for blocks, (first, _) in zip(arrived, halves)
-    ]
-    misfit = [exchange([half] * tile_count, "rtile") for half, _ in pairs]
-    residual = [half for _, half in pairs]
-    partial = []
-    for blocks, tiles in zip(misfit, halves):
-        partial = back_project(
-            ranks, blocks, green_right, green_left, freq_count, rep_count, tiles, partial
-        )
+    limits = jnp.broadcast_to(ranks[..., None, None], ranks.shape + (1, LANES))
+    predicted = predict(limits, spectrum, green_right, green_left, tile_count)
+    misfit, residual = residual_of(exchange(predicted, "rtile"), data)
+    misfit = exchange([misfit] * tile_count, "rtile")
+    partial = back_project(limits, misfit, green_right, green_left, freq_count, rep_count)
     arrived = exchange(gather(exchange(partial, "rep")), "freq")
-    return (jnp.concatenate(residual, axis=2), gradient_of(arrived, table, rhs_count))
+    return (residual, gradient_of(arrived, table, rhs_count))
 
 
 def solution(mesh):

time: 53.7 us -> 53.3 us (level)
  waiting for transfers between devices: 11.2 us -> 23.9 us
  starting transfers between devices: 26.1 us -> 17.1 us
  Pallas kernels: 14.7 us -> 11.2 us
  other arithmetic: 0.69 us -> 0 us
    ppermute x20 -> x14, waiting for transfers between devices: 11.2 us -> 23.9 us  [exchange(): arrived.append(lax.ppermute(blocks[step], axis, pairs))]
    ppermute x20 -> x14, starting transfers between devices: 26.1 us -> 17.1 us  [exchange(): arrived.append(lax.ppermute(blocks[step], axis, pairs))]
    pallas_call x6 -> x3, Pallas kernels: 7.79 us -> 4.13 us  [the longest x1 1.74 us: predict(): pl.pallas_call(functools.partial(predict_kernel, reps, parts), in_specs=[...]
    concatenate x1 -> x0, other arithmetic: 0.69 us -> none  [shards(): jnp.concatenate(residual, axis=2)]
  transfers between devices with their start and end apart: 20 -> 14, of which waited for: 9 -> 12; matrix products, arithmetic and copies ran while one was open for 1% -> 0% of each run, Pallas kernels for 7% -> 0%
where the time goes in v6:
time: 53.3 us; the launch traced here: 53.2 us
  waiting for transfers between devices  23.9 us (45%)
  starting transfers between devices  17.1 us (32%)
  Pallas kernels  11.2 us (21%)
  between operations  0.76 us (1%)
    ppermute x14, waiting for transfers between devices, exchange(): arrived.append(lax.ppermute(blocks[step], axis, pairs))  23.9 us
    ppermute x14, starting transfers between devices, exchange(): arrived.append(lax.ppermute(blocks[step], axis, pairs))  17.1 us
    pallas_call x1, Pallas kernels, spectrum_of(): pl.pallas_call(spectrum_kernel, in_specs=[pl.BlockSpec(memory_space=pltpu...  4.41 us
    pallas_call x1, Pallas kernels, gradient_of(): pl.pallas_call(gradient_kernel, in_specs=[pl.BlockSpec(memory_space=pltpu...  2.63 us
    pallas_call x1, Pallas kernels, predict(): pl.pallas_call(functools.partial(predict_kernel, reps, parts), in_specs=[...  1.74 us
    pallas_call x1, Pallas kernels, back_project(): pl.pallas_call(functools.partial(back_kernel, parts, groups, reps), in_sp...  1.65 us
  transfers between devices with their start and end apart: 14, of which 12 were waited for; matrix products, arithmetic and copies ran while one was open for 0% of the time, Pallas kernels for 0%

profile of v6, /device:TPU:0, one launch (start us, length us, event | category | flops | bytes accessed | tf_op | source)
XLA Modules:
  0.0 53.2 jit_solution(9942996730029091571)
XLA Ops:
  0.6 0.0 copy-start.3
  0.6 0.0 copy-start
  0.7 0.0 copy-start.1
  0.7 0.0 copy-start.2
  0.7 4.4 %spectrum.1 = (bf16[24,1024]{1,0:T(8,128)(2,1)S(1)}, bf16[3,2,16,128]{3,2,1,0:T(8,128)(2,1)S(1)}, bf16[3,2,16,128]{3,2,1,0:T(8,128)(2,1)S(1)}, bf16[3,2,16,128]{...) custom-call(bf16[2,4,16,32,1024]{4,3,2,1,0:T(8,128)(2,1)} %bitcast.2), custom_call_target="tpu_custom_call" | custom-call | tf_op jit(solution)/shard_map/spectrum/pallas_call | solution.py:117
  5.1 3.0 %collective-permute-start = (bf16[3,2,16,128]{3,2,1,0:T(8,128)(2,1)S(1)}, bf16[3,2,16,128]{3,2,1,0:T(8,128)(2,1)S(1)}, u32[]{:S(2)}, u32[]{:S(2)}) collective-permute-start(bf16[3,2,16,128]{3,2,1,0:T(8,128)(2,1)S(1)} %get-tuple-element.20), channel_id=1, source_target_pairs={{0,8},{8,0},{16,24},{24,16},{1,9},{9,1},{17,25},{25,17},{2,10},{10... | collective-permute-start | bytes 73736 | tf_op jit(solution)/shard_map/ppermute | solution.py:62
  8.1 1.5 %collective-permute-start.1 = (bf16[3,2,16,128]{3,2,1,0:T(8,128)(2,1)S(1)}, bf16[3,2,16,128]{3,2,1,0:T(8,128)(2,1)S(1)}, u32[]{:S(2)}, u32[]{:S(2)}) collective-permute-start(bf16[3,2,16,128]{3,2,1,0:T(8,128)(2,1)S(1)} %get-tuple-element.21), channel_id=1, source_target_pairs={{0,16},{8,24},{16,0},{24,8},{1,17},{9,25},{17,1},{25,9},{2,18},{10... | collective-permute-start | bytes 73736 | tf_op jit(solution)/shard_map/ppermute | solution.py:62
  9.6 0.0 collective-permute-start.2
  9.6 0.3 collective-permute-done.refs_1_
  9.9 2.0 %collective-permute-done.1.refs_2_ = bf16[3,2,16,128]{3,2,1,0:T(8,128)(2,1)S(1)} collective-permute-done((bf16[3,2,16,128]{3,2,1,0:T(8,128)(2,1)S(1)}, bf16[3,2,16,128]{3,2,1,0:T(8,128)(2,1)S(1)}, u32[]{:S(2)}, u32[]{:S(2)}) %collective-permute-start.1) | collective-permute-done | bytes 24608 | tf_op jit(solution)/shard_map/ppermute | solution.py:62
  11.9 2.4 %collective-permute-done.2.refs_3_ = bf16[3,2,16,128]{3,2,1,0:T(8,128)(2,1)S(1)} collective-permute-done((bf16[3,2,16,128]{3,2,1,0:T(8,128)(2,1)S(1)}, bf16[3,2,16,128]{3,2,1,0:T(8,128)(2,1)S(1)}, u32[]{:S(2)}, u32[]{:S(2)}) %collective-permute-start.2) | collective-permute-done | bytes 24608 | tf_op jit(solution)/shard_map/ppermute | solution.py:62
  14.4 0.1 collective-permute-start.3
  14.4 0.0 copy-done.3
  14.4 0.1 copy.7
  14.6 1.2 %collective-permute-done.3.refs_1_ = bf16[4,3,2,16,128]{4,3,2,1,0:T(8,128)(2,1)S(1)} collective-permute-done((bf16[4,3,2,16,128]{4,3,2,1,0:T(8,128)(2,1)S(1)}, bf16[4,3,2,16,128]{4,3,2,1,0:T(8,128)(2,1)S(1)}, u32[]{:S(2)}, u32[]{:S(2)}) %collective-permute-start.3) | collective-permute-done | bytes 98336 | tf_op jit(solution)/shard_map/ppermute | solution.py:62
  15.7 0.1 broadcast_in_dim.2.limits_ref
  15.8 0.0 copy-done
  15.8 0.0 copy-done.1
  15.8 1.7 %predict.1 = (bf16[2,24,1024]{2,1,0:T(8,128)(2,1)S(1)}, bf16[2,24,1024]{2,1,0:T(8,128)(2,1)S(1)}, bf16[2,24,1024]{2,1,0:T(8,128)(2,1)S(1)}, bf16[2,24,1024]{2,1,0:T(8,128)(2,1)S(1)}) custom-call(s32[3,4,2,1,128]{4,3,2,1,0:T(1,128)S(1)} %broadcast_in_dim.2.limits_ref, bf16[2,3,4,2,48,256]{5,4,3,2,1,0:T(8,128)(2,1)S(1)} %copy-done, ...), custom_call_target="tpu_custom_call" | custom-call | flops 150994944 | bytes 2359296 | tf_op jit(solution)/shard_map/predict/pallas_call | solution.py:234
  17.6 1.6 %collective-permute-start.4 = (bf16[2,24,1024]{2,1,0:T(8,128)(2,1)S(1)}, bf16[2,24,1024]{2,1,0:T(8,128)(2,1)S(1)}, u32[]{:S(2)}, u32[]{:S(2)}) collective-permute-start(bf16[2,24,1024]{2,1,0:T(8,128)(2,1)S(1)} %get-tuple-element.24), channel_id=1, source_target_pairs={{0,2},{2,0},{4,6},{6,4},{1,3},{3,1},{5,7},{7,5},{8,10},{10,8},{12,... | collective-permute-start | bytes 294920 | tf_op jit(solution)/shard_map/ppermute | solution.py:62
  19.2 2.6 %collective-permute-start.5 = (bf16[2,24,1024]{2,1,0:T(8,128)(2,1)S(1)}, bf16[2,24,1024]{2,1,0:T(8,128)(2,1)S(1)}, u32[]{:S(2)}, u32[]{:S(2)}) collective-permute-start(bf16[2,24,1024]{2,1,0:T(8,128)(2,1)S(1)} %get-tuple-element.25), channel_id=1, source_target_pairs={{0,4},{2,6},{4,0},{6,2},{1,5},{3,7},{5,1},{7,3},{8,12},{10,14},{12... | collective-permute-start | bytes 294920 | tf_op jit(solution)/shard_map/ppermute | solution.py:62
  21.8 0.2 collective-permute-start.6
  22.0 0.5 collective-permute-done.4.refs_1_
  22.5 7.4 %collective-permute-done.5.refs_2_ = bf16[2,24,1024]{2,1,0:T(8,128)(2,1)S(1)} collective-permute-done((bf16[2,24,1024]{2,1,0:T(8,128)(2,1)S(1)}, bf16[2,24,1024]{2,1,0:T(8,128)(2,1)S(1)}, u32[]{:S(2)}, u32[]{:S(2)}) %collective-permute-start.5) | collective-permute-done | bytes 98336 | tf_op jit(solution)/shard_map/ppermute | solution.py:62
  29.9 0.0 collective-permute-done.6.refs_3_
  29.9 0.0 copy-done.2
  29.9 0.7 %residual.1 = (bf16[2,24,1024]{2,1,0:T(8,128)(2,1)S(1)}, f32[2,24,1024]{2,1,0:T(8,128)}) custom-call(f32[2,24,1024]{2,1,0:T(8,128)S(1)} %copy-done.2, bf16[2,24,1024]{2,1,0:T(8,128)(2,1)S(1)} %get-tuple-element.23.refs_0_, bf16[2,24,1024]{2,1,0:T(8,128)(2,1)S(1)} %collective-permute-done.4.refs_1_, bf16[2,24,1024]{2,1,0:T(8,128)(2,1)S(1)} %collective-permute-done.5.refs_2_, ...), custom_call_target="tpu_custom_call" | custom-call | tf_op jit(solution)/shard_map/residual/pallas_call | solution.py:258
  30.6 2.6 %collective-permute-start.9 = (bf16[2,24,1024]{2,1,0:T(8,128)(2,1)S(1)}, bf16[2,24,1024]{2,1,0:T(8,128)(2,1)S(1)}, u32[]{:S(2)}, u32[]{:S(2)}) collective-permute-start(bf16[2,24,1024]{2,1,0:T(8,128)(2,1)S(1)} %get-tuple-element.29.refs_0_), channel_id=1, source_target_pairs={{0,6},{2,4},{4,2},{6,0},{1,7},{3,5},{5,3},{7,1},{8,14},{10,12},{12... | collective-permute-start | bytes 294920 | tf_op jit(solution)/shard_map/ppermute | solution.py:62
  33.2 0.6 %collective-permute-start.8 = (bf16[2,24,1024]{2,1,0:T(8,128)(2,1)S(1)}, bf16[2,24,1024]{2,1,0:T(8,128)(2,1)S(1)}, u32[]{:S(2)}, u32[]{:S(2)}) collective-permute-start(bf16[2,24,1024]{2,1,0:T(8,128)(2,1)S(1)} %get-tuple-element.29.refs_0_), channel_id=1, source_target_pairs={{0,4},{2,6},{4,0},{6,2},{1,5},{3,7},{5,1},{7,3},{8,12},{10,14},{12... | collective-permute-start | bytes 294920 | tf_op jit(solution)/shard_map/ppermute | solution.py:62
  33.8 1.2 %collective-permute-start.7 = (bf16[2,24,1024]{2,1,0:T(8,128)(2,1)S(1)}, bf16[2,24,1024]{2,1,0:T(8,128)(2,1)S(1)}, u32[]{:S(2)}, u32[]{:S(2)}) collective-permute-start(bf16[2,24,1024]{2,1,0:T(8,128)(2,1)S(1)} %get-tuple-element.29.refs_0_), channel_id=1, source_target_pairs={{0,2},{2,0},{4,6},{6,4},{1,3},{3,1},{5,7},{7,5},{8,10},{10,8},{12,... | collective-permute-start | bytes 294920 | tf_op jit(solution)/shard_map/ppermute | solution.py:62
  35.0 3.1 %collective-permute-done.9.refs_3_ = bf16[2,24,1024]{2,1,0:T(8,128)(2,1)S(1)} collective-permute-done((bf16[2,24,1024]{2,1,0:T(8,128)(2,1)S(1)}, bf16[2,24,1024]{2,1,0:T(8,128)(2,1)S(1)}, u32[]{:S(2)}, u32[]{:S(2)}) %collective-permute-start.9) | collective-permute-done | bytes 98336 | tf_op jit(solution)/shard_map/ppermute | solution.py:62
  38.1 3.6 %collective-permute-done.8.refs_2_ = bf16[2,24,1024]{2,1,0:T(8,128)(2,1)S(1)} collective-permute-done((bf16[2,24,1024]{2,1,0:T(8,128)(2,1)S(1)}, bf16[2,24,1024]{2,1,0:T(8,128)(2,1)S(1)}, u32[]{:S(2)}, u32[]{:S(2)}) %collective-permute-start.8) | collective-permute-done | bytes 98336 | tf_op jit(solution)/shard_map/ppermute | solution.py:62
  41.7 0.0 collective-permute-done.7.refs_1_
  41.7 1.6 %back_project.1 = (bf16[4,3,2,16,128]{4,3,2,1,0:T(8,128)(2,1)S(1)}, bf16[4,3,2,16,128]{4,3,2,1,0:T(8,128)(2,1)S(1)}) custom-call(s32[3,4,2,1,128]{4,3,2,1,0:T(1,128)S(1)} %broadcast_in_dim.2.limits_ref, bf16[2,3,4,2,48,256]{5,4,3,2,1,0:T(8,128)(2,1)S(1)} %copy-done, bf16[2,3,4,2,48,256]{5,4,3,2,1,0:T(8,128)(2,1)S(1)} %copy-done.1, ...), custom_call_target="tpu_custom_call" | custom-call | flops 150994944 | bytes 2359296 | tf_op jit(solution)/shard_map/back_project/pallas_call | solution.py:332
  43.3 0.1 collective-permute-start.10
  43.4 1.3 %collective-permute-done.10.refs_1_ = bf16[4,3,2,16,128]{4,3,2,1,0:T(8,128)(2,1)S(1)} collective-permute-done((bf16[4,3,2,16,128]{4,3,2,1,0:T(8,128)(2,1)S(1)}, bf16[4,3,2,16,128]{4,3,2,1,0:T(8,128)(2,1)S(1)}, u32[]{:S(2)}, u32[]{:S(2)}) %collective-permute-start.10) | collective-permute-done | bytes 98336 | tf_op jit(solution)/shard_map/ppermute | solution.py:62
  44.7 0.6 %collective-permute-start.11 = (bf16[3,2,16,128]{3,2,1,0:T(8,128)(2,1)S(1)}, bf16[3,2,16,128]{3,2,1,0:T(8,128)(2,1)S(1)}, u32[]{:S(2)}, u32[]{:S(2)}) collective-permute-start(bf16[3,2,16,128]{3,2,1,0:T(8,128)(2,1)S(1)} %get-tuple-element.33), channel_id=1, source_target_pairs={{0,8},{8,0},{16,24},{24,16},{1,9},{9,1},{17,25},{25,17},{2,10},{10... | collective-permute-start | bytes 73736 | tf_op jit(solution)/shard_map/ppermute | solution.py:62
  45.3 0.5 collective-permute-start.12
  45.8 2.4 %collective-permute-start.13 = (bf16[3,2,16,128]{3,2,1,0:T(8,128)(2,1)S(1)}, bf16[3,2,16,128]{3,2,1,0:T(8,128)(2,1)S(1)}, u32[]{:S(2)}, u32[]{:S(2)}) collective-permute-start(bf16[3,2,16,128]{3,2,1,0:T(8,128)(2,1)S(1)} %get-tuple-element.35), channel_id=1, source_target_pairs={{0,24},{8,16},{16,8},{24,0},{1,25},{9,17},{17,9},{25,1},{2,26},{10... | collective-permute-start | bytes 73736 | tf_op jit(solution)/shard_map/ppermute | solution.py:62
  48.3 0.3 collective-permute-done.11.refs_1_
  48.6 0.8 %collective-permute-done.12.refs_2_ = bf16[3,2,16,128]{3,2,1,0:T(8,128)(2,1)S(1)} collective-permute-done((bf16[3,2,16,128]{3,2,1,0:T(8,128)(2,1)S(1)}, bf16[3,2,16,128]{3,2,1,0:T(8,128)(2,1)S(1)}, u32[]{:S(2)}, u32[]{:S(2)}) %collective-permute-start.12) | collective-permute-done | bytes 24608 | tf_op jit(solution)/shard_map/ppermute | solution.py:62
  49.4 1.1 %collective-permute-done.13.refs_3_ = bf16[3,2,16,128]{3,2,1,0:T(8,128)(2,1)S(1)} collective-permute-done((bf16[3,2,16,128]{3,2,1,0:T(8,128)(2,1)S(1)}, bf16[3,2,16,128]{3,2,1,0:T(8,128)(2,1)S(1)}, u32[]{:S(2)}, u32[]{:S(2)}) %collective-permute-start.13) | collective-permute-done | bytes 24608 | tf_op jit(solution)/shard_map/ppermute | solution.py:62
  50.6 2.6 %gradient.1 = bf16[4,16,32,1024]{3,2,1,0:T(8,128)(2,1)} custom-call(bf16[24,1024]{1,0:T(8,128)(2,1)S(1)} %get-tuple-element.28.table_ref, bf16[3,2,16,128]{3,2,1,0:T(8,128)(2,1)S(1)} %get-tuple-element.32.refs_0_, bf16[3,2,16,128]{3,2,1,0:T(8,128)(2,1)S(1)} %collective-permute-done.11.refs_1_, bf16[3,2,16,128]{3,2,1,0:T(8,128)(2,1)S(1)} %collective-permute-done.12.refs_2_, ...), custom_call_target="tpu_custom_call" | custom-call | tf_op jit(solution)/shard_map/gradient/pallas_call | solution.py:412
  (2 shorter events, 0.0 us)
Async XLA Ops:
  0.6 13.8 %copy-start.3 = (s32[3,4,2]{1,2,0:T(2,128)S(1)}, s32[3,4,2]{1,2,0:T(2,128)}, u32[]{:S(2)}) copy-start(s32[3,4,2]{1,2,0:T(2,128)} %param.8) | copy-start | bytes 292
  0.6 15.2 %copy-start = (bf16[2,3,4,2,48,256]{5,4,3,2,1,0:T(8,128)(2,1)S(1)}, bf16[2,3,4,2,48,256]{5,4,3,2,1,0:T(8,128)(2,1)}, u32[]{:S(2)}) copy-start(bf16[2,3,4,2,48,256]{5,4,3,2,1,0:T(8,128)(2,1)} %right_ref.3) | copy-start | bytes 3538948
  0.7 15.2 %copy-start.1 = (bf16[2,3,4,2,48,256]{5,4,3,2,1,0:T(8,128)(2,1)S(1)}, bf16[2,3,4,2,48,256]{5,4,3,2,1,0:T(8,128)(2,1)}, u32[]{:S(2)}) copy-start(bf16[2,3,4,2,48,256]{5,4,3,2,1,0:T(8,128)(2,1)} %left_ref.3) | copy-start | bytes 3538948
  0.7 29.2 %copy-start.2 = (f32[2,24,1024]{2,1,0:T(8,128)S(1)}, f32[2,24,1024]{2,1,0:T(8,128)}, u32[]{:S(2)}) copy-start(f32[2,24,1024]{2,1,0:T(8,128)} %data_ref.1) | copy-start | bytes 589828
  5.1 4.8 %collective-permute-start = (bf16[3,2,16,128]{3,2,1,0:T(8,128)(2,1)S(1)}, bf16[3,2,16,128]{3,2,1,0:T(8,128)(2,1)S(1)}, u32[]{:S(2)}, u32[]{:S(2)}) collective-permute-start(bf16[3,2,16,128]{3,2,1,0:T(8,128)(2,1)S(1)} %get-tuple-element.20), channel_id=1, source_target_pairs={{0,8},{8,0},{16,24},{24,16},{1,9},{9,1},{17,25},{25,17},{2,10},{10... | collective-permute-start | bytes 73736 | tf_op jit(solution)/shard_map/ppermute | solution.py:62
  8.1 3.8 %collective-permute-start.1 = (bf16[3,2,16,128]{3,2,1,0:T(8,128)(2,1)S(1)}, bf16[3,2,16,128]{3,2,1,0:T(8,128)(2,1)S(1)}, u32[]{:S(2)}, u32[]{:S(2)}) collective-permute-start(bf16[3,2,16,128]{3,2,1,0:T(8,128)(2,1)S(1)} %get-tuple-element.21), channel_id=1, source_target_pairs={{0,16},{8,24},{16,0},{24,8},{1,17},{9,25},{17,1},{25,9},{2,18},{10... | collective-permute-start | bytes 73736 | tf_op jit(solution)/shard_map/ppermute | solution.py:62
  9.6 4.7 %collective-permute-start.2 = (bf16[3,2,16,128]{3,2,1,0:T(8,128)(2,1)S(1)}, bf16[3,2,16,128]{3,2,1,0:T(8,128)(2,1)S(1)}, u32[]{:S(2)}, u32[]{:S(2)}) collective-permute-start(bf16[3,2,16,128]{3,2,1,0:T(8,128)(2,1)S(1)} %get-tuple-element.22), channel_id=1, source_target_pairs={{0,24},{8,16},{16,8},{24,0},{1,25},{9,17},{17,9},{25,1},{2,26},{10... | collective-permute-start | bytes 73736 | tf_op jit(solution)/shard_map/ppermute | solution.py:62
  14.4 1.4 %collective-permute-start.3 = (bf16[4,3,2,16,128]{4,3,2,1,0:T(8,128)(2,1)S(1)}, bf16[4,3,2,16,128]{4,3,2,1,0:T(8,128)(2,1)S(1)}, u32[]{:S(2)}, u32[]{:S(2)}) collective-permute-start(bf16[4,3,2,16,128]{4,3,2,1,0:T(8,128)(2,1)S(1)} %pack.1.refs_0_), channel_id=1, source_target_pairs={{0,1},{1,0},{2,3},{3,2},{4,5},{5,4},{6,7},{7,6},{8,9},{9,8},{10,11... | collective-permute-start | bytes 294920 | tf_op jit(solution)/shard_map/ppermute | solution.py:62
  17.6 4.9 %collective-permute-start.4 = (bf16[2,24,1024]{2,1,0:T(8,128)(2,1)S(1)}, bf16[2,24,1024]{2,1,0:T(8,128)(2,1)S(1)}, u32[]{:S(2)}, u32[]{:S(2)}) collective-permute-start(bf16[2,24,1024]{2,1,0:T(8,128)(2,1)S(1)} %get-tuple-element.24), channel_id=1, source_target_pairs={{0,2},{2,0},{4,6},{6,4},{1,3},{3,1},{5,7},{7,5},{8,10},{10,8},{12,... | collective-permute-start | bytes 294920 | tf_op jit(solution)/shard_map/ppermute | solution.py:62
  19.2 10.7 %collective-permute-start.5 = (bf16[2,24,1024]{2,1,0:T(8,128)(2,1)S(1)}, bf16[2,24,1024]{2,1,0:T(8,128)(2,1)S(1)}, u32[]{:S(2)}, u32[]{:S(2)}) collective-permute-start(bf16[2,24,1024]{2,1,0:T(8,128)(2,1)S(1)} %get-tuple-element.25), channel_id=1, source_target_pairs={{0,4},{2,6},{4,0},{6,2},{1,5},{3,7},{5,1},{7,3},{8,12},{10,14},{12... | collective-permute-start | bytes 294920 | tf_op jit(solution)/shard_map/ppermute | solution.py:62
  21.8 8.0 %collective-permute-start.6 = (bf16[2,24,1024]{2,1,0:T(8,128)(2,1)S(1)}, bf16[2,24,1024]{2,1,0:T(8,128)(2,1)S(1)}, u32[]{:S(2)}, u32[]{:S(2)}) collective-permute-start(bf16[2,24,1024]{2,1,0:T(8,128)(2,1)S(1)} %get-tuple-element.26), channel_id=1, source_target_pairs={{0,6},{2,4},{4,2},{6,0},{1,7},{3,5},{5,3},{7,1},{8,14},{10,12},{12... | collective-permute-start | bytes 294920 | tf_op jit(solution)/shard_map/ppermute | solution.py:62
  30.6 7.5 %collective-permute-start.9 = (bf16[2,24,1024]{2,1,0:T(8,128)(2,1)S(1)}, bf16[2,24,1024]{2,1,0:T(8,128)(2,1)S(1)}, u32[]{:S(2)}, u32[]{:S(2)}) collective-permute-start(bf16[2,24,1024]{2,1,0:T(8,128)(2,1)S(1)} %get-tuple-element.29.refs_0_), channel_id=1, source_target_pairs={{0,6},{2,4},{4,2},{6,0},{1,7},{3,5},{5,3},{7,1},{8,14},{10,12},{12... | collective-permute-start | bytes 294920 | tf_op jit(solution)/shard_map/ppermute | solution.py:62
  33.2 8.4 %collective-permute-start.8 = (bf16[2,24,1024]{2,1,0:T(8,128)(2,1)S(1)}, bf16[2,24,1024]{2,1,0:T(8,128)(2,1)S(1)}, u32[]{:S(2)}, u32[]{:S(2)}) collective-permute-start(bf16[2,24,1024]{2,1,0:T(8,128)(2,1)S(1)} %get-tuple-element.29.refs_0_), channel_id=1, source_target_pairs={{0,4},{2,6},{4,0},{6,2},{1,5},{3,7},{5,1},{7,3},{8,12},{10,14},{12... | collective-permute-start | bytes 294920 | tf_op jit(solution)/shard_map/ppermute | solution.py:62
  33.8 7.8 %collective-permute-start.7 = (bf16[2,24,1024]{2,1,0:T(8,128)(2,1)S(1)}, bf16[2,24,1024]{2,1,0:T(8,128)(2,1)S(1)}, u32[]{:S(2)}, u32[]{:S(2)}) collective-permute-start(bf16[2,24,1024]{2,1,0:T(8,128)(2,1)S(1)} %get-tuple-element.29.refs_0_), channel_id=1, source_target_pairs={{0,2},{2,0},{4,6},{6,4},{1,3},{3,1},{5,7},{7,5},{8,10},{10,8},{12,... | collective-permute-start | bytes 294920 | tf_op jit(solution)/shard_map/ppermute | solution.py:62
  43.3 1.4 %collective-permute-start.10 = (bf16[4,3,2,16,128]{4,3,2,1,0:T(8,128)(2,1)S(1)}, bf16[4,3,2,16,128]{4,3,2,1,0:T(8,128)(2,1)S(1)}, u32[]{:S(2)}, u32[]{:S(2)}) collective-permute-start(bf16[4,3,2,16,128]{4,3,2,1,0:T(8,128)(2,1)S(1)} %get-tuple-element.31), channel_id=1, source_target_pairs={{0,1},{1,0},{2,3},{3,2},{4,5},{5,4},{6,7},{7,6},{8,9},{9,8},{10,11... | collective-permute-start | bytes 294920 | tf_op jit(solution)/shard_map/ppermute | solution.py:62
  44.7 3.9 %collective-permute-start.11 = (bf16[3,2,16,128]{3,2,1,0:T(8,128)(2,1)S(1)}, bf16[3,2,16,128]{3,2,1,0:T(8,128)(2,1)S(1)}, u32[]{:S(2)}, u32[]{:S(2)}) collective-permute-start(bf16[3,2,16,128]{3,2,1,0:T(8,128)(2,1)S(1)} %get-tuple-element.33), channel_id=1, source_target_pairs={{0,8},{8,0},{16,24},{24,16},{1,9},{9,1},{17,25},{25,17},{2,10},{10... | collective-permute-start | bytes 73736 | tf_op jit(solution)/shard_map/ppermute | solution.py:62
  45.3 4.1 %collective-permute-start.12 = (bf16[3,2,16,128]{3,2,1,0:T(8,128)(2,1)S(1)}, bf16[3,2,16,128]{3,2,1,0:T(8,128)(2,1)S(1)}, u32[]{:S(2)}, u32[]{:S(2)}) collective-permute-start(bf16[3,2,16,128]{3,2,1,0:T(8,128)(2,1)S(1)} %get-tuple-element.34), channel_id=1, source_target_pairs={{0,16},{8,24},{16,0},{24,8},{1,17},{9,25},{17,1},{25,9},{2,18},{10... | collective-permute-start | bytes 73736 | tf_op jit(solution)/shard_map/ppermute | solution.py:62
  45.8 4.7 %collective-permute-start.13 = (bf16[3,2,16,128]{3,2,1,0:T(8,128)(2,1)S(1)}, bf16[3,2,16,128]{3,2,1,0:T(8,128)(2,1)S(1)}, u32[]{:S(2)}, u32[]{:S(2)}) collective-permute-start(bf16[3,2,16,128]{3,2,1,0:T(8,128)(2,1)S(1)} %get-tuple-element.35), channel_id=1, source_target_pairs={{0,24},{8,16},{16,8},{24,0},{1,25},{9,17},{17,9},{25,1},{2,26},{10... | collective-permute-start | bytes 73736 | tf_op jit(solution)/shard_map/ppermute | solution.py:62

commit v7 on v6

--- a/solution.py
+++ b/solution.py
@@ -68,7 +68,7 @@
     model_ref, rows_ref, model_sems = refs[-3:]
     high, low, rhs, length = model_ref.shape
     dests = len(out_refs)
-    freqs = out_refs[0].shape[0]
+    freqs, _, _, lanes = out_refs[0].shape
     bins = 2 * dests * freqs
     chunks = model_sems.shape[0]
     part = low // chunks
@@ -91,14 +91,15 @@
     for at in range(chunks):
         for copy in copies[at]:
             copy.wait()
-        block = model_ref[:, at * part : (at + 1) * part].reshape(high * part * rhs, length)
-        sums = dot(block, table, 1, 1)
-        for row in range(part):
-            mine = jnp.concatenate(
-                [sums[(h * part + row) * rhs : (h * part + row + 1) * rhs] for h in range(high)]
+        for start in range(at * part, (at + 1) * part, 2):
+            width = min(2, (at + 1) * part - start)
+            block = jnp.concatenate(
+                [model_ref[:, start + row].reshape(lanes, length) for row in range(width)]
             )
-            place = (at * part + row) * bins
-            rows_ref[place : place + bins] = mine.T
+            sums = dot(table, block, 1, 1)
+            for row in range(width):
+                place = (start + row) * bins
+                rows_ref[place : place + bins] = sums[:, row * lanes : (row + 1) * lanes]
     me = lax.axis_index("freq")
     for at, out_ref in enumerate(out_refs):
         dest = target(me, at, dests)
@@ -198,7 +199,9 @@
                 blocks = []
                 for g in range(j * per_tile, (j + 1) * per_tile):
                     for rep in range(reps):
-                        got = spec_ref[rep, g, f, c].astype(jnp.float32)
+                        got = spec_ref[rep, g, f, c]
+                        if low % 16:
+                            got = got.astype(jnp.float32)
                         blocks += [got[:, h * rhs : (h + 1) * rhs] for h in range(high)]
                 halves.append(jnp.concatenate(blocks))
             straight = jnp.concatenate(halves, axis=1).astype(jnp.bfloat16)
@@ -247,9 +250,10 @@
 
 
 def residual_kernel(data_ref, *refs):
-    block_refs, (misfit_ref, residual_ref) = refs[:-2], refs[-2:]
+    block_refs, (misfit_ref, *part_refs) = refs[:-3], refs[-3:]
     residual = sum(block_ref[...].astype(jnp.float32) for block_ref in block_refs) - data_ref[...]
-    residual_ref[...] = residual
+    for c, part_ref in enumerate(part_refs):
+        part_ref[...] = residual[c]
     misfit_ref[...] = residual.astype(misfit_ref.dtype)
 
 
@@ -258,10 +262,11 @@
     return pl.pallas_call(
         residual_kernel,
         in_specs=[pl.BlockSpec(memory_space=pltpu.VMEM)] * (1 + len(blocks)),
-        out_specs=[pl.BlockSpec(memory_space=pltpu.VMEM)] * 2,
+        out_specs=[pl.BlockSpec(memory_space=pltpu.VMEM)] * 3,
         out_shape=[
             jax.ShapeDtypeStruct(shape, jnp.bfloat16),
-            jax.ShapeDtypeStruct(shape, jnp.float32),
+            jax.ShapeDtypeStruct(shape[1:], jnp.float32),
+            jax.ShapeDtypeStruct(shape[1:], jnp.float32),
         ],
         compiler_params=pltpu.CompilerParams(vmem_limit_bytes=VMEM_LIMIT),
         name="residual",
@@ -304,7 +309,8 @@
             right = jnp.concatenate(
                 [right_ref[c, f, :, j].reshape(row_tiles * size, tile) for c in range(2)]
             )
-            grad = dot(factors, right, 0, 0).T
+            grad = dot(factors, right, 0, 0)
+            grad = (grad if low % 16 else grad.astype(out_refs[0].dtype)).T
             for at in range(per_tile):
                 rows = at * high * low
                 for c in range(2):
@@ -344,41 +350,81 @@
     )(limits, green_right, green_left, *misfit)
 
 
-def gather_kernel(reps, *refs):
+def gather_kernel(picks, reps, *refs):
     part_refs, out_refs = refs[:reps], refs[reps:]
-    for step, out_ref in enumerate(out_refs):
-        total = sum(part_ref[step].astype(jnp.float32) for part_ref in part_refs)
-        out_ref[...] = total.astype(out_ref.dtype)
-
-
-def gather(parts):
-    shape = parts[0].shape
+    for steps, out_ref in zip(picks, out_refs):
+        for at, step in enumerate(steps):
+            total = sum(part_ref[step].astype(jnp.float32) for part_ref in part_refs)
+            out_ref[at] = total.astype(out_ref.dtype)
+
+
+def gather(parts, picks):
+    shape = parts[0].shape[1:]
     return pl.pallas_call(
-        functools.partial(gather_kernel, len(parts)),
+        functools.partial(gather_kernel, picks, len(parts)),
         in_specs=[pl.BlockSpec(memory_space=pltpu.VMEM)] * len(parts),
-        out_specs=[pl.BlockSpec(memory_space=pltpu.VMEM)] * shape[0],
-        out_shape=[jax.ShapeDtypeStruct(shape[1:], jnp.bfloat16)] * shape[0],
+        out_specs=[pl.BlockSpec(memory_space=pltpu.VMEM)] * len(picks),
+        out_shape=[
+            jax.ShapeDtypeStruct((len(steps),) + shape, jnp.bfloat16) for steps in picks
+        ],
         compiler_params=pltpu.CompilerParams(vmem_limit_bytes=VMEM_LIMIT),
         name="gather",
     )(*parts)
 
 
-def gradient_kernel(table_ref, *refs):
-    part_refs = refs[:-4]
-    out_hbm, out_ref, rows_ref, out_sems = refs[-4:]
-    groups = len(part_refs)
-    freqs, _, low, lanes = part_refs[0].shape
+def select_kernel(picks, *refs):
+    *block_refs, out_ref = refs
+    for at, (array, place) in enumerate(picks):
+        out_ref[at] = block_refs[array][place]
+
+
+def select(arrays, picks):
+    shape = (len(picks),) + arrays[0].shape[1:]
+    return pl.pallas_call(
+        functools.partial(select_kernel, picks),
+        in_specs=[pl.BlockSpec(memory_space=pltpu.VMEM)] * len(arrays),
+        out_specs=pl.BlockSpec(memory_space=pltpu.VMEM),
+        out_shape=jax.ShapeDtypeStruct(shape, arrays[0].dtype),
+        compiler_params=pltpu.CompilerParams(vmem_limit_bytes=VMEM_LIMIT),
+        name="select",
+    )(*arrays)
+
+
+def return_spectra(parts, axis):
+    count = parts[0].shape[0]
+    if count & (count - 1):
+        blocks = exchange(gather(parts, [[step] for step in range(count)]), axis)
+        return select(blocks, [(step, 0) for step in range(count)])
+    sent, kept = [[step for step in range(count) if step & 1 == bit] for bit in (1, 0)]
+    message, own = gather(parts, [sent, kept])
+    arrays = [own]
+    held = {(0, step): (0, at) for at, step in enumerate(kept)}
+    leaving = [(0, step) for step in sent]
+    bit = 1
+    while bit < count:
+        if bit > 1:
+            leaving = sorted(key for key in held if key[1] & bit)
+            message = select(arrays, [held.pop(key) for key in leaving])
+        arrays.append(lax.ppermute(message, axis, [(me, me ^ bit) for me in range(count)]))
+        for at, (source, step) in enumerate(leaving):
+            held[source ^ bit, step ^ bit] = (len(arrays) - 1, at)
+        bit *= 2
+    return select(arrays, [held[source, 0] for source in range(count)])
+
+
+def gradient_kernel(table_ref, parts_ref, out_hbm, out_ref, rows_ref, out_sems):
+    groups, freqs, _, low, lanes = parts_ref.shape
     high, _, rhs, length = out_ref.shape
     bins = table_ref.shape[0]
     chunks = out_sems.shape[0]
     part = low // chunks
     me = lax.axis_index("freq")
-    for at, part_ref in enumerate(part_refs):
+    for at in range(groups):
         g = origin(me, at, groups)
         for f in range(freqs):
             for c in range(2):
                 rows = pl.ds(c * groups * freqs + g * freqs + f, low, stride=bins)
-                rows_ref[rows, :] = part_ref[f, c].astype(jnp.float32)
+                rows_ref[rows, :] = parts_ref[at, f, c].astype(jnp.float32)
     table = table_ref[...]
     copies = []
     for at in range(chunks):
@@ -404,14 +450,14 @@
 
 
 def gradient_of(parts, table, rhs):
-    freqs, _, low, lanes = parts[0].shape
+    _, _, _, low, lanes = parts.shape
     bins, length = table.shape
     high = lanes // rhs
     chunks = math.gcd(low, 4)
     shape = (high, low, rhs, length)
     out = pl.pallas_call(
         gradient_kernel,
-        in_specs=[pl.BlockSpec(memory_space=pltpu.VMEM)] * (1 + len(parts)),
+        in_specs=[pl.BlockSpec(memory_space=pltpu.VMEM)] * 2,
         out_specs=pl.BlockSpec(memory_space=pltpu.HBM),
         out_shape=jax.ShapeDtypeStruct(shape, jnp.bfloat16),
         scratch_shapes=[
@@ -421,7 +467,7 @@
         ],
         compiler_params=pltpu.CompilerParams(vmem_limit_bytes=VMEM_LIMIT),
         name="gradient",
-    )(table, *parts)
+    )(table, parts)
     return out.reshape(1, high * low, rhs, length)
 
 
@@ -436,11 +482,11 @@
     spectrum = exchange([spectrum] * rep_count, "rep")
     limits = jnp.broadcast_to(ranks[..., None, None], ranks.shape + (1, LANES))
     predicted = predict(limits, spectrum, green_right, green_left, tile_count)
-    misfit, residual = residual_of(exchange(predicted, "rtile"), data)
+    misfit, *residual = residual_of(exchange(predicted, "rtile")[::-1], data)
     misfit = exchange([misfit] * tile_count, "rtile")
     partial = back_project(limits, misfit, green_right, green_left, freq_count, rep_count)
-    arrived = exchange(gather(exchange(partial, "rep")), "freq")
-    return (residual, gradient_of(arrived, table, rhs_count))
+    arrived = return_spectra(exchange(partial, "rep"), "freq")
+    return (jnp.stack(residual), gradient_of(arrived, table, rhs_count))
 
 
 def solution(mesh):

time: 53.3 us -> 53.7 us (level)
  waiting for transfers between devices: 23.9 us -> 27.9 us
  starting transfers between devices: 17.1 us -> 14.7 us
  Pallas kernels: 11.2 us -> 9.22 us
  other arithmetic: 0 us -> 0.69 us
    ppermute x0 -> x2, waiting for transfers between devices: none -> 6.44 us  [return_spectra(): lax.ppermute(message, axis, [(me, me ^ bit) for me in range(count)])]
    ppermute x14 -> x11, starting transfers between devices: 17.1 us -> 13.6 us  [exchange(): arrived.append(lax.ppermute(blocks[step], axis, pairs))]
    ppermute x14 -> x11, waiting for transfers between devices: 23.9 us -> 21.5 us  [exchange(): arrived.append(lax.ppermute(blocks[step], axis, pairs))]
    pallas_call x1, Pallas kernels: 4.41 us -> 3.2 us  [spectrum_of(): pl.pallas_call(spectrum_kernel, in_specs=[pl.BlockSpec(memory_space=pltpu...]
    ppermute x0 -> x2, starting transfers between devices: none -> 1.11 us  [return_spectra(): lax.ppermute(message, axis, [(me, me ^ bit) for me in range(count)])]
    another operation x0 -> x1, other arithmetic: none -> 0.69 us  [shards(): return (jnp.stack(residual), gradient_of(arrived, table, rhs_count))]
    pallas_call x1, Pallas kernels: 0.74 us -> 0.06 us  [residual_of(): pl.pallas_call(residual_kernel, in_specs=[pl.BlockSpec(memory_space=pltpu...]
  transfers between devices with their start and end apart: 14 -> 13, of which waited for: 12 -> 11; matrix products, arithmetic and copies ran while one was open for 0% -> 1% of each run, Pallas kernels for 0% -> 0%
where the time goes in v7:
time: 53.7 us; the launch traced here: 53.5 us
  waiting for transfers between devices  27.9 us (52%)
  starting transfers between devices  14.7 us (27%)
  Pallas kernels  9.22 us (17%)
  between operations  0.76 us (1%)
  other arithmetic  0.69 us (1%)
    ppermute x11, waiting for transfers between devices, exchange(): arrived.append(lax.ppermute(blocks[step], axis, pairs))  21.5 us
    ppermute x11, starting transfers between devices, exchange(): arrived.append(lax.ppermute(blocks[step], axis, pairs))  13.6 us
    ppermute x2, waiting for transfers between devices, return_spectra(): lax.ppermute(message, axis, [(me, me ^ bit) for me in range(count)])  6.44 us
    pallas_call x1, Pallas kernels, spectrum_of(): pl.pallas_call(spectrum_kernel, in_specs=[pl.BlockSpec(memory_space=pltpu...  3.2 us
    pallas_call x1, Pallas kernels, gradient_of(): pl.pallas_call(gradient_kernel, in_specs=[pl.BlockSpec(memory_space=pltpu...  2.63 us
    pallas_call x1, Pallas kernels, predict(): pl.pallas_call(functools.partial(predict_kernel, reps, parts), in_specs=[...  1.75 us
    pallas_call x1, Pallas kernels, back_project(): pl.pallas_call(functools.partial(back_kernel, parts, groups, reps), in_sp...  1.52 us
    ppermute x2, starting transfers between devices, return_spectra(): lax.ppermute(message, axis, [(me, me ^ bit) for me in range(count)])  1.11 us
  transfers between devices with their start and end apart: 13, of which 11 were waited for; matrix products, arithmetic and copies ran while one was open for 1% of the time, Pallas kernels for 0%

profile of v7, /device:TPU:0, one launch (start us, length us, event | category | flops | bytes accessed | tf_op | source)
XLA Modules:
  0.0 53.5 jit_solution(15074984199311283364)
XLA Ops:
  0.6 0.0 copy-start.3
  0.6 0.0 copy-start
  0.7 0.0 copy-start.1
  0.7 0.0 copy-start.2
  0.7 3.2 %spectrum.1 = (bf16[24,1024]{1,0:T(8,128)(2,1)S(1)}, bf16[3,2,16,128]{3,2,1,0:T(8,128)(2,1)S(1)}, bf16[3,2,16,128]{3,2,1,0:T(8,128)(2,1)S(1)}, bf16[3,2,16,128]{...) custom-call(bf16[2,4,16,32,1024]{4,3,2,1,0:T(8,128)(2,1)} %bitcast.6), custom_call_target="tpu_custom_call" | custom-call | tf_op jit(solution)/shard_map/spectrum/pallas_call | solution.py:118
  3.9 3.0 %collective-permute-start = (bf16[3,2,16,128]{3,2,1,0:T(8,128)(2,1)S(1)}, bf16[3,2,16,128]{3,2,1,0:T(8,128)(2,1)S(1)}, u32[]{:S(2)}, u32[]{:S(2)}) collective-permute-start(bf16[3,2,16,128]{3,2,1,0:T(8,128)(2,1)S(1)} %get-tuple-element.19), channel_id=1, source_target_pairs={{0,8},{8,0},{16,24},{24,16},{1,9},{9,1},{17,25},{25,17},{2,10},{10... | collective-permute-start | bytes 73736 | tf_op jit(solution)/shard_map/ppermute | solution.py:62
  6.9 1.5 %collective-permute-start.1 = (bf16[3,2,16,128]{3,2,1,0:T(8,128)(2,1)S(1)}, bf16[3,2,16,128]{3,2,1,0:T(8,128)(2,1)S(1)}, u32[]{:S(2)}, u32[]{:S(2)}) collective-permute-start(bf16[3,2,16,128]{3,2,1,0:T(8,128)(2,1)S(1)} %get-tuple-element.20), channel_id=1, source_target_pairs={{0,16},{8,24},{16,0},{24,8},{1,17},{9,25},{17,1},{25,9},{2,18},{10... | collective-permute-start | bytes 73736 | tf_op jit(solution)/shard_map/ppermute | solution.py:62
  8.4 0.0 collective-permute-start.2
  8.4 0.3 collective-permute-done.refs_1_
  8.7 2.0 %collective-permute-done.1.refs_2_ = bf16[3,2,16,128]{3,2,1,0:T(8,128)(2,1)S(1)} collective-permute-done((bf16[3,2,16,128]{3,2,1,0:T(8,128)(2,1)S(1)}, bf16[3,2,16,128]{3,2,1,0:T(8,128)(2,1)S(1)}, u32[]{:S(2)}, u32[]{:S(2)}) %collective-permute-start.1) | collective-permute-done | bytes 24608 | tf_op jit(solution)/shard_map/ppermute | solution.py:62
  10.7 2.4 %collective-permute-done.2.refs_3_ = bf16[3,2,16,128]{3,2,1,0:T(8,128)(2,1)S(1)} collective-permute-done((bf16[3,2,16,128]{3,2,1,0:T(8,128)(2,1)S(1)}, bf16[3,2,16,128]{3,2,1,0:T(8,128)(2,1)S(1)}, u32[]{:S(2)}, u32[]{:S(2)}) %collective-permute-start.2) | collective-permute-done | bytes 24608 | tf_op jit(solution)/shard_map/ppermute | solution.py:62
  13.1 0.1 collective-permute-start.3
  13.2 0.0 copy-done.3
  13.2 0.1 copy.7
  13.3 1.2 %collective-permute-done.3.refs_1_ = bf16[4,3,2,16,128]{4,3,2,1,0:T(8,128)(2,1)S(1)} collective-permute-done((bf16[4,3,2,16,128]{4,3,2,1,0:T(8,128)(2,1)S(1)}, bf16[4,3,2,16,128]{4,3,2,1,0:T(8,128)(2,1)S(1)}, u32[]{:S(2)}, u32[]{:S(2)}) %collective-permute-start.3) | collective-permute-done | bytes 98336 | tf_op jit(solution)/shard_map/ppermute | solution.py:62
  14.5 0.1 broadcast_in_dim.2.limits_ref
  14.6 0.0 copy-done
  14.6 0.0 copy-done.1
  14.6 1.7 %predict.1 = (bf16[2,24,1024]{2,1,0:T(8,128)(2,1)S(1)}, bf16[2,24,1024]{2,1,0:T(8,128)(2,1)S(1)}, bf16[2,24,1024]{2,1,0:T(8,128)(2,1)S(1)}, bf16[2,24,1024]{2,1,0:T(8,128)(2,1)S(1)}) custom-call(s32[3,4,2,1,128]{4,3,2,1,0:T(1,128)S(1)} %broadcast_in_dim.2.limits_ref, bf16[2,3,4,2,48,256]{5,4,3,2,1,0:T(8,128)(2,1)S(1)} %copy-done, ...), custom_call_target="tpu_custom_call" | custom-call | flops 150994944 | bytes 2359296 | tf_op jit(solution)/shard_map/predict/pallas_call | solution.py:237
  16.4 3.7 %collective-permute-start.4 = (bf16[2,24,1024]{2,1,0:T(8,128)(2,1)S(1)}, bf16[2,24,1024]{2,1,0:T(8,128)(2,1)S(1)}, u32[]{:S(2)}, u32[]{:S(2)}) collective-permute-start(bf16[2,24,1024]{2,1,0:T(8,128)(2,1)S(1)} %get-tuple-element.22), channel_id=1, source_target_pairs={{0,6},{2,4},{4,2},{6,0},{1,7},{3,5},{5,3},{7,1},{8,14},{10,12},{12... | collective-permute-start | bytes 294920 | tf_op jit(solution)/shard_map/ppermute | solution.py:62
  20.1 0.0 collective-permute-start.5
  20.1 0.8 %collective-permute-start.6 = (bf16[2,24,1024]{2,1,0:T(8,128)(2,1)S(1)}, bf16[2,24,1024]{2,1,0:T(8,128)(2,1)S(1)}, u32[]{:S(2)}, u32[]{:S(2)}) collective-permute-start(bf16[2,24,1024]{2,1,0:T(8,128)(2,1)S(1)} %get-tuple-element.24), channel_id=1, source_target_pairs={{0,2},{2,0},{4,6},{6,4},{1,3},{3,1},{5,7},{7,5},{8,10},{10,8},{12,... | collective-permute-start | bytes 294920 | tf_op jit(solution)/shard_map/ppermute | solution.py:62
  20.8 3.1 %collective-permute-done.4.refs_0_ = bf16[2,24,1024]{2,1,0:T(8,128)(2,1)S(1)} collective-permute-done((bf16[2,24,1024]{2,1,0:T(8,128)(2,1)S(1)}, bf16[2,24,1024]{2,1,0:T(8,128)(2,1)S(1)}, u32[]{:S(2)}, u32[]{:S(2)}) %collective-permute-start.4) | collective-permute-done | bytes 98336 | tf_op jit(solution)/shard_map/ppermute | solution.py:62
  24.0 4.7 %collective-permute-done.5.refs_1_ = bf16[2,24,1024]{2,1,0:T(8,128)(2,1)S(1)} collective-permute-done((bf16[2,24,1024]{2,1,0:T(8,128)(2,1)S(1)}, bf16[2,24,1024]{2,1,0:T(8,128)(2,1)S(1)}, u32[]{:S(2)}, u32[]{:S(2)}) %collective-permute-start.5) | collective-permute-done | bytes 98336 | tf_op jit(solution)/shard_map/ppermute | solution.py:62
  28.6 0.0 collective-permute-done.6.refs_2_
  28.6 0.0 copy-done.2
  28.6 0.1 residual.1
  28.7 2.5 %collective-permute-start.9 = (bf16[2,24,1024]{2,1,0:T(8,128)(2,1)S(1)}, bf16[2,24,1024]{2,1,0:T(8,128)(2,1)S(1)}, u32[]{:S(2)}, u32[]{:S(2)}) collective-permute-start(bf16[2,24,1024]{2,1,0:T(8,128)(2,1)S(1)} %get-tuple-element.29.refs_0_), channel_id=1, source_target_pairs={{0,6},{2,4},{4,2},{6,0},{1,7},{3,5},{5,3},{7,1},{8,14},{10,12},{12... | collective-permute-start | bytes 294920 | tf_op jit(solution)/shard_map/ppermute | solution.py:62
  31.2 0.0 collective-permute-start.8
  31.3 1.9 %collective-permute-start.7 = (bf16[2,24,1024]{2,1,0:T(8,128)(2,1)S(1)}, bf16[2,24,1024]{2,1,0:T(8,128)(2,1)S(1)}, u32[]{:S(2)}, u32[]{:S(2)}) collective-permute-start(bf16[2,24,1024]{2,1,0:T(8,128)(2,1)S(1)} %get-tuple-element.29.refs_0_), channel_id=1, source_target_pairs={{0,2},{2,0},{4,6},{6,4},{1,3},{3,1},{5,7},{7,5},{8,10},{10,8},{12,... | collective-permute-start | bytes 294920 | tf_op jit(solution)/shard_map/ppermute | solution.py:62
  33.2 3.1 %collective-permute-done.9.refs_3_ = bf16[2,24,1024]{2,1,0:T(8,128)(2,1)S(1)} collective-permute-done((bf16[2,24,1024]{2,1,0:T(8,128)(2,1)S(1)}, bf16[2,24,1024]{2,1,0:T(8,128)(2,1)S(1)}, u32[]{:S(2)}, u32[]{:S(2)}) %collective-permute-start.9) | collective-permute-done | bytes 98336 | tf_op jit(solution)/shard_map/ppermute | solution.py:62
  36.3 3.4 %collective-permute-done.8.refs_2_ = bf16[2,24,1024]{2,1,0:T(8,128)(2,1)S(1)} collective-permute-done((bf16[2,24,1024]{2,1,0:T(8,128)(2,1)S(1)}, bf16[2,24,1024]{2,1,0:T(8,128)(2,1)S(1)}, u32[]{:S(2)}, u32[]{:S(2)}) %collective-permute-start.8) | collective-permute-done | bytes 98336 | tf_op jit(solution)/shard_map/ppermute | solution.py:62
  39.7 0.0 collective-permute-done.7.refs_1_
  39.7 1.5 %back_project.1 = (bf16[4,3,2,16,128]{4,3,2,1,0:T(8,128)(2,1)S(1)}, bf16[4,3,2,16,128]{4,3,2,1,0:T(8,128)(2,1)S(1)}) custom-call(s32[3,4,2,1,128]{4,3,2,1,0:T(1,128)S(1)} %broadcast_in_dim.2.limits_ref, bf16[2,3,4,2,48,256]{5,4,3,2,1,0:T(8,128)(2,1)S(1)} %copy-done, bf16[2,3,4,2,48,256]{5,4,3,2,1,0:T(8,128)(2,1)S(1)} %copy-done.1, ...), custom_call_target="tpu_custom_call" | custom-call | flops 150994944 | bytes 2359296 | tf_op jit(solution)/shard_map/back_project/pallas_call | solution.py:338
  41.2 0.1 collective-permute-start.10
  41.3 1.3 %collective-permute-done.10.refs_1_ = bf16[4,3,2,16,128]{4,3,2,1,0:T(8,128)(2,1)S(1)} collective-permute-done((bf16[4,3,2,16,128]{4,3,2,1,0:T(8,128)(2,1)S(1)}, bf16[4,3,2,16,128]{4,3,2,1,0:T(8,128)(2,1)S(1)}, u32[]{:S(2)}, u32[]{:S(2)}) %collective-permute-start.10) | collective-permute-done | bytes 98336 | tf_op jit(solution)/shard_map/ppermute | solution.py:62
  42.6 0.6 %collective-permute-start.11 = (bf16[2,3,2,16,128]{4,3,2,1,0:T(8,128)(2,1)S(1)}, bf16[2,3,2,16,128]{4,3,2,1,0:T(8,128)(2,1)S(1)}, u32[]{:S(2)}, u32[]{:S(2)}) collective-permute-start(bf16[2,3,2,16,128]{4,3,2,1,0:T(8,128)(2,1)S(1)} %get-tuple-element.33), channel_id=1, source_target_pairs={{0,8},{8,0},{16,24},{24,16},{1,9},{9,1},{17,25},{25,17},{2,10},{10... | collective-permute-start | bytes 147464 | tf_op jit(solution)/shard_map/ppermute | solution.py:408
  43.2 3.6 %collective-permute-done.11.refs_1_ = bf16[2,3,2,16,128]{4,3,2,1,0:T(8,128)(2,1)S(1)} collective-permute-done((bf16[2,3,2,16,128]{4,3,2,1,0:T(8,128)(2,1)S(1)}, bf16[2,3,2,16,128]{4,3,2,1,0:T(8,128)(2,1)S(1)}, u32[]{:S(2)}, u32[]{:S(2)}) %collective-permute-start.11) | collective-permute-done | bytes 49184 | tf_op jit(solution)/shard_map/ppermute | solution.py:408
  46.8 0.5 collective-permute-start.12
  47.3 0.7 %pad_maximum_fusion = f32[2,24,1024]{2,1,0:T(8,128)} fusion(f32[1,24,1024]{2,1,0:T(8,128)S(1)} %bitcast.5, f32[1,24,1024]{2,1,0:T(8,128)S(1)} %bitcast.4), kind=kLoop, calls=%fused_computation | loop fusion | flops 49152 | bytes 393216 | tf_op jit(solution)/shard_map/stack | solution.py:489
  48.0 2.9 %collective-permute-done.12.refs_2_ = bf16[2,3,2,16,128]{4,3,2,1,0:T(8,128)(2,1)S(1)} collective-permute-done((bf16[2,3,2,16,128]{4,3,2,1,0:T(8,128)(2,1)S(1)}, bf16[2,3,2,16,128]{4,3,2,1,0:T(8,128)(2,1)S(1)}, u32[]{:S(2)}, u32[]{:S(2)}) %collective-permute-start.12) | collective-permute-done | bytes 49184 | tf_op jit(solution)/shard_map/ppermute | solution.py:408
  50.9 2.6 %gradient.1 = bf16[4,16,32,1024]{3,2,1,0:T(8,128)(2,1)} custom-call(bf16[24,1024]{1,0:T(8,128)(2,1)S(1)} %get-tuple-element.28.table_ref, bf16[4,3,2,16,128]{4,3,2,1,0:T(8,128)(2,1)S(1)} %select.3.parts_ref), custom_call_target="tpu_custom_call" | custom-call | tf_op jit(solution)/shard_map/gradient/pallas_call | solution.py:458
  (4 shorter events, 0.0 us)
Async XLA Ops:
  0.6 12.6 %copy-start.3 = (s32[3,4,2]{1,2,0:T(2,128)S(1)}, s32[3,4,2]{1,2,0:T(2,128)}, u32[]{:S(2)}) copy-start(s32[3,4,2]{1,2,0:T(2,128)} %param.8) | copy-start | bytes 292
  0.6 14.0 %copy-start = (bf16[2,3,4,2,48,256]{5,4,3,2,1,0:T(8,128)(2,1)S(1)}, bf16[2,3,4,2,48,256]{5,4,3,2,1,0:T(8,128)(2,1)}, u32[]{:S(2)}) copy-start(bf16[2,3,4,2,48,256]{5,4,3,2,1,0:T(8,128)(2,1)} %right_ref.3) | copy-start | bytes 3538948
  0.7 14.0 %copy-start.1 = (bf16[2,3,4,2,48,256]{5,4,3,2,1,0:T(8,128)(2,1)S(1)}, bf16[2,3,4,2,48,256]{5,4,3,2,1,0:T(8,128)(2,1)}, u32[]{:S(2)}) copy-start(bf16[2,3,4,2,48,256]{5,4,3,2,1,0:T(8,128)(2,1)} %left_ref.3) | copy-start | bytes 3538948
  0.7 28.0 %copy-start.2 = (f32[2,24,1024]{2,1,0:T(8,128)S(1)}, f32[2,24,1024]{2,1,0:T(8,128)}, u32[]{:S(2)}) copy-start(f32[2,24,1024]{2,1,0:T(8,128)} %data_ref.1) | copy-start | bytes 589828
  3.9 4.8 %collective-permute-start = (bf16[3,2,16,128]{3,2,1,0:T(8,128)(2,1)S(1)}, bf16[3,2,16,128]{3,2,1,0:T(8,128)(2,1)S(1)}, u32[]{:S(2)}, u32[]{:S(2)}) collective-permute-start(bf16[3,2,16,128]{3,2,1,0:T(8,128)(2,1)S(1)} %get-tuple-element.19), channel_id=1, source_target_pairs={{0,8},{8,0},{16,24},{24,16},{1,9},{9,1},{17,25},{25,17},{2,10},{10... | collective-permute-start | bytes 73736 | tf_op jit(solution)/shard_map/ppermute | solution.py:62
  6.9 3.8 %collective-permute-start.1 = (bf16[3,2,16,128]{3,2,1,0:T(8,128)(2,1)S(1)}, bf16[3,2,16,128]{3,2,1,0:T(8,128)(2,1)S(1)}, u32[]{:S(2)}, u32[]{:S(2)}) collective-permute-start(bf16[3,2,16,128]{3,2,1,0:T(8,128)(2,1)S(1)} %get-tuple-element.20), channel_id=1, source_target_pairs={{0,16},{8,24},{16,0},{24,8},{1,17},{9,25},{17,1},{25,9},{2,18},{10... | collective-permute-start | bytes 73736 | tf_op jit(solution)/shard_map/ppermute | solution.py:62
  8.4 4.7 %collective-permute-start.2 = (bf16[3,2,16,128]{3,2,1,0:T(8,128)(2,1)S(1)}, bf16[3,2,16,128]{3,2,1,0:T(8,128)(2,1)S(1)}, u32[]{:S(2)}, u32[]{:S(2)}) collective-permute-start(bf16[3,2,16,128]{3,2,1,0:T(8,128)(2,1)S(1)} %get-tuple-element.21), channel_id=1, source_target_pairs={{0,24},{8,16},{16,8},{24,0},{1,25},{9,17},{17,9},{25,1},{2,26},{10... | collective-permute-start | bytes 73736 | tf_op jit(solution)/shard_map/ppermute | solution.py:62
  13.1 1.4 %collective-permute-start.3 = (bf16[4,3,2,16,128]{4,3,2,1,0:T(8,128)(2,1)S(1)}, bf16[4,3,2,16,128]{4,3,2,1,0:T(8,128)(2,1)S(1)}, u32[]{:S(2)}, u32[]{:S(2)}) collective-permute-start(bf16[4,3,2,16,128]{4,3,2,1,0:T(8,128)(2,1)S(1)} %pack.1.refs_0_), channel_id=1, source_target_pairs={{0,1},{1,0},{2,3},{3,2},{4,5},{5,4},{6,7},{7,6},{8,9},{9,8},{10,11... | collective-permute-start | bytes 294920 | tf_op jit(solution)/shard_map/ppermute | solution.py:62
  16.4 7.6 %collective-permute-start.4 = (bf16[2,24,1024]{2,1,0:T(8,128)(2,1)S(1)}, bf16[2,24,1024]{2,1,0:T(8,128)(2,1)S(1)}, u32[]{:S(2)}, u32[]{:S(2)}) collective-permute-start(bf16[2,24,1024]{2,1,0:T(8,128)(2,1)S(1)} %get-tuple-element.22), channel_id=1, source_target_pairs={{0,6},{2,4},{4,2},{6,0},{1,7},{3,5},{5,3},{7,1},{8,14},{10,12},{12... | collective-permute-start | bytes 294920 | tf_op jit(solution)/shard_map/ppermute | solution.py:62
  20.1 8.6 %collective-permute-start.5 = (bf16[2,24,1024]{2,1,0:T(8,128)(2,1)S(1)}, bf16[2,24,1024]{2,1,0:T(8,128)(2,1)S(1)}, u32[]{:S(2)}, u32[]{:S(2)}) collective-permute-start(bf16[2,24,1024]{2,1,0:T(8,128)(2,1)S(1)} %get-tuple-element.23), channel_id=1, source_target_pairs={{0,4},{2,6},{4,0},{6,2},{1,5},{3,7},{5,1},{7,3},{8,12},{10,14},{12... | collective-permute-start | bytes 294920 | tf_op jit(solution)/shard_map/ppermute | solution.py:62
  20.1 8.6 %collective-permute-start.6 = (bf16[2,24,1024]{2,1,0:T(8,128)(2,1)S(1)}, bf16[2,24,1024]{2,1,0:T(8,128)(2,1)S(1)}, u32[]{:S(2)}, u32[]{:S(2)}) collective-permute-start(bf16[2,24,1024]{2,1,0:T(8,128)(2,1)S(1)} %get-tuple-element.24), channel_id=1, source_target_pairs={{0,2},{2,0},{4,6},{6,4},{1,3},{3,1},{5,7},{7,5},{8,10},{10,8},{12,... | collective-permute-start | bytes 294920 | tf_op jit(solution)/shard_map/ppermute | solution.py:62
  28.7 7.6 %collective-permute-start.9 = (bf16[2,24,1024]{2,1,0:T(8,128)(2,1)S(1)}, bf16[2,24,1024]{2,1,0:T(8,128)(2,1)S(1)}, u32[]{:S(2)}, u32[]{:S(2)}) collective-permute-start(bf16[2,24,1024]{2,1,0:T(8,128)(2,1)S(1)} %get-tuple-element.29.refs_0_), channel_id=1, source_target_pairs={{0,6},{2,4},{4,2},{6,0},{1,7},{3,5},{5,3},{7,1},{8,14},{10,12},{12... | collective-permute-start | bytes 294920 | tf_op jit(solution)/shard_map/ppermute | solution.py:62
  31.2 8.4 %collective-permute-start.8 = (bf16[2,24,1024]{2,1,0:T(8,128)(2,1)S(1)}, bf16[2,24,1024]{2,1,0:T(8,128)(2,1)S(1)}, u32[]{:S(2)}, u32[]{:S(2)}) collective-permute-start(bf16[2,24,1024]{2,1,0:T(8,128)(2,1)S(1)} %get-tuple-element.29.refs_0_), channel_id=1, source_target_pairs={{0,4},{2,6},{4,0},{6,2},{1,5},{3,7},{5,1},{7,3},{8,12},{10,14},{12... | collective-permute-start | bytes 294920 | tf_op jit(solution)/shard_map/ppermute | solution.py:62
  31.3 8.4 %collective-permute-start.7 = (bf16[2,24,1024]{2,1,0:T(8,128)(2,1)S(1)}, bf16[2,24,1024]{2,1,0:T(8,128)(2,1)S(1)}, u32[]{:S(2)}, u32[]{:S(2)}) collective-permute-start(bf16[2,24,1024]{2,1,0:T(8,128)(2,1)S(1)} %get-tuple-element.29.refs_0_), channel_id=1, source_target_pairs={{0,2},{2,0},{4,6},{6,4},{1,3},{3,1},{5,7},{7,5},{8,10},{10,8},{12,... | collective-permute-start | bytes 294920 | tf_op jit(solution)/shard_map/ppermute | solution.py:62
  41.2 1.4 %collective-permute-start.10 = (bf16[4,3,2,16,128]{4,3,2,1,0:T(8,128)(2,1)S(1)}, bf16[4,3,2,16,128]{4,3,2,1,0:T(8,128)(2,1)S(1)}, u32[]{:S(2)}, u32[]{:S(2)}) collective-permute-start(bf16[4,3,2,16,128]{4,3,2,1,0:T(8,128)(2,1)S(1)} %get-tuple-element.31), channel_id=1, source_target_pairs={{0,1},{1,0},{2,3},{3,2},{4,5},{5,4},{6,7},{7,6},{8,9},{9,8},{10,11... | collective-permute-start | bytes 294920 | tf_op jit(solution)/shard_map/ppermute | solution.py:62
  42.6 4.2 %collective-permute-start.11 = (bf16[2,3,2,16,128]{4,3,2,1,0:T(8,128)(2,1)S(1)}, bf16[2,3,2,16,128]{4,3,2,1,0:T(8,128)(2,1)S(1)}, u32[]{:S(2)}, u32[]{:S(2)}) collective-permute-start(bf16[2,3,2,16,128]{4,3,2,1,0:T(8,128)(2,1)S(1)} %get-tuple-element.33), channel_id=1, source_target_pairs={{0,8},{8,0},{16,24},{24,16},{1,9},{9,1},{17,25},{25,17},{2,10},{10... | collective-permute-start | bytes 147464 | tf_op jit(solution)/shard_map/ppermute | solution.py:408
  46.8 4.1 %collective-permute-start.12 = (bf16[2,3,2,16,128]{4,3,2,1,0:T(8,128)(2,1)S(1)}, bf16[2,3,2,16,128]{4,3,2,1,0:T(8,128)(2,1)S(1)}, u32[]{:S(2)}, u32[]{:S(2)}) collective-permute-start(bf16[2,3,2,16,128]{4,3,2,1,0:T(8,128)(2,1)S(1)} %select.2), channel_id=1, source_target_pairs={{0,16},{8,24},{16,0},{24,8},{1,17},{9,25},{17,1},{25,9},{2,18},{10... | collective-permute-start | bytes 147464 | tf_op jit(solution)/shard_map/ppermute | solution.py:408

commit v8 on v6

--- a/solution.py
+++ b/solution.py
@@ -68,18 +68,17 @@
     model_ref, rows_ref, model_sems = refs[-3:]
     high, low, rhs, length = model_ref.shape
     dests = len(out_refs)
-    freqs = out_refs[0].shape[0]
+    freqs, _, _, lanes = out_refs[0].shape
     bins = 2 * dests * freqs
     chunks = model_sems.shape[0]
     part = low // chunks
-    own = model_hbm.at[lax.axis_index("rep")]
     copies = []
     for at in range(chunks):
         rows = pl.ds(at * part, part)
         copies.append(
             [
                 pltpu.make_async_copy(
-                    own.at[h, rows], model_ref.at[h, rows], model_sems.at[at, h]
+                    model_hbm.at[h, rows], model_ref.at[h, rows], model_sems.at[at, h]
                 )
                 for h in range(high)
             ]
@@ -91,14 +90,15 @@
     for at in range(chunks):
         for copy in copies[at]:
             copy.wait()
-        block = model_ref[:, at * part : (at + 1) * part].reshape(high * part * rhs, length)
-        sums = dot(block, table, 1, 1)
-        for row in range(part):
-            mine = jnp.concatenate(
-                [sums[(h * part + row) * rhs : (h * part + row + 1) * rhs] for h in range(high)]
+        for start in range(at * part, (at + 1) * part, 2):
+            width = min(2, (at + 1) * part - start)
+            block = jnp.concatenate(
+                [model_ref[:, start + row].reshape(lanes, length) for row in range(width)]
             )
-            place = (at * part + row) * bins
-            rows_ref[place : place + bins] = mine.T
+            sums = dot(table, block, 1, 1)
+            for row in range(width):
+                place = (start + row) * bins
+                rows_ref[place : place + bins] = sums[:, row * lanes : (row + 1) * lanes]
     me = lax.axis_index("freq")
     for at, out_ref in enumerate(out_refs):
         dest = target(me, at, dests)
@@ -108,10 +108,10 @@
                 out_ref[f, c] = rows_ref[pl.ds(q, low, stride=bins), :].astype(out_ref.dtype)
 
 
-def spectrum_of(model, dests, freqs, reps):
+def spectrum_of(model, dests, freqs):
     traces, rhs, length = model.shape
     high = LANES // rhs
-    low = traces // (reps * high)
+    low = traces // high
     chunks = math.gcd(low, 4)
     bins = 2 * dests * freqs
     table, *blocks = pl.pallas_call(
@@ -127,27 +127,8 @@
         ],
         compiler_params=pltpu.CompilerParams(vmem_limit_bytes=VMEM_LIMIT),
         name="spectrum",
-    )(model.reshape(reps, high, low, rhs, length))
+    )(model.reshape(high, low, rhs, length))
     return table, blocks
-
-
-def pack_kernel(*refs):
-    block_refs, out_ref = refs[:-1], refs[-1]
-    me = lax.axis_index("freq")
-    for at, block_ref in enumerate(block_refs):
-        out_ref[origin(me, at, len(block_refs))] = block_ref[...]
-
-
-def pack(blocks):
-    shape = (len(blocks),) + blocks[0].shape
-    return pl.pallas_call(
-        pack_kernel,
-        in_specs=[pl.BlockSpec(memory_space=pltpu.VMEM)] * len(blocks),
-        out_specs=pl.BlockSpec(memory_space=pltpu.VMEM),
-        out_shape=jax.ShapeDtypeStruct(shape, blocks[0].dtype),
-        compiler_params=pltpu.CompilerParams(vmem_limit_bytes=VMEM_LIMIT),
-        name="pack",
-    )(*blocks)
 
 
 def tile_cost(count, size, tile, rhs):
@@ -178,15 +159,15 @@
     return found
 
 
-def predict_kernel(reps, parts, limits_ref, right_ref, left_ref, *refs):
-    arrived_refs, out_refs = refs[:reps], refs[reps : reps + parts]
-    spec_ref, sum_ref = refs[reps + parts :]
-    _, groups, freqs, _, low, lanes = spec_ref.shape
+def predict_kernel(groups, parts, limits_ref, right_ref, left_ref, *refs):
+    arrived_refs, out_refs = refs[:groups], refs[groups : groups + parts]
+    spec_ref, sum_ref = refs[groups + parts :]
+    _, freqs, _, low, lanes = spec_ref.shape
     row_tiles, col_tiles, size, tile = left_ref.shape[2:]
     _, pairs, _ = out_refs[0].shape
-    own = lax.axis_index("rep")
-    for at, arrived_ref in enumerate(arrived_refs):
-        spec_ref[origin(own, at, reps)] = arrived_ref[...]
+    me = lax.axis_index("freq")
+    for at, arrived_ref in enumerate(arrived_refs[::-1]):
+        spec_ref[origin(me, at, groups)] = arrived_ref[...]
     rhs = parts * pairs // freqs
     high = lanes // rhs
     per_tile = groups // col_tiles
@@ -197,9 +178,10 @@
             for c in range(2):
                 blocks = []
                 for g in range(j * per_tile, (j + 1) * per_tile):
-                    for rep in range(reps):
-                        got = spec_ref[rep, g, f, c].astype(jnp.float32)
-                        blocks += [got[:, h * rhs : (h + 1) * rhs] for h in range(high)]
+                    got = spec_ref[g, f, c]
+                    if low % 16:
+                        got = got.astype(jnp.float32)
+                    blocks += [got[:, h * rhs : (h + 1) * rhs] for h in range(high)]
                 halves.append(jnp.concatenate(blocks))
             straight = jnp.concatenate(halves, axis=1).astype(jnp.bfloat16)
             crossed = jnp.concatenate([halves[1], -halves[0]], axis=1).astype(jnp.bfloat16)
@@ -226,30 +208,31 @@
 
 def predict(limits, spectrum, green_right, green_left, parts):
     freqs, row_tiles, col_tiles, size, tile = green_left.shape[1:]
-    reps = len(spectrum)
-    groups, _, _, low, _ = spectrum[0].shape
-    rhs = LANES * reps * groups * low // (col_tiles * tile)
+    groups = len(spectrum)
+    _, _, low, _ = spectrum[0].shape
+    rhs = LANES * groups * low // (col_tiles * tile)
     pairs = freqs * rhs
     sources = row_tiles * tile
     return pl.pallas_call(
-        functools.partial(predict_kernel, reps, parts),
-        in_specs=[pl.BlockSpec(memory_space=pltpu.VMEM)] * (3 + reps),
+        functools.partial(predict_kernel, groups, parts),
+        in_specs=[pl.BlockSpec(memory_space=pltpu.VMEM)] * (3 + groups),
         out_specs=[pl.BlockSpec(memory_space=pltpu.VMEM)] * parts,
         out_shape=[jax.ShapeDtypeStruct((2, pairs // parts, sources), jnp.bfloat16)] * parts,
         scratch_shapes=[
-            pltpu.VMEM((reps,) + spectrum[0].shape, jnp.bfloat16),
+            pltpu.VMEM((groups,) + spectrum[0].shape, jnp.bfloat16),
             pltpu.VMEM((parts, 2, pairs // parts, sources), jnp.float32),
         ],
         compiler_params=pltpu.CompilerParams(vmem_limit_bytes=VMEM_LIMIT),
         cost_estimate=tile_cost(freqs * row_tiles * col_tiles, size, tile, rhs),
         name="predict",
-    )(limits, green_right, green_left, *spectrum)
+    )(limits, green_right, green_left, *spectrum[::-1])
 
 
 def residual_kernel(data_ref, *refs):
-    block_refs, (misfit_ref, residual_ref) = refs[:-2], refs[-2:]
+    block_refs, (misfit_ref, *part_refs) = refs[:-3], refs[-3:]
     residual = sum(block_ref[...].astype(jnp.float32) for block_ref in block_refs) - data_ref[...]
-    residual_ref[...] = residual
+    for c, part_ref in enumerate(part_refs):
+        part_ref[...] = residual[c]
     misfit_ref[...] = residual.astype(misfit_ref.dtype)
 
 
@@ -258,10 +241,11 @@
     return pl.pallas_call(
         residual_kernel,
         in_specs=[pl.BlockSpec(memory_space=pltpu.VMEM)] * (1 + len(blocks)),
-        out_specs=[pl.BlockSpec(memory_space=pltpu.VMEM)] * 2,
+        out_specs=[pl.BlockSpec(memory_space=pltpu.VMEM)] * 3,
         out_shape=[
             jax.ShapeDtypeStruct(shape, jnp.bfloat16),
-            jax.ShapeDtypeStruct(shape, jnp.float32),
+            jax.ShapeDtypeStruct(shape[1:], jnp.float32),
+            jax.ShapeDtypeStruct(shape[1:], jnp.float32),
         ],
         compiler_params=pltpu.CompilerParams(vmem_limit_bytes=VMEM_LIMIT),
         name="residual",
@@ -304,7 +288,8 @@
             right = jnp.concatenate(
                 [right_ref[c, f, :, j].reshape(row_tiles * size, tile) for c in range(2)]
             )
-            grad = dot(factors, right, 0, 0).T
+            grad = dot(factors, right, 0, 0)
+            grad = (grad if low % 16 else grad.astype(out_refs[0].dtype)).T
             for at in range(per_tile):
                 rows = at * high * low
                 for c in range(2):
@@ -364,8 +349,7 @@
 
 
 def gradient_kernel(table_ref, *refs):
-    part_refs = refs[:-4]
-    out_hbm, out_ref, rows_ref, out_sems = refs[-4:]
+    part_refs, (out_hbm, out_ref, rows_ref, out_sems) = refs[-5::-1], refs[-4:]
     groups = len(part_refs)
     freqs, _, low, lanes = part_refs[0].shape
     high, _, rhs, length = out_ref.shape
@@ -404,7 +388,7 @@
 
 
 def gradient_of(parts, table, rhs):
-    freqs, _, low, lanes = parts[0].shape
+    _, _, low, lanes = parts[0].shape
     bins, length = table.shape
     high = lanes // rhs
     chunks = math.gcd(low, 4)
@@ -421,7 +405,7 @@
         ],
         compiler_params=pltpu.CompilerParams(vmem_limit_bytes=VMEM_LIMIT),
         name="gradient",
-    )(table, *parts)
+    )(table, *parts[::-1])
     return out.reshape(1, high * low, rhs, length)
 
 
@@ -431,16 +415,15 @@
     rep_count = lax.axis_size("rep")
     freq_local = ranks.shape[0]
     rhs_count = model.shape[2]
-    table, spectrum = spectrum_of(model[0], freq_count, freq_local, rep_count)
-    spectrum = pack(exchange(spectrum, "freq"))
-    spectrum = exchange([spectrum] * rep_count, "rep")
+    table, spectrum = spectrum_of(model[0], freq_count, freq_local)
+    spectrum = exchange(spectrum, "freq")
     limits = jnp.broadcast_to(ranks[..., None, None], ranks.shape + (1, LANES))
     predicted = predict(limits, spectrum, green_right, green_left, tile_count)
-    misfit, residual = residual_of(exchange(predicted, "rtile"), data)
+    misfit, *residual = residual_of(exchange(predicted, "rtile")[::-1], data)
     misfit = exchange([misfit] * tile_count, "rtile")
     partial = back_project(limits, misfit, green_right, green_left, freq_count, rep_count)
     arrived = exchange(gather(exchange(partial, "rep")), "freq")
-    return (residual, gradient_of(arrived, table, rhs_count))
+    return (jnp.stack(residual), gradient_of(arrived, table, rhs_count))
 
 
 def solution(mesh):

time: 53.3 us -> 48 us (0.901)
  waiting for transfers between devices: 23.9 us -> 18.3 us
  other arithmetic: 0 us -> 0.69 us
    ppermute x14 -> x13, waiting for transfers between devices: 23.9 us -> 18.3 us  [exchange(): arrived.append(lax.ppermute(blocks[step], axis, pairs))]
    another operation x0 -> x1, other arithmetic: none -> 0.69 us  [shards(): return (jnp.stack(residual), gradient_of(arrived, table, rhs_count))]
    pallas_call x1, Pallas kernels: 0.74 us -> 0.06 us  [residual_of(): pl.pallas_call(residual_kernel, in_specs=[pl.BlockSpec(memory_space=pltpu...]
    ppermute x14 -> x13, starting transfers between devices: 17.1 us -> 17.1 us  [exchange(): arrived.append(lax.ppermute(blocks[step], axis, pairs))]
    pallas_call x2 -> x1, Pallas kernels: 1.75 us -> 1.74 us  [predict(): pl.pallas_call(functools.partial(predict_kernel, groups, parts), in_specs...]
  transfers between devices with their start and end apart: 14 -> 13, of which waited for: 12 -> 11; matrix products, arithmetic and copies ran while one was open for 0% -> 2% of each run, Pallas kernels for 0% -> 0%
where the time goes in v8:
time: 48 us; the launch traced here: 47.8 us
  waiting for transfers between devices  18.3 us (38%)
  starting transfers between devices  17.1 us (36%)
  Pallas kernels  10.8 us (22%)
  between operations  0.74 us (2%)
  other arithmetic  0.69 us (1%)
    ppermute x13, waiting for transfers between devices, exchange(): arrived.append(lax.ppermute(blocks[step], axis, pairs))  18.3 us
    ppermute x13, starting transfers between devices, exchange(): arrived.append(lax.ppermute(blocks[step], axis, pairs))  17.1 us
    pallas_call x1, Pallas kernels, spectrum_of(): pl.pallas_call(spectrum_kernel, in_specs=[pl.BlockSpec(memory_space=pltpu...  4.77 us
    pallas_call x1, Pallas kernels, gradient_of(): pl.pallas_call(gradient_kernel, in_specs=[pl.BlockSpec(memory_space=pltpu...  2.62 us
    pallas_call x1, Pallas kernels, predict(): pl.pallas_call(functools.partial(predict_kernel, groups, parts), in_specs...  1.74 us
    pallas_call x1, Pallas kernels, back_project(): pl.pallas_call(functools.partial(back_kernel, parts, groups, reps), in_sp...  1.53 us
  transfers between devices with their start and end apart: 13, of which 11 were waited for; matrix products, arithmetic and copies ran while one was open for 2% of the time, Pallas kernels for 0%

profile of v8, /device:TPU:0, one launch (start us, length us, event | category | flops | bytes accessed | tf_op | source)
XLA Modules:
  0.0 47.8 jit_solution(6752167059754959965)
XLA Ops:
  0.6 0.0 copy-start.3
  0.6 0.0 copy-start
  0.7 0.0 copy-start.1
  0.7 0.0 copy-start.2
  0.7 4.8 %spectrum.1 = (bf16[24,1024]{1,0:T(8,128)(2,1)S(1)}, bf16[3,2,32,128]{3,2,1,0:T(8,128)(2,1)S(1)}, bf16[3,2,32,128]{3,2,1,0:T(8,128)(2,1)S(1)}, bf16[3,2,32,128]{...) custom-call(bf16[4,32,32,1024]{3,2,1,0:T(8,128)(2,1)} %bitcast.6), custom_call_target="tpu_custom_call" | custom-call | tf_op jit(solution)/shard_map/spectrum/pallas_call | solution.py:117
  5.4 4.0 %collective-permute-start = (bf16[3,2,32,128]{3,2,1,0:T(8,128)(2,1)S(1)}, bf16[3,2,32,128]{3,2,1,0:T(8,128)(2,1)S(1)}, u32[]{:S(2)}, u32[]{:S(2)}) collective-permute-start(bf16[3,2,32,128]{3,2,1,0:T(8,128)(2,1)S(1)} %get-tuple-element.20), channel_id=1, source_target_pairs={{0,24},{8,16},{16,8},{24,0},{1,25},{9,17},{17,9},{25,1},{2,26},{10... | collective-permute-start | bytes 147464 | tf_op jit(solution)/shard_map/ppermute | solution.py:62
  9.4 0.5 %collective-permute-start.1 = (bf16[3,2,32,128]{3,2,1,0:T(8,128)(2,1)S(1)}, bf16[3,2,32,128]{3,2,1,0:T(8,128)(2,1)S(1)}, u32[]{:S(2)}, u32[]{:S(2)}) collective-permute-start(bf16[3,2,32,128]{3,2,1,0:T(8,128)(2,1)S(1)} %get-tuple-element.21), channel_id=1, source_target_pairs={{0,16},{8,24},{16,0},{24,8},{1,17},{9,25},{17,1},{25,9},{2,18},{10... | collective-permute-start | bytes 147464 | tf_op jit(solution)/shard_map/ppermute | solution.py:62
  9.9 0.1 collective-permute-start.2
  10.1 0.0 copy-done.3
  10.1 0.1 copy.7
  10.2 1.3 %collective-permute-done.refs_0_ = bf16[3,2,32,128]{3,2,1,0:T(8,128)(2,1)S(1)} collective-permute-done((bf16[3,2,32,128]{3,2,1,0:T(8,128)(2,1)S(1)}, bf16[3,2,32,128]{3,2,1,0:T(8,128)(2,1)S(1)}, u32[]{:S(2)}, u32[]{:S(2)}) %collective-permute-start) | collective-permute-done | bytes 49184 | tf_op jit(solution)/shard_map/ppermute | solution.py:62
  11.5 2.0 %collective-permute-done.1.refs_1_ = bf16[3,2,32,128]{3,2,1,0:T(8,128)(2,1)S(1)} collective-permute-done((bf16[3,2,32,128]{3,2,1,0:T(8,128)(2,1)S(1)}, bf16[3,2,32,128]{3,2,1,0:T(8,128)(2,1)S(1)}, u32[]{:S(2)}, u32[]{:S(2)}) %collective-permute-start.1) | collective-permute-done | bytes 49184 | tf_op jit(solution)/shard_map/ppermute | solution.py:62
  13.5 0.5 %collective-permute-done.2.refs_2_ = bf16[3,2,32,128]{3,2,1,0:T(8,128)(2,1)S(1)} collective-permute-done((bf16[3,2,32,128]{3,2,1,0:T(8,128)(2,1)S(1)}, bf16[3,2,32,128]{3,2,1,0:T(8,128)(2,1)S(1)}, u32[]{:S(2)}, u32[]{:S(2)}) %collective-permute-start.2) | collective-permute-done | bytes 49184 | tf_op jit(solution)/shard_map/ppermute | solution.py:62
  14.0 0.1 broadcast_in_dim.2.limits_ref
  14.1 0.0 copy-done
  14.1 0.0 copy-done.1
  14.1 1.7 %predict.1 = (bf16[2,24,1024]{2,1,0:T(8,128)(2,1)S(1)}, bf16[2,24,1024]{2,1,0:T(8,128)(2,1)S(1)}, bf16[2,24,1024]{2,1,0:T(8,128)(2,1)S(1)}, bf16[2,24,1024]{2,1,0:T(8,128)(2,1)S(1)}) custom-call(s32[3,4,2,1,128]{4,3,2,1,0:T(1,128)S(1)} %broadcast_in_dim.2.limits_ref, bf16[2,3,4,2,48,256]{5,4,3,2,1,0:T(8,128)(2,1)S(1)} %copy-done, ...), custom_call_target="tpu_custom_call" | custom-call | flops 150994944 | bytes 2359296 | tf_op jit(solution)/shard_map/predict/pallas_call | solution.py:216
  15.9 3.7 %collective-permute-start.3 = (bf16[2,24,1024]{2,1,0:T(8,128)(2,1)S(1)}, bf16[2,24,1024]{2,1,0:T(8,128)(2,1)S(1)}, u32[]{:S(2)}, u32[]{:S(2)}) collective-permute-start(bf16[2,24,1024]{2,1,0:T(8,128)(2,1)S(1)} %get-tuple-element.24), channel_id=1, source_target_pairs={{0,6},{2,4},{4,2},{6,0},{1,7},{3,5},{5,3},{7,1},{8,14},{10,12},{12... | collective-permute-start | bytes 294920 | tf_op jit(solution)/shard_map/ppermute | solution.py:62
  19.5 0.0 collective-permute-start.4
  19.6 0.8 %collective-permute-start.5 = (bf16[2,24,1024]{2,1,0:T(8,128)(2,1)S(1)}, bf16[2,24,1024]{2,1,0:T(8,128)(2,1)S(1)}, u32[]{:S(2)}, u32[]{:S(2)}) collective-permute-start(bf16[2,24,1024]{2,1,0:T(8,128)(2,1)S(1)} %get-tuple-element.26), channel_id=1, source_target_pairs={{0,2},{2,0},{4,6},{6,4},{1,3},{3,1},{5,7},{7,5},{8,10},{10,8},{12,... | collective-permute-start | bytes 294920 | tf_op jit(solution)/shard_map/ppermute | solution.py:62
  20.3 2.1 %collective-permute-done.3.refs_0_ = bf16[2,24,1024]{2,1,0:T(8,128)(2,1)S(1)} collective-permute-done((bf16[2,24,1024]{2,1,0:T(8,128)(2,1)S(1)}, bf16[2,24,1024]{2,1,0:T(8,128)(2,1)S(1)}, u32[]{:S(2)}, u32[]{:S(2)}) %collective-permute-start.3) | collective-permute-done | bytes 98336 | tf_op jit(solution)/shard_map/ppermute | solution.py:62
  22.4 4.0 %collective-permute-done.4.refs_1_ = bf16[2,24,1024]{2,1,0:T(8,128)(2,1)S(1)} collective-permute-done((bf16[2,24,1024]{2,1,0:T(8,128)(2,1)S(1)}, bf16[2,24,1024]{2,1,0:T(8,128)(2,1)S(1)}, u32[]{:S(2)}, u32[]{:S(2)}) %collective-permute-start.4) | collective-permute-done | bytes 98336 | tf_op jit(solution)/shard_map/ppermute | solution.py:62
  26.4 0.0 collective-permute-done.5.refs_2_
  26.4 0.0 copy-done.2
  26.4 0.1 residual.1
  26.5 2.6 %collective-permute-start.8 = (bf16[2,24,1024]{2,1,0:T(8,128)(2,1)S(1)}, bf16[2,24,1024]{2,1,0:T(8,128)(2,1)S(1)}, u32[]{:S(2)}, u32[]{:S(2)}) collective-permute-start(bf16[2,24,1024]{2,1,0:T(8,128)(2,1)S(1)} %get-tuple-element.31.refs_0_), channel_id=1, source_target_pairs={{0,6},{2,4},{4,2},{6,0},{1,7},{3,5},{5,3},{7,1},{8,14},{10,12},{12... | collective-permute-start | bytes 294920 | tf_op jit(solution)/shard_map/ppermute | solution.py:62
  29.1 0.0 collective-permute-start.7
  29.1 1.8 %collective-permute-start.6 = (bf16[2,24,1024]{2,1,0:T(8,128)(2,1)S(1)}, bf16[2,24,1024]{2,1,0:T(8,128)(2,1)S(1)}, u32[]{:S(2)}, u32[]{:S(2)}) collective-permute-start(bf16[2,24,1024]{2,1,0:T(8,128)(2,1)S(1)} %get-tuple-element.31.refs_0_), channel_id=1, source_target_pairs={{0,2},{2,0},{4,6},{6,4},{1,3},{3,1},{5,7},{7,5},{8,10},{10,8},{12,... | collective-permute-start | bytes 294920 | tf_op jit(solution)/shard_map/ppermute | solution.py:62
  30.9 3.1 %collective-permute-done.8.refs_3_ = bf16[2,24,1024]{2,1,0:T(8,128)(2,1)S(1)} collective-permute-done((bf16[2,24,1024]{2,1,0:T(8,128)(2,1)S(1)}, bf16[2,24,1024]{2,1,0:T(8,128)(2,1)S(1)}, u32[]{:S(2)}, u32[]{:S(2)}) %collective-permute-start.8) | collective-permute-done | bytes 98336 | tf_op jit(solution)/shard_map/ppermute | solution.py:62
  34.1 2.5 %collective-permute-done.7.refs_2_ = bf16[2,24,1024]{2,1,0:T(8,128)(2,1)S(1)} collective-permute-done((bf16[2,24,1024]{2,1,0:T(8,128)(2,1)S(1)}, bf16[2,24,1024]{2,1,0:T(8,128)(2,1)S(1)}, u32[]{:S(2)}, u32[]{:S(2)}) %collective-permute-start.7) | collective-permute-done | bytes 98336 | tf_op jit(solution)/shard_map/ppermute | solution.py:62
  36.6 0.0 collective-permute-done.6.refs_1_
  36.6 1.5 %back_project.1 = (bf16[4,3,2,16,128]{4,3,2,1,0:T(8,128)(2,1)S(1)}, bf16[4,3,2,16,128]{4,3,2,1,0:T(8,128)(2,1)S(1)}) custom-call(s32[3,4,2,1,128]{4,3,2,1,0:T(1,128)S(1)} %broadcast_in_dim.2.limits_ref, bf16[2,3,4,2,48,256]{5,4,3,2,1,0:T(8,128)(2,1)S(1)} %copy-done, bf16[2,3,4,2,48,256]{5,4,3,2,1,0:T(8,128)(2,1)S(1)} %copy-done.1, ...), custom_call_target="tpu_custom_call" | custom-call | flops 150994944 | bytes 2359296 | tf_op jit(solution)/shard_map/back_project/pallas_call | solution.py:317
  38.1 0.1 collective-permute-start.9
  38.2 1.3 %collective-permute-done.9.refs_1_ = bf16[4,3,2,16,128]{4,3,2,1,0:T(8,128)(2,1)S(1)} collective-permute-done((bf16[4,3,2,16,128]{4,3,2,1,0:T(8,128)(2,1)S(1)}, bf16[4,3,2,16,128]{4,3,2,1,0:T(8,128)(2,1)S(1)}, u32[]{:S(2)}, u32[]{:S(2)}) %collective-permute-start.9) | collective-permute-done | bytes 98336 | tf_op jit(solution)/shard_map/ppermute | solution.py:62
  39.5 1.8 %collective-permute-start.10 = (bf16[3,2,16,128]{3,2,1,0:T(8,128)(2,1)S(1)}, bf16[3,2,16,128]{3,2,1,0:T(8,128)(2,1)S(1)}, u32[]{:S(2)}, u32[]{:S(2)}) collective-permute-start(bf16[3,2,16,128]{3,2,1,0:T(8,128)(2,1)S(1)} %get-tuple-element.34), channel_id=1, source_target_pairs={{0,24},{8,16},{16,8},{24,0},{1,25},{9,17},{17,9},{25,1},{2,26},{10... | collective-permute-start | bytes 73736 | tf_op jit(solution)/shard_map/ppermute | solution.py:62
  41.3 0.1 collective-permute-start.11
  41.4 1.7 %collective-permute-start.12 = (bf16[3,2,16,128]{3,2,1,0:T(8,128)(2,1)S(1)}, bf16[3,2,16,128]{3,2,1,0:T(8,128)(2,1)S(1)}, u32[]{:S(2)}, u32[]{:S(2)}) collective-permute-start(bf16[3,2,16,128]{3,2,1,0:T(8,128)(2,1)S(1)} %get-tuple-element.36), channel_id=1, source_target_pairs={{0,8},{8,0},{16,24},{24,16},{1,9},{9,1},{17,25},{25,17},{2,10},{10... | collective-permute-start | bytes 73736 | tf_op jit(solution)/shard_map/ppermute | solution.py:62
  43.1 0.7 %pad_maximum_fusion = f32[2,24,1024]{2,1,0:T(8,128)} fusion(f32[1,24,1024]{2,1,0:T(8,128)S(1)} %bitcast.5, f32[1,24,1024]{2,1,0:T(8,128)S(1)} %bitcast.4), kind=kLoop, calls=%fused_computation | loop fusion | flops 49152 | bytes 393216 | tf_op jit(solution)/shard_map/stack | solution.py:426
  43.8 0.5 %collective-permute-done.10.refs_0_ = bf16[3,2,16,128]{3,2,1,0:T(8,128)(2,1)S(1)} collective-permute-done((bf16[3,2,16,128]{3,2,1,0:T(8,128)(2,1)S(1)}, bf16[3,2,16,128]{3,2,1,0:T(8,128)(2,1)S(1)}, u32[]{:S(2)}, u32[]{:S(2)}) %collective-permute-start.10) | collective-permute-done | bytes 24608 | tf_op jit(solution)/shard_map/ppermute | solution.py:62
  44.3 0.8 %collective-permute-done.11.refs_1_ = bf16[3,2,16,128]{3,2,1,0:T(8,128)(2,1)S(1)} collective-permute-done((bf16[3,2,16,128]{3,2,1,0:T(8,128)(2,1)S(1)}, bf16[3,2,16,128]{3,2,1,0:T(8,128)(2,1)S(1)}, u32[]{:S(2)}, u32[]{:S(2)}) %collective-permute-start.11) | collective-permute-done | bytes 24608 | tf_op jit(solution)/shard_map/ppermute | solution.py:62
  45.2 0.1 collective-permute-done.12.refs_2_
  45.2 2.6 %gradient.1 = bf16[4,16,32,1024]{3,2,1,0:T(8,128)(2,1)} custom-call(bf16[24,1024]{1,0:T(8,128)(2,1)S(1)} %get-tuple-element.30.table_ref, bf16[3,2,16,128]{3,2,1,0:T(8,128)(2,1)S(1)} %collective-permute-done.10.refs_0_, bf16[3,2,16,128]{3,2,1,0:T(8,128)(2,1)S(1)} %collective-permute-done.11.refs_1_, ...), custom_call_target="tpu_custom_call" | custom-call | tf_op jit(solution)/shard_map/gradient/pallas_call | solution.py:396
  (1 shorter events, 0.0 us)
Async XLA Ops:
  0.6 9.4 %copy-start.3 = (s32[3,4,2]{1,2,0:T(2,128)S(1)}, s32[3,4,2]{1,2,0:T(2,128)}, u32[]{:S(2)}) copy-start(s32[3,4,2]{1,2,0:T(2,128)} %param.8) | copy-start | bytes 292
  0.6 13.5 %copy-start = (bf16[2,3,4,2,48,256]{5,4,3,2,1,0:T(8,128)(2,1)S(1)}, bf16[2,3,4,2,48,256]{5,4,3,2,1,0:T(8,128)(2,1)}, u32[]{:S(2)}) copy-start(bf16[2,3,4,2,48,256]{5,4,3,2,1,0:T(8,128)(2,1)} %right_ref.3) | copy-start | bytes 3538948
  0.7 13.5 %copy-start.1 = (bf16[2,3,4,2,48,256]{5,4,3,2,1,0:T(8,128)(2,1)S(1)}, bf16[2,3,4,2,48,256]{5,4,3,2,1,0:T(8,128)(2,1)}, u32[]{:S(2)}) copy-start(bf16[2,3,4,2,48,256]{5,4,3,2,1,0:T(8,128)(2,1)} %left_ref.3) | copy-start | bytes 3538948
  0.7 25.7 %copy-start.2 = (f32[2,24,1024]{2,1,0:T(8,128)S(1)}, f32[2,24,1024]{2,1,0:T(8,128)}, u32[]{:S(2)}) copy-start(f32[2,24,1024]{2,1,0:T(8,128)} %data_ref.1) | copy-start | bytes 589828
  5.4 6.0 %collective-permute-start = (bf16[3,2,32,128]{3,2,1,0:T(8,128)(2,1)S(1)}, bf16[3,2,32,128]{3,2,1,0:T(8,128)(2,1)S(1)}, u32[]{:S(2)}, u32[]{:S(2)}) collective-permute-start(bf16[3,2,32,128]{3,2,1,0:T(8,128)(2,1)S(1)} %get-tuple-element.20), channel_id=1, source_target_pairs={{0,24},{8,16},{16,8},{24,0},{1,25},{9,17},{17,9},{25,1},{2,26},{10... | collective-permute-start | bytes 147464 | tf_op jit(solution)/shard_map/ppermute | solution.py:62
  9.4 4.1 %collective-permute-start.1 = (bf16[3,2,32,128]{3,2,1,0:T(8,128)(2,1)S(1)}, bf16[3,2,32,128]{3,2,1,0:T(8,128)(2,1)S(1)}, u32[]{:S(2)}, u32[]{:S(2)}) collective-permute-start(bf16[3,2,32,128]{3,2,1,0:T(8,128)(2,1)S(1)} %get-tuple-element.21), channel_id=1, source_target_pairs={{0,16},{8,24},{16,0},{24,8},{1,17},{9,25},{17,1},{25,9},{2,18},{10... | collective-permute-start | bytes 147464 | tf_op jit(solution)/shard_map/ppermute | solution.py:62
  9.9 4.1 %collective-permute-start.2 = (bf16[3,2,32,128]{3,2,1,0:T(8,128)(2,1)S(1)}, bf16[3,2,32,128]{3,2,1,0:T(8,128)(2,1)S(1)}, u32[]{:S(2)}, u32[]{:S(2)}) collective-permute-start(bf16[3,2,32,128]{3,2,1,0:T(8,128)(2,1)S(1)} %get-tuple-element.22), channel_id=1, source_target_pairs={{0,8},{8,0},{16,24},{24,16},{1,9},{9,1},{17,25},{25,17},{2,10},{10... | collective-permute-start | bytes 147464 | tf_op jit(solution)/shard_map/ppermute | solution.py:62
  15.9 6.5 %collective-permute-start.3 = (bf16[2,24,1024]{2,1,0:T(8,128)(2,1)S(1)}, bf16[2,24,1024]{2,1,0:T(8,128)(2,1)S(1)}, u32[]{:S(2)}, u32[]{:S(2)}) collective-permute-start(bf16[2,24,1024]{2,1,0:T(8,128)(2,1)S(1)} %get-tuple-element.24), channel_id=1, source_target_pairs={{0,6},{2,4},{4,2},{6,0},{1,7},{3,5},{5,3},{7,1},{8,14},{10,12},{12... | collective-permute-start | bytes 294920 | tf_op jit(solution)/shard_map/ppermute | solution.py:62
  19.5 6.8 %collective-permute-start.4 = (bf16[2,24,1024]{2,1,0:T(8,128)(2,1)S(1)}, bf16[2,24,1024]{2,1,0:T(8,128)(2,1)S(1)}, u32[]{:S(2)}, u32[]{:S(2)}) collective-permute-start(bf16[2,24,1024]{2,1,0:T(8,128)(2,1)S(1)} %get-tuple-element.25), channel_id=1, source_target_pairs={{0,4},{2,6},{4,0},{6,2},{1,5},{3,7},{5,1},{7,3},{8,12},{10,14},{12... | collective-permute-start | bytes 294920 | tf_op jit(solution)/shard_map/ppermute | solution.py:62
  19.6 6.8 %collective-permute-start.5 = (bf16[2,24,1024]{2,1,0:T(8,128)(2,1)S(1)}, bf16[2,24,1024]{2,1,0:T(8,128)(2,1)S(1)}, u32[]{:S(2)}, u32[]{:S(2)}) collective-permute-start(bf16[2,24,1024]{2,1,0:T(8,128)(2,1)S(1)} %get-tuple-element.26), channel_id=1, source_target_pairs={{0,2},{2,0},{4,6},{6,4},{1,3},{3,1},{5,7},{7,5},{8,10},{10,8},{12,... | collective-permute-start | bytes 294920 | tf_op jit(solution)/shard_map/ppermute | solution.py:62
  26.5 7.6 %collective-permute-start.8 = (bf16[2,24,1024]{2,1,0:T(8,128)(2,1)S(1)}, bf16[2,24,1024]{2,1,0:T(8,128)(2,1)S(1)}, u32[]{:S(2)}, u32[]{:S(2)}) collective-permute-start(bf16[2,24,1024]{2,1,0:T(8,128)(2,1)S(1)} %get-tuple-element.31.refs_0_), channel_id=1, source_target_pairs={{0,6},{2,4},{4,2},{6,0},{1,7},{3,5},{5,3},{7,1},{8,14},{10,12},{12... | collective-permute-start | bytes 294920 | tf_op jit(solution)/shard_map/ppermute | solution.py:62
  29.1 7.5 %collective-permute-start.7 = (bf16[2,24,1024]{2,1,0:T(8,128)(2,1)S(1)}, bf16[2,24,1024]{2,1,0:T(8,128)(2,1)S(1)}, u32[]{:S(2)}, u32[]{:S(2)}) collective-permute-start(bf16[2,24,1024]{2,1,0:T(8,128)(2,1)S(1)} %get-tuple-element.31.refs_0_), channel_id=1, source_target_pairs={{0,4},{2,6},{4,0},{6,2},{1,5},{3,7},{5,1},{7,3},{8,12},{10,14},{12... | collective-permute-start | bytes 294920 | tf_op jit(solution)/shard_map/ppermute | solution.py:62
  29.1 7.5 %collective-permute-start.6 = (bf16[2,24,1024]{2,1,0:T(8,128)(2,1)S(1)}, bf16[2,24,1024]{2,1,0:T(8,128)(2,1)S(1)}, u32[]{:S(2)}, u32[]{:S(2)}) collective-permute-start(bf16[2,24,1024]{2,1,0:T(8,128)(2,1)S(1)} %get-tuple-element.31.refs_0_), channel_id=1, source_target_pairs={{0,2},{2,0},{4,6},{6,4},{1,3},{3,1},{5,7},{7,5},{8,10},{10,8},{12,... | collective-permute-start | bytes 294920 | tf_op jit(solution)/shard_map/ppermute | solution.py:62
  38.1 1.4 %collective-permute-start.9 = (bf16[4,3,2,16,128]{4,3,2,1,0:T(8,128)(2,1)S(1)}, bf16[4,3,2,16,128]{4,3,2,1,0:T(8,128)(2,1)S(1)}, u32[]{:S(2)}, u32[]{:S(2)}) collective-permute-start(bf16[4,3,2,16,128]{4,3,2,1,0:T(8,128)(2,1)S(1)} %get-tuple-element.33), channel_id=1, source_target_pairs={{0,1},{1,0},{2,3},{3,2},{4,5},{5,4},{6,7},{7,6},{8,9},{9,8},{10,11... | collective-permute-start | bytes 294920 | tf_op jit(solution)/shard_map/ppermute | solution.py:62
  39.5 4.8 %collective-permute-start.10 = (bf16[3,2,16,128]{3,2,1,0:T(8,128)(2,1)S(1)}, bf16[3,2,16,128]{3,2,1,0:T(8,128)(2,1)S(1)}, u32[]{:S(2)}, u32[]{:S(2)}) collective-permute-start(bf16[3,2,16,128]{3,2,1,0:T(8,128)(2,1)S(1)} %get-tuple-element.34), channel_id=1, source_target_pairs={{0,24},{8,16},{16,8},{24,0},{1,25},{9,17},{17,9},{25,1},{2,26},{10... | collective-permute-start | bytes 73736 | tf_op jit(solution)/shard_map/ppermute | solution.py:62
  41.3 3.8 %collective-permute-start.11 = (bf16[3,2,16,128]{3,2,1,0:T(8,128)(2,1)S(1)}, bf16[3,2,16,128]{3,2,1,0:T(8,128)(2,1)S(1)}, u32[]{:S(2)}, u32[]{:S(2)}) collective-permute-start(bf16[3,2,16,128]{3,2,1,0:T(8,128)(2,1)S(1)} %get-tuple-element.35), channel_id=1, source_target_pairs={{0,16},{8,24},{16,0},{24,8},{1,17},{9,25},{17,1},{25,9},{2,18},{10... | collective-permute-start | bytes 73736 | tf_op jit(solution)/shard_map/ppermute | solution.py:62
  41.4 3.8 %collective-permute-start.12 = (bf16[3,2,16,128]{3,2,1,0:T(8,128)(2,1)S(1)}, bf16[3,2,16,128]{3,2,1,0:T(8,128)(2,1)S(1)}, u32[]{:S(2)}, u32[]{:S(2)}) collective-permute-start(bf16[3,2,16,128]{3,2,1,0:T(8,128)(2,1)S(1)} %get-tuple-element.36), channel_id=1, source_target_pairs={{0,8},{8,0},{16,24},{24,16},{1,9},{9,1},{17,25},{25,17},{2,10},{10... | collective-permute-start | bytes 73736 | tf_op jit(solution)/shard_map/ppermute | solution.py:62

commit v9 on v8

--- a/solution.py
+++ b/solution.py
@@ -112,7 +112,7 @@
     traces, rhs, length = model.shape
     high = LANES // rhs
     low = traces // high
-    chunks = math.gcd(low, 4)
+    chunks = math.gcd(low, 8)
     bins = 2 * dests * freqs
     table, *blocks = pl.pallas_call(
         spectrum_kernel,
@@ -159,11 +159,13 @@
     return found
 
 
-def predict_kernel(groups, parts, limits_ref, right_ref, left_ref, *refs):
+def predict_kernel(groups, parts, tiles, limits_ref, right_ref, left_ref, *refs):
     arrived_refs, out_refs = refs[:groups], refs[groups : groups + parts]
     spec_ref, sum_ref = refs[groups + parts :]
     _, freqs, _, low, lanes = spec_ref.shape
-    row_tiles, col_tiles, size, tile = left_ref.shape[2:]
+    col_tiles, size, tile = left_ref.shape[3:]
+    begin, end = tiles
+    row_tiles = end - begin
     _, pairs, _ = out_refs[0].shape
     me = lax.axis_index("freq")
     for at, arrived_ref in enumerate(arrived_refs[::-1]):
@@ -185,14 +187,16 @@
                 halves.append(jnp.concatenate(blocks))
             straight = jnp.concatenate(halves, axis=1).astype(jnp.bfloat16)
             crossed = jnp.concatenate([halves[1], -halves[0]], axis=1).astype(jnp.bfloat16)
-            right = [right_ref[c, f, :, j].reshape(row_tiles * size, tile) for c in range(2)]
+            right = [
+                right_ref[c, f, begin:end, j].reshape(row_tiles * size, tile) for c in range(2)
+            ]
             product = dot(right[0], straight, 1, 0) + dot(right[1], crossed, 1, 0)
-            places = [(f, i, j) for i in range(row_tiles)]
+            places = [(f, i, j) for i in range(begin, end)]
             projected.append(masked(product, limits_ref, places, size))
         for i in range(row_tiles):
             straight = [projected[j][i] for j in range(col_tiles)]
             factors = jnp.concatenate(straight + [turned(part) for part in straight])
-            left = left_ref[:, f, i].reshape(2 * col_tiles * size, tile)
+            left = left_ref[:, f, begin + i].reshape(2 * col_tiles * size, tile)
             predicted = dot(factors, left, 0, 0)
             for c in range(2):
                 row = c * rhs
@@ -206,15 +210,16 @@
         out_ref[...] = sum_ref[target(me, at, parts)].astype(out_ref.dtype)
 
 
-def predict(limits, spectrum, green_right, green_left, parts):
-    freqs, row_tiles, col_tiles, size, tile = green_left.shape[1:]
+def predict(limits, spectrum, green_right, green_left, parts, tiles):
+    freqs, _, col_tiles, size, tile = green_left.shape[1:]
+    row_tiles = tiles[1] - tiles[0]
     groups = len(spectrum)
     _, _, low, _ = spectrum[0].shape
     rhs = LANES * groups * low // (col_tiles * tile)
     pairs = freqs * rhs
     sources = row_tiles * tile
     return pl.pallas_call(
-        functools.partial(predict_kernel, groups, parts),
+        functools.partial(predict_kernel, groups, parts, tiles),
         in_specs=[pl.BlockSpec(memory_space=pltpu.VMEM)] * (3 + groups),
         out_specs=[pl.BlockSpec(memory_space=pltpu.VMEM)] * parts,
         out_shape=[jax.ShapeDtypeStruct((2, pairs // parts, sources), jnp.bfloat16)] * parts,
@@ -228,39 +233,46 @@
     )(limits, green_right, green_left, *spectrum[::-1])
 
 
-def residual_kernel(data_ref, *refs):
-    block_refs, (misfit_ref, *part_refs) = refs[:-3], refs[-3:]
-    residual = sum(block_ref[...].astype(jnp.float32) for block_ref in block_refs) - data_ref[...]
-    for c, part_ref in enumerate(part_refs):
-        part_ref[...] = residual[c]
+def residual_kernel(column, data_ref, *refs):
+    block_refs, (misfit_ref, residual_ref) = refs[:-2], refs[-2:]
+    observed = data_ref[:, :, column : column + residual_ref.shape[2]]
+    residual = sum(block_ref[...].astype(jnp.float32) for block_ref in block_refs) - observed
+    residual_ref[...] = residual
     misfit_ref[...] = residual.astype(misfit_ref.dtype)
 
 
-def residual_of(blocks, data):
+def residual_of(blocks, data, column):
     shape = blocks[0].shape
     return pl.pallas_call(
-        residual_kernel,
+        functools.partial(residual_kernel, column),
         in_specs=[pl.BlockSpec(memory_space=pltpu.VMEM)] * (1 + len(blocks)),
-        out_specs=[pl.BlockSpec(memory_space=pltpu.VMEM)] * 3,
+        out_specs=[pl.BlockSpec(memory_space=pltpu.VMEM)] * 2,
         out_shape=[
             jax.ShapeDtypeStruct(shape, jnp.bfloat16),
-            jax.ShapeDtypeStruct(shape[1:], jnp.float32),
-            jax.ShapeDtypeStruct(shape[1:], jnp.float32),
+            jax.ShapeDtypeStruct(shape, jnp.float32),
         ],
         compiler_params=pltpu.CompilerParams(vmem_limit_bytes=VMEM_LIMIT),
         name="residual",
     )(data, *blocks)
 
 
-def back_kernel(parts, groups, reps, limits_ref, right_ref, left_ref, *refs):
-    misfit_refs, out_refs = refs[:parts], refs[parts : parts + reps]
-    misfit_all_ref, grad_ref = refs[parts + reps :]
+def back_kernel(parts, groups, reps, tiles, limits_ref, right_ref, left_ref, *refs):
     _, freqs, row_tiles, col_tiles, size, tile = left_ref.shape
+    begin, end = tiles
+    carried, final = begin > 0, end == row_tiles
+    row_tiles = end - begin
+    misfit_refs, refs = refs[:parts], refs[parts:]
+    if carried:
+        carried_ref, refs = refs[0], refs[1:]
     _, pairs, _ = misfit_refs[0].shape
     rhs = parts * pairs // freqs
-    _, _, _, low, lanes = out_refs[0].shape
-    high = lanes // rhs
-    per_tile = groups * reps // col_tiles
+    if final:
+        out_refs, (misfit_all_ref, grad_ref) = refs[:reps], refs[reps:]
+        _, _, _, low, lanes = out_refs[0].shape
+        high = lanes // rhs
+        per_tile = groups * reps // col_tiles
+    else:
+        carry_ref, misfit_all_ref = refs
     me = lax.axis_index("rtile")
     for at, misfit_ref in enumerate(misfit_refs):
         misfit_all_ref[origin(me, at, parts)] = misfit_ref[...].astype(jnp.float32)
@@ -278,17 +290,22 @@
             ]
             straight = jnp.concatenate(rows).astype(jnp.bfloat16)
             crossed = jnp.concatenate([rows[1], -rows[0]]).astype(jnp.bfloat16)
-            left = [left_ref[c, f, i].reshape(col_tiles * size, tile) for c in range(2)]
+            left = [left_ref[c, f, begin + i].reshape(col_tiles * size, tile) for c in range(2)]
             product = dot(left[0], straight, 1, 1) + dot(left[1], crossed, 1, 1)
-            places = [(f, i, j) for j in range(col_tiles)]
+            places = [(f, begin + i, j) for j in range(col_tiles)]
             back.append(masked(product, limits_ref, places, size))
         for j in range(col_tiles):
             straight = [part[j] for part in back]
             factors = jnp.concatenate(straight + [turned(part) for part in straight])
             right = jnp.concatenate(
-                [right_ref[c, f, :, j].reshape(row_tiles * size, tile) for c in range(2)]
+                [right_ref[c, f, begin:end, j].reshape(row_tiles * size, tile) for c in range(2)]
             )
             grad = dot(factors, right, 0, 0)
+            if carried:
+                grad = grad + carried_ref[f, j]
+            if not final:
+                carry_ref[f, j] = grad
+                continue
             grad = (grad if low % 16 else grad.astype(out_refs[0].dtype)).T
             for at in range(per_tile):
                 rows = at * high * low
@@ -300,6 +317,8 @@
                     grad_ref[j * per_tile + at, f, c] = jnp.concatenate(blocks, axis=1).astype(
                         grad_ref.dtype
                     )
+    if not final:
+        return
     me, own = lax.axis_index("freq"), lax.axis_index("rep")
     for at, out_ref in enumerate(out_refs):
         rep = target(own, at, reps)
@@ -307,26 +326,29 @@
             out_ref[step] = grad_ref[target(me, step, groups) * reps + rep]
 
 
-def back_project(limits, misfit, green_right, green_left, groups, reps):
+def back_project(limits, misfit, green_right, green_left, groups, reps, tiles, carried):
     parts = len(misfit)
     _, pairs, sources = misfit[0].shape
     freqs, row_tiles, col_tiles, size, tile = green_left.shape[1:]
     rhs = parts * pairs // freqs
-    low = col_tiles * tile * rhs // (groups * reps * LANES)
-    block = (freqs, 2, low, LANES)
+    scratch = [pltpu.VMEM((parts, 2, pairs, sources), jnp.float32)]
+    if tiles[1] == row_tiles:
+        low = col_tiles * tile * rhs // (groups * reps * LANES)
+        block = (freqs, 2, low, LANES)
+        out_shape = [jax.ShapeDtypeStruct((groups,) + block, jnp.bfloat16)] * reps
+        scratch.append(pltpu.VMEM((groups * reps,) + block, jnp.bfloat16))
+    else:
+        out_shape = [jax.ShapeDtypeStruct((freqs, col_tiles, 2 * rhs, tile), jnp.float32)]
     return pl.pallas_call(
-        functools.partial(back_kernel, parts, groups, reps),
-        in_specs=[pl.BlockSpec(memory_space=pltpu.VMEM)] * (3 + parts),
-        out_specs=[pl.BlockSpec(memory_space=pltpu.VMEM)] * reps,
-        out_shape=[jax.ShapeDtypeStruct((groups,) + block, jnp.bfloat16)] * reps,
-        scratch_shapes=[
-            pltpu.VMEM((parts, 2, pairs, sources), jnp.float32),
-            pltpu.VMEM((groups * reps,) + block, jnp.bfloat16),
-        ],
-        compiler_params=pltpu.CompilerParams(vmem_limit_bytes=VMEM_LIMIT),
-        cost_estimate=tile_cost(freqs * row_tiles * col_tiles, size, tile, rhs),
+        functools.partial(back_kernel, parts, groups, reps, tiles),
+        in_specs=[pl.BlockSpec(memory_space=pltpu.VMEM)] * (3 + parts + len(carried)),
+        out_specs=[pl.BlockSpec(memory_space=pltpu.VMEM)] * len(out_shape),
+        out_shape=out_shape,
+        scratch_shapes=scratch,
+        compiler_params=pltpu.CompilerParams(vmem_limit_bytes=VMEM_LIMIT),
+        cost_estimate=tile_cost(freqs * (tiles[1] - tiles[0]) * col_tiles, size, tile, rhs),
         name="back_project",
-    )(limits, green_right, green_left, *misfit)
+    )(limits, green_right, green_left, *misfit, *carried)
 
 
 def gather_kernel(reps, *refs):
@@ -418,12 +440,24 @@
     table, spectrum = spectrum_of(model[0], freq_count, freq_local)
     spectrum = exchange(spectrum, "freq")
     limits = jnp.broadcast_to(ranks[..., None, None], ranks.shape + (1, LANES))
-    predicted = predict(limits, spectrum, green_right, green_left, tile_count)
-    misfit, *residual = residual_of(exchange(predicted, "rtile")[::-1], data)
-    misfit = exchange([misfit] * tile_count, "rtile")
-    partial = back_project(limits, misfit, green_right, green_left, freq_count, rep_count)
+    row_tiles, _, _, tile = green_left.shape[2:]
+    halves = [(0, row_tiles // 2), (row_tiles // 2, row_tiles)]
+    predicted = [
+        predict(limits, spectrum, green_right, green_left, tile_count, tiles) for tiles in halves
+    ]
+    residual = [
+        residual_of(exchange(blocks, "rtile")[::-1], data, first * tile)
+        for blocks, (first, _) in zip(predicted, halves)
+    ]
+    misfit = [exchange([half] * tile_count, "rtile") for half, _ in residual]
+    partial = []
+    for blocks, tiles in zip(misfit, halves):
+        partial = back_project(
+            limits, blocks, green_right, green_left, freq_count, rep_count, tiles, partial
+        )
     arrived = exchange(gather(exchange(partial, "rep")), "freq")
-    return (jnp.stack(residual), gradient_of(arrived, table, rhs_count))
+    residual = jnp.concatenate([half for _, half in residual], axis=2)
+    return (residual, gradient_of(arrived, table, rhs_count))
 
 
 def solution(mesh):

time: 48 us -> 50.6 us (1.054)
  starting transfers between devices: 17.1 us -> 26 us
  waiting for transfers between devices: 18.3 us -> 9.91 us
  Pallas kernels: 10.8 us -> 12.8 us
    ppermute x13 -> x19, starting transfers between devices: 17.1 us -> 26 us  [exchange(): arrived.append(lax.ppermute(blocks[step], axis, pairs))]
    ppermute x13 -> x19, waiting for transfers between devices: 18.3 us -> 9.91 us  [exchange(): arrived.append(lax.ppermute(blocks[step], axis, pairs))]
    pallas_call x3 -> x6, Pallas kernels: 3.33 us -> 5.09 us  [the longest x2 2.6 us: predict(): pl.pallas_call(functools.partial(predict_kernel, groups, parts, tiles), i...]
    another operation x1 -> x0, other arithmetic: 0.69 us -> none  [shards(): return (jnp.stack(residual), gradient_of(arrived, table, rhs_count))]
    concatenate x0 -> x1, other arithmetic: none -> 0.69 us  [shards(): residual = jnp.concatenate([half for _, half in residual], axis=2)]
  transfers between devices with their start and end apart: 13 -> 19, of which waited for: 11 -> 11; matrix products, arithmetic and copies ran while one was open for 2% -> 2% of each run, Pallas kernels for 0% -> 5%
where the time goes in v9:
time: 50.6 us; the launch traced here: 50.4 us
  starting transfers between devices  26 us (51%)
  Pallas kernels  12.8 us (25%)
  waiting for transfers between devices  9.91 us (20%)
  between operations  0.76 us (2%)
  other arithmetic  0.69 us (1%)
    ppermute x19, starting transfers between devices, exchange(): arrived.append(lax.ppermute(blocks[step], axis, pairs))  26 us
    ppermute x19, waiting for transfers between devices, exchange(): arrived.append(lax.ppermute(blocks[step], axis, pairs))  9.91 us
    pallas_call x1, Pallas kernels, spectrum_of(): pl.pallas_call(spectrum_kernel, in_specs=[pl.BlockSpec(memory_space=pltpu...  5.06 us
    pallas_call x1, Pallas kernels, gradient_of(): pl.pallas_call(gradient_kernel, in_specs=[pl.BlockSpec(memory_space=pltpu...  2.63 us
    pallas_call x2, Pallas kernels, predict(): pl.pallas_call(functools.partial(predict_kernel, groups, parts, tiles), i...  2.6 us
    pallas_call x2, Pallas kernels, back_project(): pl.pallas_call(functools.partial(back_kernel, parts, groups, reps, tiles)...  2.43 us
  transfers between devices with their start and end apart: 19, of which 11 were waited for; matrix products, arithmetic and copies ran while one was open for 2% of the time, Pallas kernels for 5%

profile of v9, /device:TPU:0, one launch (start us, length us, event | category | flops | bytes accessed | tf_op | source)
XLA Modules:
  0.0 50.4 jit_solution(9431285557925998428)
XLA Ops:
  0.6 0.0 copy-start.3
  0.6 0.0 copy-start
  0.7 0.0 copy-start.1
  0.7 5.1 %spectrum.1 = (bf16[24,1024]{1,0:T(8,128)(2,1)S(1)}, bf16[3,2,32,128]{3,2,1,0:T(8,128)(2,1)S(1)}, bf16[3,2,32,128]{3,2,1,0:T(8,128)(2,1)S(1)}, bf16[3,2,32,128]{...) custom-call(bf16[4,32,32,1024]{3,2,1,0:T(8,128)(2,1)} %bitcast.2), custom_call_target="tpu_custom_call" | custom-call | tf_op jit(solution)/shard_map/spectrum/pallas_call | solution.py:117
  5.7 0.0 copy-start.2
  5.7 4.0 %collective-permute-start = (bf16[3,2,32,128]{3,2,1,0:T(8,128)(2,1)S(1)}, bf16[3,2,32,128]{3,2,1,0:T(8,128)(2,1)S(1)}, u32[]{:S(2)}, u32[]{:S(2)}) collective-permute-start(bf16[3,2,32,128]{3,2,1,0:T(8,128)(2,1)S(1)} %get-tuple-element.25), channel_id=1, source_target_pairs={{0,24},{8,16},{16,8},{24,0},{1,25},{9,17},{17,9},{25,1},{2,26},{10... | collective-permute-start | bytes 147464 | tf_op jit(solution)/shard_map/ppermute | solution.py:62
  9.7 0.5 %collective-permute-start.1 = (bf16[3,2,32,128]{3,2,1,0:T(8,128)(2,1)S(1)}, bf16[3,2,32,128]{3,2,1,0:T(8,128)(2,1)S(1)}, u32[]{:S(2)}, u32[]{:S(2)}) collective-permute-start(bf16[3,2,32,128]{3,2,1,0:T(8,128)(2,1)S(1)} %get-tuple-element.26), channel_id=1, source_target_pairs={{0,16},{8,24},{16,0},{24,8},{1,17},{9,25},{17,1},{25,9},{2,18},{10... | collective-permute-start | bytes 147464 | tf_op jit(solution)/shard_map/ppermute | solution.py:62
  10.2 0.1 collective-permute-start.2
  10.3 0.0 copy-done.3
  10.3 0.1 copy.7
  10.4 1.3 %collective-permute-done.refs_0_ = bf16[3,2,32,128]{3,2,1,0:T(8,128)(2,1)S(1)} collective-permute-done((bf16[3,2,32,128]{3,2,1,0:T(8,128)(2,1)S(1)}, bf16[3,2,32,128]{3,2,1,0:T(8,128)(2,1)S(1)}, u32[]{:S(2)}, u32[]{:S(2)}) %collective-permute-start) | collective-permute-done | bytes 49184 | tf_op jit(solution)/shard_map/ppermute | solution.py:62
  11.8 2.0 %collective-permute-done.1.refs_1_ = bf16[3,2,32,128]{3,2,1,0:T(8,128)(2,1)S(1)} collective-permute-done((bf16[3,2,32,128]{3,2,1,0:T(8,128)(2,1)S(1)}, bf16[3,2,32,128]{3,2,1,0:T(8,128)(2,1)S(1)}, u32[]{:S(2)}, u32[]{:S(2)}) %collective-permute-start.1) | collective-permute-done | bytes 49184 | tf_op jit(solution)/shard_map/ppermute | solution.py:62
  13.8 0.5 %collective-permute-done.2.refs_2_ = bf16[3,2,32,128]{3,2,1,0:T(8,128)(2,1)S(1)} collective-permute-done((bf16[3,2,32,128]{3,2,1,0:T(8,128)(2,1)S(1)}, bf16[3,2,32,128]{3,2,1,0:T(8,128)(2,1)S(1)}, u32[]{:S(2)}, u32[]{:S(2)}) %collective-permute-start.2) | collective-permute-done | bytes 49184 | tf_op jit(solution)/shard_map/ppermute | solution.py:62
  14.3 0.1 broadcast_in_dim.2.limits_ref
  14.4 0.0 copy-done
  14.4 0.0 copy-done.1
  14.4 1.3 %predict.2 = (bf16[2,24,512]{2,1,0:T(8,128)(2,1)S(1)}, bf16[2,24,512]{2,1,0:T(8,128)(2,1)S(1)}, bf16[2,24,512]{2,1,0:T(8,128)(2,1)S(1)}, bf16[2,24,512]{2,1,0:T(8,128)(2,1)S(1)}) custom-call(s32[3,4,2,1,128]{4,3,2,1,0:T(1,128)S(1)} %broadcast_in_dim.2.limits_ref, bf16[2,3,4,2,48,256]{5,4,3,2,1,0:T(8,128)(2,1)S(1)} %copy-done, ...), custom_call_target="tpu_custom_call" | custom-call | flops 75497472 | bytes 1179648 | tf_op jit(solution)/shard_map/predict/pallas_call | solution.py:221
  15.7 3.7 %collective-permute-start.3 = (bf16[2,24,512]{2,1,0:T(8,128)(2,1)S(1)}, bf16[2,24,512]{2,1,0:T(8,128)(2,1)S(1)}, u32[]{:S(2)}, u32[]{:S(2)}) collective-permute-start(bf16[2,24,512]{2,1,0:T(8,128)(2,1)S(1)} %get-tuple-element.29), channel_id=1, source_target_pairs={{0,6},{2,4},{4,2},{6,0},{1,7},{3,5},{5,3},{7,1},{8,14},{10,12},{12... | collective-permute-start | bytes 147464 | tf_op jit(solution)/shard_map/ppermute | solution.py:62
  19.4 0.0 collective-permute-start.4
  19.4 0.8 %collective-permute-start.5 = (bf16[2,24,512]{2,1,0:T(8,128)(2,1)S(1)}, bf16[2,24,512]{2,1,0:T(8,128)(2,1)S(1)}, u32[]{:S(2)}, u32[]{:S(2)}) collective-permute-start(bf16[2,24,512]{2,1,0:T(8,128)(2,1)S(1)} %get-tuple-element.31), channel_id=1, source_target_pairs={{0,2},{2,0},{4,6},{6,4},{1,3},{3,1},{5,7},{7,5},{8,10},{10,8},{12,... | collective-permute-start | bytes 147464 | tf_op jit(solution)/shard_map/ppermute | solution.py:62
  20.2 1.3 %predict.3 = (bf16[2,24,512]{2,1,0:T(8,128)(2,1)S(1)}, bf16[2,24,512]{2,1,0:T(8,128)(2,1)S(1)}, bf16[2,24,512]{2,1,0:T(8,128)(2,1)S(1)}, bf16[2,24,512]{2,1,0:T(8,128)(2,1)S(1)}) custom-call(s32[3,4,2,1,128]{4,3,2,1,0:T(1,128)S(1)} %broadcast_in_dim.2.limits_ref, bf16[2,3,4,2,48,256]{5,4,3,2,1,0:T(8,128)(2,1)S(1)} %copy-done, ...), custom_call_target="tpu_custom_call" | custom-call | flops 75497472 | bytes 1179648 | tf_op jit(solution)/shard_map/predict/pallas_call | solution.py:221
  21.5 3.7 %collective-permute-start.6 = (bf16[2,24,512]{2,1,0:T(8,128)(2,1)S(1)}, bf16[2,24,512]{2,1,0:T(8,128)(2,1)S(1)}, u32[]{:S(2)}, u32[]{:S(2)}) collective-permute-start(bf16[2,24,512]{2,1,0:T(8,128)(2,1)S(1)} %get-tuple-element.34), channel_id=1, source_target_pairs={{0,6},{2,4},{4,2},{6,0},{1,7},{3,5},{5,3},{7,1},{8,14},{10,12},{12... | collective-permute-start | bytes 147464 | tf_op jit(solution)/shard_map/ppermute | solution.py:62
  25.2 0.0 collective-permute-start.7
  25.2 0.0 collective-permute-done.3.refs_0_
  25.2 0.7 %collective-permute-start.8 = (bf16[2,24,512]{2,1,0:T(8,128)(2,1)S(1)}, bf16[2,24,512]{2,1,0:T(8,128)(2,1)S(1)}, u32[]{:S(2)}, u32[]{:S(2)}) collective-permute-start(bf16[2,24,512]{2,1,0:T(8,128)(2,1)S(1)} %get-tuple-element.36), channel_id=1, source_target_pairs={{0,2},{2,0},{4,6},{6,4},{1,3},{3,1},{5,7},{7,5},{8,10},{10,8},{12,... | collective-permute-start | bytes 147464 | tf_op jit(solution)/shard_map/ppermute | solution.py:62
  25.9 0.0 collective-permute-done.4.refs_1_
  25.9 0.0 collective-permute-done.5.refs_2_
  25.9 0.0 copy-done.2
  26.0 3.7 %collective-permute-start.14 = (bf16[2,24,512]{2,1,0:T(8,128)(2,1)S(1)}, bf16[2,24,512]{2,1,0:T(8,128)(2,1)S(1)}, u32[]{:S(2)}, u32[]{:S(2)}) collective-permute-start(bf16[2,24,512]{2,1,0:T(8,128)(2,1)S(1)} %get-tuple-element.41.refs_0_), channel_id=1, source_target_pairs={{0,6},{2,4},{4,2},{6,0},{1,7},{3,5},{5,3},{7,1},{8,14},{10,12},{12... | collective-permute-start | bytes 147464 | tf_op jit(solution)/shard_map/ppermute | solution.py:62
  29.7 0.0 collective-permute-start.13
  29.7 0.0 collective-permute-done.6.refs_0_
  29.7 0.7 %collective-permute-start.12 = (bf16[2,24,512]{2,1,0:T(8,128)(2,1)S(1)}, bf16[2,24,512]{2,1,0:T(8,128)(2,1)S(1)}, u32[]{:S(2)}, u32[]{:S(2)}) collective-permute-start(bf16[2,24,512]{2,1,0:T(8,128)(2,1)S(1)} %get-tuple-element.41.refs_0_), channel_id=1, source_target_pairs={{0,2},{2,0},{4,6},{6,4},{1,3},{3,1},{5,7},{7,5},{8,10},{10,8},{12,... | collective-permute-start | bytes 147464 | tf_op jit(solution)/shard_map/ppermute | solution.py:62
  30.4 0.3 collective-permute-done.7.refs_1_
  30.7 0.1 collective-permute-done.8.refs_2_
  30.9 3.3 %collective-permute-start.11 = (bf16[2,24,512]{2,1,0:T(8,128)(2,1)S(1)}, bf16[2,24,512]{2,1,0:T(8,128)(2,1)S(1)}, u32[]{:S(2)}, u32[]{:S(2)}) collective-permute-start(bf16[2,24,512]{2,1,0:T(8,128)(2,1)S(1)} %get-tuple-element.40.refs_0_), channel_id=1, source_target_pairs={{0,6},{2,4},{4,2},{6,0},{1,7},{3,5},{5,3},{7,1},{8,14},{10,12},{12... | collective-permute-start | bytes 147464 | tf_op jit(solution)/shard_map/ppermute | solution.py:62
  34.2 0.0 collective-permute-start.10
  34.2 0.0 collective-permute-done.14.refs_3_
  34.2 1.1 %collective-permute-start.9 = (bf16[2,24,512]{2,1,0:T(8,128)(2,1)S(1)}, bf16[2,24,512]{2,1,0:T(8,128)(2,1)S(1)}, u32[]{:S(2)}, u32[]{:S(2)}) collective-permute-start(bf16[2,24,512]{2,1,0:T(8,128)(2,1)S(1)} %get-tuple-element.40.refs_0_), channel_id=1, source_target_pairs={{0,2},{2,0},{4,6},{6,4},{1,3},{3,1},{5,7},{7,5},{8,10},{10,8},{12,... | collective-permute-start | bytes 147464 | tf_op jit(solution)/shard_map/ppermute | solution.py:62
  35.3 0.0 collective-permute-done.13.refs_2_
  35.3 0.0 collective-permute-done.12.refs_1_
  35.3 1.1 %back_project.2.refs_4_ = f32[3,2,64,256]{3,2,1,0:T(8,128)S(1)} custom-call(s32[3,4,2,1,128]{4,3,2,1,0:T(1,128)S(1)} %broadcast_in_dim.2.limits_ref, bf16[2,3,4,2,48,256]{5,4,3,2,1,0:T(8,128)(2,1)S(1)} %copy-done, bf16[2,3,4,2,48,256]{5,4,3,2,1,0:T(8,128)(2,1)S(1)} %copy-done.1, bf16[2,24,512]{2,1,0:T(8,128)(2,1)S(1)} %get-tuple-element.41.refs_0_, ...), custom_call_target="tpu_custom_call" | custom-call | flops 75497472 | bytes 1179648 | tf_op jit(solution)/shard_map/back_project/pallas_call | solution.py:342
  36.5 0.4 collective-permute-done.11.refs_3_
  36.8 2.3 %collective-permute-done.10.refs_2_ = bf16[2,24,512]{2,1,0:T(8,128)(2,1)S(1)} collective-permute-done((bf16[2,24,512]{2,1,0:T(8,128)(2,1)S(1)}, bf16[2,24,512]{2,1,0:T(8,128)(2,1)S(1)}, u32[]{:S(2)}, u32[]{:S(2)}) %collective-permute-start.10) | collective-permute-done | bytes 49184 | tf_op jit(solution)/shard_map/ppermute | solution.py:62
  39.2 0.0 collective-permute-done.9.refs_1_
  39.2 1.3 %back_project.3 = (bf16[4,3,2,16,128]{4,3,2,1,0:T(8,128)(2,1)S(1)}, bf16[4,3,2,16,128]{4,3,2,1,0:T(8,128)(2,1)S(1)}) custom-call(s32[3,4,2,1,128]{4,3,2,1,0:T(1,128)S(1)} %broadcast_in_dim.2.limits_ref, bf16[2,3,4,2,48,256]{5,4,3,2,1,0:T(8,128)(2,1)S(1)} %copy-done, bf16[2,3,4,2,48,256]{5,4,3,2,1,0:T(8,128)(2,1)S(1)} %copy-done.1, ...), custom_call_target="tpu_custom_call" | custom-call | flops 75497472 | bytes 1179648 | tf_op jit(solution)/shard_map/back_project/pallas_call | solution.py:342
  40.5 0.1 collective-permute-start.15
  40.6 1.3 %collective-permute-done.15.refs_1_ = bf16[4,3,2,16,128]{4,3,2,1,0:T(8,128)(2,1)S(1)} collective-permute-done((bf16[4,3,2,16,128]{4,3,2,1,0:T(8,128)(2,1)S(1)}, bf16[4,3,2,16,128]{4,3,2,1,0:T(8,128)(2,1)S(1)}, u32[]{:S(2)}, u32[]{:S(2)}) %collective-permute-start.15) | collective-permute-done | bytes 98336 | tf_op jit(solution)/shard_map/ppermute | solution.py:62
  41.9 1.6 %collective-permute-start.16 = (bf16[3,2,16,128]{3,2,1,0:T(8,128)(2,1)S(1)}, bf16[3,2,16,128]{3,2,1,0:T(8,128)(2,1)S(1)}, u32[]{:S(2)}, u32[]{:S(2)}) collective-permute-start(bf16[3,2,16,128]{3,2,1,0:T(8,128)(2,1)S(1)} %get-tuple-element.44), channel_id=1, source_target_pairs={{0,24},{8,16},{16,8},{24,0},{1,25},{9,17},{17,9},{25,1},{2,26},{10... | collective-permute-start | bytes 73736 | tf_op jit(solution)/shard_map/ppermute | solution.py:62
  43.4 0.5 %collective-permute-start.17 = (bf16[3,2,16,128]{3,2,1,0:T(8,128)(2,1)S(1)}, bf16[3,2,16,128]{3,2,1,0:T(8,128)(2,1)S(1)}, u32[]{:S(2)}, u32[]{:S(2)}) collective-permute-start(bf16[3,2,16,128]{3,2,1,0:T(8,128)(2,1)S(1)} %get-tuple-element.45), channel_id=1, source_target_pairs={{0,16},{8,24},{16,0},{24,8},{1,17},{9,25},{17,1},{25,9},{2,18},{10... | collective-permute-start | bytes 73736 | tf_op jit(solution)/shard_map/ppermute | solution.py:62
  44.0 1.5 %collective-permute-start.18 = (bf16[3,2,16,128]{3,2,1,0:T(8,128)(2,1)S(1)}, bf16[3,2,16,128]{3,2,1,0:T(8,128)(2,1)S(1)}, u32[]{:S(2)}, u32[]{:S(2)}) collective-permute-start(bf16[3,2,16,128]{3,2,1,0:T(8,128)(2,1)S(1)} %get-tuple-element.46), channel_id=1, source_target_pairs={{0,8},{8,0},{16,24},{24,16},{1,9},{9,1},{17,25},{25,17},{2,10},{10... | collective-permute-start | bytes 73736 | tf_op jit(solution)/shard_map/ppermute | solution.py:62
  45.4 0.7 %pad_maximum_fusion = f32[2,24,1024]{2,1,0:T(8,128)} fusion(f32[2,24,512]{2,1,0:T(8,128)S(1)} %get-tuple-element.38, f32[2,24,512]{2,1,0:T(8,128)S(1)} %get-tuple-element.33), kind=kLoop, calls=%fused_computation | loop fusion | flops 49152 | bytes 393216 | tf_op jit(solution)/shard_map/concatenate | solution.py:459
  46.1 0.5 %collective-permute-done.16.refs_0_ = bf16[3,2,16,128]{3,2,1,0:T(8,128)(2,1)S(1)} collective-permute-done((bf16[3,2,16,128]{3,2,1,0:T(8,128)(2,1)S(1)}, bf16[3,2,16,128]{3,2,1,0:T(8,128)(2,1)S(1)}, u32[]{:S(2)}, u32[]{:S(2)}) %collective-permute-start.16) | collective-permute-done | bytes 24608 | tf_op jit(solution)/shard_map/ppermute | solution.py:62
  46.7 0.6 %collective-permute-done.17.refs_1_ = bf16[3,2,16,128]{3,2,1,0:T(8,128)(2,1)S(1)} collective-permute-done((bf16[3,2,16,128]{3,2,1,0:T(8,128)(2,1)S(1)}, bf16[3,2,16,128]{3,2,1,0:T(8,128)(2,1)S(1)}, u32[]{:S(2)}, u32[]{:S(2)}) %collective-permute-start.17) | collective-permute-done | bytes 24608 | tf_op jit(solution)/shard_map/ppermute | solution.py:62
  47.3 0.5 %collective-permute-done.18.refs_2_ = bf16[3,2,16,128]{3,2,1,0:T(8,128)(2,1)S(1)} collective-permute-done((bf16[3,2,16,128]{3,2,1,0:T(8,128)(2,1)S(1)}, bf16[3,2,16,128]{3,2,1,0:T(8,128)(2,1)S(1)}, u32[]{:S(2)}, u32[]{:S(2)}) %collective-permute-start.18) | collective-permute-done | bytes 24608 | tf_op jit(solution)/shard_map/ppermute | solution.py:62
  47.8 2.6 %gradient.1 = bf16[4,16,32,1024]{3,2,1,0:T(8,128)(2,1)} custom-call(bf16[24,1024]{1,0:T(8,128)(2,1)S(1)} %get-tuple-element.39.table_ref, bf16[3,2,16,128]{3,2,1,0:T(8,128)(2,1)S(1)} %collective-permute-done.16.refs_0_, bf16[3,2,16,128]{3,2,1,0:T(8,128)(2,1)S(1)} %collective-permute-done.17.refs_1_, ...), custom_call_target="tpu_custom_call" | custom-call | tf_op jit(solution)/shard_map/gradient/pallas_call | solution.py:418
  (3 shorter events, 0.1 us)
Async XLA Ops:
  0.6 9.7 %copy-start.3 = (s32[3,4,2]{1,2,0:T(2,128)S(1)}, s32[3,4,2]{1,2,0:T(2,128)}, u32[]{:S(2)}) copy-start(s32[3,4,2]{1,2,0:T(2,128)} %param.8) | copy-start | bytes 292
  0.6 13.7 %copy-start = (bf16[2,3,4,2,48,256]{5,4,3,2,1,0:T(8,128)(2,1)S(1)}, bf16[2,3,4,2,48,256]{5,4,3,2,1,0:T(8,128)(2,1)}, u32[]{:S(2)}) copy-start(bf16[2,3,4,2,48,256]{5,4,3,2,1,0:T(8,128)(2,1)} %right_ref.7) | copy-start | bytes 3538948
  0.7 13.7 %copy-start.1 = (bf16[2,3,4,2,48,256]{5,4,3,2,1,0:T(8,128)(2,1)S(1)}, bf16[2,3,4,2,48,256]{5,4,3,2,1,0:T(8,128)(2,1)}, u32[]{:S(2)}) copy-start(bf16[2,3,4,2,48,256]{5,4,3,2,1,0:T(8,128)(2,1)} %left_ref.7) | copy-start | bytes 3538948
  5.7 20.2 %copy-start.2 = (f32[2,24,1024]{2,1,0:T(8,128)S(1)}, f32[2,24,1024]{2,1,0:T(8,128)}, u32[]{:S(2)}) copy-start(f32[2,24,1024]{2,1,0:T(8,128)} %data_ref.3) | copy-start | bytes 589828
  5.7 6.0 %collective-permute-start = (bf16[3,2,32,128]{3,2,1,0:T(8,128)(2,1)S(1)}, bf16[3,2,32,128]{3,2,1,0:T(8,128)(2,1)S(1)}, u32[]{:S(2)}, u32[]{:S(2)}) collective-permute-start(bf16[3,2,32,128]{3,2,1,0:T(8,128)(2,1)S(1)} %get-tuple-element.25), channel_id=1, source_target_pairs={{0,24},{8,16},{16,8},{24,0},{1,25},{9,17},{17,9},{25,1},{2,26},{10... | collective-permute-start | bytes 147464 | tf_op jit(solution)/shard_map/ppermute | solution.py:62
  9.7 4.1 %collective-permute-start.1 = (bf16[3,2,32,128]{3,2,1,0:T(8,128)(2,1)S(1)}, bf16[3,2,32,128]{3,2,1,0:T(8,128)(2,1)S(1)}, u32[]{:S(2)}, u32[]{:S(2)}) collective-permute-start(bf16[3,2,32,128]{3,2,1,0:T(8,128)(2,1)S(1)} %get-tuple-element.26), channel_id=1, source_target_pairs={{0,16},{8,24},{16,0},{24,8},{1,17},{9,25},{17,1},{25,9},{2,18},{10... | collective-permute-start | bytes 147464 | tf_op jit(solution)/shard_map/ppermute | solution.py:62
  10.2 4.1 %collective-permute-start.2 = (bf16[3,2,32,128]{3,2,1,0:T(8,128)(2,1)S(1)}, bf16[3,2,32,128]{3,2,1,0:T(8,128)(2,1)S(1)}, u32[]{:S(2)}, u32[]{:S(2)}) collective-permute-start(bf16[3,2,32,128]{3,2,1,0:T(8,128)(2,1)S(1)} %get-tuple-element.27), channel_id=1, source_target_pairs={{0,8},{8,0},{16,24},{24,16},{1,9},{9,1},{17,25},{25,17},{2,10},{10... | collective-permute-start | bytes 147464 | tf_op jit(solution)/shard_map/ppermute | solution.py:62
  15.7 9.5 %collective-permute-start.3 = (bf16[2,24,512]{2,1,0:T(8,128)(2,1)S(1)}, bf16[2,24,512]{2,1,0:T(8,128)(2,1)S(1)}, u32[]{:S(2)}, u32[]{:S(2)}) collective-permute-start(bf16[2,24,512]{2,1,0:T(8,128)(2,1)S(1)} %get-tuple-element.29), channel_id=1, source_target_pairs={{0,6},{2,4},{4,2},{6,0},{1,7},{3,5},{5,3},{7,1},{8,14},{10,12},{12... | collective-permute-start | bytes 147464 | tf_op jit(solution)/shard_map/ppermute | solution.py:62
  19.4 6.5 %collective-permute-start.4 = (bf16[2,24,512]{2,1,0:T(8,128)(2,1)S(1)}, bf16[2,24,512]{2,1,0:T(8,128)(2,1)S(1)}, u32[]{:S(2)}, u32[]{:S(2)}) collective-permute-start(bf16[2,24,512]{2,1,0:T(8,128)(2,1)S(1)} %get-tuple-element.30), channel_id=1, source_target_pairs={{0,4},{2,6},{4,0},{6,2},{1,5},{3,7},{5,1},{7,3},{8,12},{10,14},{12... | collective-permute-start | bytes 147464 | tf_op jit(solution)/shard_map/ppermute | solution.py:62
  19.4 6.5 %collective-permute-start.5 = (bf16[2,24,512]{2,1,0:T(8,128)(2,1)S(1)}, bf16[2,24,512]{2,1,0:T(8,128)(2,1)S(1)}, u32[]{:S(2)}, u32[]{:S(2)}) collective-permute-start(bf16[2,24,512]{2,1,0:T(8,128)(2,1)S(1)} %get-tuple-element.31), channel_id=1, source_target_pairs={{0,2},{2,0},{4,6},{6,4},{1,3},{3,1},{5,7},{7,5},{8,10},{10,8},{12,... | collective-permute-start | bytes 147464 | tf_op jit(solution)/shard_map/ppermute | solution.py:62
  21.5 8.2 %collective-permute-start.6 = (bf16[2,24,512]{2,1,0:T(8,128)(2,1)S(1)}, bf16[2,24,512]{2,1,0:T(8,128)(2,1)S(1)}, u32[]{:S(2)}, u32[]{:S(2)}) collective-permute-start(bf16[2,24,512]{2,1,0:T(8,128)(2,1)S(1)} %get-tuple-element.34), channel_id=1, source_target_pairs={{0,6},{2,4},{4,2},{6,0},{1,7},{3,5},{5,3},{7,1},{8,14},{10,12},{12... | collective-permute-start | bytes 147464 | tf_op jit(solution)/shard_map/ppermute | solution.py:62
  25.2 5.6 %collective-permute-start.7 = (bf16[2,24,512]{2,1,0:T(8,128)(2,1)S(1)}, bf16[2,24,512]{2,1,0:T(8,128)(2,1)S(1)}, u32[]{:S(2)}, u32[]{:S(2)}) collective-permute-start(bf16[2,24,512]{2,1,0:T(8,128)(2,1)S(1)} %get-tuple-element.35), channel_id=1, source_target_pairs={{0,4},{2,6},{4,0},{6,2},{1,5},{3,7},{5,1},{7,3},{8,12},{10,14},{12... | collective-permute-start | bytes 147464 | tf_op jit(solution)/shard_map/ppermute | solution.py:62
  25.2 5.7 %collective-permute-start.8 = (bf16[2,24,512]{2,1,0:T(8,128)(2,1)S(1)}, bf16[2,24,512]{2,1,0:T(8,128)(2,1)S(1)}, u32[]{:S(2)}, u32[]{:S(2)}) collective-permute-start(bf16[2,24,512]{2,1,0:T(8,128)(2,1)S(1)} %get-tuple-element.36), channel_id=1, source_target_pairs={{0,2},{2,0},{4,6},{6,4},{1,3},{3,1},{5,7},{7,5},{8,10},{10,8},{12,... | collective-permute-start | bytes 147464 | tf_op jit(solution)/shard_map/ppermute | solution.py:62
  26.0 8.2 %collective-permute-start.14 = (bf16[2,24,512]{2,1,0:T(8,128)(2,1)S(1)}, bf16[2,24,512]{2,1,0:T(8,128)(2,1)S(1)}, u32[]{:S(2)}, u32[]{:S(2)}) collective-permute-start(bf16[2,24,512]{2,1,0:T(8,128)(2,1)S(1)} %get-tuple-element.41.refs_0_), channel_id=1, source_target_pairs={{0,6},{2,4},{4,2},{6,0},{1,7},{3,5},{5,3},{7,1},{8,14},{10,12},{12... | collective-permute-start | bytes 147464 | tf_op jit(solution)/shard_map/ppermute | solution.py:62
  29.7 5.6 %collective-permute-start.13 = (bf16[2,24,512]{2,1,0:T(8,128)(2,1)S(1)}, bf16[2,24,512]{2,1,0:T(8,128)(2,1)S(1)}, u32[]{:S(2)}, u32[]{:S(2)}) collective-permute-start(bf16[2,24,512]{2,1,0:T(8,128)(2,1)S(1)} %get-tuple-element.41.refs_0_), channel_id=1, source_target_pairs={{0,4},{2,6},{4,0},{6,2},{1,5},{3,7},{5,1},{7,3},{8,12},{10,14},{12... | collective-permute-start | bytes 147464 | tf_op jit(solution)/shard_map/ppermute | solution.py:62
  29.7 5.6 %collective-permute-start.12 = (bf16[2,24,512]{2,1,0:T(8,128)(2,1)S(1)}, bf16[2,24,512]{2,1,0:T(8,128)(2,1)S(1)}, u32[]{:S(2)}, u32[]{:S(2)}) collective-permute-start(bf16[2,24,512]{2,1,0:T(8,128)(2,1)S(1)} %get-tuple-element.41.refs_0_), channel_id=1, source_target_pairs={{0,2},{2,0},{4,6},{6,4},{1,3},{3,1},{5,7},{7,5},{8,10},{10,8},{12,... | collective-permute-start | bytes 147464 | tf_op jit(solution)/shard_map/ppermute | solution.py:62
  30.9 6.0 %collective-permute-start.11 = (bf16[2,24,512]{2,1,0:T(8,128)(2,1)S(1)}, bf16[2,24,512]{2,1,0:T(8,128)(2,1)S(1)}, u32[]{:S(2)}, u32[]{:S(2)}) collective-permute-start(bf16[2,24,512]{2,1,0:T(8,128)(2,1)S(1)} %get-tuple-element.40.refs_0_), channel_id=1, source_target_pairs={{0,6},{2,4},{4,2},{6,0},{1,7},{3,5},{5,3},{7,1},{8,14},{10,12},{12... | collective-permute-start | bytes 147464 | tf_op jit(solution)/shard_map/ppermute | solution.py:62
  34.2 5.0 %collective-permute-start.10 = (bf16[2,24,512]{2,1,0:T(8,128)(2,1)S(1)}, bf16[2,24,512]{2,1,0:T(8,128)(2,1)S(1)}, u32[]{:S(2)}, u32[]{:S(2)}) collective-permute-start(bf16[2,24,512]{2,1,0:T(8,128)(2,1)S(1)} %get-tuple-element.40.refs_0_), channel_id=1, source_target_pairs={{0,4},{2,6},{4,0},{6,2},{1,5},{3,7},{5,1},{7,3},{8,12},{10,14},{12... | collective-permute-start | bytes 147464 | tf_op jit(solution)/shard_map/ppermute | solution.py:62
  34.2 5.0 %collective-permute-start.9 = (bf16[2,24,512]{2,1,0:T(8,128)(2,1)S(1)}, bf16[2,24,512]{2,1,0:T(8,128)(2,1)S(1)}, u32[]{:S(2)}, u32[]{:S(2)}) collective-permute-start(bf16[2,24,512]{2,1,0:T(8,128)(2,1)S(1)} %get-tuple-element.40.refs_0_), channel_id=1, source_target_pairs={{0,2},{2,0},{4,6},{6,4},{1,3},{3,1},{5,7},{7,5},{8,10},{10,8},{12,... | collective-permute-start | bytes 147464 | tf_op jit(solution)/shard_map/ppermute | solution.py:62
  40.5 1.4 %collective-permute-start.15 = (bf16[4,3,2,16,128]{4,3,2,1,0:T(8,128)(2,1)S(1)}, bf16[4,3,2,16,128]{4,3,2,1,0:T(8,128)(2,1)S(1)}, u32[]{:S(2)}, u32[]{:S(2)}) collective-permute-start(bf16[4,3,2,16,128]{4,3,2,1,0:T(8,128)(2,1)S(1)} %get-tuple-element.43), channel_id=1, source_target_pairs={{0,1},{1,0},{2,3},{3,2},{4,5},{5,4},{6,7},{7,6},{8,9},{9,8},{10,11... | collective-permute-start | bytes 294920 | tf_op jit(solution)/shard_map/ppermute | solution.py:62
  41.9 4.8 %collective-permute-start.16 = (bf16[3,2,16,128]{3,2,1,0:T(8,128)(2,1)S(1)}, bf16[3,2,16,128]{3,2,1,0:T(8,128)(2,1)S(1)}, u32[]{:S(2)}, u32[]{:S(2)}) collective-permute-start(bf16[3,2,16,128]{3,2,1,0:T(8,128)(2,1)S(1)} %get-tuple-element.44), channel_id=1, source_target_pairs={{0,24},{8,16},{16,8},{24,0},{1,25},{9,17},{17,9},{25,1},{2,26},{10... | collective-permute-start | bytes 73736 | tf_op jit(solution)/shard_map/ppermute | solution.py:62
  43.4 3.8 %collective-permute-start.17 = (bf16[3,2,16,128]{3,2,1,0:T(8,128)(2,1)S(1)}, bf16[3,2,16,128]{3,2,1,0:T(8,128)(2,1)S(1)}, u32[]{:S(2)}, u32[]{:S(2)}) collective-permute-start(bf16[3,2,16,128]{3,2,1,0:T(8,128)(2,1)S(1)} %get-tuple-element.45), channel_id=1, source_target_pairs={{0,16},{8,24},{16,0},{24,8},{1,17},{9,25},{17,1},{25,9},{2,18},{10... | collective-permute-start | bytes 73736 | tf_op jit(solution)/shard_map/ppermute | solution.py:62
  44.0 3.8 %collective-permute-start.18 = (bf16[3,2,16,128]{3,2,1,0:T(8,128)(2,1)S(1)}, bf16[3,2,16,128]{3,2,1,0:T(8,128)(2,1)S(1)}, u32[]{:S(2)}, u32[]{:S(2)}) collective-permute-start(bf16[3,2,16,128]{3,2,1,0:T(8,128)(2,1)S(1)} %get-tuple-element.46), channel_id=1, source_target_pairs={{0,8},{8,0},{16,24},{24,16},{1,9},{9,1},{17,25},{25,17},{2,10},{10... | collective-permute-start | bytes 73736 | tf_op jit(solution)/shard_map/ppermute | solution.py:62

commit v10 on v8

--- a/solution.py
+++ b/solution.py
@@ -63,6 +63,44 @@
     return [blocks[0]] + arrived[::-1]
 
 
+def swap(block, axis, count, step):
+    return lax.ppermute(block, axis, [(me, me ^ step) for me in range(count)])
+
+
+def add_kernel(first_ref, second_ref, out_ref):
+    total = first_ref[...].astype(jnp.float32) + second_ref[...].astype(jnp.float32)
+    out_ref[...] = total.astype(out_ref.dtype)
+
+
+def add(first, second):
+    return pl.pallas_call(
+        add_kernel,
+        in_specs=[pl.BlockSpec(memory_space=pltpu.VMEM)] * 2,
+        out_specs=pl.BlockSpec(memory_space=pltpu.VMEM),
+        out_shape=jax.ShapeDtypeStruct(first.shape, first.dtype),
+        compiler_params=pltpu.CompilerParams(vmem_limit_bytes=VMEM_LIMIT),
+        name="add",
+    )(first, second)
+
+
+def scatter_sums(blocks, axis):
+    count = len(blocks)
+    if count != 4:
+        return exchange(blocks, axis)[::-1]
+    far = swap(blocks[3], axis, count, 1)
+    near = swap(blocks[1], axis, count, 1)
+    across = swap(add(blocks[2], far), axis, count, 2)
+    return [across, near, blocks[0]]
+
+
+def collect(block, axis, count):
+    if count != 4:
+        return exchange([block] * count, axis)
+    across = swap(block, axis, count, 2)
+    near = swap(block, axis, count, 1)
+    return [block, near, across, swap(across, axis, count, 1)]
+
+
 def spectrum_kernel(model_hbm, table_out_ref, *refs):
     out_refs = refs[:-3]
     model_ref, rows_ref, model_sems = refs[-3:]
@@ -76,20 +114,15 @@
     for at in range(chunks):
         rows = pl.ds(at * part, part)
         copies.append(
-            [
-                pltpu.make_async_copy(
-                    model_hbm.at[h, rows], model_ref.at[h, rows], model_sems.at[at, h]
-                )
-                for h in range(high)
-            ]
+            pltpu.make_async_copy(
+                model_hbm.at[:, rows], model_ref.at[:, rows], model_sems.at[at]
+            )
         )
-        for copy in copies[-1]:
-            copy.start()
+        copies[-1].start()
     table = tables(bins, length)
     table_out_ref[...] = table
     for at in range(chunks):
-        for copy in copies[at]:
-            copy.wait()
+        copies[at].wait()
         for start in range(at * part, (at + 1) * part, 2):
             width = min(2, (at + 1) * part - start)
             block = jnp.concatenate(
@@ -123,7 +156,7 @@
         scratch_shapes=[
             pltpu.VMEM((high, low, rhs, length), model.dtype),
             pltpu.VMEM((low * bins, LANES), jnp.float32),
-            pltpu.SemaphoreType.DMA((chunks, high)),
+            pltpu.SemaphoreType.DMA((chunks,)),
         ],
         compiler_params=pltpu.CompilerParams(vmem_limit_bytes=VMEM_LIMIT),
         name="spectrum",
@@ -171,8 +204,8 @@
     rhs = parts * pairs // freqs
     high = lanes // rhs
     per_tile = groups // col_tiles
-    for f in range(freqs):
-        projected = []
+    products = {}
+    for f in range(freqs):
         for j in range(col_tiles):
             halves = []
             for c in range(2):
@@ -183,17 +216,23 @@
                         got = got.astype(jnp.float32)
                     blocks += [got[:, h * rhs : (h + 1) * rhs] for h in range(high)]
                 halves.append(jnp.concatenate(blocks))
-            straight = jnp.concatenate(halves, axis=1).astype(jnp.bfloat16)
-            crossed = jnp.concatenate([halves[1], -halves[0]], axis=1).astype(jnp.bfloat16)
+            first = jnp.concatenate(halves, axis=1).astype(jnp.bfloat16)
+            second = jnp.concatenate([halves[1], -halves[0]], axis=1).astype(jnp.bfloat16)
             right = [right_ref[c, f, :, j].reshape(row_tiles * size, tile) for c in range(2)]
-            product = dot(right[0], straight, 1, 0) + dot(right[1], crossed, 1, 0)
-            places = [(f, i, j) for i in range(row_tiles)]
-            projected.append(masked(product, limits_ref, places, size))
+            products[f, j] = dot(right[0], first, 1, 0) + dot(right[1], second, 1, 0)
+    factors = {}
+    for f in range(freqs):
+        projected = [
+            masked(products[f, j], limits_ref, [(f, i, j) for i in range(row_tiles)], size)
+            for j in range(col_tiles)
+        ]
         for i in range(row_tiles):
             straight = [projected[j][i] for j in range(col_tiles)]
-            factors = jnp.concatenate(straight + [turned(part) for part in straight])
+            factors[f, i] = jnp.concatenate(straight + [turned(part) for part in straight])
+    for f in range(freqs):
+        for i in range(row_tiles):
             left = left_ref[:, f, i].reshape(2 * col_tiles * size, tile)
-            predicted = dot(factors, left, 0, 0)
+            predicted = dot(factors[f, i], left, 0, 0)
             for c in range(2):
                 row = c * rhs
                 for part, start, length in spans(f * rhs, rhs, pairs):
@@ -264,8 +303,8 @@
     me = lax.axis_index("rtile")
     for at, misfit_ref in enumerate(misfit_refs):
         misfit_all_ref[origin(me, at, parts)] = misfit_ref[...].astype(jnp.float32)
-    for f in range(freqs):
-        back = []
+    products = {}
+    for f in range(freqs):
         for i in range(row_tiles):
             rows = [
                 jnp.concatenate(
@@ -276,19 +315,25 @@
                 )
                 for c in range(2)
             ]
-            straight = jnp.concatenate(rows).astype(jnp.bfloat16)
-            crossed = jnp.concatenate([rows[1], -rows[0]]).astype(jnp.bfloat16)
+            first = jnp.concatenate(rows).astype(jnp.bfloat16)
+            second = jnp.concatenate([rows[1], -rows[0]]).astype(jnp.bfloat16)
             left = [left_ref[c, f, i].reshape(col_tiles * size, tile) for c in range(2)]
-            product = dot(left[0], straight, 1, 1) + dot(left[1], crossed, 1, 1)
-            places = [(f, i, j) for j in range(col_tiles)]
-            back.append(masked(product, limits_ref, places, size))
+            products[f, i] = dot(left[0], first, 1, 1) + dot(left[1], second, 1, 1)
+    factors = {}
+    for f in range(freqs):
+        back = [
+            masked(products[f, i], limits_ref, [(f, i, j) for j in range(col_tiles)], size)
+            for i in range(row_tiles)
+        ]
         for j in range(col_tiles):
             straight = [part[j] for part in back]
-            factors = jnp.concatenate(straight + [turned(part) for part in straight])
+            factors[f, j] = jnp.concatenate(straight + [turned(part) for part in straight])
+    for f in range(freqs):
+        for j in range(col_tiles):
             right = jnp.concatenate(
                 [right_ref[c, f, :, j].reshape(row_tiles * size, tile) for c in range(2)]
             )
-            grad = dot(factors, right, 0, 0)
+            grad = dot(factors[f, j], right, 0, 0)
             grad = (grad if low % 16 else grad.astype(out_refs[0].dtype)).T
             for at in range(per_tile):
                 rows = at * high * low
@@ -376,13 +421,10 @@
                 high, rhs, length
             )
         rows = pl.ds(at * part, part)
-        for h in range(high):
-            copies.append(
-                pltpu.make_async_copy(
-                    out_ref.at[h, rows], out_hbm.at[h, rows], out_sems.at[at, h]
-                )
-            )
-            copies[-1].start()
+        copies.append(
+            pltpu.make_async_copy(out_ref.at[:, rows], out_hbm.at[:, rows], out_sems.at[at])
+        )
+        copies[-1].start()
     for copy in copies:
         copy.wait()
 
@@ -401,7 +443,7 @@
         scratch_shapes=[
             pltpu.VMEM(shape, jnp.bfloat16),
             pltpu.VMEM((low * bins, lanes), jnp.float32),
-            pltpu.SemaphoreType.DMA((chunks, high)),
+            pltpu.SemaphoreType.DMA((chunks,)),
         ],
         compiler_params=pltpu.CompilerParams(vmem_limit_bytes=VMEM_LIMIT),
         name="gradient",
@@ -419,8 +461,8 @@
     spectrum = exchange(spectrum, "freq")
     limits = jnp.broadcast_to(ranks[..., None, None], ranks.shape + (1, LANES))
     predicted = predict(limits, spectrum, green_right, green_left, tile_count)
-    misfit, *residual = residual_of(exchange(predicted, "rtile")[::-1], data)
-    misfit = exchange([misfit] * tile_count, "rtile")
+    misfit, *residual = residual_of(scatter_sums(predicted, "rtile"), data)
+    misfit = collect(misfit, "rtile", tile_count)
     partial = back_project(limits, misfit, green_right, green_left, freq_count, rep_count)
     arrived = exchange(gather(exchange(partial, "rep")), "freq")
     return (jnp.stack(residual), gradient_of(arrived, table, rhs_count))

time: 48 us -> 50.2 us (1.046)
  starting transfers between devices: 17.1 us -> 22.1 us
  waiting for transfers between devices: 18.3 us -> 16.4 us
  Pallas kernels: 10.8 us -> 9.9 us
    ppermute x0 -> x6, starting transfers between devices: none -> 13.9 us  [swap(): return lax.ppermute(block, axis, [(me, me ^ step) for me in range(count)])]
    ppermute x13 -> x7, waiting for transfers between devices: 18.3 us -> 7.31 us  [exchange(): arrived.append(lax.ppermute(blocks[step], axis, pairs))]
    ppermute x0 -> x6, waiting for transfers between devices: none -> 9.08 us  [swap(): return lax.ppermute(block, axis, [(me, me ^ step) for me in range(count)])]
    ppermute x13 -> x7, starting transfers between devices: 17.1 us -> 8.23 us  [exchange(): arrived.append(lax.ppermute(blocks[step], axis, pairs))]
  transfers between devices with their start and end apart: 13 -> 13, of which waited for: 11 -> 10; matrix products, arithmetic and copies ran while one was open for 2% -> 2% of each run, Pallas kernels for 0% -> 0%
where the time goes in v10:
time: 50.2 us; the launch traced here: 50 us
  starting transfers between devices  22.1 us (44%)
  waiting for transfers between devices  16.4 us (33%)
  Pallas kernels  9.9 us (20%)
  between operations  0.74 us (1%)
  other arithmetic  0.69 us (1%)
    ppermute x6, starting transfers between devices, swap(): return lax.ppermute(block, axis, [(me, me ^ step) for me in range(count)])  13.9 us
    ppermute x6, waiting for transfers between devices, swap(): return lax.ppermute(block, axis, [(me, me ^ step) for me in range(count)])  9.08 us
    ppermute x7, starting transfers between devices, exchange(): arrived.append(lax.ppermute(blocks[step], axis, pairs))  8.23 us
    ppermute x7, waiting for transfers between devices, exchange(): arrived.append(lax.ppermute(blocks[step], axis, pairs))  7.31 us
    pallas_call x1, Pallas kernels, spectrum_of(): pl.pallas_call(spectrum_kernel, in_specs=[pl.BlockSpec(memory_space=pltpu...  4.73 us
    pallas_call x1, Pallas kernels, gradient_of(): pl.pallas_call(gradient_kernel, in_specs=[pl.BlockSpec(memory_space=pltpu...  2.54 us
    pallas_call x1, Pallas kernels, predict(): pl.pallas_call(functools.partial(predict_kernel, groups, parts), in_specs...  1.34 us
    pallas_call x1, Pallas kernels, back_project(): pl.pallas_call(functools.partial(back_kernel, parts, groups, reps), in_sp...  1.2 us
  transfers between devices with their start and end apart: 13, of which 10 were waited for; matrix products, arithmetic and copies ran while one was open for 2% of the time, Pallas kernels for 0%

profile of v10, /device:TPU:0, one launch (start us, length us, event | category | flops | bytes accessed | tf_op | source)
XLA Modules:
  0.0 50.0 jit_solution(12536167663264535794)
XLA Ops:
  0.6 0.0 copy-start.3
  0.6 0.0 copy-start
  0.7 0.0 copy-start.1
  0.7 0.0 copy-start.2
  0.7 4.7 %spectrum.1 = (bf16[24,1024]{1,0:T(8,128)(2,1)S(1)}, bf16[3,2,32,128]{3,2,1,0:T(8,128)(2,1)S(1)}, bf16[3,2,32,128]{3,2,1,0:T(8,128)(2,1)S(1)}, bf16[3,2,32,128]{...) custom-call(bf16[4,32,32,1024]{3,2,1,0:T(8,128)(2,1)} %bitcast.6), custom_call_target="tpu_custom_call" | custom-call | tf_op jit(solution)/shard_map/spectrum/pallas_call | solution.py:150
  5.4 4.0 %collective-permute-start = (bf16[3,2,32,128]{3,2,1,0:T(8,128)(2,1)S(1)}, bf16[3,2,32,128]{3,2,1,0:T(8,128)(2,1)S(1)}, u32[]{:S(2)}, u32[]{:S(2)}) collective-permute-start(bf16[3,2,32,128]{3,2,1,0:T(8,128)(2,1)S(1)} %get-tuple-element.20), channel_id=1, source_target_pairs={{0,24},{8,16},{16,8},{24,0},{1,25},{9,17},{17,9},{25,1},{2,26},{10... | collective-permute-start | bytes 147464 | tf_op jit(solution)/shard_map/ppermute | solution.py:62
  9.4 0.5 %collective-permute-start.1 = (bf16[3,2,32,128]{3,2,1,0:T(8,128)(2,1)S(1)}, bf16[3,2,32,128]{3,2,1,0:T(8,128)(2,1)S(1)}, u32[]{:S(2)}, u32[]{:S(2)}) collective-permute-start(bf16[3,2,32,128]{3,2,1,0:T(8,128)(2,1)S(1)} %get-tuple-element.21), channel_id=1, source_target_pairs={{0,16},{8,24},{16,0},{24,8},{1,17},{9,25},{17,1},{25,9},{2,18},{10... | collective-permute-start | bytes 147464 | tf_op jit(solution)/shard_map/ppermute | solution.py:62
  9.9 0.1 collective-permute-start.2
  10.0 0.0 copy-done.3
  10.0 0.1 copy.7
  10.1 1.3 %collective-permute-done.refs_0_ = bf16[3,2,32,128]{3,2,1,0:T(8,128)(2,1)S(1)} collective-permute-done((bf16[3,2,32,128]{3,2,1,0:T(8,128)(2,1)S(1)}, bf16[3,2,32,128]{3,2,1,0:T(8,128)(2,1)S(1)}, u32[]{:S(2)}, u32[]{:S(2)}) %collective-permute-start) | collective-permute-done | bytes 49184 | tf_op jit(solution)/shard_map/ppermute | solution.py:62
  11.4 2.0 %collective-permute-done.1.refs_1_ = bf16[3,2,32,128]{3,2,1,0:T(8,128)(2,1)S(1)} collective-permute-done((bf16[3,2,32,128]{3,2,1,0:T(8,128)(2,1)S(1)}, bf16[3,2,32,128]{3,2,1,0:T(8,128)(2,1)S(1)}, u32[]{:S(2)}, u32[]{:S(2)}) %collective-permute-start.1) | collective-permute-done | bytes 49184 | tf_op jit(solution)/shard_map/ppermute | solution.py:62
  13.5 0.5 %collective-permute-done.2.refs_2_ = bf16[3,2,32,128]{3,2,1,0:T(8,128)(2,1)S(1)} collective-permute-done((bf16[3,2,32,128]{3,2,1,0:T(8,128)(2,1)S(1)}, bf16[3,2,32,128]{3,2,1,0:T(8,128)(2,1)S(1)}, u32[]{:S(2)}, u32[]{:S(2)}) %collective-permute-start.2) | collective-permute-done | bytes 49184 | tf_op jit(solution)/shard_map/ppermute | solution.py:62
  14.0 0.1 broadcast_in_dim.2.limits_ref
  14.0 0.0 copy-done
  14.1 0.0 copy-done.1
  14.1 1.3 %predict.1 = (bf16[2,24,1024]{2,1,0:T(8,128)(2,1)S(1)}, bf16[2,24,1024]{2,1,0:T(8,128)(2,1)S(1)}, bf16[2,24,1024]{2,1,0:T(8,128)(2,1)S(1)}, bf16[2,24,1024]{2,1,0:T(8,128)(2,1)S(1)}) custom-call(s32[3,4,2,1,128]{4,3,2,1,0:T(1,128)S(1)} %broadcast_in_dim.2.limits_ref, bf16[2,3,4,2,48,256]{5,4,3,2,1,0:T(8,128)(2,1)S(1)} %copy-done, ...), custom_call_target="tpu_custom_call" | custom-call | flops 150994944 | bytes 2359296 | tf_op jit(solution)/shard_map/predict/pallas_call | solution.py:255
  15.4 1.6 %collective-permute-start.3 = (bf16[2,24,1024]{2,1,0:T(8,128)(2,1)S(1)}, bf16[2,24,1024]{2,1,0:T(8,128)(2,1)S(1)}, u32[]{:S(2)}, u32[]{:S(2)}) collective-permute-start(bf16[2,24,1024]{2,1,0:T(8,128)(2,1)S(1)} %get-tuple-element.25), channel_id=1, source_target_pairs={{0,2},{2,0},{4,6},{6,4},{1,3},{3,1},{5,7},{7,5},{8,10},{10,8},{12,... | collective-permute-start | bytes 294920 | tf_op jit(solution)/shard_map/ppermute | solution.py:67
  17.1 0.5 collective-permute-start.5
  17.5 2.6 %collective-permute-done.3.second_ref = bf16[2,24,1024]{2,1,0:T(8,128)(2,1)S(1)} collective-permute-done((bf16[2,24,1024]{2,1,0:T(8,128)(2,1)S(1)}, bf16[2,24,1024]{2,1,0:T(8,128)(2,1)S(1)}, u32[]{:S(2)}, u32[]{:S(2)}) %collective-permute-start.3) | collective-permute-done | bytes 98336 | tf_op jit(solution)/shard_map/ppermute | solution.py:67
  20.1 2.9 %collective-permute-start.4 = (bf16[2,24,1024]{2,1,0:T(8,128)(2,1)S(1)}, bf16[2,24,1024]{2,1,0:T(8,128)(2,1)S(1)}, u32[]{:S(2)}, u32[]{:S(2)}) collective-permute-start(bf16[2,24,1024]{2,1,0:T(8,128)(2,1)S(1)} %add.1), channel_id=1, source_target_pairs={{0,4},{2,6},{4,0},{6,2},{1,5},{3,7},{5,1},{7,3},{8,12},{10,14},{12... | collective-permute-start | bytes 294920 | tf_op jit(solution)/shard_map/ppermute | solution.py:67
  23.0 0.0 collective-permute-done.5.refs_1_
  23.0 3.9 %collective-permute-done.4.refs_0_ = bf16[2,24,1024]{2,1,0:T(8,128)(2,1)S(1)} collective-permute-done((bf16[2,24,1024]{2,1,0:T(8,128)(2,1)S(1)}, bf16[2,24,1024]{2,1,0:T(8,128)(2,1)S(1)}, u32[]{:S(2)}, u32[]{:S(2)}) %collective-permute-start.4) | collective-permute-done | bytes 98336 | tf_op jit(solution)/shard_map/ppermute | solution.py:67
  26.9 0.0 copy-done.2
  27.0 2.1 %collective-permute-start.7 = (bf16[2,24,1024]{2,1,0:T(8,128)(2,1)S(1)}, bf16[2,24,1024]{2,1,0:T(8,128)(2,1)S(1)}, u32[]{:S(2)}, u32[]{:S(2)}) collective-permute-start(bf16[2,24,1024]{2,1,0:T(8,128)(2,1)S(1)} %get-tuple-element.31.refs_0_), channel_id=1, source_target_pairs={{0,4},{2,6},{4,0},{6,2},{1,5},{3,7},{5,1},{7,3},{8,12},{10,14},{12... | collective-permute-start | bytes 294920 | tf_op jit(solution)/shard_map/ppermute | solution.py:67
  29.1 3.8 %collective-permute-start.6 = (bf16[2,24,1024]{2,1,0:T(8,128)(2,1)S(1)}, bf16[2,24,1024]{2,1,0:T(8,128)(2,1)S(1)}, u32[]{:S(2)}, u32[]{:S(2)}) collective-permute-start(bf16[2,24,1024]{2,1,0:T(8,128)(2,1)S(1)} %get-tuple-element.31.refs_0_), channel_id=1, source_target_pairs={{0,2},{2,0},{4,6},{6,4},{1,3},{3,1},{5,7},{7,5},{8,10},{10,8},{12,... | collective-permute-start | bytes 294920 | tf_op jit(solution)/shard_map/ppermute | solution.py:67
  32.9 0.0 collective-permute-done.7.refs_2_
  32.9 3.0 %collective-permute-start.8 = (bf16[2,24,1024]{2,1,0:T(8,128)(2,1)S(1)}, bf16[2,24,1024]{2,1,0:T(8,128)(2,1)S(1)}, u32[]{:S(2)}, u32[]{:S(2)}) collective-permute-start(bf16[2,24,1024]{2,1,0:T(8,128)(2,1)S(1)} %collective-permute-done.7.refs_2_), channel_id=1, source_target_pairs={{0,2},{2,0},{4,6},{6,4},{1,3},{3,1},{5,7},{7,5},{8,10},{10,8},{12,... | collective-permute-start | bytes 294920 | tf_op jit(solution)/shard_map/ppermute | solution.py:67
  35.9 0.0 collective-permute-done.6.refs_1_
  35.9 2.6 %collective-permute-done.8.refs_3_ = bf16[2,24,1024]{2,1,0:T(8,128)(2,1)S(1)} collective-permute-done((bf16[2,24,1024]{2,1,0:T(8,128)(2,1)S(1)}, bf16[2,24,1024]{2,1,0:T(8,128)(2,1)S(1)}, u32[]{:S(2)}, u32[]{:S(2)}) %collective-permute-start.8) | collective-permute-done | bytes 98336 | tf_op jit(solution)/shard_map/ppermute | solution.py:67
  38.5 1.2 %back_project.1 = (bf16[4,3,2,16,128]{4,3,2,1,0:T(8,128)(2,1)S(1)}, bf16[4,3,2,16,128]{4,3,2,1,0:T(8,128)(2,1)S(1)}) custom-call(s32[3,4,2,1,128]{4,3,2,1,0:T(1,128)S(1)} %broadcast_in_dim.2.limits_ref, bf16[2,3,4,2,48,256]{5,4,3,2,1,0:T(8,128)(2,1)S(1)} %copy-done, bf16[2,3,4,2,48,256]{5,4,3,2,1,0:T(8,128)(2,1)S(1)} %copy-done.1, ...), custom_call_target="tpu_custom_call" | custom-call | flops 150994944 | bytes 2359296 | tf_op jit(solution)/shard_map/back_project/pallas_call | solution.py:362
  39.7 0.1 collective-permute-start.9
  39.8 1.3 %collective-permute-done.9.refs_1_ = bf16[4,3,2,16,128]{4,3,2,1,0:T(8,128)(2,1)S(1)} collective-permute-done((bf16[4,3,2,16,128]{4,3,2,1,0:T(8,128)(2,1)S(1)}, bf16[4,3,2,16,128]{4,3,2,1,0:T(8,128)(2,1)S(1)}, u32[]{:S(2)}, u32[]{:S(2)}) %collective-permute-start.9) | collective-permute-done | bytes 98336 | tf_op jit(solution)/shard_map/ppermute | solution.py:62
  41.1 1.6 %collective-permute-start.10 = (bf16[3,2,16,128]{3,2,1,0:T(8,128)(2,1)S(1)}, bf16[3,2,16,128]{3,2,1,0:T(8,128)(2,1)S(1)}, u32[]{:S(2)}, u32[]{:S(2)}) collective-permute-start(bf16[3,2,16,128]{3,2,1,0:T(8,128)(2,1)S(1)} %get-tuple-element.34), channel_id=1, source_target_pairs={{0,24},{8,16},{16,8},{24,0},{1,25},{9,17},{17,9},{25,1},{2,26},{10... | collective-permute-start | bytes 73736 | tf_op jit(solution)/shard_map/ppermute | solution.py:62
  42.7 1.0 %collective-permute-start.11 = (bf16[3,2,16,128]{3,2,1,0:T(8,128)(2,1)S(1)}, bf16[3,2,16,128]{3,2,1,0:T(8,128)(2,1)S(1)}, u32[]{:S(2)}, u32[]{:S(2)}) collective-permute-start(bf16[3,2,16,128]{3,2,1,0:T(8,128)(2,1)S(1)} %get-tuple-element.35), channel_id=1, source_target_pairs={{0,16},{8,24},{16,0},{24,8},{1,17},{9,25},{17,1},{25,9},{2,18},{10... | collective-permute-start | bytes 73736 | tf_op jit(solution)/shard_map/ppermute | solution.py:62
  43.7 1.0 %collective-permute-start.12 = (bf16[3,2,16,128]{3,2,1,0:T(8,128)(2,1)S(1)}, bf16[3,2,16,128]{3,2,1,0:T(8,128)(2,1)S(1)}, u32[]{:S(2)}, u32[]{:S(2)}) collective-permute-start(bf16[3,2,16,128]{3,2,1,0:T(8,128)(2,1)S(1)} %get-tuple-element.36), channel_id=1, source_target_pairs={{0,8},{8,0},{16,24},{24,16},{1,9},{9,1},{17,25},{25,17},{2,10},{10... | collective-permute-start | bytes 73736 | tf_op jit(solution)/shard_map/ppermute | solution.py:62
  44.6 0.7 %pad_maximum_fusion = f32[2,24,1024]{2,1,0:T(8,128)} fusion(f32[1,24,1024]{2,1,0:T(8,128)S(1)} %bitcast.5, f32[1,24,1024]{2,1,0:T(8,128)S(1)} %bitcast.4), kind=kLoop, calls=%fused_computation | loop fusion | flops 49152 | bytes 393216 | tf_op jit(solution)/shard_map/stack | solution.py:468
  45.3 0.5 %collective-permute-done.10.refs_0_ = bf16[3,2,16,128]{3,2,1,0:T(8,128)(2,1)S(1)} collective-permute-done((bf16[3,2,16,128]{3,2,1,0:T(8,128)(2,1)S(1)}, bf16[3,2,16,128]{3,2,1,0:T(8,128)(2,1)S(1)}, u32[]{:S(2)}, u32[]{:S(2)}) %collective-permute-start.10) | collective-permute-done | bytes 24608 | tf_op jit(solution)/shard_map/ppermute | solution.py:62
  45.9 0.6 %collective-permute-done.11.refs_1_ = bf16[3,2,16,128]{3,2,1,0:T(8,128)(2,1)S(1)} collective-permute-done((bf16[3,2,16,128]{3,2,1,0:T(8,128)(2,1)S(1)}, bf16[3,2,16,128]{3,2,1,0:T(8,128)(2,1)S(1)}, u32[]{:S(2)}, u32[]{:S(2)}) %collective-permute-start.11) | collective-permute-done | bytes 24608 | tf_op jit(solution)/shard_map/ppermute | solution.py:62
  46.5 1.0 %collective-permute-done.12.refs_2_ = bf16[3,2,16,128]{3,2,1,0:T(8,128)(2,1)S(1)} collective-permute-done((bf16[3,2,16,128]{3,2,1,0:T(8,128)(2,1)S(1)}, bf16[3,2,16,128]{3,2,1,0:T(8,128)(2,1)S(1)}, u32[]{:S(2)}, u32[]{:S(2)}) %collective-permute-start.12) | collective-permute-done | bytes 24608 | tf_op jit(solution)/shard_map/ppermute | solution.py:62
  47.5 2.5 %gradient.1 = bf16[4,16,32,1024]{3,2,1,0:T(8,128)(2,1)} custom-call(bf16[24,1024]{1,0:T(8,128)(2,1)S(1)} %get-tuple-element.30.table_ref, bf16[3,2,16,128]{3,2,1,0:T(8,128)(2,1)S(1)} %collective-permute-done.10.refs_0_, bf16[3,2,16,128]{3,2,1,0:T(8,128)(2,1)S(1)} %collective-permute-done.11.refs_1_, ...), custom_call_target="tpu_custom_call" | custom-call | tf_op jit(solution)/shard_map/gradient/pallas_call | solution.py:438
  (3 shorter events, 0.1 us)
Async XLA Ops:
  0.6 9.4 %copy-start.3 = (s32[3,4,2]{1,2,0:T(2,128)S(1)}, s32[3,4,2]{1,2,0:T(2,128)}, u32[]{:S(2)}) copy-start(s32[3,4,2]{1,2,0:T(2,128)} %param.8) | copy-start | bytes 292
  0.6 13.4 %copy-start = (bf16[2,3,4,2,48,256]{5,4,3,2,1,0:T(8,128)(2,1)S(1)}, bf16[2,3,4,2,48,256]{5,4,3,2,1,0:T(8,128)(2,1)}, u32[]{:S(2)}) copy-start(bf16[2,3,4,2,48,256]{5,4,3,2,1,0:T(8,128)(2,1)} %right_ref.3) | copy-start | bytes 3538948
  0.7 13.4 %copy-start.1 = (bf16[2,3,4,2,48,256]{5,4,3,2,1,0:T(8,128)(2,1)S(1)}, bf16[2,3,4,2,48,256]{5,4,3,2,1,0:T(8,128)(2,1)}, u32[]{:S(2)}) copy-start(bf16[2,3,4,2,48,256]{5,4,3,2,1,0:T(8,128)(2,1)} %left_ref.3) | copy-start | bytes 3538948
  0.7 26.3 %copy-start.2 = (f32[2,24,1024]{2,1,0:T(8,128)S(1)}, f32[2,24,1024]{2,1,0:T(8,128)}, u32[]{:S(2)}) copy-start(f32[2,24,1024]{2,1,0:T(8,128)} %data_ref.1) | copy-start | bytes 589828
  5.4 6.0 %collective-permute-start = (bf16[3,2,32,128]{3,2,1,0:T(8,128)(2,1)S(1)}, bf16[3,2,32,128]{3,2,1,0:T(8,128)(2,1)S(1)}, u32[]{:S(2)}, u32[]{:S(2)}) collective-permute-start(bf16[3,2,32,128]{3,2,1,0:T(8,128)(2,1)S(1)} %get-tuple-element.20), channel_id=1, source_target_pairs={{0,24},{8,16},{16,8},{24,0},{1,25},{9,17},{17,9},{25,1},{2,26},{10... | collective-permute-start | bytes 147464 | tf_op jit(solution)/shard_map/ppermute | solution.py:62
  9.4 4.1 %collective-permute-start.1 = (bf16[3,2,32,128]{3,2,1,0:T(8,128)(2,1)S(1)}, bf16[3,2,32,128]{3,2,1,0:T(8,128)(2,1)S(1)}, u32[]{:S(2)}, u32[]{:S(2)}) collective-permute-start(bf16[3,2,32,128]{3,2,1,0:T(8,128)(2,1)S(1)} %get-tuple-element.21), channel_id=1, source_target_pairs={{0,16},{8,24},{16,0},{24,8},{1,17},{9,25},{17,1},{25,9},{2,18},{10... | collective-permute-start | bytes 147464 | tf_op jit(solution)/shard_map/ppermute | solution.py:62
  9.9 4.1 %collective-permute-start.2 = (bf16[3,2,32,128]{3,2,1,0:T(8,128)(2,1)S(1)}, bf16[3,2,32,128]{3,2,1,0:T(8,128)(2,1)S(1)}, u32[]{:S(2)}, u32[]{:S(2)}) collective-permute-start(bf16[3,2,32,128]{3,2,1,0:T(8,128)(2,1)S(1)} %get-tuple-element.22), channel_id=1, source_target_pairs={{0,8},{8,0},{16,24},{24,16},{1,9},{9,1},{17,25},{25,17},{2,10},{10... | collective-permute-start | bytes 147464 | tf_op jit(solution)/shard_map/ppermute | solution.py:62
  15.4 4.7 %collective-permute-start.3 = (bf16[2,24,1024]{2,1,0:T(8,128)(2,1)S(1)}, bf16[2,24,1024]{2,1,0:T(8,128)(2,1)S(1)}, u32[]{:S(2)}, u32[]{:S(2)}) collective-permute-start(bf16[2,24,1024]{2,1,0:T(8,128)(2,1)S(1)} %get-tuple-element.25), channel_id=1, source_target_pairs={{0,2},{2,0},{4,6},{6,4},{1,3},{3,1},{5,7},{7,5},{8,10},{10,8},{12,... | collective-permute-start | bytes 294920 | tf_op jit(solution)/shard_map/ppermute | solution.py:67
  17.1 6.0 %collective-permute-start.5 = (bf16[2,24,1024]{2,1,0:T(8,128)(2,1)S(1)}, bf16[2,24,1024]{2,1,0:T(8,128)(2,1)S(1)}, u32[]{:S(2)}, u32[]{:S(2)}) collective-permute-start(bf16[2,24,1024]{2,1,0:T(8,128)(2,1)S(1)} %get-tuple-element.26), channel_id=1, source_target_pairs={{0,2},{2,0},{4,6},{6,4},{1,3},{3,1},{5,7},{7,5},{8,10},{10,8},{12,... | collective-permute-start | bytes 294920 | tf_op jit(solution)/shard_map/ppermute | solution.py:67
  20.1 6.8 %collective-permute-start.4 = (bf16[2,24,1024]{2,1,0:T(8,128)(2,1)S(1)}, bf16[2,24,1024]{2,1,0:T(8,128)(2,1)S(1)}, u32[]{:S(2)}, u32[]{:S(2)}) collective-permute-start(bf16[2,24,1024]{2,1,0:T(8,128)(2,1)S(1)} %add.1), channel_id=1, source_target_pairs={{0,4},{2,6},{4,0},{6,2},{1,5},{3,7},{5,1},{7,3},{8,12},{10,14},{12... | collective-permute-start | bytes 294920 | tf_op jit(solution)/shard_map/ppermute | solution.py:67
  27.0 6.0 %collective-permute-start.7 = (bf16[2,24,1024]{2,1,0:T(8,128)(2,1)S(1)}, bf16[2,24,1024]{2,1,0:T(8,128)(2,1)S(1)}, u32[]{:S(2)}, u32[]{:S(2)}) collective-permute-start(bf16[2,24,1024]{2,1,0:T(8,128)(2,1)S(1)} %get-tuple-element.31.refs_0_), channel_id=1, source_target_pairs={{0,4},{2,6},{4,0},{6,2},{1,5},{3,7},{5,1},{7,3},{8,12},{10,14},{12... | collective-permute-start | bytes 294920 | tf_op jit(solution)/shard_map/ppermute | solution.py:67
  29.1 6.8 %collective-permute-start.6 = (bf16[2,24,1024]{2,1,0:T(8,128)(2,1)S(1)}, bf16[2,24,1024]{2,1,0:T(8,128)(2,1)S(1)}, u32[]{:S(2)}, u32[]{:S(2)}) collective-permute-start(bf16[2,24,1024]{2,1,0:T(8,128)(2,1)S(1)} %get-tuple-element.31.refs_0_), channel_id=1, source_target_pairs={{0,2},{2,0},{4,6},{6,4},{1,3},{3,1},{5,7},{7,5},{8,10},{10,8},{12,... | collective-permute-start | bytes 294920 | tf_op jit(solution)/shard_map/ppermute | solution.py:67
  32.9 5.5 %collective-permute-start.8 = (bf16[2,24,1024]{2,1,0:T(8,128)(2,1)S(1)}, bf16[2,24,1024]{2,1,0:T(8,128)(2,1)S(1)}, u32[]{:S(2)}, u32[]{:S(2)}) collective-permute-start(bf16[2,24,1024]{2,1,0:T(8,128)(2,1)S(1)} %collective-permute-done.7.refs_2_), channel_id=1, source_target_pairs={{0,2},{2,0},{4,6},{6,4},{1,3},{3,1},{5,7},{7,5},{8,10},{10,8},{12,... | collective-permute-start | bytes 294920 | tf_op jit(solution)/shard_map/ppermute | solution.py:67
  39.7 1.4 %collective-permute-start.9 = (bf16[4,3,2,16,128]{4,3,2,1,0:T(8,128)(2,1)S(1)}, bf16[4,3,2,16,128]{4,3,2,1,0:T(8,128)(2,1)S(1)}, u32[]{:S(2)}, u32[]{:S(2)}) collective-permute-start(bf16[4,3,2,16,128]{4,3,2,1,0:T(8,128)(2,1)S(1)} %get-tuple-element.33), channel_id=1, source_target_pairs={{0,1},{1,0},{2,3},{3,2},{4,5},{5,4},{6,7},{7,6},{8,9},{9,8},{10,11... | collective-permute-start | bytes 294920 | tf_op jit(solution)/shard_map/ppermute | solution.py:62
  41.1 4.8 %collective-permute-start.10 = (bf16[3,2,16,128]{3,2,1,0:T(8,128)(2,1)S(1)}, bf16[3,2,16,128]{3,2,1,0:T(8,128)(2,1)S(1)}, u32[]{:S(2)}, u32[]{:S(2)}) collective-permute-start(bf16[3,2,16,128]{3,2,1,0:T(8,128)(2,1)S(1)} %get-tuple-element.34), channel_id=1, source_target_pairs={{0,24},{8,16},{16,8},{24,0},{1,25},{9,17},{17,9},{25,1},{2,26},{10... | collective-permute-start | bytes 73736 | tf_op jit(solution)/shard_map/ppermute | solution.py:62
  42.7 3.8 %collective-permute-start.11 = (bf16[3,2,16,128]{3,2,1,0:T(8,128)(2,1)S(1)}, bf16[3,2,16,128]{3,2,1,0:T(8,128)(2,1)S(1)}, u32[]{:S(2)}, u32[]{:S(2)}) collective-permute-start(bf16[3,2,16,128]{3,2,1,0:T(8,128)(2,1)S(1)} %get-tuple-element.35), channel_id=1, source_target_pairs={{0,16},{8,24},{16,0},{24,8},{1,17},{9,25},{17,1},{25,9},{2,18},{10... | collective-permute-start | bytes 73736 | tf_op jit(solution)/shard_map/ppermute | solution.py:62
  43.7 3.8 %collective-permute-start.12 = (bf16[3,2,16,128]{3,2,1,0:T(8,128)(2,1)S(1)}, bf16[3,2,16,128]{3,2,1,0:T(8,128)(2,1)S(1)}, u32[]{:S(2)}, u32[]{:S(2)}) collective-permute-start(bf16[3,2,16,128]{3,2,1,0:T(8,128)(2,1)S(1)} %get-tuple-element.36), channel_id=1, source_target_pairs={{0,8},{8,0},{16,24},{24,16},{1,9},{9,1},{17,25},{25,17},{2,10},{10... | collective-permute-start | bytes 73736 | tf_op jit(solution)/shard_map/ppermute | solution.py:62

commit v11 on v10

--- a/solution.py
+++ b/solution.py
@@ -61,44 +61,6 @@
         pairs = [(me, me ^ step if count & (count - 1) == 0 else (me + step) % count) for me in range(count)]
         arrived.append(lax.ppermute(blocks[step], axis, pairs))
     return [blocks[0]] + arrived[::-1]
-
-
-def swap(block, axis, count, step):
-    return lax.ppermute(block, axis, [(me, me ^ step) for me in range(count)])
-
-
-def add_kernel(first_ref, second_ref, out_ref):
-    total = first_ref[...].astype(jnp.float32) + second_ref[...].astype(jnp.float32)
-    out_ref[...] = total.astype(out_ref.dtype)
-
-
-def add(first, second):
-    return pl.pallas_call(
-        add_kernel,
-        in_specs=[pl.BlockSpec(memory_space=pltpu.VMEM)] * 2,
-        out_specs=pl.BlockSpec(memory_space=pltpu.VMEM),
-        out_shape=jax.ShapeDtypeStruct(first.shape, first.dtype),
-        compiler_params=pltpu.CompilerParams(vmem_limit_bytes=VMEM_LIMIT),
-        name="add",
-    )(first, second)
-
-
-def scatter_sums(blocks, axis):
-    count = len(blocks)
-    if count != 4:
-        return exchange(blocks, axis)[::-1]
-    far = swap(blocks[3], axis, count, 1)
-    near = swap(blocks[1], axis, count, 1)
-    across = swap(add(blocks[2], far), axis, count, 2)
-    return [across, near, blocks[0]]
-
-
-def collect(block, axis, count):
-    if count != 4:
-        return exchange([block] * count, axis)
-    across = swap(block, axis, count, 2)
-    near = swap(block, axis, count, 1)
-    return [block, near, across, swap(across, axis, count, 1)]
 
 
 def spectrum_kernel(model_hbm, table_out_ref, *refs):
@@ -192,46 +154,85 @@
     return found
 
 
-def predict_kernel(groups, parts, limits_ref, right_ref, left_ref, *refs):
-    arrived_refs, out_refs = refs[:groups], refs[groups : groups + parts]
-    spec_ref, sum_ref = refs[groups + parts :]
-    _, freqs, _, low, lanes = spec_ref.shape
-    row_tiles, col_tiles, size, tile = left_ref.shape[2:]
+def project_tile(j, block_refs, tile_ref, limits_ref, right_ref):
+    freqs, _, low, lanes = block_refs[0].shape
+    _, _, row_tiles, _, size, tile = right_ref.shape
+    high = tile // (len(block_refs) * low)
+    rhs = lanes // high
+    me = lax.axis_index("freq")
+    for at, block_ref in enumerate(block_refs):
+        tile_ref[(me ^ at) & (len(block_refs) - 1)] = block_ref[...]
+    products = []
+    for f in range(freqs):
+        halves = []
+        for c in range(2):
+            blocks = []
+            for g in range(len(block_refs)):
+                got = tile_ref[g, f, c]
+                if low % 16:
+                    got = got.astype(jnp.float32)
+                blocks += [got[:, h * rhs : (h + 1) * rhs] for h in range(high)]
+            halves.append(jnp.concatenate(blocks))
+        first = jnp.concatenate(halves, axis=1).astype(jnp.bfloat16)
+        second = jnp.concatenate([halves[1], -halves[0]], axis=1).astype(jnp.bfloat16)
+        right = [right_ref[c, f, :, j].reshape(row_tiles * size, tile) for c in range(2)]
+        products.append(dot(right[0], first, 1, 0) + dot(right[1], second, 1, 0))
+    return [
+        masked(product, limits_ref, [(f, i, j) for i in range(row_tiles)], size)
+        for f, product in enumerate(products)
+    ]
+
+
+def project_kernel(count, limits_ref, right_ref, *refs):
+    block_refs, (out_ref, tile_ref) = refs[:count], refs[count:]
+    j = lax.div(lax.axis_index("freq"), count)
+    for f, parts in enumerate(project_tile(j, block_refs, tile_ref, limits_ref, right_ref)):
+        for i, part in enumerate(parts):
+            out_ref[f, i] = part
+
+
+def project(limits, blocks, green_right):
+    _, freqs, row_tiles, _, size, tile = green_right.shape
+    _, _, low, _ = blocks[0].shape
+    columns = 2 * LANES * len(blocks) * low // tile
+    return pl.pallas_call(
+        functools.partial(project_kernel, len(blocks)),
+        in_specs=[pl.BlockSpec(memory_space=pltpu.VMEM)] * (2 + len(blocks)),
+        out_specs=pl.BlockSpec(memory_space=pltpu.VMEM),
+        out_shape=jax.ShapeDtypeStruct((freqs, row_tiles, size, columns), jnp.bfloat16),
+        scratch_shapes=[pltpu.VMEM((len(blocks),) + blocks[0].shape, jnp.bfloat16)],
+        compiler_params=pltpu.CompilerParams(vmem_limit_bytes=VMEM_LIMIT),
+        cost_estimate=tile_cost(freqs * row_tiles, size, tile, columns // 4),
+        name="project",
+    )(limits, green_right, *blocks)
+
+
+def predict_kernel(groups, parts, limits_ref, right_ref, left_ref, own_ref, *refs):
+    _, freqs, row_tiles, col_tiles, size, tile = left_ref.shape
+    per_tile = groups // col_tiles
+    others = groups - per_tile
+    block_refs, out_refs, (tile_ref, sum_ref) = (
+        refs[:others][::-1],
+        refs[others : others + parts],
+        refs[others + parts :],
+    )
     _, pairs, _ = out_refs[0].shape
-    me = lax.axis_index("freq")
-    for at, arrived_ref in enumerate(arrived_refs[::-1]):
-        spec_ref[origin(me, at, groups)] = arrived_ref[...]
     rhs = parts * pairs // freqs
-    high = lanes // rhs
-    per_tile = groups // col_tiles
-    products = {}
-    for f in range(freqs):
-        for j in range(col_tiles):
-            halves = []
-            for c in range(2):
-                blocks = []
-                for g in range(j * per_tile, (j + 1) * per_tile):
-                    got = spec_ref[g, f, c]
-                    if low % 16:
-                        got = got.astype(jnp.float32)
-                    blocks += [got[:, h * rhs : (h + 1) * rhs] for h in range(high)]
-                halves.append(jnp.concatenate(blocks))
-            first = jnp.concatenate(halves, axis=1).astype(jnp.bfloat16)
-            second = jnp.concatenate([halves[1], -halves[0]], axis=1).astype(jnp.bfloat16)
-            right = [right_ref[c, f, :, j].reshape(row_tiles * size, tile) for c in range(2)]
-            products[f, j] = dot(right[0], first, 1, 0) + dot(right[1], second, 1, 0)
+    own = lax.div(lax.axis_index("freq"), per_tile)
+    tiles = [own]
+    projected = [[[own_ref[f, i] for i in range(row_tiles)] for f in range(freqs)]]
+    for step in range(1, col_tiles):
+        blocks = block_refs[(step - 1) * per_tile : step * per_tile]
+        tiles.append(own ^ step)
+        projected.append(project_tile(own ^ step, blocks, tile_ref, limits_ref, right_ref))
     factors = {}
     for f in range(freqs):
-        projected = [
-            masked(products[f, j], limits_ref, [(f, i, j) for i in range(row_tiles)], size)
-            for j in range(col_tiles)
-        ]
         for i in range(row_tiles):
-            straight = [projected[j][i] for j in range(col_tiles)]
+            straight = [part[f][i] for part in projected]
             factors[f, i] = jnp.concatenate(straight + [turned(part) for part in straight])
     for f in range(freqs):
         for i in range(row_tiles):
-            left = left_ref[:, f, i].reshape(2 * col_tiles * size, tile)
+            left = jnp.concatenate([left_ref[c, f, i, j] for c in range(2) for j in tiles])
             predicted = dot(factors[f, i], left, 0, 0)
             for c in range(2):
                 row = c * rhs
@@ -245,26 +246,24 @@
         out_ref[...] = sum_ref[target(me, at, parts)].astype(out_ref.dtype)
 
 
-def predict(limits, spectrum, green_right, green_left, parts):
+def predict(limits, own, blocks, green_right, green_left, parts):
     freqs, row_tiles, col_tiles, size, tile = green_left.shape[1:]
-    groups = len(spectrum)
-    _, _, low, _ = spectrum[0].shape
-    rhs = LANES * groups * low // (col_tiles * tile)
-    pairs = freqs * rhs
+    groups = len(blocks) * col_tiles // (col_tiles - 1)
+    pairs = freqs * own.shape[3] // 2
     sources = row_tiles * tile
     return pl.pallas_call(
         functools.partial(predict_kernel, groups, parts),
-        in_specs=[pl.BlockSpec(memory_space=pltpu.VMEM)] * (3 + groups),
+        in_specs=[pl.BlockSpec(memory_space=pltpu.VMEM)] * (4 + len(blocks)),
         out_specs=[pl.BlockSpec(memory_space=pltpu.VMEM)] * parts,
         out_shape=[jax.ShapeDtypeStruct((2, pairs // parts, sources), jnp.bfloat16)] * parts,
         scratch_shapes=[
-            pltpu.VMEM((groups,) + spectrum[0].shape, jnp.bfloat16),
+            pltpu.VMEM((groups // col_tiles,) + blocks[0].shape, jnp.bfloat16),
             pltpu.VMEM((parts, 2, pairs // parts, sources), jnp.float32),
         ],
         compiler_params=pltpu.CompilerParams(vmem_limit_bytes=VMEM_LIMIT),
-        cost_estimate=tile_cost(freqs * row_tiles * col_tiles, size, tile, rhs),
+        cost_estimate=tile_cost(freqs * row_tiles * col_tiles, size, tile, pairs // freqs),
         name="predict",
-    )(limits, green_right, green_left, *spectrum[::-1])
+    )(limits, green_right, green_left, own, *blocks[::-1])
 
 
 def residual_kernel(data_ref, *refs):
@@ -409,17 +408,20 @@
                 rows = pl.ds(c * groups * freqs + g * freqs + f, low, stride=bins)
                 rows_ref[rows, :] = part_ref[f, c].astype(jnp.float32)
     table = table_ref[...]
+    width = math.gcd(length, 256)
     copies = []
     for at in range(chunks):
         coefficients = jnp.concatenate(
             [rows_ref[row * bins : (row + 1) * bins] for row in range(at * part, (at + 1) * part)],
             axis=1,
         ).astype(jnp.bfloat16)
-        traces = dot(coefficients, table, 0, 0).astype(out_ref.dtype)
-        for row in range(part):
-            out_ref[:, at * part + row] = traces[row * lanes : (row + 1) * lanes].reshape(
-                high, rhs, length
-            )
+        for column in range(0, length, width):
+            columns = slice(column, column + width)
+            traces = dot(coefficients, table[:, columns], 0, 0).astype(out_ref.dtype)
+            for row in range(part):
+                out_ref[:, at * part + row, :, columns] = traces[
+                    row * lanes : (row + 1) * lanes
+                ].reshape(high, rhs, width)
         rows = pl.ds(at * part, part)
         copies.append(
             pltpu.make_async_copy(out_ref.at[:, rows], out_hbm.at[:, rows], out_sems.at[at])
@@ -460,9 +462,11 @@
     table, spectrum = spectrum_of(model[0], freq_count, freq_local)
     spectrum = exchange(spectrum, "freq")
     limits = jnp.broadcast_to(ranks[..., None, None], ranks.shape + (1, LANES))
-    predicted = predict(limits, spectrum, green_right, green_left, tile_count)
-    misfit, *residual = residual_of(scatter_sums(predicted, "rtile"), data)
-    misfit = collect(misfit, "rtile", tile_count)
+    per_tile = freq_count // green_right.shape[3]
+    own = project(limits, spectrum[:per_tile], green_right)
+    predicted = predict(limits, own, spectrum[per_tile:], green_right, green_left, tile_count)
+    misfit, *residual = residual_of(exchange(predicted, "rtile")[::-1], data)
+    misfit = exchange([misfit] * tile_count, "rtile")
     partial = back_project(limits, misfit, green_right, green_left, freq_count, rep_count)
     arrived = exchange(gather(exchange(partial, "rep")), "freq")
     return (jnp.stack(residual), gradient_of(arrived, table, rhs_count))

time: 50.2 us -> 48.2 us (0.960)
  starting transfers between devices: 22.1 us -> 17.1 us
  waiting for transfers between devices: 16.4 us -> 19.2 us
    ppermute x6 -> x0, starting transfers between devices: 13.9 us -> none  [swap(): return lax.ppermute(block, axis, [(me, me ^ step) for me in range(count)])]
    ppermute x7 -> x13, waiting for transfers between devices: 7.31 us -> 19.2 us  [exchange(): arrived.append(lax.ppermute(blocks[step], axis, pairs))]
    ppermute x6 -> x0, waiting for transfers between devices: 9.08 us -> none  [swap(): return lax.ppermute(block, axis, [(me, me ^ step) for me in range(count)])]
    ppermute x7 -> x13, starting transfers between devices: 8.23 us -> 17.1 us  [exchange(): arrived.append(lax.ppermute(blocks[step], axis, pairs))]
    pallas_call x1, Pallas kernels: 0.03 us -> 0.57 us  [project(): pl.pallas_call(functools.partial(project_kernel, len(blocks)), in_specs=[...]
  transfers between devices with their start and end apart: 13 -> 13, of which waited for: 10 -> 11; matrix products, arithmetic and copies ran while one was open for 2% -> 2% of each run, Pallas kernels for 0% -> 1%
where the time goes in v11:
time: 48.2 us; the launch traced here: 48 us
  waiting for transfers between devices  19.2 us (40%)
  starting transfers between devices  17.1 us (35%)
  Pallas kernels  10.1 us (21%)
  between operations  0.74 us (2%)
  other arithmetic  0.7 us (1%)
    ppermute x13, waiting for transfers between devices, exchange(): arrived.append(lax.ppermute(blocks[step], axis, pairs))  19.2 us
    ppermute x13, starting transfers between devices, exchange(): arrived.append(lax.ppermute(blocks[step], axis, pairs))  17.1 us
    pallas_call x1, Pallas kernels, spectrum_of(): pl.pallas_call(spectrum_kernel, in_specs=[pl.BlockSpec(memory_space=pltpu...  4.73 us
    pallas_call x1, Pallas kernels, gradient_of(): pl.pallas_call(gradient_kernel, in_specs=[pl.BlockSpec(memory_space=pltpu...  2.53 us
    pallas_call x1, Pallas kernels, back_project(): pl.pallas_call(functools.partial(back_kernel, parts, groups, reps), in_sp...  1.2 us
    pallas_call x1, Pallas kernels, predict(): pl.pallas_call(functools.partial(predict_kernel, groups, parts), in_specs...  0.99 us
  transfers between devices with their start and end apart: 13, of which 11 were waited for; matrix products, arithmetic and copies ran while one was open for 2% of the time, Pallas kernels for 1%

profile of v11, /device:TPU:0, one launch (start us, length us, event | category | flops | bytes accessed | tf_op | source)
XLA Modules:
  0.0 48.0 jit_solution(11937173398469120296)
XLA Ops:
  0.6 0.0 copy-start.3
  0.6 0.0 copy-start
  0.7 0.0 copy-start.1
  0.7 0.0 copy-start.2
  0.7 4.7 %spectrum.1 = (bf16[24,1024]{1,0:T(8,128)(2,1)S(1)}, bf16[3,2,32,128]{3,2,1,0:T(8,128)(2,1)S(1)}, bf16[3,2,32,128]{3,2,1,0:T(8,128)(2,1)S(1)}, bf16[3,2,32,128]{...) custom-call(bf16[4,32,32,1024]{3,2,1,0:T(8,128)(2,1)} %bitcast.6), custom_call_target="tpu_custom_call" | custom-call | tf_op jit(solution)/shard_map/spectrum/pallas_call | solution.py:112
  5.4 3.0 %collective-permute-start = (bf16[3,2,32,128]{3,2,1,0:T(8,128)(2,1)S(1)}, bf16[3,2,32,128]{3,2,1,0:T(8,128)(2,1)S(1)}, u32[]{:S(2)}, u32[]{:S(2)}) collective-permute-start(bf16[3,2,32,128]{3,2,1,0:T(8,128)(2,1)S(1)} %get-tuple-element.21), channel_id=1, source_target_pairs={{0,8},{8,0},{16,24},{24,16},{1,9},{9,1},{17,25},{25,17},{2,10},{10... | collective-permute-start | bytes 147464 | tf_op jit(solution)/shard_map/ppermute | solution.py:62
  8.4 1.5 %collective-permute-start.1 = (bf16[3,2,32,128]{3,2,1,0:T(8,128)(2,1)S(1)}, bf16[3,2,32,128]{3,2,1,0:T(8,128)(2,1)S(1)}, u32[]{:S(2)}, u32[]{:S(2)}) collective-permute-start(bf16[3,2,32,128]{3,2,1,0:T(8,128)(2,1)S(1)} %get-tuple-element.22), channel_id=1, source_target_pairs={{0,24},{8,16},{16,8},{24,0},{1,25},{9,17},{17,9},{25,1},{2,26},{10... | collective-permute-start | bytes 147464 | tf_op jit(solution)/shard_map/ppermute | solution.py:62
  9.9 0.0 collective-permute-start.2
  9.9 0.0 copy-done.3
  10.0 0.1 copy.7
  10.1 0.4 collective-permute-done.refs_1_
  10.5 0.1 broadcast_in_dim.2.limits_ref
  10.6 0.0 copy-done
  10.6 0.6 %project.1.own_ref = bf16[3,4,48,64]{3,2,1,0:T(8,128)(2,1)S(1)} custom-call(s32[3,4,2,1,128]{4,3,2,1,0:T(1,128)S(1)} %broadcast_in_dim.2.limits_ref, bf16[2,3,4,2,48,256]{5,4,3,2,1,0:T(8,128)(2,1)S(1)} %copy-done, bf16[3,2,32,128]{3,2,1,0:T(8,128)(2,1)S(1)} %get-tuple-element.20.refs_0_, bf16[3,2,32,128]{3,2,1,0:T(8,128)(2,1)S(1)} %collective-permute-done.refs_1_), custom_call_target="tpu_custom_call" | custom-call | flops 37748736 | bytes 1179648 | tf_op jit(solution)/shard_map/project/pallas_call | solution.py:198
  11.2 2.2 %collective-permute-done.1.refs_0_ = bf16[3,2,32,128]{3,2,1,0:T(8,128)(2,1)S(1)} collective-permute-done((bf16[3,2,32,128]{3,2,1,0:T(8,128)(2,1)S(1)}, bf16[3,2,32,128]{3,2,1,0:T(8,128)(2,1)S(1)}, u32[]{:S(2)}, u32[]{:S(2)}) %collective-permute-start.1) | collective-permute-done | bytes 49184 | tf_op jit(solution)/shard_map/ppermute | solution.py:62
  13.4 0.6 %collective-permute-done.2.refs_1_ = bf16[3,2,32,128]{3,2,1,0:T(8,128)(2,1)S(1)} collective-permute-done((bf16[3,2,32,128]{3,2,1,0:T(8,128)(2,1)S(1)}, bf16[3,2,32,128]{3,2,1,0:T(8,128)(2,1)S(1)}, u32[]{:S(2)}, u32[]{:S(2)}) %collective-permute-start.2) | collective-permute-done | bytes 49184 | tf_op jit(solution)/shard_map/ppermute | solution.py:62
  14.0 0.0 copy-done.1
  14.0 1.0 %predict.1 = (bf16[2,24,1024]{2,1,0:T(8,128)(2,1)S(1)}, bf16[2,24,1024]{2,1,0:T(8,128)(2,1)S(1)}, bf16[2,24,1024]{2,1,0:T(8,128)(2,1)S(1)}, bf16[2,24,1024]{2,1,0:T(8,128)(2,1)S(1)}) custom-call(s32[3,4,2,1,128]{4,3,2,1,0:T(1,128)S(1)} %broadcast_in_dim.2.limits_ref, bf16[2,3,4,2,48,256]{5,4,3,2,1,0:T(8,128)(2,1)S(1)} %copy-done, ...), custom_call_target="tpu_custom_call" | custom-call | flops 150994944 | bytes 2359296 | tf_op jit(solution)/shard_map/predict/pallas_call | solution.py:254
  15.0 3.7 %collective-permute-start.3 = (bf16[2,24,1024]{2,1,0:T(8,128)(2,1)S(1)}, bf16[2,24,1024]{2,1,0:T(8,128)(2,1)S(1)}, u32[]{:S(2)}, u32[]{:S(2)}) collective-permute-start(bf16[2,24,1024]{2,1,0:T(8,128)(2,1)S(1)} %get-tuple-element.24), channel_id=1, source_target_pairs={{0,6},{2,4},{4,2},{6,0},{1,7},{3,5},{5,3},{7,1},{8,14},{10,12},{12... | collective-permute-start | bytes 294920 | tf_op jit(solution)/shard_map/ppermute | solution.py:62
  18.7 0.0 collective-permute-start.4
  18.7 0.8 %collective-permute-start.5 = (bf16[2,24,1024]{2,1,0:T(8,128)(2,1)S(1)}, bf16[2,24,1024]{2,1,0:T(8,128)(2,1)S(1)}, u32[]{:S(2)}, u32[]{:S(2)}) collective-permute-start(bf16[2,24,1024]{2,1,0:T(8,128)(2,1)S(1)} %get-tuple-element.26), channel_id=1, source_target_pairs={{0,2},{2,0},{4,6},{6,4},{1,3},{3,1},{5,7},{7,5},{8,10},{10,8},{12,... | collective-permute-start | bytes 294920 | tf_op jit(solution)/shard_map/ppermute | solution.py:62
  19.4 2.2 %collective-permute-done.3.refs_0_ = bf16[2,24,1024]{2,1,0:T(8,128)(2,1)S(1)} collective-permute-done((bf16[2,24,1024]{2,1,0:T(8,128)(2,1)S(1)}, bf16[2,24,1024]{2,1,0:T(8,128)(2,1)S(1)}, u32[]{:S(2)}, u32[]{:S(2)}) %collective-permute-start.3) | collective-permute-done | bytes 98336 | tf_op jit(solution)/shard_map/ppermute | solution.py:62
  21.6 4.1 %collective-permute-done.4.refs_1_ = bf16[2,24,1024]{2,1,0:T(8,128)(2,1)S(1)} collective-permute-done((bf16[2,24,1024]{2,1,0:T(8,128)(2,1)S(1)}, bf16[2,24,1024]{2,1,0:T(8,128)(2,1)S(1)}, u32[]{:S(2)}, u32[]{:S(2)}) %collective-permute-start.4) | collective-permute-done | bytes 98336 | tf_op jit(solution)/shard_map/ppermute | solution.py:62
  25.7 0.0 collective-permute-done.5.refs_2_
  25.7 0.0 copy-done.2
  25.7 0.1 residual.1
  25.8 2.5 %collective-permute-start.8 = (bf16[2,24,1024]{2,1,0:T(8,128)(2,1)S(1)}, bf16[2,24,1024]{2,1,0:T(8,128)(2,1)S(1)}, u32[]{:S(2)}, u32[]{:S(2)}) collective-permute-start(bf16[2,24,1024]{2,1,0:T(8,128)(2,1)S(1)} %get-tuple-element.31.refs_0_), channel_id=1, source_target_pairs={{0,6},{2,4},{4,2},{6,0},{1,7},{3,5},{5,3},{7,1},{8,14},{10,12},{12... | collective-permute-start | bytes 294920 | tf_op jit(solution)/shard_map/ppermute | solution.py:62
  28.3 0.0 collective-permute-start.7
  28.3 1.9 %collective-permute-start.6 = (bf16[2,24,1024]{2,1,0:T(8,128)(2,1)S(1)}, bf16[2,24,1024]{2,1,0:T(8,128)(2,1)S(1)}, u32[]{:S(2)}, u32[]{:S(2)}) collective-permute-start(bf16[2,24,1024]{2,1,0:T(8,128)(2,1)S(1)} %get-tuple-element.31.refs_0_), channel_id=1, source_target_pairs={{0,2},{2,0},{4,6},{6,4},{1,3},{3,1},{5,7},{7,5},{8,10},{10,8},{12,... | collective-permute-start | bytes 294920 | tf_op jit(solution)/shard_map/ppermute | solution.py:62
  30.2 3.1 %collective-permute-done.8.refs_3_ = bf16[2,24,1024]{2,1,0:T(8,128)(2,1)S(1)} collective-permute-done((bf16[2,24,1024]{2,1,0:T(8,128)(2,1)S(1)}, bf16[2,24,1024]{2,1,0:T(8,128)(2,1)S(1)}, u32[]{:S(2)}, u32[]{:S(2)}) %collective-permute-start.8) | collective-permute-done | bytes 98336 | tf_op jit(solution)/shard_map/ppermute | solution.py:62
  33.4 2.5 %collective-permute-done.7.refs_2_ = bf16[2,24,1024]{2,1,0:T(8,128)(2,1)S(1)} collective-permute-done((bf16[2,24,1024]{2,1,0:T(8,128)(2,1)S(1)}, bf16[2,24,1024]{2,1,0:T(8,128)(2,1)S(1)}, u32[]{:S(2)}, u32[]{:S(2)}) %collective-permute-start.7) | collective-permute-done | bytes 98336 | tf_op jit(solution)/shard_map/ppermute | solution.py:62
  35.9 0.0 collective-permute-done.6.refs_1_
  35.9 1.2 %back_project.1 = (bf16[4,3,2,16,128]{4,3,2,1,0:T(8,128)(2,1)S(1)}, bf16[4,3,2,16,128]{4,3,2,1,0:T(8,128)(2,1)S(1)}) custom-call(s32[3,4,2,1,128]{4,3,2,1,0:T(1,128)S(1)} %broadcast_in_dim.2.limits_ref, bf16[2,3,4,2,48,256]{5,4,3,2,1,0:T(8,128)(2,1)S(1)} %copy-done, bf16[2,3,4,2,48,256]{5,4,3,2,1,0:T(8,128)(2,1)S(1)} %copy-done.1, ...), custom_call_target="tpu_custom_call" | custom-call | flops 150994944 | bytes 2359296 | tf_op jit(solution)/shard_map/back_project/pallas_call | solution.py:361
  37.1 0.1 collective-permute-start.9
  37.2 1.3 %collective-permute-done.9.refs_1_ = bf16[4,3,2,16,128]{4,3,2,1,0:T(8,128)(2,1)S(1)} collective-permute-done((bf16[4,3,2,16,128]{4,3,2,1,0:T(8,128)(2,1)S(1)}, bf16[4,3,2,16,128]{4,3,2,1,0:T(8,128)(2,1)S(1)}, u32[]{:S(2)}, u32[]{:S(2)}) %collective-permute-start.9) | collective-permute-done | bytes 98336 | tf_op jit(solution)/shard_map/ppermute | solution.py:62
  38.5 1.5 %collective-permute-start.10 = (bf16[3,2,16,128]{3,2,1,0:T(8,128)(2,1)S(1)}, bf16[3,2,16,128]{3,2,1,0:T(8,128)(2,1)S(1)}, u32[]{:S(2)}, u32[]{:S(2)}) collective-permute-start(bf16[3,2,16,128]{3,2,1,0:T(8,128)(2,1)S(1)} %get-tuple-element.34), channel_id=1, source_target_pairs={{0,24},{8,16},{16,8},{24,0},{1,25},{9,17},{17,9},{25,1},{2,26},{10... | collective-permute-start | bytes 73736 | tf_op jit(solution)/shard_map/ppermute | solution.py:62
  40.0 1.6 %collective-permute-start.11 = (bf16[3,2,16,128]{3,2,1,0:T(8,128)(2,1)S(1)}, bf16[3,2,16,128]{3,2,1,0:T(8,128)(2,1)S(1)}, u32[]{:S(2)}, u32[]{:S(2)}) collective-permute-start(bf16[3,2,16,128]{3,2,1,0:T(8,128)(2,1)S(1)} %get-tuple-element.35), channel_id=1, source_target_pairs={{0,16},{8,24},{16,0},{24,8},{1,17},{9,25},{17,1},{25,9},{2,18},{10... | collective-permute-start | bytes 73736 | tf_op jit(solution)/shard_map/ppermute | solution.py:62
  41.7 0.4 collective-permute-start.12
  42.1 0.7 %pad_maximum_fusion = f32[2,24,1024]{2,1,0:T(8,128)} fusion(f32[1,24,1024]{2,1,0:T(8,128)S(1)} %bitcast.5, f32[1,24,1024]{2,1,0:T(8,128)S(1)} %bitcast.4), kind=kLoop, calls=%fused_computation | loop fusion | flops 49152 | bytes 393216 | tf_op jit(solution)/shard_map/stack | solution.py:472
  42.8 0.5 %collective-permute-done.10.refs_0_ = bf16[3,2,16,128]{3,2,1,0:T(8,128)(2,1)S(1)} collective-permute-done((bf16[3,2,16,128]{3,2,1,0:T(8,128)(2,1)S(1)}, bf16[3,2,16,128]{3,2,1,0:T(8,128)(2,1)S(1)}, u32[]{:S(2)}, u32[]{:S(2)}) %collective-permute-start.10) | collective-permute-done | bytes 24608 | tf_op jit(solution)/shard_map/ppermute | solution.py:62
  43.3 0.6 %collective-permute-done.11.refs_1_ = bf16[3,2,16,128]{3,2,1,0:T(8,128)(2,1)S(1)} collective-permute-done((bf16[3,2,16,128]{3,2,1,0:T(8,128)(2,1)S(1)}, bf16[3,2,16,128]{3,2,1,0:T(8,128)(2,1)S(1)}, u32[]{:S(2)}, u32[]{:S(2)}) %collective-permute-start.11) | collective-permute-done | bytes 24608 | tf_op jit(solution)/shard_map/ppermute | solution.py:62
  43.9 1.6 %collective-permute-done.12.refs_2_ = bf16[3,2,16,128]{3,2,1,0:T(8,128)(2,1)S(1)} collective-permute-done((bf16[3,2,16,128]{3,2,1,0:T(8,128)(2,1)S(1)}, bf16[3,2,16,128]{3,2,1,0:T(8,128)(2,1)S(1)}, u32[]{:S(2)}, u32[]{:S(2)}) %collective-permute-start.12) | collective-permute-done | bytes 24608 | tf_op jit(solution)/shard_map/ppermute | solution.py:62
  45.5 2.5 %gradient.1 = bf16[4,16,32,1024]{3,2,1,0:T(8,128)(2,1)} custom-call(bf16[24,1024]{1,0:T(8,128)(2,1)S(1)} %get-tuple-element.30.table_ref, bf16[3,2,16,128]{3,2,1,0:T(8,128)(2,1)S(1)} %collective-permute-done.10.refs_0_, bf16[3,2,16,128]{3,2,1,0:T(8,128)(2,1)S(1)} %collective-permute-done.11.refs_1_, ...), custom_call_target="tpu_custom_call" | custom-call | tf_op jit(solution)/shard_map/gradient/pallas_call | solution.py:440
  (1 shorter events, 0.0 us)
Async XLA Ops:
  0.6 9.3 %copy-start.3 = (s32[3,4,2]{1,2,0:T(2,128)S(1)}, s32[3,4,2]{1,2,0:T(2,128)}, u32[]{:S(2)}) copy-start(s32[3,4,2]{1,2,0:T(2,128)} %param.8) | copy-start | bytes 292
  0.6 9.9 %copy-start = (bf16[2,3,4,2,48,256]{5,4,3,2,1,0:T(8,128)(2,1)S(1)}, bf16[2,3,4,2,48,256]{5,4,3,2,1,0:T(8,128)(2,1)}, u32[]{:S(2)}) copy-start(bf16[2,3,4,2,48,256]{5,4,3,2,1,0:T(8,128)(2,1)} %right_ref.5) | copy-start | bytes 3538948
  0.7 13.3 %copy-start.1 = (bf16[2,3,4,2,48,256]{5,4,3,2,1,0:T(8,128)(2,1)S(1)}, bf16[2,3,4,2,48,256]{5,4,3,2,1,0:T(8,128)(2,1)}, u32[]{:S(2)}) copy-start(bf16[2,3,4,2,48,256]{5,4,3,2,1,0:T(8,128)(2,1)} %left_ref.3) | copy-start | bytes 3538948
  0.7 25.1 %copy-start.2 = (f32[2,24,1024]{2,1,0:T(8,128)S(1)}, f32[2,24,1024]{2,1,0:T(8,128)}, u32[]{:S(2)}) copy-start(f32[2,24,1024]{2,1,0:T(8,128)} %data_ref.1) | copy-start | bytes 589828
  5.4 5.1 %collective-permute-start = (bf16[3,2,32,128]{3,2,1,0:T(8,128)(2,1)S(1)}, bf16[3,2,32,128]{3,2,1,0:T(8,128)(2,1)S(1)}, u32[]{:S(2)}, u32[]{:S(2)}) collective-permute-start(bf16[3,2,32,128]{3,2,1,0:T(8,128)(2,1)S(1)} %get-tuple-element.21), channel_id=1, source_target_pairs={{0,8},{8,0},{16,24},{24,16},{1,9},{9,1},{17,25},{25,17},{2,10},{10... | collective-permute-start | bytes 147464 | tf_op jit(solution)/shard_map/ppermute | solution.py:62
  8.4 5.0 %collective-permute-start.1 = (bf16[3,2,32,128]{3,2,1,0:T(8,128)(2,1)S(1)}, bf16[3,2,32,128]{3,2,1,0:T(8,128)(2,1)S(1)}, u32[]{:S(2)}, u32[]{:S(2)}) collective-permute-start(bf16[3,2,32,128]{3,2,1,0:T(8,128)(2,1)S(1)} %get-tuple-element.22), channel_id=1, source_target_pairs={{0,24},{8,16},{16,8},{24,0},{1,25},{9,17},{17,9},{25,1},{2,26},{10... | collective-permute-start | bytes 147464 | tf_op jit(solution)/shard_map/ppermute | solution.py:62
  9.9 4.1 %collective-permute-start.2 = (bf16[3,2,32,128]{3,2,1,0:T(8,128)(2,1)S(1)}, bf16[3,2,32,128]{3,2,1,0:T(8,128)(2,1)S(1)}, u32[]{:S(2)}, u32[]{:S(2)}) collective-permute-start(bf16[3,2,32,128]{3,2,1,0:T(8,128)(2,1)S(1)} %get-tuple-element.23), channel_id=1, source_target_pairs={{0,16},{8,24},{16,0},{24,8},{1,17},{9,25},{17,1},{25,9},{2,18},{10... | collective-permute-start | bytes 147464 | tf_op jit(solution)/shard_map/ppermute | solution.py:62
  15.0 6.6 %collective-permute-start.3 = (bf16[2,24,1024]{2,1,0:T(8,128)(2,1)S(1)}, bf16[2,24,1024]{2,1,0:T(8,128)(2,1)S(1)}, u32[]{:S(2)}, u32[]{:S(2)}) collective-permute-start(bf16[2,24,1024]{2,1,0:T(8,128)(2,1)S(1)} %get-tuple-element.24), channel_id=1, source_target_pairs={{0,6},{2,4},{4,2},{6,0},{1,7},{3,5},{5,3},{7,1},{8,14},{10,12},{12... | collective-permute-start | bytes 294920 | tf_op jit(solution)/shard_map/ppermute | solution.py:62
  18.7 7.0 %collective-permute-start.4 = (bf16[2,24,1024]{2,1,0:T(8,128)(2,1)S(1)}, bf16[2,24,1024]{2,1,0:T(8,128)(2,1)S(1)}, u32[]{:S(2)}, u32[]{:S(2)}) collective-permute-start(bf16[2,24,1024]{2,1,0:T(8,128)(2,1)S(1)} %get-tuple-element.25), channel_id=1, source_target_pairs={{0,4},{2,6},{4,0},{6,2},{1,5},{3,7},{5,1},{7,3},{8,12},{10,14},{12... | collective-permute-start | bytes 294920 | tf_op jit(solution)/shard_map/ppermute | solution.py:62
  18.7 7.0 %collective-permute-start.5 = (bf16[2,24,1024]{2,1,0:T(8,128)(2,1)S(1)}, bf16[2,24,1024]{2,1,0:T(8,128)(2,1)S(1)}, u32[]{:S(2)}, u32[]{:S(2)}) collective-permute-start(bf16[2,24,1024]{2,1,0:T(8,128)(2,1)S(1)} %get-tuple-element.26), channel_id=1, source_target_pairs={{0,2},{2,0},{4,6},{6,4},{1,3},{3,1},{5,7},{7,5},{8,10},{10,8},{12,... | collective-permute-start | bytes 294920 | tf_op jit(solution)/shard_map/ppermute | solution.py:62
  25.8 7.6 %collective-permute-start.8 = (bf16[2,24,1024]{2,1,0:T(8,128)(2,1)S(1)}, bf16[2,24,1024]{2,1,0:T(8,128)(2,1)S(1)}, u32[]{:S(2)}, u32[]{:S(2)}) collective-permute-start(bf16[2,24,1024]{2,1,0:T(8,128)(2,1)S(1)} %get-tuple-element.31.refs_0_), channel_id=1, source_target_pairs={{0,6},{2,4},{4,2},{6,0},{1,7},{3,5},{5,3},{7,1},{8,14},{10,12},{12... | collective-permute-start | bytes 294920 | tf_op jit(solution)/shard_map/ppermute | solution.py:62
  28.3 7.6 %collective-permute-start.7 = (bf16[2,24,1024]{2,1,0:T(8,128)(2,1)S(1)}, bf16[2,24,1024]{2,1,0:T(8,128)(2,1)S(1)}, u32[]{:S(2)}, u32[]{:S(2)}) collective-permute-start(bf16[2,24,1024]{2,1,0:T(8,128)(2,1)S(1)} %get-tuple-element.31.refs_0_), channel_id=1, source_target_pairs={{0,4},{2,6},{4,0},{6,2},{1,5},{3,7},{5,1},{7,3},{8,12},{10,14},{12... | collective-permute-start | bytes 294920 | tf_op jit(solution)/shard_map/ppermute | solution.py:62
  28.3 7.6 %collective-permute-start.6 = (bf16[2,24,1024]{2,1,0:T(8,128)(2,1)S(1)}, bf16[2,24,1024]{2,1,0:T(8,128)(2,1)S(1)}, u32[]{:S(2)}, u32[]{:S(2)}) collective-permute-start(bf16[2,24,1024]{2,1,0:T(8,128)(2,1)S(1)} %get-tuple-element.31.refs_0_), channel_id=1, source_target_pairs={{0,2},{2,0},{4,6},{6,4},{1,3},{3,1},{5,7},{7,5},{8,10},{10,8},{12,... | collective-permute-start | bytes 294920 | tf_op jit(solution)/shard_map/ppermute | solution.py:62
  37.1 1.4 %collective-permute-start.9 = (bf16[4,3,2,16,128]{4,3,2,1,0:T(8,128)(2,1)S(1)}, bf16[4,3,2,16,128]{4,3,2,1,0:T(8,128)(2,1)S(1)}, u32[]{:S(2)}, u32[]{:S(2)}) collective-permute-start(bf16[4,3,2,16,128]{4,3,2,1,0:T(8,128)(2,1)S(1)} %get-tuple-element.33), channel_id=1, source_target_pairs={{0,1},{1,0},{2,3},{3,2},{4,5},{5,4},{6,7},{7,6},{8,9},{9,8},{10,11... | collective-permute-start | bytes 294920 | tf_op jit(solution)/shard_map/ppermute | solution.py:62
  38.5 4.8 %collective-permute-start.10 = (bf16[3,2,16,128]{3,2,1,0:T(8,128)(2,1)S(1)}, bf16[3,2,16,128]{3,2,1,0:T(8,128)(2,1)S(1)}, u32[]{:S(2)}, u32[]{:S(2)}) collective-permute-start(bf16[3,2,16,128]{3,2,1,0:T(8,128)(2,1)S(1)} %get-tuple-element.34), channel_id=1, source_target_pairs={{0,24},{8,16},{16,8},{24,0},{1,25},{9,17},{17,9},{25,1},{2,26},{10... | collective-permute-start | bytes 73736 | tf_op jit(solution)/shard_map/ppermute | solution.py:62
  40.0 3.8 %collective-permute-start.11 = (bf16[3,2,16,128]{3,2,1,0:T(8,128)(2,1)S(1)}, bf16[3,2,16,128]{3,2,1,0:T(8,128)(2,1)S(1)}, u32[]{:S(2)}, u32[]{:S(2)}) collective-permute-start(bf16[3,2,16,128]{3,2,1,0:T(8,128)(2,1)S(1)} %get-tuple-element.35), channel_id=1, source_target_pairs={{0,16},{8,24},{16,0},{24,8},{1,17},{9,25},{17,1},{25,9},{2,18},{10... | collective-permute-start | bytes 73736 | tf_op jit(solution)/shard_map/ppermute | solution.py:62
  41.7 3.8 %collective-permute-start.12 = (bf16[3,2,16,128]{3,2,1,0:T(8,128)(2,1)S(1)}, bf16[3,2,16,128]{3,2,1,0:T(8,128)(2,1)S(1)}, u32[]{:S(2)}, u32[]{:S(2)}) collective-permute-start(bf16[3,2,16,128]{3,2,1,0:T(8,128)(2,1)S(1)} %get-tuple-element.36), channel_id=1, source_target_pairs={{0,8},{8,0},{16,24},{24,16},{1,9},{9,1},{17,25},{25,17},{2,10},{10... | collective-permute-start | bytes 73736 | tf_op jit(solution)/shard_map/ppermute | solution.py:62

commit v12 on v11

--- a/solution.py
+++ b/solution.py
@@ -61,6 +61,10 @@
         pairs = [(me, me ^ step if count & (count - 1) == 0 else (me + step) % count) for me in range(count)]
         arrived.append(lax.ppermute(blocks[step], axis, pairs))
     return [blocks[0]] + arrived[::-1]
+
+
+def shared_steps(groups, reps):
+    return groups == 4 and reps == 2
 
 
 def spectrum_kernel(model_hbm, table_out_ref, *refs):
@@ -347,8 +351,12 @@
     me, own = lax.axis_index("freq"), lax.axis_index("rep")
     for at, out_ref in enumerate(out_refs):
         rep = target(own, at, reps)
-        for step in range(groups):
-            out_ref[step] = grad_ref[target(me, step, groups) * reps + rep]
+        if shared_steps(groups, reps):
+            places = [((1 + rep), 0), ((1 + rep), 1), (3, rep), (0, rep)]
+        else:
+            places = [(step, rep) for step in range(groups)]
+        for slot, (step, core) in enumerate(places):
+            out_ref[slot] = grad_ref[target(me, step, groups) * reps + core]
 
 
 def back_project(limits, misfit, green_right, green_left, groups, reps):
@@ -375,38 +383,76 @@
 
 def gather_kernel(reps, *refs):
     part_refs, out_refs = refs[:reps], refs[reps:]
-    for step, out_ref in enumerate(out_refs):
-        total = sum(part_ref[step].astype(jnp.float32) for part_ref in part_refs)
-        out_ref[...] = total.astype(out_ref.dtype)
-
-
-def gather(parts):
-    shape = parts[0].shape
+    slot = 0
+    for out_ref in out_refs:
+        for at in range(out_ref.shape[0]):
+            total = sum(part_ref[slot].astype(jnp.float32) for part_ref in part_refs)
+            out_ref[at] = total.astype(out_ref.dtype)
+            slot += 1
+
+
+def gather(parts, counts):
+    shape = parts[0].shape[1:]
     return pl.pallas_call(
         functools.partial(gather_kernel, len(parts)),
         in_specs=[pl.BlockSpec(memory_space=pltpu.VMEM)] * len(parts),
-        out_specs=[pl.BlockSpec(memory_space=pltpu.VMEM)] * shape[0],
-        out_shape=[jax.ShapeDtypeStruct(shape[1:], jnp.bfloat16)] * shape[0],
+        out_specs=[pl.BlockSpec(memory_space=pltpu.VMEM)] * len(counts),
+        out_shape=[jax.ShapeDtypeStruct((count,) + shape, jnp.bfloat16) for count in counts],
         compiler_params=pltpu.CompilerParams(vmem_limit_bytes=VMEM_LIMIT),
         name="gather",
     )(*parts)
 
 
-def gradient_kernel(table_ref, *refs):
+def other_kernel(pair_ref, out_ref):
+    out_ref[0] = pair_ref[1 - lax.axis_index("rep")]
+
+
+def other(pair):
+    return pl.pallas_call(
+        other_kernel,
+        in_specs=[pl.BlockSpec(memory_space=pltpu.VMEM)],
+        out_specs=pl.BlockSpec(memory_space=pltpu.VMEM),
+        out_shape=jax.ShapeDtypeStruct((1,) + pair.shape[1:], pair.dtype),
+        compiler_params=pltpu.CompilerParams(vmem_limit_bytes=VMEM_LIMIT),
+        name="other",
+    )(pair)
+
+
+def return_spectra(parts):
+    groups, reps = parts[0].shape[0], len(parts)
+    parts = exchange(parts, "rep")
+    if not shared_steps(groups, reps):
+        return exchange(gather(parts, [1] * groups), "freq")
+    pair, last, own = gather(parts, [2, 1, 1])
+    devices = [(chip, core) for chip in range(groups) for core in range(reps)]
+    near = [(chip * reps + core, (chip ^ (1 + core)) * reps + core) for chip, core in devices]
+    far = [(chip * reps + core, (chip ^ 3) * reps + core) for chip, core in devices]
+    pair = lax.ppermute(pair, ("freq", "rep"), near)
+    last = lax.ppermute(last, ("freq", "rep"), far)
+    swapped = lax.ppermute(other(pair), "rep", [(0, 1), (1, 0)])
+    return [own, pair, swapped, last]
+
+
+def gradient_kernel(reps, table_ref, *refs):
     part_refs, (out_hbm, out_ref, rows_ref, out_sems) = refs[-5::-1], refs[-4:]
     groups = len(part_refs)
-    freqs, _, low, lanes = part_refs[0].shape
+    _, freqs, _, low, lanes = part_refs[0].shape
     high, _, rhs, length = out_ref.shape
     bins = table_ref.shape[0]
     chunks = out_sems.shape[0]
     part = low // chunks
     me = lax.axis_index("freq")
-    for at, part_ref in enumerate(part_refs):
-        g = origin(me, at, groups)
+    if shared_steps(groups, reps):
+        core = lax.axis_index("rep")
+        places = [(0, 0), (1 + core, core), (2 - core, 0), (3, 0)]
+    else:
+        places = [(step, 0) for step in range(groups)]
+    for part_ref, (step, place) in zip(part_refs, places):
+        g = origin(me, step, groups)
         for f in range(freqs):
             for c in range(2):
                 rows = pl.ds(c * groups * freqs + g * freqs + f, low, stride=bins)
-                rows_ref[rows, :] = part_ref[f, c].astype(jnp.float32)
+                rows_ref[rows, :] = part_ref[place, f, c].astype(jnp.float32)
     table = table_ref[...]
     width = math.gcd(length, 256)
     copies = []
@@ -431,14 +477,14 @@
         copy.wait()
 
 
-def gradient_of(parts, table, rhs):
-    _, _, low, lanes = parts[0].shape
+def gradient_of(parts, table, rhs, reps):
+    _, _, _, low, lanes = parts[0].shape
     bins, length = table.shape
     high = lanes // rhs
     chunks = math.gcd(low, 4)
     shape = (high, low, rhs, length)
     out = pl.pallas_call(
-        gradient_kernel,
+        functools.partial(gradient_kernel, reps),
         in_specs=[pl.BlockSpec(memory_space=pltpu.VMEM)] * (1 + len(parts)),
         out_specs=pl.BlockSpec(memory_space=pltpu.HBM),
         out_shape=jax.ShapeDtypeStruct(shape, jnp.bfloat16),
@@ -468,8 +514,8 @@
     misfit, *residual = residual_of(exchange(predicted, "rtile")[::-1], data)
     misfit = exchange([misfit] * tile_count, "rtile")
     partial = back_project(limits, misfit, green_right, green_left, freq_count, rep_count)
-    arrived = exchange(gather(exchange(partial, "rep")), "freq")
-    return (jnp.stack(residual), gradient_of(arrived, table, rhs_count))
+    arrived = return_spectra(partial)
+    return (jnp.stack(residual), gradient_of(arrived, table, rhs_count, rep_count))
 
 
 def solution(mesh):

time: 48.2 us -> 47.6 us (0.988)
  starting transfers between devices: 17.1 us -> 15.9 us
  waiting for transfers between devices: 19.2 us -> 19.9 us
    ppermute x13 -> x10, starting transfers between devices: 17.1 us -> 13.5 us  [exchange(): arrived.append(lax.ppermute(blocks[step], axis, pairs))]
    ppermute x0 -> x3, waiting for transfers between devices: none -> 3.37 us  [the longest x1 2.07 us: return_spectra(): pair = lax.ppermute(pair, ('freq', 'rep'), near)]
    ppermute x13 -> x10, waiting for transfers between devices: 19.2 us -> 16.5 us  [exchange(): arrived.append(lax.ppermute(blocks[step], axis, pairs))]
    ppermute x0 -> x3, starting transfers between devices: none -> 2.34 us  [the longest x1 1.69 us: return_spectra(): pair = lax.ppermute(pair, ('freq', 'rep'), near)]
    pallas_call x1 -> x2, Pallas kernels: 2.53 us -> 2.54 us  [the longest x1 2.54 us: gradient_of(): pl.pallas_call(functools.partial(gradient_kernel, reps), in_specs=[pl.Blo...]
  transfers between devices with their start and end apart: 13 -> 13, of which waited for: 11 -> 10; matrix products, arithmetic and copies ran while one was open for 2% -> 2% of each run, Pallas kernels for 1% -> 1%
where the time goes in v12:
time: 47.6 us; the launch traced here: 47.5 us
  waiting for transfers between devices  19.9 us (42%)
  starting transfers between devices  15.9 us (33%)
  Pallas kernels  10.1 us (21%)
  between operations  0.74 us (2%)
  other arithmetic  0.7 us (1%)
    ppermute x10, waiting for transfers between devices, exchange(): arrived.append(lax.ppermute(blocks[step], axis, pairs))  16.5 us
    ppermute x10, starting transfers between devices, exchange(): arrived.append(lax.ppermute(blocks[step], axis, pairs))  13.5 us
    pallas_call x1, Pallas kernels, spectrum_of(): pl.pallas_call(spectrum_kernel, in_specs=[pl.BlockSpec(memory_space=pltpu...  4.73 us
    pallas_call x1, Pallas kernels, gradient_of(): pl.pallas_call(functools.partial(gradient_kernel, reps), in_specs=[pl.Blo...  2.54 us
    ppermute x1, waiting for transfers between devices, return_spectra(): pair = lax.ppermute(pair, ('freq', 'rep'), near)  2.07 us
    ppermute x1, starting transfers between devices, return_spectra(): pair = lax.ppermute(pair, ('freq', 'rep'), near)  1.69 us
    ppermute x1, waiting for transfers between devices, return_spectra(): last = lax.ppermute(last, ('freq', 'rep'), far)  1.3 us
    pallas_call x1, Pallas kernels, back_project(): pl.pallas_call(functools.partial(back_kernel, parts, groups, reps), in_sp...  1.2 us
  transfers between devices with their start and end apart: 13, of which 10 were waited for; matrix products, arithmetic and copies ran while one was open for 2% of the time, Pallas kernels for 1%

profile of v12, /device:TPU:0, one launch (start us, length us, event | category | flops | bytes accessed | tf_op | source)
XLA Modules:
  0.0 47.5 jit_solution(17216797090900210804)
XLA Ops:
  0.6 0.0 copy-start.3
  0.6 0.0 copy-start
  0.7 0.0 copy-start.1
  0.7 0.0 copy-start.2
  0.7 4.7 %spectrum.1 = (bf16[24,1024]{1,0:T(8,128)(2,1)S(1)}, bf16[3,2,32,128]{3,2,1,0:T(8,128)(2,1)S(1)}, bf16[3,2,32,128]{3,2,1,0:T(8,128)(2,1)S(1)}, bf16[3,2,32,128]{...) custom-call(bf16[4,32,32,1024]{3,2,1,0:T(8,128)(2,1)} %bitcast.6), custom_call_target="tpu_custom_call" | custom-call | tf_op jit(solution)/shard_map/spectrum/pallas_call | solution.py:116
  5.4 3.0 %collective-permute-start = (bf16[3,2,32,128]{3,2,1,0:T(8,128)(2,1)S(1)}, bf16[3,2,32,128]{3,2,1,0:T(8,128)(2,1)S(1)}, u32[]{:S(2)}, u32[]{:S(2)}) collective-permute-start(bf16[3,2,32,128]{3,2,1,0:T(8,128)(2,1)S(1)} %get-tuple-element.20), channel_id=1, source_target_pairs={{0,8},{8,0},{16,24},{24,16},{1,9},{9,1},{17,25},{25,17},{2,10},{10... | collective-permute-start | bytes 147464 | tf_op jit(solution)/shard_map/ppermute | solution.py:62
  8.4 1.5 %collective-permute-start.1 = (bf16[3,2,32,128]{3,2,1,0:T(8,128)(2,1)S(1)}, bf16[3,2,32,128]{3,2,1,0:T(8,128)(2,1)S(1)}, u32[]{:S(2)}, u32[]{:S(2)}) collective-permute-start(bf16[3,2,32,128]{3,2,1,0:T(8,128)(2,1)S(1)} %get-tuple-element.21), channel_id=1, source_target_pairs={{0,24},{8,16},{16,8},{24,0},{1,25},{9,17},{17,9},{25,1},{2,26},{10... | collective-permute-start | bytes 147464 | tf_op jit(solution)/shard_map/ppermute | solution.py:62
  9.9 0.0 collective-permute-start.2
  9.9 0.0 copy-done.3
  10.0 0.1 copy.7
  10.1 0.4 collective-permute-done.refs_1_
  10.5 0.1 broadcast_in_dim.2.limits_ref
  10.6 0.0 copy-done
  10.6 0.6 %project.1.own_ref = bf16[3,4,48,64]{3,2,1,0:T(8,128)(2,1)S(1)} custom-call(s32[3,4,2,1,128]{4,3,2,1,0:T(1,128)S(1)} %broadcast_in_dim.2.limits_ref, bf16[2,3,4,2,48,256]{5,4,3,2,1,0:T(8,128)(2,1)S(1)} %copy-done, bf16[3,2,32,128]{3,2,1,0:T(8,128)(2,1)S(1)} %get-tuple-element.19.refs_0_, bf16[3,2,32,128]{3,2,1,0:T(8,128)(2,1)S(1)} %collective-permute-done.refs_1_), custom_call_target="tpu_custom_call" | custom-call | flops 37748736 | bytes 1179648 | tf_op jit(solution)/shard_map/project/pallas_call | solution.py:202
  11.2 2.2 %collective-permute-done.1.refs_0_ = bf16[3,2,32,128]{3,2,1,0:T(8,128)(2,1)S(1)} collective-permute-done((bf16[3,2,32,128]{3,2,1,0:T(8,128)(2,1)S(1)}, bf16[3,2,32,128]{3,2,1,0:T(8,128)(2,1)S(1)}, u32[]{:S(2)}, u32[]{:S(2)}) %collective-permute-start.1) | collective-permute-done | bytes 49184 | tf_op jit(solution)/shard_map/ppermute | solution.py:62
  13.4 0.6 %collective-permute-done.2.refs_1_ = bf16[3,2,32,128]{3,2,1,0:T(8,128)(2,1)S(1)} collective-permute-done((bf16[3,2,32,128]{3,2,1,0:T(8,128)(2,1)S(1)}, bf16[3,2,32,128]{3,2,1,0:T(8,128)(2,1)S(1)}, u32[]{:S(2)}, u32[]{:S(2)}) %collective-permute-start.2) | collective-permute-done | bytes 49184 | tf_op jit(solution)/shard_map/ppermute | solution.py:62
  14.0 0.0 copy-done.1
  14.0 1.0 %predict.1 = (bf16[2,24,1024]{2,1,0:T(8,128)(2,1)S(1)}, bf16[2,24,1024]{2,1,0:T(8,128)(2,1)S(1)}, bf16[2,24,1024]{2,1,0:T(8,128)(2,1)S(1)}, bf16[2,24,1024]{2,1,0:T(8,128)(2,1)S(1)}) custom-call(s32[3,4,2,1,128]{4,3,2,1,0:T(1,128)S(1)} %broadcast_in_dim.2.limits_ref, bf16[2,3,4,2,48,256]{5,4,3,2,1,0:T(8,128)(2,1)S(1)} %copy-done, ...), custom_call_target="tpu_custom_call" | custom-call | flops 150994944 | bytes 2359296 | tf_op jit(solution)/shard_map/predict/pallas_call | solution.py:258
  15.0 3.7 %collective-permute-start.3 = (bf16[2,24,1024]{2,1,0:T(8,128)(2,1)S(1)}, bf16[2,24,1024]{2,1,0:T(8,128)(2,1)S(1)}, u32[]{:S(2)}, u32[]{:S(2)}) collective-permute-start(bf16[2,24,1024]{2,1,0:T(8,128)(2,1)S(1)} %get-tuple-element.23), channel_id=1, source_target_pairs={{0,6},{2,4},{4,2},{6,0},{1,7},{3,5},{5,3},{7,1},{8,14},{10,12},{12... | collective-permute-start | bytes 294920 | tf_op jit(solution)/shard_map/ppermute | solution.py:62
  18.7 0.0 collective-permute-start.4
  18.7 0.8 %collective-permute-start.5 = (bf16[2,24,1024]{2,1,0:T(8,128)(2,1)S(1)}, bf16[2,24,1024]{2,1,0:T(8,128)(2,1)S(1)}, u32[]{:S(2)}, u32[]{:S(2)}) collective-permute-start(bf16[2,24,1024]{2,1,0:T(8,128)(2,1)S(1)} %get-tuple-element.25), channel_id=1, source_target_pairs={{0,2},{2,0},{4,6},{6,4},{1,3},{3,1},{5,7},{7,5},{8,10},{10,8},{12,... | collective-permute-start | bytes 294920 | tf_op jit(solution)/shard_map/ppermute | solution.py:62
  19.4 2.2 %collective-permute-done.3.refs_0_ = bf16[2,24,1024]{2,1,0:T(8,128)(2,1)S(1)} collective-permute-done((bf16[2,24,1024]{2,1,0:T(8,128)(2,1)S(1)}, bf16[2,24,1024]{2,1,0:T(8,128)(2,1)S(1)}, u32[]{:S(2)}, u32[]{:S(2)}) %collective-permute-start.3) | collective-permute-done | bytes 98336 | tf_op jit(solution)/shard_map/ppermute | solution.py:62
  21.6 4.1 %collective-permute-done.4.refs_1_ = bf16[2,24,1024]{2,1,0:T(8,128)(2,1)S(1)} collective-permute-done((bf16[2,24,1024]{2,1,0:T(8,128)(2,1)S(1)}, bf16[2,24,1024]{2,1,0:T(8,128)(2,1)S(1)}, u32[]{:S(2)}, u32[]{:S(2)}) %collective-permute-start.4) | collective-permute-done | bytes 98336 | tf_op jit(solution)/shard_map/ppermute | solution.py:62
  25.7 0.0 collective-permute-done.5.refs_2_
  25.7 0.0 copy-done.2
  25.7 0.1 residual.1
  25.8 2.5 %collective-permute-start.8 = (bf16[2,24,1024]{2,1,0:T(8,128)(2,1)S(1)}, bf16[2,24,1024]{2,1,0:T(8,128)(2,1)S(1)}, u32[]{:S(2)}, u32[]{:S(2)}) collective-permute-start(bf16[2,24,1024]{2,1,0:T(8,128)(2,1)S(1)} %get-tuple-element.30.refs_0_), channel_id=1, source_target_pairs={{0,6},{2,4},{4,2},{6,0},{1,7},{3,5},{5,3},{7,1},{8,14},{10,12},{12... | collective-permute-start | bytes 294920 | tf_op jit(solution)/shard_map/ppermute | solution.py:62
  28.3 0.0 collective-permute-start.7
  28.3 1.9 %collective-permute-start.6 = (bf16[2,24,1024]{2,1,0:T(8,128)(2,1)S(1)}, bf16[2,24,1024]{2,1,0:T(8,128)(2,1)S(1)}, u32[]{:S(2)}, u32[]{:S(2)}) collective-permute-start(bf16[2,24,1024]{2,1,0:T(8,128)(2,1)S(1)} %get-tuple-element.30.refs_0_), channel_id=1, source_target_pairs={{0,2},{2,0},{4,6},{6,4},{1,3},{3,1},{5,7},{7,5},{8,10},{10,8},{12,... | collective-permute-start | bytes 294920 | tf_op jit(solution)/shard_map/ppermute | solution.py:62
  30.2 3.1 %collective-permute-done.8.refs_3_ = bf16[2,24,1024]{2,1,0:T(8,128)(2,1)S(1)} collective-permute-done((bf16[2,24,1024]{2,1,0:T(8,128)(2,1)S(1)}, bf16[2,24,1024]{2,1,0:T(8,128)(2,1)S(1)}, u32[]{:S(2)}, u32[]{:S(2)}) %collective-permute-start.8) | collective-permute-done | bytes 98336 | tf_op jit(solution)/shard_map/ppermute | solution.py:62
  33.4 2.5 %collective-permute-done.7.refs_2_ = bf16[2,24,1024]{2,1,0:T(8,128)(2,1)S(1)} collective-permute-done((bf16[2,24,1024]{2,1,0:T(8,128)(2,1)S(1)}, bf16[2,24,1024]{2,1,0:T(8,128)(2,1)S(1)}, u32[]{:S(2)}, u32[]{:S(2)}) %collective-permute-start.7) | collective-permute-done | bytes 98336 | tf_op jit(solution)/shard_map/ppermute | solution.py:62
  35.9 0.0 collective-permute-done.6.refs_1_
  35.9 1.2 %back_project.1 = (bf16[4,3,2,16,128]{4,3,2,1,0:T(8,128)(2,1)S(1)}, bf16[4,3,2,16,128]{4,3,2,1,0:T(8,128)(2,1)S(1)}) custom-call(s32[3,4,2,1,128]{4,3,2,1,0:T(1,128)S(1)} %broadcast_in_dim.2.limits_ref, bf16[2,3,4,2,48,256]{5,4,3,2,1,0:T(8,128)(2,1)S(1)} %copy-done, bf16[2,3,4,2,48,256]{5,4,3,2,1,0:T(8,128)(2,1)S(1)} %copy-done.1, ...), custom_call_target="tpu_custom_call" | custom-call | flops 150994944 | bytes 2359296 | tf_op jit(solution)/shard_map/back_project/pallas_call | solution.py:369
  37.1 0.1 collective-permute-start.9
  37.2 1.3 %collective-permute-done.9.refs_1_ = bf16[4,3,2,16,128]{4,3,2,1,0:T(8,128)(2,1)S(1)} collective-permute-done((bf16[4,3,2,16,128]{4,3,2,1,0:T(8,128)(2,1)S(1)}, bf16[4,3,2,16,128]{4,3,2,1,0:T(8,128)(2,1)S(1)}, u32[]{:S(2)}, u32[]{:S(2)}) %collective-permute-start.9) | collective-permute-done | bytes 98336 | tf_op jit(solution)/shard_map/ppermute | solution.py:62
  38.5 1.7 %collective-permute-start.11 = (bf16[2,3,2,16,128]{4,3,2,1,0:T(8,128)(2,1)S(1)}, bf16[2,3,2,16,128]{4,3,2,1,0:T(8,128)(2,1)S(1)}, u32[]{:S(2)}, u32[]{:S(2)}) collective-permute-start(bf16[2,3,2,16,128]{4,3,2,1,0:T(8,128)(2,1)S(1)} %get-tuple-element.34), channel_id=1, source_target_pairs={{0,8},{1,17},{8,0},{9,25},{16,24},{17,1},{24,16},{25,9},{2,10},{3,... | collective-permute-start | bytes 147464 | tf_op jit(solution)/shard_map/ppermute | solution.py:430
  40.2 0.7 %collective-permute-start.10 = (bf16[1,3,2,16,128]{4,3,2,1,0:T(8,128)(2,1)S(1)}, bf16[1,3,2,16,128]{4,3,2,1,0:T(8,128)(2,1)S(1)}, u32[]{:S(2)}, u32[]{:S(2)}) collective-permute-start(bf16[1,3,2,16,128]{4,3,2,1,0:T(8,128)(2,1)S(1)} %get-tuple-element.33), channel_id=1, source_target_pairs={{0,24},{1,25},{8,16},{9,17},{16,8},{17,9},{24,0},{25,1},{2,26},{3,... | collective-permute-start | bytes 73736 | tf_op jit(solution)/shard_map/ppermute | solution.py:431
  40.8 2.1 %collective-permute-done.11.pair_ref.refs_2_ = bf16[2,3,2,16,128]{4,3,2,1,0:T(8,128)(2,1)S(1)} collective-permute-done((bf16[2,3,2,16,128]{4,3,2,1,0:T(8,128)(2,1)S(1)}, bf16[2,3,2,16,128]{4,3,2,1,0:T(8,128)(2,1)S(1)}, u32[]{:S(2)}, u32[]{:S(2)}) %collective-permute-start.11) | collective-permute-done | bytes 49184 | tf_op jit(solution)/shard_map/ppermute | solution.py:430
  42.9 0.0 collective-permute-start.12
  42.9 0.7 %pad_maximum_fusion = f32[2,24,1024]{2,1,0:T(8,128)} fusion(f32[1,24,1024]{2,1,0:T(8,128)S(1)} %bitcast.5, f32[1,24,1024]{2,1,0:T(8,128)S(1)} %bitcast.4), kind=kLoop, calls=%fused_computation | loop fusion | flops 49152 | bytes 393216 | tf_op jit(solution)/shard_map/stack | solution.py:518
  43.6 1.3 %collective-permute-done.10.refs_0_ = bf16[1,3,2,16,128]{4,3,2,1,0:T(8,128)(2,1)S(1)} collective-permute-done((bf16[1,3,2,16,128]{4,3,2,1,0:T(8,128)(2,1)S(1)}, bf16[1,3,2,16,128]{4,3,2,1,0:T(8,128)(2,1)S(1)}, u32[]{:S(2)}, u32[]{:S(2)}) %collective-permute-start.10) | collective-permute-done | bytes 24608 | tf_op jit(solution)/shard_map/ppermute | solution.py:431
  44.9 0.0 collective-permute-done.12.refs_1_
  44.9 2.5 %gradient.1 = bf16[4,16,32,1024]{3,2,1,0:T(8,128)(2,1)} custom-call(bf16[24,1024]{1,0:T(8,128)(2,1)S(1)} %get-tuple-element.29.table_ref, bf16[1,3,2,16,128]{4,3,2,1,0:T(8,128)(2,1)S(1)} %collective-permute-done.10.refs_0_, bf16[1,3,2,16,128]{4,3,2,1,0:T(8,128)(2,1)S(1)} %collective-permute-done.12.refs_1_, ...), custom_call_target="tpu_custom_call" | custom-call | tf_op jit(solution)/shard_map/gradient/pallas_call | solution.py:486
  (2 shorter events, 0.0 us)
Async XLA Ops:
  0.6 9.3 %copy-start.3 = (s32[3,4,2]{1,2,0:T(2,128)S(1)}, s32[3,4,2]{1,2,0:T(2,128)}, u32[]{:S(2)}) copy-start(s32[3,4,2]{1,2,0:T(2,128)} %param.8) | copy-start | bytes 292
  0.6 9.9 %copy-start = (bf16[2,3,4,2,48,256]{5,4,3,2,1,0:T(8,128)(2,1)S(1)}, bf16[2,3,4,2,48,256]{5,4,3,2,1,0:T(8,128)(2,1)}, u32[]{:S(2)}) copy-start(bf16[2,3,4,2,48,256]{5,4,3,2,1,0:T(8,128)(2,1)} %right_ref.5) | copy-start | bytes 3538948
  0.7 13.3 %copy-start.1 = (bf16[2,3,4,2,48,256]{5,4,3,2,1,0:T(8,128)(2,1)S(1)}, bf16[2,3,4,2,48,256]{5,4,3,2,1,0:T(8,128)(2,1)}, u32[]{:S(2)}) copy-start(bf16[2,3,4,2,48,256]{5,4,3,2,1,0:T(8,128)(2,1)} %left_ref.3) | copy-start | bytes 3538948
  0.7 25.1 %copy-start.2 = (f32[2,24,1024]{2,1,0:T(8,128)S(1)}, f32[2,24,1024]{2,1,0:T(8,128)}, u32[]{:S(2)}) copy-start(f32[2,24,1024]{2,1,0:T(8,128)} %data_ref.1) | copy-start | bytes 589828
  5.4 5.1 %collective-permute-start = (bf16[3,2,32,128]{3,2,1,0:T(8,128)(2,1)S(1)}, bf16[3,2,32,128]{3,2,1,0:T(8,128)(2,1)S(1)}, u32[]{:S(2)}, u32[]{:S(2)}) collective-permute-start(bf16[3,2,32,128]{3,2,1,0:T(8,128)(2,1)S(1)} %get-tuple-element.20), channel_id=1, source_target_pairs={{0,8},{8,0},{16,24},{24,16},{1,9},{9,1},{17,25},{25,17},{2,10},{10... | collective-permute-start | bytes 147464 | tf_op jit(solution)/shard_map/ppermute | solution.py:62
  8.4 5.0 %collective-permute-start.1 = (bf16[3,2,32,128]{3,2,1,0:T(8,128)(2,1)S(1)}, bf16[3,2,32,128]{3,2,1,0:T(8,128)(2,1)S(1)}, u32[]{:S(2)}, u32[]{:S(2)}) collective-permute-start(bf16[3,2,32,128]{3,2,1,0:T(8,128)(2,1)S(1)} %get-tuple-element.21), channel_id=1, source_target_pairs={{0,24},{8,16},{16,8},{24,0},{1,25},{9,17},{17,9},{25,1},{2,26},{10... | collective-permute-start | bytes 147464 | tf_op jit(solution)/shard_map/ppermute | solution.py:62
  9.9 4.1 %collective-permute-start.2 = (bf16[3,2,32,128]{3,2,1,0:T(8,128)(2,1)S(1)}, bf16[3,2,32,128]{3,2,1,0:T(8,128)(2,1)S(1)}, u32[]{:S(2)}, u32[]{:S(2)}) collective-permute-start(bf16[3,2,32,128]{3,2,1,0:T(8,128)(2,1)S(1)} %get-tuple-element.22), channel_id=1, source_target_pairs={{0,16},{8,24},{16,0},{24,8},{1,17},{9,25},{17,1},{25,9},{2,18},{10... | collective-permute-start | bytes 147464 | tf_op jit(solution)/shard_map/ppermute | solution.py:62
  15.0 6.6 %collective-permute-start.3 = (bf16[2,24,1024]{2,1,0:T(8,128)(2,1)S(1)}, bf16[2,24,1024]{2,1,0:T(8,128)(2,1)S(1)}, u32[]{:S(2)}, u32[]{:S(2)}) collective-permute-start(bf16[2,24,1024]{2,1,0:T(8,128)(2,1)S(1)} %get-tuple-element.23), channel_id=1, source_target_pairs={{0,6},{2,4},{4,2},{6,0},{1,7},{3,5},{5,3},{7,1},{8,14},{10,12},{12... | collective-permute-start | bytes 294920 | tf_op jit(solution)/shard_map/ppermute | solution.py:62
  18.7 7.0 %collective-permute-start.4 = (bf16[2,24,1024]{2,1,0:T(8,128)(2,1)S(1)}, bf16[2,24,1024]{2,1,0:T(8,128)(2,1)S(1)}, u32[]{:S(2)}, u32[]{:S(2)}) collective-permute-start(bf16[2,24,1024]{2,1,0:T(8,128)(2,1)S(1)} %get-tuple-element.24), channel_id=1, source_target_pairs={{0,4},{2,6},{4,0},{6,2},{1,5},{3,7},{5,1},{7,3},{8,12},{10,14},{12... | collective-permute-start | bytes 294920 | tf_op jit(solution)/shard_map/ppermute | solution.py:62
  18.7 7.0 %collective-permute-start.5 = (bf16[2,24,1024]{2,1,0:T(8,128)(2,1)S(1)}, bf16[2,24,1024]{2,1,0:T(8,128)(2,1)S(1)}, u32[]{:S(2)}, u32[]{:S(2)}) collective-permute-start(bf16[2,24,1024]{2,1,0:T(8,128)(2,1)S(1)} %get-tuple-element.25), channel_id=1, source_target_pairs={{0,2},{2,0},{4,6},{6,4},{1,3},{3,1},{5,7},{7,5},{8,10},{10,8},{12,... | collective-permute-start | bytes 294920 | tf_op jit(solution)/shard_map/ppermute | solution.py:62
  25.8 7.6 %collective-permute-start.8 = (bf16[2,24,1024]{2,1,0:T(8,128)(2,1)S(1)}, bf16[2,24,1024]{2,1,0:T(8,128)(2,1)S(1)}, u32[]{:S(2)}, u32[]{:S(2)}) collective-permute-start(bf16[2,24,1024]{2,1,0:T(8,128)(2,1)S(1)} %get-tuple-element.30.refs_0_), channel_id=1, source_target_pairs={{0,6},{2,4},{4,2},{6,0},{1,7},{3,5},{5,3},{7,1},{8,14},{10,12},{12... | collective-permute-start | bytes 294920 | tf_op jit(solution)/shard_map/ppermute | solution.py:62
  28.3 7.6 %collective-permute-start.7 = (bf16[2,24,1024]{2,1,0:T(8,128)(2,1)S(1)}, bf16[2,24,1024]{2,1,0:T(8,128)(2,1)S(1)}, u32[]{:S(2)}, u32[]{:S(2)}) collective-permute-start(bf16[2,24,1024]{2,1,0:T(8,128)(2,1)S(1)} %get-tuple-element.30.refs_0_), channel_id=1, source_target_pairs={{0,4},{2,6},{4,0},{6,2},{1,5},{3,7},{5,1},{7,3},{8,12},{10,14},{12... | collective-permute-start | bytes 294920 | tf_op jit(solution)/shard_map/ppermute | solution.py:62
  28.3 7.6 %collective-permute-start.6 = (bf16[2,24,1024]{2,1,0:T(8,128)(2,1)S(1)}, bf16[2,24,1024]{2,1,0:T(8,128)(2,1)S(1)}, u32[]{:S(2)}, u32[]{:S(2)}) collective-permute-start(bf16[2,24,1024]{2,1,0:T(8,128)(2,1)S(1)} %get-tuple-element.30.refs_0_), channel_id=1, source_target_pairs={{0,2},{2,0},{4,6},{6,4},{1,3},{3,1},{5,7},{7,5},{8,10},{10,8},{12,... | collective-permute-start | bytes 294920 | tf_op jit(solution)/shard_map/ppermute | solution.py:62
  37.1 1.4 %collective-permute-start.9 = (bf16[4,3,2,16,128]{4,3,2,1,0:T(8,128)(2,1)S(1)}, bf16[4,3,2,16,128]{4,3,2,1,0:T(8,128)(2,1)S(1)}, u32[]{:S(2)}, u32[]{:S(2)}) collective-permute-start(bf16[4,3,2,16,128]{4,3,2,1,0:T(8,128)(2,1)S(1)} %get-tuple-element.32), channel_id=1, source_target_pairs={{0,1},{1,0},{2,3},{3,2},{4,5},{5,4},{6,7},{7,6},{8,9},{9,8},{10,11... | collective-permute-start | bytes 294920 | tf_op jit(solution)/shard_map/ppermute | solution.py:62
  38.5 4.4 %collective-permute-start.11 = (bf16[2,3,2,16,128]{4,3,2,1,0:T(8,128)(2,1)S(1)}, bf16[2,3,2,16,128]{4,3,2,1,0:T(8,128)(2,1)S(1)}, u32[]{:S(2)}, u32[]{:S(2)}) collective-permute-start(bf16[2,3,2,16,128]{4,3,2,1,0:T(8,128)(2,1)S(1)} %get-tuple-element.34), channel_id=1, source_target_pairs={{0,8},{1,17},{8,0},{9,25},{16,24},{17,1},{24,16},{25,9},{2,10},{3,... | collective-permute-start | bytes 147464 | tf_op jit(solution)/shard_map/ppermute | solution.py:430
  40.2 4.7 %collective-permute-start.10 = (bf16[1,3,2,16,128]{4,3,2,1,0:T(8,128)(2,1)S(1)}, bf16[1,3,2,16,128]{4,3,2,1,0:T(8,128)(2,1)S(1)}, u32[]{:S(2)}, u32[]{:S(2)}) collective-permute-start(bf16[1,3,2,16,128]{4,3,2,1,0:T(8,128)(2,1)S(1)} %get-tuple-element.33), channel_id=1, source_target_pairs={{0,24},{1,25},{8,16},{9,17},{16,8},{17,9},{24,0},{25,1},{2,26},{3,... | collective-permute-start | bytes 73736 | tf_op jit(solution)/shard_map/ppermute | solution.py:431
  42.9 2.0 %collective-permute-start.12 = (bf16[1,3,2,16,128]{4,3,2,1,0:T(8,128)(2,1)S(1)}, bf16[1,3,2,16,128]{4,3,2,1,0:T(8,128)(2,1)S(1)}, u32[]{:S(2)}, u32[]{:S(2)}) collective-permute-start(bf16[1,3,2,16,128]{4,3,2,1,0:T(8,128)(2,1)S(1)} %other.1), channel_id=1, source_target_pairs={{0,1},{1,0},{2,3},{3,2},{4,5},{5,4},{6,7},{7,6},{8,9},{9,8},{10,11... | collective-permute-start | bytes 73736 | tf_op jit(solution)/shard_map/ppermute | solution.py:432

commit v13 on v12

--- a/solution.py
+++ b/solution.py
@@ -63,6 +63,12 @@
     return [blocks[0]] + arrived[::-1]
 
 
+def ramp(count):
+    step = max(count // 4, 1)
+    cuts = [0] + list(range(step // 2 or step, count, step)) + [count]
+    return [(start, end - start) for start, end in zip(cuts, cuts[1:])]
+
+
 def shared_steps(groups, reps):
     return groups == 4 and reps == 2
 
@@ -74,11 +80,10 @@
     dests = len(out_refs)
     freqs, _, _, lanes = out_refs[0].shape
     bins = 2 * dests * freqs
-    chunks = model_sems.shape[0]
-    part = low // chunks
+    chunks = ramp(low)
     copies = []
-    for at in range(chunks):
-        rows = pl.ds(at * part, part)
+    for at, (start, length_of) in enumerate(chunks):
+        rows = pl.ds(start, length_of)
         copies.append(
             pltpu.make_async_copy(
                 model_hbm.at[:, rows], model_ref.at[:, rows], model_sems.at[at]
@@ -87,10 +92,10 @@
         copies[-1].start()
     table = tables(bins, length)
     table_out_ref[...] = table
-    for at in range(chunks):
-        copies[at].wait()
-        for start in range(at * part, (at + 1) * part, 2):
-            width = min(2, (at + 1) * part - start)
+    for copy, (begin, length_of) in zip(copies, chunks):
+        copy.wait()
+        for start in range(begin, begin + length_of, 2):
+            width = min(2, begin + length_of - start)
             block = jnp.concatenate(
                 [model_ref[:, start + row].reshape(lanes, length) for row in range(width)]
             )
@@ -111,7 +116,7 @@
     traces, rhs, length = model.shape
     high = LANES // rhs
     low = traces // high
-    chunks = math.gcd(low, 4)
+    chunks = len(ramp(low))
     bins = 2 * dests * freqs
     table, *blocks = pl.pallas_call(
         spectrum_kernel,
@@ -136,6 +141,26 @@
         bytes_accessed=count * 2 * 4 * size * tile,
         transcendentals=0,
     )
+
+
+def limits_kernel(ranks_ref, table_ref, out_ref):
+    freqs, row_tiles, col_tiles = ranks_ref.shape
+    for f in range(freqs):
+        for i in range(row_tiles):
+            for j in range(col_tiles):
+                rank = ranks_ref[f, i : i + 1, j : j + 1]
+                out_ref[f, i, j] = jnp.broadcast_to(rank, (1, LANES))
+
+
+def limits_of(ranks, table):
+    return pl.pallas_call(
+        limits_kernel,
+        in_specs=[pl.BlockSpec(memory_space=pltpu.VMEM)] * 2,
+        out_specs=pl.BlockSpec(memory_space=pltpu.VMEM),
+        out_shape=jax.ShapeDtypeStruct(ranks.shape + (1, LANES), jnp.int32),
+        compiler_params=pltpu.CompilerParams(vmem_limit_bytes=VMEM_LIMIT),
+        name="limits",
+    )(ranks, table)
 
 
 def masked(product, limits_ref, places, size):
@@ -439,8 +464,6 @@
     _, freqs, _, low, lanes = part_refs[0].shape
     high, _, rhs, length = out_ref.shape
     bins = table_ref.shape[0]
-    chunks = out_sems.shape[0]
-    part = low // chunks
     me = lax.axis_index("freq")
     if shared_steps(groups, reps):
         core = lax.axis_index("rep")
@@ -456,19 +479,19 @@
     table = table_ref[...]
     width = math.gcd(length, 256)
     copies = []
-    for at in range(chunks):
+    for at, (start, part) in enumerate(ramp(low)):
         coefficients = jnp.concatenate(
-            [rows_ref[row * bins : (row + 1) * bins] for row in range(at * part, (at + 1) * part)],
+            [rows_ref[row * bins : (row + 1) * bins] for row in range(start, start + part)],
             axis=1,
         ).astype(jnp.bfloat16)
         for column in range(0, length, width):
             columns = slice(column, column + width)
             traces = dot(coefficients, table[:, columns], 0, 0).astype(out_ref.dtype)
             for row in range(part):
-                out_ref[:, at * part + row, :, columns] = traces[
+                out_ref[:, start + row, :, columns] = traces[
                     row * lanes : (row + 1) * lanes
                 ].reshape(high, rhs, width)
-        rows = pl.ds(at * part, part)
+        rows = pl.ds(start, part)
         copies.append(
             pltpu.make_async_copy(out_ref.at[:, rows], out_hbm.at[:, rows], out_sems.at[at])
         )
@@ -481,7 +504,7 @@
     _, _, _, low, lanes = parts[0].shape
     bins, length = table.shape
     high = lanes // rhs
-    chunks = math.gcd(low, 4)
+    chunks = len(ramp(low))
     shape = (high, low, rhs, length)
     out = pl.pallas_call(
         functools.partial(gradient_kernel, reps),
@@ -507,7 +530,7 @@
     rhs_count = model.shape[2]
     table, spectrum = spectrum_of(model[0], freq_count, freq_local)
     spectrum = exchange(spectrum, "freq")
-    limits = jnp.broadcast_to(ranks[..., None, None], ranks.shape + (1, LANES))
+    limits = limits_of(ranks, table)
     per_tile = freq_count // green_right.shape[3]
     own = project(limits, spectrum[:per_tile], green_right)
     predicted = predict(limits, own, spectrum[per_tile:], green_right, green_left, tile_count)

time: 47.6 us -> 47.6 us (level)
  no operation moved by 1% of the time
where the time goes in v13:
time: 47.6 us; the launch traced here: 47.5 us
  waiting for transfers between devices  19.8 us (42%)
  starting transfers between devices  15.9 us (33%)
  Pallas kernels  10.2 us (21%)
  between operations  0.73 us (2%)
  other arithmetic  0.7 us (1%)
    ppermute x10, waiting for transfers between devices, exchange(): arrived.append(lax.ppermute(blocks[step], axis, pairs))  16.5 us
    ppermute x10, starting transfers between devices, exchange(): arrived.append(lax.ppermute(blocks[step], axis, pairs))  13.5 us
    pallas_call x1, Pallas kernels, spectrum_of(): pl.pallas_call(spectrum_kernel, in_specs=[pl.BlockSpec(memory_space=pltpu...  4.75 us
    pallas_call x1, Pallas kernels, gradient_of(): pl.pallas_call(functools.partial(gradient_kernel, reps), in_specs=[pl.Blo...  2.51 us
    ppermute x1, waiting for transfers between devices, return_spectra(): pair = lax.ppermute(pair, ('freq', 'rep'), near)  2.06 us
    ppermute x1, starting transfers between devices, return_spectra(): pair = lax.ppermute(pair, ('freq', 'rep'), near)  1.7 us
    ppermute x1, waiting for transfers between devices, return_spectra(): last = lax.ppermute(last, ('freq', 'rep'), far)  1.31 us
    pallas_call x1, Pallas kernels, back_project(): pl.pallas_call(functools.partial(back_kernel, parts, groups, reps), in_sp...  1.2 us
  transfers between devices with their start and end apart: 13, of which 10 were waited for; matrix products, arithmetic and copies ran while one was open for 2% of the time, Pallas kernels for 1%

profile of v13, /device:TPU:0, one launch (start us, length us, event | category | flops | bytes accessed | tf_op | source)
XLA Modules:
  0.0 47.5 jit_solution(18338476257616375548)
XLA Ops:
  0.6 0.0 copy-start.3
  0.6 0.0 copy-start
  0.7 0.0 copy-start.1
  0.7 0.0 copy-start.2
  0.7 4.7 %spectrum.1 = (bf16[24,1024]{1,0:T(8,128)(2,1)S(1)}, bf16[3,2,32,128]{3,2,1,0:T(8,128)(2,1)S(1)}, bf16[3,2,32,128]{3,2,1,0:T(8,128)(2,1)S(1)}, bf16[3,2,32,128]{...) custom-call(bf16[4,32,32,1024]{3,2,1,0:T(8,128)(2,1)} %bitcast.6), custom_call_target="tpu_custom_call" | custom-call | tf_op jit(solution)/shard_map/spectrum/pallas_call | solution.py:121
  5.4 3.0 %collective-permute-start = (bf16[3,2,32,128]{3,2,1,0:T(8,128)(2,1)S(1)}, bf16[3,2,32,128]{3,2,1,0:T(8,128)(2,1)S(1)}, u32[]{:S(2)}, u32[]{:S(2)}) collective-permute-start(bf16[3,2,32,128]{3,2,1,0:T(8,128)(2,1)S(1)} %get-tuple-element.21), channel_id=1, source_target_pairs={{0,8},{8,0},{16,24},{24,16},{1,9},{9,1},{17,25},{25,17},{2,10},{10... | collective-permute-start | bytes 147464 | tf_op jit(solution)/shard_map/ppermute | solution.py:62
  8.4 1.5 %collective-permute-start.1 = (bf16[3,2,32,128]{3,2,1,0:T(8,128)(2,1)S(1)}, bf16[3,2,32,128]{3,2,1,0:T(8,128)(2,1)S(1)}, u32[]{:S(2)}, u32[]{:S(2)}) collective-permute-start(bf16[3,2,32,128]{3,2,1,0:T(8,128)(2,1)S(1)} %get-tuple-element.22), channel_id=1, source_target_pairs={{0,24},{8,16},{16,8},{24,0},{1,25},{9,17},{17,9},{25,1},{2,26},{10... | collective-permute-start | bytes 147464 | tf_op jit(solution)/shard_map/ppermute | solution.py:62
  9.9 0.0 collective-permute-start.2
  10.0 0.0 copy-done.3
  10.0 0.1 copy.7.ranks_ref
  10.1 0.1 limits.1.limits_ref
  10.2 0.3 collective-permute-done.refs_1_
  10.5 0.0 copy-done
  10.5 0.6 %project.1.own_ref = bf16[3,4,48,64]{3,2,1,0:T(8,128)(2,1)S(1)} custom-call(s32[3,4,2,1,128]{4,3,2,1,0:T(1,128)S(1)} %limits.1.limits_ref, bf16[2,3,4,2,48,256]{5,4,3,2,1,0:T(8,128)(2,1)S(1)} %copy-done, bf16[3,2,32,128]{3,2,1,0:T(8,128)(2,1)S(1)} %get-tuple-element.20.refs_0_, bf16[3,2,32,128]{3,2,1,0:T(8,128)(2,1)S(1)} %collective-permute-done.refs_1_), custom_call_target="tpu_custom_call" | custom-call | flops 37748736 | bytes 1179648 | tf_op jit(solution)/shard_map/project/pallas_call | solution.py:227
  11.1 2.3 %collective-permute-done.1.refs_0_ = bf16[3,2,32,128]{3,2,1,0:T(8,128)(2,1)S(1)} collective-permute-done((bf16[3,2,32,128]{3,2,1,0:T(8,128)(2,1)S(1)}, bf16[3,2,32,128]{3,2,1,0:T(8,128)(2,1)S(1)}, u32[]{:S(2)}, u32[]{:S(2)}) %collective-permute-start.1) | collective-permute-done | bytes 49184 | tf_op jit(solution)/shard_map/ppermute | solution.py:62
  13.4 0.6 %collective-permute-done.2.refs_1_ = bf16[3,2,32,128]{3,2,1,0:T(8,128)(2,1)S(1)} collective-permute-done((bf16[3,2,32,128]{3,2,1,0:T(8,128)(2,1)S(1)}, bf16[3,2,32,128]{3,2,1,0:T(8,128)(2,1)S(1)}, u32[]{:S(2)}, u32[]{:S(2)}) %collective-permute-start.2) | collective-permute-done | bytes 49184 | tf_op jit(solution)/shard_map/ppermute | solution.py:62
  14.0 0.0 copy-done.1
  14.0 1.0 %predict.1 = (bf16[2,24,1024]{2,1,0:T(8,128)(2,1)S(1)}, bf16[2,24,1024]{2,1,0:T(8,128)(2,1)S(1)}, bf16[2,24,1024]{2,1,0:T(8,128)(2,1)S(1)}, bf16[2,24,1024]{2,1,0:T(8,128)(2,1)S(1)}) custom-call(s32[3,4,2,1,128]{4,3,2,1,0:T(1,128)S(1)} %limits.1.limits_ref, bf16[2,3,4,2,48,256]{5,4,3,2,1,0:T(8,128)(2,1)S(1)} %copy-done, ...), custom_call_target="tpu_custom_call" | custom-call | flops 150994944 | bytes 2359296 | tf_op jit(solution)/shard_map/predict/pallas_call | solution.py:283
  15.0 3.7 %collective-permute-start.3 = (bf16[2,24,1024]{2,1,0:T(8,128)(2,1)S(1)}, bf16[2,24,1024]{2,1,0:T(8,128)(2,1)S(1)}, u32[]{:S(2)}, u32[]{:S(2)}) collective-permute-start(bf16[2,24,1024]{2,1,0:T(8,128)(2,1)S(1)} %get-tuple-element.24), channel_id=1, source_target_pairs={{0,6},{2,4},{4,2},{6,0},{1,7},{3,5},{5,3},{7,1},{8,14},{10,12},{12... | collective-permute-start | bytes 294920 | tf_op jit(solution)/shard_map/ppermute | solution.py:62
  18.7 0.0 collective-permute-start.4
  18.7 0.8 %collective-permute-start.5 = (bf16[2,24,1024]{2,1,0:T(8,128)(2,1)S(1)}, bf16[2,24,1024]{2,1,0:T(8,128)(2,1)S(1)}, u32[]{:S(2)}, u32[]{:S(2)}) collective-permute-start(bf16[2,24,1024]{2,1,0:T(8,128)(2,1)S(1)} %get-tuple-element.26), channel_id=1, source_target_pairs={{0,2},{2,0},{4,6},{6,4},{1,3},{3,1},{5,7},{7,5},{8,10},{10,8},{12,... | collective-permute-start | bytes 294920 | tf_op jit(solution)/shard_map/ppermute | solution.py:62
  19.5 2.1 %collective-permute-done.3.refs_0_ = bf16[2,24,1024]{2,1,0:T(8,128)(2,1)S(1)} collective-permute-done((bf16[2,24,1024]{2,1,0:T(8,128)(2,1)S(1)}, bf16[2,24,1024]{2,1,0:T(8,128)(2,1)S(1)}, u32[]{:S(2)}, u32[]{:S(2)}) %collective-permute-start.3) | collective-permute-done | bytes 98336 | tf_op jit(solution)/shard_map/ppermute | solution.py:62
  21.6 4.1 %collective-permute-done.4.refs_1_ = bf16[2,24,1024]{2,1,0:T(8,128)(2,1)S(1)} collective-permute-done((bf16[2,24,1024]{2,1,0:T(8,128)(2,1)S(1)}, bf16[2,24,1024]{2,1,0:T(8,128)(2,1)S(1)}, u32[]{:S(2)}, u32[]{:S(2)}) %collective-permute-start.4) | collective-permute-done | bytes 98336 | tf_op jit(solution)/shard_map/ppermute | solution.py:62
  25.7 0.0 collective-permute-done.5.refs_2_
  25.7 0.0 copy-done.2
  25.7 0.1 residual.1
  25.8 2.5 %collective-permute-start.8 = (bf16[2,24,1024]{2,1,0:T(8,128)(2,1)S(1)}, bf16[2,24,1024]{2,1,0:T(8,128)(2,1)S(1)}, u32[]{:S(2)}, u32[]{:S(2)}) collective-permute-start(bf16[2,24,1024]{2,1,0:T(8,128)(2,1)S(1)} %get-tuple-element.30.refs_0_), channel_id=1, source_target_pairs={{0,6},{2,4},{4,2},{6,0},{1,7},{3,5},{5,3},{7,1},{8,14},{10,12},{12... | collective-permute-start | bytes 294920 | tf_op jit(solution)/shard_map/ppermute | solution.py:62
  28.3 0.0 collective-permute-start.7
  28.3 1.9 %collective-permute-start.6 = (bf16[2,24,1024]{2,1,0:T(8,128)(2,1)S(1)}, bf16[2,24,1024]{2,1,0:T(8,128)(2,1)S(1)}, u32[]{:S(2)}, u32[]{:S(2)}) collective-permute-start(bf16[2,24,1024]{2,1,0:T(8,128)(2,1)S(1)} %get-tuple-element.30.refs_0_), channel_id=1, source_target_pairs={{0,2},{2,0},{4,6},{6,4},{1,3},{3,1},{5,7},{7,5},{8,10},{10,8},{12,... | collective-permute-start | bytes 294920 | tf_op jit(solution)/shard_map/ppermute | solution.py:62
  30.3 3.1 %collective-permute-done.8.refs_3_ = bf16[2,24,1024]{2,1,0:T(8,128)(2,1)S(1)} collective-permute-done((bf16[2,24,1024]{2,1,0:T(8,128)(2,1)S(1)}, bf16[2,24,1024]{2,1,0:T(8,128)(2,1)S(1)}, u32[]{:S(2)}, u32[]{:S(2)}) %collective-permute-start.8) | collective-permute-done | bytes 98336 | tf_op jit(solution)/shard_map/ppermute | solution.py:62
  33.4 2.5 %collective-permute-done.7.refs_2_ = bf16[2,24,1024]{2,1,0:T(8,128)(2,1)S(1)} collective-permute-done((bf16[2,24,1024]{2,1,0:T(8,128)(2,1)S(1)}, bf16[2,24,1024]{2,1,0:T(8,128)(2,1)S(1)}, u32[]{:S(2)}, u32[]{:S(2)}) %collective-permute-start.7) | collective-permute-done | bytes 98336 | tf_op jit(solution)/shard_map/ppermute | solution.py:62
  35.9 0.0 collective-permute-done.6.refs_1_
  35.9 1.2 %back_project.1 = (bf16[4,3,2,16,128]{4,3,2,1,0:T(8,128)(2,1)S(1)}, bf16[4,3,2,16,128]{4,3,2,1,0:T(8,128)(2,1)S(1)}) custom-call(s32[3,4,2,1,128]{4,3,2,1,0:T(1,128)S(1)} %limits.1.limits_ref, bf16[2,3,4,2,48,256]{5,4,3,2,1,0:T(8,128)(2,1)S(1)} %copy-done, bf16[2,3,4,2,48,256]{5,4,3,2,1,0:T(8,128)(2,1)S(1)} %copy-done.1, ...), custom_call_target="tpu_custom_call" | custom-call | flops 150994944 | bytes 2359296 | tf_op jit(solution)/shard_map/back_project/pallas_call | solution.py:394
  37.1 0.1 collective-permute-start.9
  37.2 1.3 %collective-permute-done.9.refs_1_ = bf16[4,3,2,16,128]{4,3,2,1,0:T(8,128)(2,1)S(1)} collective-permute-done((bf16[4,3,2,16,128]{4,3,2,1,0:T(8,128)(2,1)S(1)}, bf16[4,3,2,16,128]{4,3,2,1,0:T(8,128)(2,1)S(1)}, u32[]{:S(2)}, u32[]{:S(2)}) %collective-permute-start.9) | collective-permute-done | bytes 98336 | tf_op jit(solution)/shard_map/ppermute | solution.py:62
  38.5 1.7 %collective-permute-start.11 = (bf16[2,3,2,16,128]{4,3,2,1,0:T(8,128)(2,1)S(1)}, bf16[2,3,2,16,128]{4,3,2,1,0:T(8,128)(2,1)S(1)}, u32[]{:S(2)}, u32[]{:S(2)}) collective-permute-start(bf16[2,3,2,16,128]{4,3,2,1,0:T(8,128)(2,1)S(1)} %get-tuple-element.34), channel_id=1, source_target_pairs={{0,8},{1,17},{8,0},{9,25},{16,24},{17,1},{24,16},{25,9},{2,10},{3,... | collective-permute-start | bytes 147464 | tf_op jit(solution)/shard_map/ppermute | solution.py:455
  40.2 0.7 %collective-permute-start.10 = (bf16[1,3,2,16,128]{4,3,2,1,0:T(8,128)(2,1)S(1)}, bf16[1,3,2,16,128]{4,3,2,1,0:T(8,128)(2,1)S(1)}, u32[]{:S(2)}, u32[]{:S(2)}) collective-permute-start(bf16[1,3,2,16,128]{4,3,2,1,0:T(8,128)(2,1)S(1)} %get-tuple-element.33), channel_id=1, source_target_pairs={{0,24},{1,25},{8,16},{9,17},{16,8},{17,9},{24,0},{25,1},{2,26},{3,... | collective-permute-start | bytes 73736 | tf_op jit(solution)/shard_map/ppermute | solution.py:456
  40.9 2.1 %collective-permute-done.11.pair_ref.refs_2_ = bf16[2,3,2,16,128]{4,3,2,1,0:T(8,128)(2,1)S(1)} collective-permute-done((bf16[2,3,2,16,128]{4,3,2,1,0:T(8,128)(2,1)S(1)}, bf16[2,3,2,16,128]{4,3,2,1,0:T(8,128)(2,1)S(1)}, u32[]{:S(2)}, u32[]{:S(2)}) %collective-permute-start.11) | collective-permute-done | bytes 49184 | tf_op jit(solution)/shard_map/ppermute | solution.py:455
  42.9 0.0 collective-permute-start.12
  42.9 0.7 %pad_maximum_fusion = f32[2,24,1024]{2,1,0:T(8,128)} fusion(f32[1,24,1024]{2,1,0:T(8,128)S(1)} %bitcast.5, f32[1,24,1024]{2,1,0:T(8,128)S(1)} %bitcast.4), kind=kLoop, calls=%fused_computation | loop fusion | flops 49152 | bytes 393216 | tf_op jit(solution)/shard_map/stack | solution.py:541
  43.6 1.3 %collective-permute-done.10.refs_0_ = bf16[1,3,2,16,128]{4,3,2,1,0:T(8,128)(2,1)S(1)} collective-permute-done((bf16[1,3,2,16,128]{4,3,2,1,0:T(8,128)(2,1)S(1)}, bf16[1,3,2,16,128]{4,3,2,1,0:T(8,128)(2,1)S(1)}, u32[]{:S(2)}, u32[]{:S(2)}) %collective-permute-start.10) | collective-permute-done | bytes 24608 | tf_op jit(solution)/shard_map/ppermute | solution.py:456
  44.9 0.0 collective-permute-done.12.refs_1_
  44.9 2.5 %gradient.1 = bf16[4,16,32,1024]{3,2,1,0:T(8,128)(2,1)} custom-call(bf16[24,1024]{1,0:T(8,128)(2,1)S(1)} %get-tuple-element.19.table_ref, bf16[1,3,2,16,128]{4,3,2,1,0:T(8,128)(2,1)S(1)} %collective-permute-done.10.refs_0_, bf16[1,3,2,16,128]{4,3,2,1,0:T(8,128)(2,1)S(1)} %collective-permute-done.12.refs_1_, ...), custom_call_target="tpu_custom_call" | custom-call | tf_op jit(solution)/shard_map/gradient/pallas_call | solution.py:509
  (2 shorter events, 0.0 us)
Async XLA Ops:
  0.6 9.3 %copy-start.3 = (s32[3,4,2]{1,2,0:T(2,128)S(1)}, s32[3,4,2]{1,2,0:T(2,128)}, u32[]{:S(2)}) copy-start(s32[3,4,2]{1,2,0:T(2,128)} %param.8) | copy-start | bytes 292
  0.6 9.9 %copy-start = (bf16[2,3,4,2,48,256]{5,4,3,2,1,0:T(8,128)(2,1)S(1)}, bf16[2,3,4,2,48,256]{5,4,3,2,1,0:T(8,128)(2,1)}, u32[]{:S(2)}) copy-start(bf16[2,3,4,2,48,256]{5,4,3,2,1,0:T(8,128)(2,1)} %right_ref.5) | copy-start | bytes 3538948
  0.7 13.4 %copy-start.1 = (bf16[2,3,4,2,48,256]{5,4,3,2,1,0:T(8,128)(2,1)S(1)}, bf16[2,3,4,2,48,256]{5,4,3,2,1,0:T(8,128)(2,1)}, u32[]{:S(2)}) copy-start(bf16[2,3,4,2,48,256]{5,4,3,2,1,0:T(8,128)(2,1)} %left_ref.3) | copy-start | bytes 3538948
  0.7 25.1 %copy-start.2 = (f32[2,24,1024]{2,1,0:T(8,128)S(1)}, f32[2,24,1024]{2,1,0:T(8,128)}, u32[]{:S(2)}) copy-start(f32[2,24,1024]{2,1,0:T(8,128)} %data_ref.1) | copy-start | bytes 589828
  5.4 5.1 %collective-permute-start = (bf16[3,2,32,128]{3,2,1,0:T(8,128)(2,1)S(1)}, bf16[3,2,32,128]{3,2,1,0:T(8,128)(2,1)S(1)}, u32[]{:S(2)}, u32[]{:S(2)}) collective-permute-start(bf16[3,2,32,128]{3,2,1,0:T(8,128)(2,1)S(1)} %get-tuple-element.21), channel_id=1, source_target_pairs={{0,8},{8,0},{16,24},{24,16},{1,9},{9,1},{17,25},{25,17},{2,10},{10... | collective-permute-start | bytes 147464 | tf_op jit(solution)/shard_map/ppermute | solution.py:62
  8.4 5.0 %collective-permute-start.1 = (bf16[3,2,32,128]{3,2,1,0:T(8,128)(2,1)S(1)}, bf16[3,2,32,128]{3,2,1,0:T(8,128)(2,1)S(1)}, u32[]{:S(2)}, u32[]{:S(2)}) collective-permute-start(bf16[3,2,32,128]{3,2,1,0:T(8,128)(2,1)S(1)} %get-tuple-element.22), channel_id=1, source_target_pairs={{0,24},{8,16},{16,8},{24,0},{1,25},{9,17},{17,9},{25,1},{2,26},{10... | collective-permute-start | bytes 147464 | tf_op jit(solution)/shard_map/ppermute | solution.py:62
  9.9 4.1 %collective-permute-start.2 = (bf16[3,2,32,128]{3,2,1,0:T(8,128)(2,1)S(1)}, bf16[3,2,32,128]{3,2,1,0:T(8,128)(2,1)S(1)}, u32[]{:S(2)}, u32[]{:S(2)}) collective-permute-start(bf16[3,2,32,128]{3,2,1,0:T(8,128)(2,1)S(1)} %get-tuple-element.23), channel_id=1, source_target_pairs={{0,16},{8,24},{16,0},{24,8},{1,17},{9,25},{17,1},{25,9},{2,18},{10... | collective-permute-start | bytes 147464 | tf_op jit(solution)/shard_map/ppermute | solution.py:62
  15.0 6.6 %collective-permute-start.3 = (bf16[2,24,1024]{2,1,0:T(8,128)(2,1)S(1)}, bf16[2,24,1024]{2,1,0:T(8,128)(2,1)S(1)}, u32[]{:S(2)}, u32[]{:S(2)}) collective-permute-start(bf16[2,24,1024]{2,1,0:T(8,128)(2,1)S(1)} %get-tuple-element.24), channel_id=1, source_target_pairs={{0,6},{2,4},{4,2},{6,0},{1,7},{3,5},{5,3},{7,1},{8,14},{10,12},{12... | collective-permute-start | bytes 294920 | tf_op jit(solution)/shard_map/ppermute | solution.py:62
  18.7 7.0 %collective-permute-start.4 = (bf16[2,24,1024]{2,1,0:T(8,128)(2,1)S(1)}, bf16[2,24,1024]{2,1,0:T(8,128)(2,1)S(1)}, u32[]{:S(2)}, u32[]{:S(2)}) collective-permute-start(bf16[2,24,1024]{2,1,0:T(8,128)(2,1)S(1)} %get-tuple-element.25), channel_id=1, source_target_pairs={{0,4},{2,6},{4,0},{6,2},{1,5},{3,7},{5,1},{7,3},{8,12},{10,14},{12... | collective-permute-start | bytes 294920 | tf_op jit(solution)/shard_map/ppermute | solution.py:62
  18.7 7.0 %collective-permute-start.5 = (bf16[2,24,1024]{2,1,0:T(8,128)(2,1)S(1)}, bf16[2,24,1024]{2,1,0:T(8,128)(2,1)S(1)}, u32[]{:S(2)}, u32[]{:S(2)}) collective-permute-start(bf16[2,24,1024]{2,1,0:T(8,128)(2,1)S(1)} %get-tuple-element.26), channel_id=1, source_target_pairs={{0,2},{2,0},{4,6},{6,4},{1,3},{3,1},{5,7},{7,5},{8,10},{10,8},{12,... | collective-permute-start | bytes 294920 | tf_op jit(solution)/shard_map/ppermute | solution.py:62
  25.8 7.6 %collective-permute-start.8 = (bf16[2,24,1024]{2,1,0:T(8,128)(2,1)S(1)}, bf16[2,24,1024]{2,1,0:T(8,128)(2,1)S(1)}, u32[]{:S(2)}, u32[]{:S(2)}) collective-permute-start(bf16[2,24,1024]{2,1,0:T(8,128)(2,1)S(1)} %get-tuple-element.30.refs_0_), channel_id=1, source_target_pairs={{0,6},{2,4},{4,2},{6,0},{1,7},{3,5},{5,3},{7,1},{8,14},{10,12},{12... | collective-permute-start | bytes 294920 | tf_op jit(solution)/shard_map/ppermute | solution.py:62
  28.3 7.6 %collective-permute-start.7 = (bf16[2,24,1024]{2,1,0:T(8,128)(2,1)S(1)}, bf16[2,24,1024]{2,1,0:T(8,128)(2,1)S(1)}, u32[]{:S(2)}, u32[]{:S(2)}) collective-permute-start(bf16[2,24,1024]{2,1,0:T(8,128)(2,1)S(1)} %get-tuple-element.30.refs_0_), channel_id=1, source_target_pairs={{0,4},{2,6},{4,0},{6,2},{1,5},{3,7},{5,1},{7,3},{8,12},{10,14},{12... | collective-permute-start | bytes 294920 | tf_op jit(solution)/shard_map/ppermute | solution.py:62
  28.3 7.6 %collective-permute-start.6 = (bf16[2,24,1024]{2,1,0:T(8,128)(2,1)S(1)}, bf16[2,24,1024]{2,1,0:T(8,128)(2,1)S(1)}, u32[]{:S(2)}, u32[]{:S(2)}) collective-permute-start(bf16[2,24,1024]{2,1,0:T(8,128)(2,1)S(1)} %get-tuple-element.30.refs_0_), channel_id=1, source_target_pairs={{0,2},{2,0},{4,6},{6,4},{1,3},{3,1},{5,7},{7,5},{8,10},{10,8},{12,... | collective-permute-start | bytes 294920 | tf_op jit(solution)/shard_map/ppermute | solution.py:62
  37.1 1.4 %collective-permute-start.9 = (bf16[4,3,2,16,128]{4,3,2,1,0:T(8,128)(2,1)S(1)}, bf16[4,3,2,16,128]{4,3,2,1,0:T(8,128)(2,1)S(1)}, u32[]{:S(2)}, u32[]{:S(2)}) collective-permute-start(bf16[4,3,2,16,128]{4,3,2,1,0:T(8,128)(2,1)S(1)} %get-tuple-element.32), channel_id=1, source_target_pairs={{0,1},{1,0},{2,3},{3,2},{4,5},{5,4},{6,7},{7,6},{8,9},{9,8},{10,11... | collective-permute-start | bytes 294920 | tf_op jit(solution)/shard_map/ppermute | solution.py:62
  38.5 4.4 %collective-permute-start.11 = (bf16[2,3,2,16,128]{4,3,2,1,0:T(8,128)(2,1)S(1)}, bf16[2,3,2,16,128]{4,3,2,1,0:T(8,128)(2,1)S(1)}, u32[]{:S(2)}, u32[]{:S(2)}) collective-permute-start(bf16[2,3,2,16,128]{4,3,2,1,0:T(8,128)(2,1)S(1)} %get-tuple-element.34), channel_id=1, source_target_pairs={{0,8},{1,17},{8,0},{9,25},{16,24},{17,1},{24,16},{25,9},{2,10},{3,... | collective-permute-start | bytes 147464 | tf_op jit(solution)/shard_map/ppermute | solution.py:455
  40.2 4.7 %collective-permute-start.10 = (bf16[1,3,2,16,128]{4,3,2,1,0:T(8,128)(2,1)S(1)}, bf16[1,3,2,16,128]{4,3,2,1,0:T(8,128)(2,1)S(1)}, u32[]{:S(2)}, u32[]{:S(2)}) collective-permute-start(bf16[1,3,2,16,128]{4,3,2,1,0:T(8,128)(2,1)S(1)} %get-tuple-element.33), channel_id=1, source_target_pairs={{0,24},{1,25},{8,16},{9,17},{16,8},{17,9},{24,0},{25,1},{2,26},{3,... | collective-permute-start | bytes 73736 | tf_op jit(solution)/shard_map/ppermute | solution.py:456
  42.9 2.0 %collective-permute-start.12 = (bf16[1,3,2,16,128]{4,3,2,1,0:T(8,128)(2,1)S(1)}, bf16[1,3,2,16,128]{4,3,2,1,0:T(8,128)(2,1)S(1)}, u32[]{:S(2)}, u32[]{:S(2)}) collective-permute-start(bf16[1,3,2,16,128]{4,3,2,1,0:T(8,128)(2,1)S(1)} %other.1), channel_id=1, source_target_pairs={{0,1},{1,0},{2,3},{3,2},{4,5},{5,4},{6,7},{7,6},{8,9},{9,8},{10,11... | collective-permute-start | bytes 73736 | tf_op jit(solution)/shard_map/ppermute | solution.py:457

commit v14 on v13

--- a/solution.py
+++ b/solution.py
@@ -89,7 +89,7 @@
                 model_hbm.at[:, rows], model_ref.at[:, rows], model_sems.at[at]
             )
         )
-        copies[-1].start()
+        copies[-1].start(priority=at % 2)
     table = tables(bins, length)
     table_out_ref[...] = table
     for copy, (begin, length_of) in zip(copies, chunks):
@@ -495,7 +495,7 @@
         copies.append(
             pltpu.make_async_copy(out_ref.at[:, rows], out_hbm.at[:, rows], out_sems.at[at])
         )
-        copies[-1].start()
+        copies[-1].start(priority=at % 2)
     for copy in copies:
         copy.wait()
 

time: 47.6 us -> 48.5 us (1.019)
  Pallas kernels: 10.2 us -> 11.1 us
    pallas_call x1, Pallas kernels: 4.75 us -> 5.69 us  [spectrum_of(): pl.pallas_call(spectrum_kernel, in_specs=[pl.BlockSpec(memory_space=pltpu...]
where the time goes in v14:
time: 48.5 us; the launch traced here: 48.4 us
  waiting for transfers between devices  19.9 us (41%)
  starting transfers between devices  15.9 us (33%)
  Pallas kernels  11.1 us (23%)
  between operations  0.73 us (2%)
  other arithmetic  0.7 us (1%)
    ppermute x10, waiting for transfers between devices, exchange(): arrived.append(lax.ppermute(blocks[step], axis, pairs))  16.5 us
    ppermute x10, starting transfers between devices, exchange(): arrived.append(lax.ppermute(blocks[step], axis, pairs))  13.5 us
    pallas_call x1, Pallas kernels, spectrum_of(): pl.pallas_call(spectrum_kernel, in_specs=[pl.BlockSpec(memory_space=pltpu...  5.69 us
    pallas_call x1, Pallas kernels, gradient_of(): pl.pallas_call(functools.partial(gradient_kernel, reps), in_specs=[pl.Blo...  2.51 us
    ppermute x1, waiting for transfers between devices, return_spectra(): pair = lax.ppermute(pair, ('freq', 'rep'), near)  2.07 us
    ppermute x1, starting transfers between devices, return_spectra(): pair = lax.ppermute(pair, ('freq', 'rep'), near)  1.69 us
    ppermute x1, waiting for transfers between devices, return_spectra(): last = lax.ppermute(last, ('freq', 'rep'), far)  1.31 us
    pallas_call x1, Pallas kernels, back_project(): pl.pallas_call(functools.partial(back_kernel, parts, groups, reps), in_sp...  1.19 us
  transfers between devices with their start and end apart: 13, of which 10 were waited for; matrix products, arithmetic and copies ran while one was open for 2% of the time, Pallas kernels for 1%

profile of v14, /device:TPU:0, one launch (start us, length us, event | category | flops | bytes accessed | tf_op | source)
XLA Modules:
  0.0 48.4 jit_solution(11616789036203432328)
XLA Ops:
  0.6 0.0 copy-start.3
  0.6 0.0 copy-start
  0.7 0.0 copy-start.1
  0.7 0.0 copy-start.2
  0.7 5.7 %spectrum.1 = (bf16[24,1024]{1,0:T(8,128)(2,1)S(1)}, bf16[3,2,32,128]{3,2,1,0:T(8,128)(2,1)S(1)}, bf16[3,2,32,128]{3,2,1,0:T(8,128)(2,1)S(1)}, bf16[3,2,32,128]{...) custom-call(bf16[4,32,32,1024]{3,2,1,0:T(8,128)(2,1)} %bitcast.6), custom_call_target="tpu_custom_call" | custom-call | tf_op jit(solution)/shard_map/spectrum/pallas_call | solution.py:121
  6.4 3.0 %collective-permute-start = (bf16[3,2,32,128]{3,2,1,0:T(8,128)(2,1)S(1)}, bf16[3,2,32,128]{3,2,1,0:T(8,128)(2,1)S(1)}, u32[]{:S(2)}, u32[]{:S(2)}) collective-permute-start(bf16[3,2,32,128]{3,2,1,0:T(8,128)(2,1)S(1)} %get-tuple-element.21), channel_id=1, source_target_pairs={{0,8},{8,0},{16,24},{24,16},{1,9},{9,1},{17,25},{25,17},{2,10},{10... | collective-permute-start | bytes 147464 | tf_op jit(solution)/shard_map/ppermute | solution.py:62
  9.4 1.5 %collective-permute-start.1 = (bf16[3,2,32,128]{3,2,1,0:T(8,128)(2,1)S(1)}, bf16[3,2,32,128]{3,2,1,0:T(8,128)(2,1)S(1)}, u32[]{:S(2)}, u32[]{:S(2)}) collective-permute-start(bf16[3,2,32,128]{3,2,1,0:T(8,128)(2,1)S(1)} %get-tuple-element.22), channel_id=1, source_target_pairs={{0,24},{8,16},{16,8},{24,0},{1,25},{9,17},{17,9},{25,1},{2,26},{10... | collective-permute-start | bytes 147464 | tf_op jit(solution)/shard_map/ppermute | solution.py:62
  10.9 0.0 collective-permute-start.2
  10.9 0.0 copy-done.3
  10.9 0.1 copy.7.ranks_ref
  11.0 0.1 limits.1.limits_ref
  11.1 0.3 collective-permute-done.refs_1_
  11.4 0.0 copy-done
  11.4 0.6 %project.1.own_ref = bf16[3,4,48,64]{3,2,1,0:T(8,128)(2,1)S(1)} custom-call(s32[3,4,2,1,128]{4,3,2,1,0:T(1,128)S(1)} %limits.1.limits_ref, bf16[2,3,4,2,48,256]{5,4,3,2,1,0:T(8,128)(2,1)S(1)} %copy-done, bf16[3,2,32,128]{3,2,1,0:T(8,128)(2,1)S(1)} %get-tuple-element.20.refs_0_, bf16[3,2,32,128]{3,2,1,0:T(8,128)(2,1)S(1)} %collective-permute-done.refs_1_), custom_call_target="tpu_custom_call" | custom-call | flops 37748736 | bytes 1179648 | tf_op jit(solution)/shard_map/project/pallas_call | solution.py:227
  12.0 2.3 %collective-permute-done.1.refs_0_ = bf16[3,2,32,128]{3,2,1,0:T(8,128)(2,1)S(1)} collective-permute-done((bf16[3,2,32,128]{3,2,1,0:T(8,128)(2,1)S(1)}, bf16[3,2,32,128]{3,2,1,0:T(8,128)(2,1)S(1)}, u32[]{:S(2)}, u32[]{:S(2)}) %collective-permute-start.1) | collective-permute-done | bytes 49184 | tf_op jit(solution)/shard_map/ppermute | solution.py:62
  14.4 0.6 %collective-permute-done.2.refs_1_ = bf16[3,2,32,128]{3,2,1,0:T(8,128)(2,1)S(1)} collective-permute-done((bf16[3,2,32,128]{3,2,1,0:T(8,128)(2,1)S(1)}, bf16[3,2,32,128]{3,2,1,0:T(8,128)(2,1)S(1)}, u32[]{:S(2)}, u32[]{:S(2)}) %collective-permute-start.2) | collective-permute-done | bytes 49184 | tf_op jit(solution)/shard_map/ppermute | solution.py:62
  15.0 0.0 copy-done.1
  15.0 1.0 %predict.1 = (bf16[2,24,1024]{2,1,0:T(8,128)(2,1)S(1)}, bf16[2,24,1024]{2,1,0:T(8,128)(2,1)S(1)}, bf16[2,24,1024]{2,1,0:T(8,128)(2,1)S(1)}, bf16[2,24,1024]{2,1,0:T(8,128)(2,1)S(1)}) custom-call(s32[3,4,2,1,128]{4,3,2,1,0:T(1,128)S(1)} %limits.1.limits_ref, bf16[2,3,4,2,48,256]{5,4,3,2,1,0:T(8,128)(2,1)S(1)} %copy-done, ...), custom_call_target="tpu_custom_call" | custom-call | flops 150994944 | bytes 2359296 | tf_op jit(solution)/shard_map/predict/pallas_call | solution.py:283
  16.0 3.7 %collective-permute-start.3 = (bf16[2,24,1024]{2,1,0:T(8,128)(2,1)S(1)}, bf16[2,24,1024]{2,1,0:T(8,128)(2,1)S(1)}, u32[]{:S(2)}, u32[]{:S(2)}) collective-permute-start(bf16[2,24,1024]{2,1,0:T(8,128)(2,1)S(1)} %get-tuple-element.24), channel_id=1, source_target_pairs={{0,6},{2,4},{4,2},{6,0},{1,7},{3,5},{5,3},{7,1},{8,14},{10,12},{12... | collective-permute-start | bytes 294920 | tf_op jit(solution)/shard_map/ppermute | solution.py:62
  19.7 0.0 collective-permute-start.4
  19.7 0.8 %collective-permute-start.5 = (bf16[2,24,1024]{2,1,0:T(8,128)(2,1)S(1)}, bf16[2,24,1024]{2,1,0:T(8,128)(2,1)S(1)}, u32[]{:S(2)}, u32[]{:S(2)}) collective-permute-start(bf16[2,24,1024]{2,1,0:T(8,128)(2,1)S(1)} %get-tuple-element.26), channel_id=1, source_target_pairs={{0,2},{2,0},{4,6},{6,4},{1,3},{3,1},{5,7},{7,5},{8,10},{10,8},{12,... | collective-permute-start | bytes 294920 | tf_op jit(solution)/shard_map/ppermute | solution.py:62
  20.4 2.2 %collective-permute-done.3.refs_0_ = bf16[2,24,1024]{2,1,0:T(8,128)(2,1)S(1)} collective-permute-done((bf16[2,24,1024]{2,1,0:T(8,128)(2,1)S(1)}, bf16[2,24,1024]{2,1,0:T(8,128)(2,1)S(1)}, u32[]{:S(2)}, u32[]{:S(2)}) %collective-permute-start.3) | collective-permute-done | bytes 98336 | tf_op jit(solution)/shard_map/ppermute | solution.py:62
  22.6 4.1 %collective-permute-done.4.refs_1_ = bf16[2,24,1024]{2,1,0:T(8,128)(2,1)S(1)} collective-permute-done((bf16[2,24,1024]{2,1,0:T(8,128)(2,1)S(1)}, bf16[2,24,1024]{2,1,0:T(8,128)(2,1)S(1)}, u32[]{:S(2)}, u32[]{:S(2)}) %collective-permute-start.4) | collective-permute-done | bytes 98336 | tf_op jit(solution)/shard_map/ppermute | solution.py:62
  26.7 0.0 collective-permute-done.5.refs_2_
  26.7 0.0 copy-done.2
  26.7 0.1 residual.1
  26.7 2.5 %collective-permute-start.8 = (bf16[2,24,1024]{2,1,0:T(8,128)(2,1)S(1)}, bf16[2,24,1024]{2,1,0:T(8,128)(2,1)S(1)}, u32[]{:S(2)}, u32[]{:S(2)}) collective-permute-start(bf16[2,24,1024]{2,1,0:T(8,128)(2,1)S(1)} %get-tuple-element.30.refs_0_), channel_id=1, source_target_pairs={{0,6},{2,4},{4,2},{6,0},{1,7},{3,5},{5,3},{7,1},{8,14},{10,12},{12... | collective-permute-start | bytes 294920 | tf_op jit(solution)/shard_map/ppermute | solution.py:62
  29.3 0.0 collective-permute-start.7
  29.3 1.9 %collective-permute-start.6 = (bf16[2,24,1024]{2,1,0:T(8,128)(2,1)S(1)}, bf16[2,24,1024]{2,1,0:T(8,128)(2,1)S(1)}, u32[]{:S(2)}, u32[]{:S(2)}) collective-permute-start(bf16[2,24,1024]{2,1,0:T(8,128)(2,1)S(1)} %get-tuple-element.30.refs_0_), channel_id=1, source_target_pairs={{0,2},{2,0},{4,6},{6,4},{1,3},{3,1},{5,7},{7,5},{8,10},{10,8},{12,... | collective-permute-start | bytes 294920 | tf_op jit(solution)/shard_map/ppermute | solution.py:62
  31.2 3.1 %collective-permute-done.8.refs_3_ = bf16[2,24,1024]{2,1,0:T(8,128)(2,1)S(1)} collective-permute-done((bf16[2,24,1024]{2,1,0:T(8,128)(2,1)S(1)}, bf16[2,24,1024]{2,1,0:T(8,128)(2,1)S(1)}, u32[]{:S(2)}, u32[]{:S(2)}) %collective-permute-start.8) | collective-permute-done | bytes 98336 | tf_op jit(solution)/shard_map/ppermute | solution.py:62
  34.3 2.5 %collective-permute-done.7.refs_2_ = bf16[2,24,1024]{2,1,0:T(8,128)(2,1)S(1)} collective-permute-done((bf16[2,24,1024]{2,1,0:T(8,128)(2,1)S(1)}, bf16[2,24,1024]{2,1,0:T(8,128)(2,1)S(1)}, u32[]{:S(2)}, u32[]{:S(2)}) %collective-permute-start.7) | collective-permute-done | bytes 98336 | tf_op jit(solution)/shard_map/ppermute | solution.py:62
  36.9 0.0 collective-permute-done.6.refs_1_
  36.9 1.2 %back_project.1 = (bf16[4,3,2,16,128]{4,3,2,1,0:T(8,128)(2,1)S(1)}, bf16[4,3,2,16,128]{4,3,2,1,0:T(8,128)(2,1)S(1)}) custom-call(s32[3,4,2,1,128]{4,3,2,1,0:T(1,128)S(1)} %limits.1.limits_ref, bf16[2,3,4,2,48,256]{5,4,3,2,1,0:T(8,128)(2,1)S(1)} %copy-done, bf16[2,3,4,2,48,256]{5,4,3,2,1,0:T(8,128)(2,1)S(1)} %copy-done.1, ...), custom_call_target="tpu_custom_call" | custom-call | flops 150994944 | bytes 2359296 | tf_op jit(solution)/shard_map/back_project/pallas_call | solution.py:394
  38.1 0.1 collective-permute-start.9
  38.2 1.3 %collective-permute-done.9.refs_1_ = bf16[4,3,2,16,128]{4,3,2,1,0:T(8,128)(2,1)S(1)} collective-permute-done((bf16[4,3,2,16,128]{4,3,2,1,0:T(8,128)(2,1)S(1)}, bf16[4,3,2,16,128]{4,3,2,1,0:T(8,128)(2,1)S(1)}, u32[]{:S(2)}, u32[]{:S(2)}) %collective-permute-start.9) | collective-permute-done | bytes 98336 | tf_op jit(solution)/shard_map/ppermute | solution.py:62
  39.5 1.7 %collective-permute-start.11 = (bf16[2,3,2,16,128]{4,3,2,1,0:T(8,128)(2,1)S(1)}, bf16[2,3,2,16,128]{4,3,2,1,0:T(8,128)(2,1)S(1)}, u32[]{:S(2)}, u32[]{:S(2)}) collective-permute-start(bf16[2,3,2,16,128]{4,3,2,1,0:T(8,128)(2,1)S(1)} %get-tuple-element.34), channel_id=1, source_target_pairs={{0,8},{1,17},{8,0},{9,25},{16,24},{17,1},{24,16},{25,9},{2,10},{3,... | collective-permute-start | bytes 147464 | tf_op jit(solution)/shard_map/ppermute | solution.py:455
  41.2 0.6 %collective-permute-start.10 = (bf16[1,3,2,16,128]{4,3,2,1,0:T(8,128)(2,1)S(1)}, bf16[1,3,2,16,128]{4,3,2,1,0:T(8,128)(2,1)S(1)}, u32[]{:S(2)}, u32[]{:S(2)}) collective-permute-start(bf16[1,3,2,16,128]{4,3,2,1,0:T(8,128)(2,1)S(1)} %get-tuple-element.33), channel_id=1, source_target_pairs={{0,24},{1,25},{8,16},{9,17},{16,8},{17,9},{24,0},{25,1},{2,26},{3,... | collective-permute-start | bytes 73736 | tf_op jit(solution)/shard_map/ppermute | solution.py:456
  41.8 2.1 %collective-permute-done.11.pair_ref.refs_2_ = bf16[2,3,2,16,128]{4,3,2,1,0:T(8,128)(2,1)S(1)} collective-permute-done((bf16[2,3,2,16,128]{4,3,2,1,0:T(8,128)(2,1)S(1)}, bf16[2,3,2,16,128]{4,3,2,1,0:T(8,128)(2,1)S(1)}, u32[]{:S(2)}, u32[]{:S(2)}) %collective-permute-start.11) | collective-permute-done | bytes 49184 | tf_op jit(solution)/shard_map/ppermute | solution.py:455
  43.9 0.0 collective-permute-start.12
  43.9 0.7 %pad_maximum_fusion = f32[2,24,1024]{2,1,0:T(8,128)} fusion(f32[1,24,1024]{2,1,0:T(8,128)S(1)} %bitcast.5, f32[1,24,1024]{2,1,0:T(8,128)S(1)} %bitcast.4), kind=kLoop, calls=%fused_computation | loop fusion | flops 49152 | bytes 393216 | tf_op jit(solution)/shard_map/stack | solution.py:541
  44.6 1.3 %collective-permute-done.10.refs_0_ = bf16[1,3,2,16,128]{4,3,2,1,0:T(8,128)(2,1)S(1)} collective-permute-done((bf16[1,3,2,16,128]{4,3,2,1,0:T(8,128)(2,1)S(1)}, bf16[1,3,2,16,128]{4,3,2,1,0:T(8,128)(2,1)S(1)}, u32[]{:S(2)}, u32[]{:S(2)}) %collective-permute-start.10) | collective-permute-done | bytes 24608 | tf_op jit(solution)/shard_map/ppermute | solution.py:456
  45.9 0.0 collective-permute-done.12.refs_1_
  45.9 2.5 %gradient.1 = bf16[4,16,32,1024]{3,2,1,0:T(8,128)(2,1)} custom-call(bf16[24,1024]{1,0:T(8,128)(2,1)S(1)} %get-tuple-element.19.table_ref, bf16[1,3,2,16,128]{4,3,2,1,0:T(8,128)(2,1)S(1)} %collective-permute-done.10.refs_0_, bf16[1,3,2,16,128]{4,3,2,1,0:T(8,128)(2,1)S(1)} %collective-permute-done.12.refs_1_, ...), custom_call_target="tpu_custom_call" | custom-call | tf_op jit(solution)/shard_map/gradient/pallas_call | solution.py:509
  (2 shorter events, 0.0 us)
Async XLA Ops:
  0.6 10.3 %copy-start.3 = (s32[3,4,2]{1,2,0:T(2,128)S(1)}, s32[3,4,2]{1,2,0:T(2,128)}, u32[]{:S(2)}) copy-start(s32[3,4,2]{1,2,0:T(2,128)} %param.8) | copy-start | bytes 292
  0.6 10.8 %copy-start = (bf16[2,3,4,2,48,256]{5,4,3,2,1,0:T(8,128)(2,1)S(1)}, bf16[2,3,4,2,48,256]{5,4,3,2,1,0:T(8,128)(2,1)}, u32[]{:S(2)}) copy-start(bf16[2,3,4,2,48,256]{5,4,3,2,1,0:T(8,128)(2,1)} %right_ref.5) | copy-start | bytes 3538948
  0.7 14.3 %copy-start.1 = (bf16[2,3,4,2,48,256]{5,4,3,2,1,0:T(8,128)(2,1)S(1)}, bf16[2,3,4,2,48,256]{5,4,3,2,1,0:T(8,128)(2,1)}, u32[]{:S(2)}) copy-start(bf16[2,3,4,2,48,256]{5,4,3,2,1,0:T(8,128)(2,1)} %left_ref.3) | copy-start | bytes 3538948
  0.7 26.0 %copy-start.2 = (f32[2,24,1024]{2,1,0:T(8,128)S(1)}, f32[2,24,1024]{2,1,0:T(8,128)}, u32[]{:S(2)}) copy-start(f32[2,24,1024]{2,1,0:T(8,128)} %data_ref.1) | copy-start | bytes 589828
  6.4 5.1 %collective-permute-start = (bf16[3,2,32,128]{3,2,1,0:T(8,128)(2,1)S(1)}, bf16[3,2,32,128]{3,2,1,0:T(8,128)(2,1)S(1)}, u32[]{:S(2)}, u32[]{:S(2)}) collective-permute-start(bf16[3,2,32,128]{3,2,1,0:T(8,128)(2,1)S(1)} %get-tuple-element.21), channel_id=1, source_target_pairs={{0,8},{8,0},{16,24},{24,16},{1,9},{9,1},{17,25},{25,17},{2,10},{10... | collective-permute-start | bytes 147464 | tf_op jit(solution)/shard_map/ppermute | solution.py:62
  9.4 5.0 %collective-permute-start.1 = (bf16[3,2,32,128]{3,2,1,0:T(8,128)(2,1)S(1)}, bf16[3,2,32,128]{3,2,1,0:T(8,128)(2,1)S(1)}, u32[]{:S(2)}, u32[]{:S(2)}) collective-permute-start(bf16[3,2,32,128]{3,2,1,0:T(8,128)(2,1)S(1)} %get-tuple-element.22), channel_id=1, source_target_pairs={{0,24},{8,16},{16,8},{24,0},{1,25},{9,17},{17,9},{25,1},{2,26},{10... | collective-permute-start | bytes 147464 | tf_op jit(solution)/shard_map/ppermute | solution.py:62
  10.9 4.1 %collective-permute-start.2 = (bf16[3,2,32,128]{3,2,1,0:T(8,128)(2,1)S(1)}, bf16[3,2,32,128]{3,2,1,0:T(8,128)(2,1)S(1)}, u32[]{:S(2)}, u32[]{:S(2)}) collective-permute-start(bf16[3,2,32,128]{3,2,1,0:T(8,128)(2,1)S(1)} %get-tuple-element.23), channel_id=1, source_target_pairs={{0,16},{8,24},{16,0},{24,8},{1,17},{9,25},{17,1},{25,9},{2,18},{10... | collective-permute-start | bytes 147464 | tf_op jit(solution)/shard_map/ppermute | solution.py:62
  16.0 6.6 %collective-permute-start.3 = (bf16[2,24,1024]{2,1,0:T(8,128)(2,1)S(1)}, bf16[2,24,1024]{2,1,0:T(8,128)(2,1)S(1)}, u32[]{:S(2)}, u32[]{:S(2)}) collective-permute-start(bf16[2,24,1024]{2,1,0:T(8,128)(2,1)S(1)} %get-tuple-element.24), channel_id=1, source_target_pairs={{0,6},{2,4},{4,2},{6,0},{1,7},{3,5},{5,3},{7,1},{8,14},{10,12},{12... | collective-permute-start | bytes 294920 | tf_op jit(solution)/shard_map/ppermute | solution.py:62
  19.7 7.0 %collective-permute-start.4 = (bf16[2,24,1024]{2,1,0:T(8,128)(2,1)S(1)}, bf16[2,24,1024]{2,1,0:T(8,128)(2,1)S(1)}, u32[]{:S(2)}, u32[]{:S(2)}) collective-permute-start(bf16[2,24,1024]{2,1,0:T(8,128)(2,1)S(1)} %get-tuple-element.25), channel_id=1, source_target_pairs={{0,4},{2,6},{4,0},{6,2},{1,5},{3,7},{5,1},{7,3},{8,12},{10,14},{12... | collective-permute-start | bytes 294920 | tf_op jit(solution)/shard_map/ppermute | solution.py:62
  19.7 7.0 %collective-permute-start.5 = (bf16[2,24,1024]{2,1,0:T(8,128)(2,1)S(1)}, bf16[2,24,1024]{2,1,0:T(8,128)(2,1)S(1)}, u32[]{:S(2)}, u32[]{:S(2)}) collective-permute-start(bf16[2,24,1024]{2,1,0:T(8,128)(2,1)S(1)} %get-tuple-element.26), channel_id=1, source_target_pairs={{0,2},{2,0},{4,6},{6,4},{1,3},{3,1},{5,7},{7,5},{8,10},{10,8},{12,... | collective-permute-start | bytes 294920 | tf_op jit(solution)/shard_map/ppermute | solution.py:62
  26.7 7.6 %collective-permute-start.8 = (bf16[2,24,1024]{2,1,0:T(8,128)(2,1)S(1)}, bf16[2,24,1024]{2,1,0:T(8,128)(2,1)S(1)}, u32[]{:S(2)}, u32[]{:S(2)}) collective-permute-start(bf16[2,24,1024]{2,1,0:T(8,128)(2,1)S(1)} %get-tuple-element.30.refs_0_), channel_id=1, source_target_pairs={{0,6},{2,4},{4,2},{6,0},{1,7},{3,5},{5,3},{7,1},{8,14},{10,12},{12... | collective-permute-start | bytes 294920 | tf_op jit(solution)/shard_map/ppermute | solution.py:62
  29.3 7.6 %collective-permute-start.7 = (bf16[2,24,1024]{2,1,0:T(8,128)(2,1)S(1)}, bf16[2,24,1024]{2,1,0:T(8,128)(2,1)S(1)}, u32[]{:S(2)}, u32[]{:S(2)}) collective-permute-start(bf16[2,24,1024]{2,1,0:T(8,128)(2,1)S(1)} %get-tuple-element.30.refs_0_), channel_id=1, source_target_pairs={{0,4},{2,6},{4,0},{6,2},{1,5},{3,7},{5,1},{7,3},{8,12},{10,14},{12... | collective-permute-start | bytes 294920 | tf_op jit(solution)/shard_map/ppermute | solution.py:62
  29.3 7.6 %collective-permute-start.6 = (bf16[2,24,1024]{2,1,0:T(8,128)(2,1)S(1)}, bf16[2,24,1024]{2,1,0:T(8,128)(2,1)S(1)}, u32[]{:S(2)}, u32[]{:S(2)}) collective-permute-start(bf16[2,24,1024]{2,1,0:T(8,128)(2,1)S(1)} %get-tuple-element.30.refs_0_), channel_id=1, source_target_pairs={{0,2},{2,0},{4,6},{6,4},{1,3},{3,1},{5,7},{7,5},{8,10},{10,8},{12,... | collective-permute-start | bytes 294920 | tf_op jit(solution)/shard_map/ppermute | solution.py:62
  38.1 1.4 %collective-permute-start.9 = (bf16[4,3,2,16,128]{4,3,2,1,0:T(8,128)(2,1)S(1)}, bf16[4,3,2,16,128]{4,3,2,1,0:T(8,128)(2,1)S(1)}, u32[]{:S(2)}, u32[]{:S(2)}) collective-permute-start(bf16[4,3,2,16,128]{4,3,2,1,0:T(8,128)(2,1)S(1)} %get-tuple-element.32), channel_id=1, source_target_pairs={{0,1},{1,0},{2,3},{3,2},{4,5},{5,4},{6,7},{7,6},{8,9},{9,8},{10,11... | collective-permute-start | bytes 294920 | tf_op jit(solution)/shard_map/ppermute | solution.py:62
  39.5 4.4 %collective-permute-start.11 = (bf16[2,3,2,16,128]{4,3,2,1,0:T(8,128)(2,1)S(1)}, bf16[2,3,2,16,128]{4,3,2,1,0:T(8,128)(2,1)S(1)}, u32[]{:S(2)}, u32[]{:S(2)}) collective-permute-start(bf16[2,3,2,16,128]{4,3,2,1,0:T(8,128)(2,1)S(1)} %get-tuple-element.34), channel_id=1, source_target_pairs={{0,8},{1,17},{8,0},{9,25},{16,24},{17,1},{24,16},{25,9},{2,10},{3,... | collective-permute-start | bytes 147464 | tf_op jit(solution)/shard_map/ppermute | solution.py:455
  41.2 4.7 %collective-permute-start.10 = (bf16[1,3,2,16,128]{4,3,2,1,0:T(8,128)(2,1)S(1)}, bf16[1,3,2,16,128]{4,3,2,1,0:T(8,128)(2,1)S(1)}, u32[]{:S(2)}, u32[]{:S(2)}) collective-permute-start(bf16[1,3,2,16,128]{4,3,2,1,0:T(8,128)(2,1)S(1)} %get-tuple-element.33), channel_id=1, source_target_pairs={{0,24},{1,25},{8,16},{9,17},{16,8},{17,9},{24,0},{25,1},{2,26},{3,... | collective-permute-start | bytes 73736 | tf_op jit(solution)/shard_map/ppermute | solution.py:456
  43.9 2.0 %collective-permute-start.12 = (bf16[1,3,2,16,128]{4,3,2,1,0:T(8,128)(2,1)S(1)}, bf16[1,3,2,16,128]{4,3,2,1,0:T(8,128)(2,1)S(1)}, u32[]{:S(2)}, u32[]{:S(2)}) collective-permute-start(bf16[1,3,2,16,128]{4,3,2,1,0:T(8,128)(2,1)S(1)} %other.1), channel_id=1, source_target_pairs={{0,1},{1,0},{2,3},{3,2},{4,5},{5,4},{6,7},{7,6},{8,9},{9,8},{10,11... | collective-permute-start | bytes 73736 | tf_op jit(solution)/shard_map/ppermute | solution.py:457

commit v15 on v13

--- a/solution.py
+++ b/solution.py
@@ -89,7 +89,7 @@
                 model_hbm.at[:, rows], model_ref.at[:, rows], model_sems.at[at]
             )
         )
-        copies[-1].start()
+        copies[-1].start(priority=1)
     table = tables(bins, length)
     table_out_ref[...] = table
     for copy, (begin, length_of) in zip(copies, chunks):

time: 47.6 us -> 47.6 us (level)
  no operation moved by 1% of the time
where the time goes in v15:
time: 47.6 us; the launch traced here: 47.5 us
  waiting for transfers between devices  19.8 us (42%)
  starting transfers between devices  15.9 us (33%)
  Pallas kernels  10.2 us (21%)
  between operations  0.73 us (2%)
  other arithmetic  0.7 us (1%)
    ppermute x10, waiting for transfers between devices, exchange(): arrived.append(lax.ppermute(blocks[step], axis, pairs))  16.5 us
    ppermute x10, starting transfers between devices, exchange(): arrived.append(lax.ppermute(blocks[step], axis, pairs))  13.5 us
    pallas_call x1, Pallas kernels, spectrum_of(): pl.pallas_call(spectrum_kernel, in_specs=[pl.BlockSpec(memory_space=pltpu...  4.75 us
    pallas_call x1, Pallas kernels, gradient_of(): pl.pallas_call(functools.partial(gradient_kernel, reps), in_specs=[pl.Blo...  2.51 us
    ppermute x1, waiting for transfers between devices, return_spectra(): pair = lax.ppermute(pair, ('freq', 'rep'), near)  2.06 us
    ppermute x1, starting transfers between devices, return_spectra(): pair = lax.ppermute(pair, ('freq', 'rep'), near)  1.7 us
    ppermute x1, waiting for transfers between devices, return_spectra(): last = lax.ppermute(last, ('freq', 'rep'), far)  1.31 us
    pallas_call x1, Pallas kernels, back_project(): pl.pallas_call(functools.partial(back_kernel, parts, groups, reps), in_sp...  1.2 us
  transfers between devices with their start and end apart: 13, of which 10 were waited for; matrix products, arithmetic and copies ran while one was open for 2% of the time, Pallas kernels for 1%

profile of v15, /device:TPU:0, one launch (start us, length us, event | category | flops | bytes accessed | tf_op | source)
XLA Modules:
  0.0 47.5 jit_solution(5436664352580322471)
XLA Ops:
  0.6 0.0 copy-start.3
  0.6 0.0 copy-start
  0.7 0.0 copy-start.1
  0.7 0.0 copy-start.2
  0.7 4.7 %spectrum.1 = (bf16[24,1024]{1,0:T(8,128)(2,1)S(1)}, bf16[3,2,32,128]{3,2,1,0:T(8,128)(2,1)S(1)}, bf16[3,2,32,128]{3,2,1,0:T(8,128)(2,1)S(1)}, bf16[3,2,32,128]{...) custom-call(bf16[4,32,32,1024]{3,2,1,0:T(8,128)(2,1)} %bitcast.6), custom_call_target="tpu_custom_call" | custom-call | tf_op jit(solution)/shard_map/spectrum/pallas_call | solution.py:121
  5.4 3.0 %collective-permute-start = (bf16[3,2,32,128]{3,2,1,0:T(8,128)(2,1)S(1)}, bf16[3,2,32,128]{3,2,1,0:T(8,128)(2,1)S(1)}, u32[]{:S(2)}, u32[]{:S(2)}) collective-permute-start(bf16[3,2,32,128]{3,2,1,0:T(8,128)(2,1)S(1)} %get-tuple-element.21), channel_id=1, source_target_pairs={{0,8},{8,0},{16,24},{24,16},{1,9},{9,1},{17,25},{25,17},{2,10},{10... | collective-permute-start | bytes 147464 | tf_op jit(solution)/shard_map/ppermute | solution.py:62
  8.4 1.5 %collective-permute-start.1 = (bf16[3,2,32,128]{3,2,1,0:T(8,128)(2,1)S(1)}, bf16[3,2,32,128]{3,2,1,0:T(8,128)(2,1)S(1)}, u32[]{:S(2)}, u32[]{:S(2)}) collective-permute-start(bf16[3,2,32,128]{3,2,1,0:T(8,128)(2,1)S(1)} %get-tuple-element.22), channel_id=1, source_target_pairs={{0,24},{8,16},{16,8},{24,0},{1,25},{9,17},{17,9},{25,1},{2,26},{10... | collective-permute-start | bytes 147464 | tf_op jit(solution)/shard_map/ppermute | solution.py:62
  9.9 0.0 collective-permute-start.2
  10.0 0.0 copy-done.3
  10.0 0.1 copy.7.ranks_ref
  10.1 0.1 limits.1.limits_ref
  10.2 0.3 collective-permute-done.refs_1_
  10.5 0.0 copy-done
  10.5 0.6 %project.1.own_ref = bf16[3,4,48,64]{3,2,1,0:T(8,128)(2,1)S(1)} custom-call(s32[3,4,2,1,128]{4,3,2,1,0:T(1,128)S(1)} %limits.1.limits_ref, bf16[2,3,4,2,48,256]{5,4,3,2,1,0:T(8,128)(2,1)S(1)} %copy-done, bf16[3,2,32,128]{3,2,1,0:T(8,128)(2,1)S(1)} %get-tuple-element.20.refs_0_, bf16[3,2,32,128]{3,2,1,0:T(8,128)(2,1)S(1)} %collective-permute-done.refs_1_), custom_call_target="tpu_custom_call" | custom-call | flops 37748736 | bytes 1179648 | tf_op jit(solution)/shard_map/project/pallas_call | solution.py:227
  11.1 2.3 %collective-permute-done.1.refs_0_ = bf16[3,2,32,128]{3,2,1,0:T(8,128)(2,1)S(1)} collective-permute-done((bf16[3,2,32,128]{3,2,1,0:T(8,128)(2,1)S(1)}, bf16[3,2,32,128]{3,2,1,0:T(8,128)(2,1)S(1)}, u32[]{:S(2)}, u32[]{:S(2)}) %collective-permute-start.1) | collective-permute-done | bytes 49184 | tf_op jit(solution)/shard_map/ppermute | solution.py:62
  13.4 0.6 %collective-permute-done.2.refs_1_ = bf16[3,2,32,128]{3,2,1,0:T(8,128)(2,1)S(1)} collective-permute-done((bf16[3,2,32,128]{3,2,1,0:T(8,128)(2,1)S(1)}, bf16[3,2,32,128]{3,2,1,0:T(8,128)(2,1)S(1)}, u32[]{:S(2)}, u32[]{:S(2)}) %collective-permute-start.2) | collective-permute-done | bytes 49184 | tf_op jit(solution)/shard_map/ppermute | solution.py:62
  14.0 0.0 copy-done.1
  14.0 1.0 %predict.1 = (bf16[2,24,1024]{2,1,0:T(8,128)(2,1)S(1)}, bf16[2,24,1024]{2,1,0:T(8,128)(2,1)S(1)}, bf16[2,24,1024]{2,1,0:T(8,128)(2,1)S(1)}, bf16[2,24,1024]{2,1,0:T(8,128)(2,1)S(1)}) custom-call(s32[3,4,2,1,128]{4,3,2,1,0:T(1,128)S(1)} %limits.1.limits_ref, bf16[2,3,4,2,48,256]{5,4,3,2,1,0:T(8,128)(2,1)S(1)} %copy-done, ...), custom_call_target="tpu_custom_call" | custom-call | flops 150994944 | bytes 2359296 | tf_op jit(solution)/shard_map/predict/pallas_call | solution.py:283
  15.0 3.7 %collective-permute-start.3 = (bf16[2,24,1024]{2,1,0:T(8,128)(2,1)S(1)}, bf16[2,24,1024]{2,1,0:T(8,128)(2,1)S(1)}, u32[]{:S(2)}, u32[]{:S(2)}) collective-permute-start(bf16[2,24,1024]{2,1,0:T(8,128)(2,1)S(1)} %get-tuple-element.24), channel_id=1, source_target_pairs={{0,6},{2,4},{4,2},{6,0},{1,7},{3,5},{5,3},{7,1},{8,14},{10,12},{12... | collective-permute-start | bytes 294920 | tf_op jit(solution)/shard_map/ppermute | solution.py:62
  18.7 0.0 collective-permute-start.4
  18.7 0.8 %collective-permute-start.5 = (bf16[2,24,1024]{2,1,0:T(8,128)(2,1)S(1)}, bf16[2,24,1024]{2,1,0:T(8,128)(2,1)S(1)}, u32[]{:S(2)}, u32[]{:S(2)}) collective-permute-start(bf16[2,24,1024]{2,1,0:T(8,128)(2,1)S(1)} %get-tuple-element.26), channel_id=1, source_target_pairs={{0,2},{2,0},{4,6},{6,4},{1,3},{3,1},{5,7},{7,5},{8,10},{10,8},{12,... | collective-permute-start | bytes 294920 | tf_op jit(solution)/shard_map/ppermute | solution.py:62
  19.5 2.1 %collective-permute-done.3.refs_0_ = bf16[2,24,1024]{2,1,0:T(8,128)(2,1)S(1)} collective-permute-done((bf16[2,24,1024]{2,1,0:T(8,128)(2,1)S(1)}, bf16[2,24,1024]{2,1,0:T(8,128)(2,1)S(1)}, u32[]{:S(2)}, u32[]{:S(2)}) %collective-permute-start.3) | collective-permute-done | bytes 98336 | tf_op jit(solution)/shard_map/ppermute | solution.py:62
  21.6 4.1 %collective-permute-done.4.refs_1_ = bf16[2,24,1024]{2,1,0:T(8,128)(2,1)S(1)} collective-permute-done((bf16[2,24,1024]{2,1,0:T(8,128)(2,1)S(1)}, bf16[2,24,1024]{2,1,0:T(8,128)(2,1)S(1)}, u32[]{:S(2)}, u32[]{:S(2)}) %collective-permute-start.4) | collective-permute-done | bytes 98336 | tf_op jit(solution)/shard_map/ppermute | solution.py:62
  25.7 0.0 collective-permute-done.5.refs_2_
  25.7 0.0 copy-done.2
  25.7 0.1 residual.1
  25.8 2.5 %collective-permute-start.8 = (bf16[2,24,1024]{2,1,0:T(8,128)(2,1)S(1)}, bf16[2,24,1024]{2,1,0:T(8,128)(2,1)S(1)}, u32[]{:S(2)}, u32[]{:S(2)}) collective-permute-start(bf16[2,24,1024]{2,1,0:T(8,128)(2,1)S(1)} %get-tuple-element.30.refs_0_), channel_id=1, source_target_pairs={{0,6},{2,4},{4,2},{6,0},{1,7},{3,5},{5,3},{7,1},{8,14},{10,12},{12... | collective-permute-start | bytes 294920 | tf_op jit(solution)/shard_map/ppermute | solution.py:62
  28.3 0.0 collective-permute-start.7
  28.3 1.9 %collective-permute-start.6 = (bf16[2,24,1024]{2,1,0:T(8,128)(2,1)S(1)}, bf16[2,24,1024]{2,1,0:T(8,128)(2,1)S(1)}, u32[]{:S(2)}, u32[]{:S(2)}) collective-permute-start(bf16[2,24,1024]{2,1,0:T(8,128)(2,1)S(1)} %get-tuple-element.30.refs_0_), channel_id=1, source_target_pairs={{0,2},{2,0},{4,6},{6,4},{1,3},{3,1},{5,7},{7,5},{8,10},{10,8},{12,... | collective-permute-start | bytes 294920 | tf_op jit(solution)/shard_map/ppermute | solution.py:62
  30.3 3.1 %collective-permute-done.8.refs_3_ = bf16[2,24,1024]{2,1,0:T(8,128)(2,1)S(1)} collective-permute-done((bf16[2,24,1024]{2,1,0:T(8,128)(2,1)S(1)}, bf16[2,24,1024]{2,1,0:T(8,128)(2,1)S(1)}, u32[]{:S(2)}, u32[]{:S(2)}) %collective-permute-start.8) | collective-permute-done | bytes 98336 | tf_op jit(solution)/shard_map/ppermute | solution.py:62
  33.4 2.5 %collective-permute-done.7.refs_2_ = bf16[2,24,1024]{2,1,0:T(8,128)(2,1)S(1)} collective-permute-done((bf16[2,24,1024]{2,1,0:T(8,128)(2,1)S(1)}, bf16[2,24,1024]{2,1,0:T(8,128)(2,1)S(1)}, u32[]{:S(2)}, u32[]{:S(2)}) %collective-permute-start.7) | collective-permute-done | bytes 98336 | tf_op jit(solution)/shard_map/ppermute | solution.py:62
  35.9 0.0 collective-permute-done.6.refs_1_
  35.9 1.2 %back_project.1 = (bf16[4,3,2,16,128]{4,3,2,1,0:T(8,128)(2,1)S(1)}, bf16[4,3,2,16,128]{4,3,2,1,0:T(8,128)(2,1)S(1)}) custom-call(s32[3,4,2,1,128]{4,3,2,1,0:T(1,128)S(1)} %limits.1.limits_ref, bf16[2,3,4,2,48,256]{5,4,3,2,1,0:T(8,128)(2,1)S(1)} %copy-done, bf16[2,3,4,2,48,256]{5,4,3,2,1,0:T(8,128)(2,1)S(1)} %copy-done.1, ...), custom_call_target="tpu_custom_call" | custom-call | flops 150994944 | bytes 2359296 | tf_op jit(solution)/shard_map/back_project/pallas_call | solution.py:394
  37.1 0.1 collective-permute-start.9
  37.2 1.3 %collective-permute-done.9.refs_1_ = bf16[4,3,2,16,128]{4,3,2,1,0:T(8,128)(2,1)S(1)} collective-permute-done((bf16[4,3,2,16,128]{4,3,2,1,0:T(8,128)(2,1)S(1)}, bf16[4,3,2,16,128]{4,3,2,1,0:T(8,128)(2,1)S(1)}, u32[]{:S(2)}, u32[]{:S(2)}) %collective-permute-start.9) | collective-permute-done | bytes 98336 | tf_op jit(solution)/shard_map/ppermute | solution.py:62
  38.5 1.7 %collective-permute-start.11 = (bf16[2,3,2,16,128]{4,3,2,1,0:T(8,128)(2,1)S(1)}, bf16[2,3,2,16,128]{4,3,2,1,0:T(8,128)(2,1)S(1)}, u32[]{:S(2)}, u32[]{:S(2)}) collective-permute-start(bf16[2,3,2,16,128]{4,3,2,1,0:T(8,128)(2,1)S(1)} %get-tuple-element.34), channel_id=1, source_target_pairs={{0,8},{1,17},{8,0},{9,25},{16,24},{17,1},{24,16},{25,9},{2,10},{3,... | collective-permute-start | bytes 147464 | tf_op jit(solution)/shard_map/ppermute | solution.py:455
  40.2 0.7 %collective-permute-start.10 = (bf16[1,3,2,16,128]{4,3,2,1,0:T(8,128)(2,1)S(1)}, bf16[1,3,2,16,128]{4,3,2,1,0:T(8,128)(2,1)S(1)}, u32[]{:S(2)}, u32[]{:S(2)}) collective-permute-start(bf16[1,3,2,16,128]{4,3,2,1,0:T(8,128)(2,1)S(1)} %get-tuple-element.33), channel_id=1, source_target_pairs={{0,24},{1,25},{8,16},{9,17},{16,8},{17,9},{24,0},{25,1},{2,26},{3,... | collective-permute-start | bytes 73736 | tf_op jit(solution)/shard_map/ppermute | solution.py:456
  40.9 2.1 %collective-permute-done.11.pair_ref.refs_2_ = bf16[2,3,2,16,128]{4,3,2,1,0:T(8,128)(2,1)S(1)} collective-permute-done((bf16[2,3,2,16,128]{4,3,2,1,0:T(8,128)(2,1)S(1)}, bf16[2,3,2,16,128]{4,3,2,1,0:T(8,128)(2,1)S(1)}, u32[]{:S(2)}, u32[]{:S(2)}) %collective-permute-start.11) | collective-permute-done | bytes 49184 | tf_op jit(solution)/shard_map/ppermute | solution.py:455
  42.9 0.0 collective-permute-start.12
  42.9 0.7 %pad_maximum_fusion = f32[2,24,1024]{2,1,0:T(8,128)} fusion(f32[1,24,1024]{2,1,0:T(8,128)S(1)} %bitcast.5, f32[1,24,1024]{2,1,0:T(8,128)S(1)} %bitcast.4), kind=kLoop, calls=%fused_computation | loop fusion | flops 49152 | bytes 393216 | tf_op jit(solution)/shard_map/stack | solution.py:541
  43.6 1.3 %collective-permute-done.10.refs_0_ = bf16[1,3,2,16,128]{4,3,2,1,0:T(8,128)(2,1)S(1)} collective-permute-done((bf16[1,3,2,16,128]{4,3,2,1,0:T(8,128)(2,1)S(1)}, bf16[1,3,2,16,128]{4,3,2,1,0:T(8,128)(2,1)S(1)}, u32[]{:S(2)}, u32[]{:S(2)}) %collective-permute-start.10) | collective-permute-done | bytes 24608 | tf_op jit(solution)/shard_map/ppermute | solution.py:456
  44.9 0.0 collective-permute-done.12.refs_1_
  44.9 2.5 %gradient.1 = bf16[4,16,32,1024]{3,2,1,0:T(8,128)(2,1)} custom-call(bf16[24,1024]{1,0:T(8,128)(2,1)S(1)} %get-tuple-element.19.table_ref, bf16[1,3,2,16,128]{4,3,2,1,0:T(8,128)(2,1)S(1)} %collective-permute-done.10.refs_0_, bf16[1,3,2,16,128]{4,3,2,1,0:T(8,128)(2,1)S(1)} %collective-permute-done.12.refs_1_, ...), custom_call_target="tpu_custom_call" | custom-call | tf_op jit(solution)/shard_map/gradient/pallas_call | solution.py:509
  (2 shorter events, 0.0 us)
Async XLA Ops:
  0.6 9.3 %copy-start.3 = (s32[3,4,2]{1,2,0:T(2,128)S(1)}, s32[3,4,2]{1,2,0:T(2,128)}, u32[]{:S(2)}) copy-start(s32[3,4,2]{1,2,0:T(2,128)} %param.8) | copy-start | bytes 292
  0.6 9.9 %copy-start = (bf16[2,3,4,2,48,256]{5,4,3,2,1,0:T(8,128)(2,1)S(1)}, bf16[2,3,4,2,48,256]{5,4,3,2,1,0:T(8,128)(2,1)}, u32[]{:S(2)}) copy-start(bf16[2,3,4,2,48,256]{5,4,3,2,1,0:T(8,128)(2,1)} %right_ref.5) | copy-start | bytes 3538948
  0.7 13.4 %copy-start.1 = (bf16[2,3,4,2,48,256]{5,4,3,2,1,0:T(8,128)(2,1)S(1)}, bf16[2,3,4,2,48,256]{5,4,3,2,1,0:T(8,128)(2,1)}, u32[]{:S(2)}) copy-start(bf16[2,3,4,2,48,256]{5,4,3,2,1,0:T(8,128)(2,1)} %left_ref.3) | copy-start | bytes 3538948
  0.7 25.1 %copy-start.2 = (f32[2,24,1024]{2,1,0:T(8,128)S(1)}, f32[2,24,1024]{2,1,0:T(8,128)}, u32[]{:S(2)}) copy-start(f32[2,24,1024]{2,1,0:T(8,128)} %data_ref.1) | copy-start | bytes 589828
  5.4 5.1 %collective-permute-start = (bf16[3,2,32,128]{3,2,1,0:T(8,128)(2,1)S(1)}, bf16[3,2,32,128]{3,2,1,0:T(8,128)(2,1)S(1)}, u32[]{:S(2)}, u32[]{:S(2)}) collective-permute-start(bf16[3,2,32,128]{3,2,1,0:T(8,128)(2,1)S(1)} %get-tuple-element.21), channel_id=1, source_target_pairs={{0,8},{8,0},{16,24},{24,16},{1,9},{9,1},{17,25},{25,17},{2,10},{10... | collective-permute-start | bytes 147464 | tf_op jit(solution)/shard_map/ppermute | solution.py:62
  8.4 5.0 %collective-permute-start.1 = (bf16[3,2,32,128]{3,2,1,0:T(8,128)(2,1)S(1)}, bf16[3,2,32,128]{3,2,1,0:T(8,128)(2,1)S(1)}, u32[]{:S(2)}, u32[]{:S(2)}) collective-permute-start(bf16[3,2,32,128]{3,2,1,0:T(8,128)(2,1)S(1)} %get-tuple-element.22), channel_id=1, source_target_pairs={{0,24},{8,16},{16,8},{24,0},{1,25},{9,17},{17,9},{25,1},{2,26},{10... | collective-permute-start | bytes 147464 | tf_op jit(solution)/shard_map/ppermute | solution.py:62
  9.9 4.1 %collective-permute-start.2 = (bf16[3,2,32,128]{3,2,1,0:T(8,128)(2,1)S(1)}, bf16[3,2,32,128]{3,2,1,0:T(8,128)(2,1)S(1)}, u32[]{:S(2)}, u32[]{:S(2)}) collective-permute-start(bf16[3,2,32,128]{3,2,1,0:T(8,128)(2,1)S(1)} %get-tuple-element.23), channel_id=1, source_target_pairs={{0,16},{8,24},{16,0},{24,8},{1,17},{9,25},{17,1},{25,9},{2,18},{10... | collective-permute-start | bytes 147464 | tf_op jit(solution)/shard_map/ppermute | solution.py:62
  15.0 6.6 %collective-permute-start.3 = (bf16[2,24,1024]{2,1,0:T(8,128)(2,1)S(1)}, bf16[2,24,1024]{2,1,0:T(8,128)(2,1)S(1)}, u32[]{:S(2)}, u32[]{:S(2)}) collective-permute-start(bf16[2,24,1024]{2,1,0:T(8,128)(2,1)S(1)} %get-tuple-element.24), channel_id=1, source_target_pairs={{0,6},{2,4},{4,2},{6,0},{1,7},{3,5},{5,3},{7,1},{8,14},{10,12},{12... | collective-permute-start | bytes 294920 | tf_op jit(solution)/shard_map/ppermute | solution.py:62
  18.7 7.0 %collective-permute-start.4 = (bf16[2,24,1024]{2,1,0:T(8,128)(2,1)S(1)}, bf16[2,24,1024]{2,1,0:T(8,128)(2,1)S(1)}, u32[]{:S(2)}, u32[]{:S(2)}) collective-permute-start(bf16[2,24,1024]{2,1,0:T(8,128)(2,1)S(1)} %get-tuple-element.25), channel_id=1, source_target_pairs={{0,4},{2,6},{4,0},{6,2},{1,5},{3,7},{5,1},{7,3},{8,12},{10,14},{12... | collective-permute-start | bytes 294920 | tf_op jit(solution)/shard_map/ppermute | solution.py:62
  18.7 7.0 %collective-permute-start.5 = (bf16[2,24,1024]{2,1,0:T(8,128)(2,1)S(1)}, bf16[2,24,1024]{2,1,0:T(8,128)(2,1)S(1)}, u32[]{:S(2)}, u32[]{:S(2)}) collective-permute-start(bf16[2,24,1024]{2,1,0:T(8,128)(2,1)S(1)} %get-tuple-element.26), channel_id=1, source_target_pairs={{0,2},{2,0},{4,6},{6,4},{1,3},{3,1},{5,7},{7,5},{8,10},{10,8},{12,... | collective-permute-start | bytes 294920 | tf_op jit(solution)/shard_map/ppermute | solution.py:62
  25.8 7.6 %collective-permute-start.8 = (bf16[2,24,1024]{2,1,0:T(8,128)(2,1)S(1)}, bf16[2,24,1024]{2,1,0:T(8,128)(2,1)S(1)}, u32[]{:S(2)}, u32[]{:S(2)}) collective-permute-start(bf16[2,24,1024]{2,1,0:T(8,128)(2,1)S(1)} %get-tuple-element.30.refs_0_), channel_id=1, source_target_pairs={{0,6},{2,4},{4,2},{6,0},{1,7},{3,5},{5,3},{7,1},{8,14},{10,12},{12... | collective-permute-start | bytes 294920 | tf_op jit(solution)/shard_map/ppermute | solution.py:62
  28.3 7.6 %collective-permute-start.7 = (bf16[2,24,1024]{2,1,0:T(8,128)(2,1)S(1)}, bf16[2,24,1024]{2,1,0:T(8,128)(2,1)S(1)}, u32[]{:S(2)}, u32[]{:S(2)}) collective-permute-start(bf16[2,24,1024]{2,1,0:T(8,128)(2,1)S(1)} %get-tuple-element.30.refs_0_), channel_id=1, source_target_pairs={{0,4},{2,6},{4,0},{6,2},{1,5},{3,7},{5,1},{7,3},{8,12},{10,14},{12... | collective-permute-start | bytes 294920 | tf_op jit(solution)/shard_map/ppermute | solution.py:62
  28.3 7.6 %collective-permute-start.6 = (bf16[2,24,1024]{2,1,0:T(8,128)(2,1)S(1)}, bf16[2,24,1024]{2,1,0:T(8,128)(2,1)S(1)}, u32[]{:S(2)}, u32[]{:S(2)}) collective-permute-start(bf16[2,24,1024]{2,1,0:T(8,128)(2,1)S(1)} %get-tuple-element.30.refs_0_), channel_id=1, source_target_pairs={{0,2},{2,0},{4,6},{6,4},{1,3},{3,1},{5,7},{7,5},{8,10},{10,8},{12,... | collective-permute-start | bytes 294920 | tf_op jit(solution)/shard_map/ppermute | solution.py:62
  37.1 1.4 %collective-permute-start.9 = (bf16[4,3,2,16,128]{4,3,2,1,0:T(8,128)(2,1)S(1)}, bf16[4,3,2,16,128]{4,3,2,1,0:T(8,128)(2,1)S(1)}, u32[]{:S(2)}, u32[]{:S(2)}) collective-permute-start(bf16[4,3,2,16,128]{4,3,2,1,0:T(8,128)(2,1)S(1)} %get-tuple-element.32), channel_id=1, source_target_pairs={{0,1},{1,0},{2,3},{3,2},{4,5},{5,4},{6,7},{7,6},{8,9},{9,8},{10,11... | collective-permute-start | bytes 294920 | tf_op jit(solution)/shard_map/ppermute | solution.py:62
  38.5 4.4 %collective-permute-start.11 = (bf16[2,3,2,16,128]{4,3,2,1,0:T(8,128)(2,1)S(1)}, bf16[2,3,2,16,128]{4,3,2,1,0:T(8,128)(2,1)S(1)}, u32[]{:S(2)}, u32[]{:S(2)}) collective-permute-start(bf16[2,3,2,16,128]{4,3,2,1,0:T(8,128)(2,1)S(1)} %get-tuple-element.34), channel_id=1, source_target_pairs={{0,8},{1,17},{8,0},{9,25},{16,24},{17,1},{24,16},{25,9},{2,10},{3,... | collective-permute-start | bytes 147464 | tf_op jit(solution)/shard_map/ppermute | solution.py:455
  40.2 4.7 %collective-permute-start.10 = (bf16[1,3,2,16,128]{4,3,2,1,0:T(8,128)(2,1)S(1)}, bf16[1,3,2,16,128]{4,3,2,1,0:T(8,128)(2,1)S(1)}, u32[]{:S(2)}, u32[]{:S(2)}) collective-permute-start(bf16[1,3,2,16,128]{4,3,2,1,0:T(8,128)(2,1)S(1)} %get-tuple-element.33), channel_id=1, source_target_pairs={{0,24},{1,25},{8,16},{9,17},{16,8},{17,9},{24,0},{25,1},{2,26},{3,... | collective-permute-start | bytes 73736 | tf_op jit(solution)/shard_map/ppermute | solution.py:456
  42.9 2.0 %collective-permute-start.12 = (bf16[1,3,2,16,128]{4,3,2,1,0:T(8,128)(2,1)S(1)}, bf16[1,3,2,16,128]{4,3,2,1,0:T(8,128)(2,1)S(1)}, u32[]{:S(2)}, u32[]{:S(2)}) collective-permute-start(bf16[1,3,2,16,128]{4,3,2,1,0:T(8,128)(2,1)S(1)} %other.1), channel_id=1, source_target_pairs={{0,1},{1,0},{2,3},{3,2},{4,5},{5,4},{6,7},{7,6},{8,9},{9,8},{10,11... | collective-permute-start | bytes 73736 | tf_op jit(solution)/shard_map/ppermute | solution.py:457

commit v16 on v13

--- a/solution.py
+++ b/solution.py
@@ -17,8 +17,13 @@
     sample = lax.broadcasted_iota(jnp.int32, (bins, length), 1)
     is_sine = row >= bins // 2
     freq_bin = jnp.where(is_sine, row - bins // 2, row) + 1
-    phase = lax.rem(freq_bin * sample, length) + jnp.where(is_sine, length // 4, 0)
-    quarter = lax.div(phase + length // 8, length // 4)
+    phase = freq_bin * sample + jnp.where(is_sine, length // 4, 0)
+    if length & (length - 1) == 0:
+        phase = phase & (length - 1)
+        quarter = (phase + length // 8) >> (length.bit_length() - 3)
+    else:
+        phase = lax.rem(phase, length)
+        quarter = lax.div(phase + length // 8, length // 4)
     angle = (phase - quarter * (length // 4)).astype(jnp.float32) * (2.0 * math.pi / length)
     square = angle * angle
     even = 1.0

time: 47.6 us -> 47.6 us (level)
  no operation moved by 1% of the time
where the time goes in v16:
time: 47.6 us; the launch traced here: 47.5 us
  waiting for transfers between devices  19.8 us (42%)
  starting transfers between devices  15.9 us (33%)
  Pallas kernels  10.2 us (21%)
  between operations  0.73 us (2%)
  other arithmetic  0.7 us (1%)
    ppermute x10, waiting for transfers between devices, exchange(): arrived.append(lax.ppermute(blocks[step], axis, pairs))  16.5 us
    ppermute x10, starting transfers between devices, exchange(): arrived.append(lax.ppermute(blocks[step], axis, pairs))  13.5 us
    pallas_call x1, Pallas kernels, spectrum_of(): pl.pallas_call(spectrum_kernel, in_specs=[pl.BlockSpec(memory_space=pltpu...  4.75 us
    pallas_call x1, Pallas kernels, gradient_of(): pl.pallas_call(functools.partial(gradient_kernel, reps), in_specs=[pl.Blo...  2.51 us
    ppermute x1, waiting for transfers between devices, return_spectra(): pair = lax.ppermute(pair, ('freq', 'rep'), near)  2.06 us
    ppermute x1, starting transfers between devices, return_spectra(): pair = lax.ppermute(pair, ('freq', 'rep'), near)  1.7 us
    ppermute x1, waiting for transfers between devices, return_spectra(): last = lax.ppermute(last, ('freq', 'rep'), far)  1.31 us
    pallas_call x1, Pallas kernels, back_project(): pl.pallas_call(functools.partial(back_kernel, parts, groups, reps), in_sp...  1.2 us
  transfers between devices with their start and end apart: 13, of which 10 were waited for; matrix products, arithmetic and copies ran while one was open for 2% of the time, Pallas kernels for 1%

profile of v16, /device:TPU:0, one launch (start us, length us, event | category | flops | bytes accessed | tf_op | source)
XLA Modules:
  0.0 47.5 jit_solution(12260057486265887898)
XLA Ops:
  0.6 0.0 copy-start.3
  0.6 0.0 copy-start
  0.7 0.0 copy-start.1
  0.7 0.0 copy-start.2
  0.7 4.7 %spectrum.1 = (bf16[24,1024]{1,0:T(8,128)(2,1)S(1)}, bf16[3,2,32,128]{3,2,1,0:T(8,128)(2,1)S(1)}, bf16[3,2,32,128]{3,2,1,0:T(8,128)(2,1)S(1)}, bf16[3,2,32,128]{...) custom-call(bf16[4,32,32,1024]{3,2,1,0:T(8,128)(2,1)} %bitcast.6), custom_call_target="tpu_custom_call" | custom-call | tf_op jit(solution)/shard_map/spectrum/pallas_call | solution.py:126
  5.4 3.0 %collective-permute-start = (bf16[3,2,32,128]{3,2,1,0:T(8,128)(2,1)S(1)}, bf16[3,2,32,128]{3,2,1,0:T(8,128)(2,1)S(1)}, u32[]{:S(2)}, u32[]{:S(2)}) collective-permute-start(bf16[3,2,32,128]{3,2,1,0:T(8,128)(2,1)S(1)} %get-tuple-element.21), channel_id=1, source_target_pairs={{0,8},{8,0},{16,24},{24,16},{1,9},{9,1},{17,25},{25,17},{2,10},{10... | collective-permute-start | bytes 147464 | tf_op jit(solution)/shard_map/ppermute | solution.py:67
  8.4 1.5 %collective-permute-start.1 = (bf16[3,2,32,128]{3,2,1,0:T(8,128)(2,1)S(1)}, bf16[3,2,32,128]{3,2,1,0:T(8,128)(2,1)S(1)}, u32[]{:S(2)}, u32[]{:S(2)}) collective-permute-start(bf16[3,2,32,128]{3,2,1,0:T(8,128)(2,1)S(1)} %get-tuple-element.22), channel_id=1, source_target_pairs={{0,24},{8,16},{16,8},{24,0},{1,25},{9,17},{17,9},{25,1},{2,26},{10... | collective-permute-start | bytes 147464 | tf_op jit(solution)/shard_map/ppermute | solution.py:67
  9.9 0.0 collective-permute-start.2
  10.0 0.0 copy-done.3
  10.0 0.1 copy.7.ranks_ref
  10.1 0.1 limits.1.limits_ref
  10.2 0.3 collective-permute-done.refs_1_
  10.5 0.0 copy-done
  10.5 0.6 %project.1.own_ref = bf16[3,4,48,64]{3,2,1,0:T(8,128)(2,1)S(1)} custom-call(s32[3,4,2,1,128]{4,3,2,1,0:T(1,128)S(1)} %limits.1.limits_ref, bf16[2,3,4,2,48,256]{5,4,3,2,1,0:T(8,128)(2,1)S(1)} %copy-done, bf16[3,2,32,128]{3,2,1,0:T(8,128)(2,1)S(1)} %get-tuple-element.20.refs_0_, bf16[3,2,32,128]{3,2,1,0:T(8,128)(2,1)S(1)} %collective-permute-done.refs_1_), custom_call_target="tpu_custom_call" | custom-call | flops 37748736 | bytes 1179648 | tf_op jit(solution)/shard_map/project/pallas_call | solution.py:232
  11.1 2.3 %collective-permute-done.1.refs_0_ = bf16[3,2,32,128]{3,2,1,0:T(8,128)(2,1)S(1)} collective-permute-done((bf16[3,2,32,128]{3,2,1,0:T(8,128)(2,1)S(1)}, bf16[3,2,32,128]{3,2,1,0:T(8,128)(2,1)S(1)}, u32[]{:S(2)}, u32[]{:S(2)}) %collective-permute-start.1) | collective-permute-done | bytes 49184 | tf_op jit(solution)/shard_map/ppermute | solution.py:67
  13.4 0.6 %collective-permute-done.2.refs_1_ = bf16[3,2,32,128]{3,2,1,0:T(8,128)(2,1)S(1)} collective-permute-done((bf16[3,2,32,128]{3,2,1,0:T(8,128)(2,1)S(1)}, bf16[3,2,32,128]{3,2,1,0:T(8,128)(2,1)S(1)}, u32[]{:S(2)}, u32[]{:S(2)}) %collective-permute-start.2) | collective-permute-done | bytes 49184 | tf_op jit(solution)/shard_map/ppermute | solution.py:67
  14.0 0.0 copy-done.1
  14.0 1.0 %predict.1 = (bf16[2,24,1024]{2,1,0:T(8,128)(2,1)S(1)}, bf16[2,24,1024]{2,1,0:T(8,128)(2,1)S(1)}, bf16[2,24,1024]{2,1,0:T(8,128)(2,1)S(1)}, bf16[2,24,1024]{2,1,0:T(8,128)(2,1)S(1)}) custom-call(s32[3,4,2,1,128]{4,3,2,1,0:T(1,128)S(1)} %limits.1.limits_ref, bf16[2,3,4,2,48,256]{5,4,3,2,1,0:T(8,128)(2,1)S(1)} %copy-done, ...), custom_call_target="tpu_custom_call" | custom-call | flops 150994944 | bytes 2359296 | tf_op jit(solution)/shard_map/predict/pallas_call | solution.py:288
  15.0 3.7 %collective-permute-start.3 = (bf16[2,24,1024]{2,1,0:T(8,128)(2,1)S(1)}, bf16[2,24,1024]{2,1,0:T(8,128)(2,1)S(1)}, u32[]{:S(2)}, u32[]{:S(2)}) collective-permute-start(bf16[2,24,1024]{2,1,0:T(8,128)(2,1)S(1)} %get-tuple-element.24), channel_id=1, source_target_pairs={{0,6},{2,4},{4,2},{6,0},{1,7},{3,5},{5,3},{7,1},{8,14},{10,12},{12... | collective-permute-start | bytes 294920 | tf_op jit(solution)/shard_map/ppermute | solution.py:67
  18.7 0.0 collective-permute-start.4
  18.7 0.8 %collective-permute-start.5 = (bf16[2,24,1024]{2,1,0:T(8,128)(2,1)S(1)}, bf16[2,24,1024]{2,1,0:T(8,128)(2,1)S(1)}, u32[]{:S(2)}, u32[]{:S(2)}) collective-permute-start(bf16[2,24,1024]{2,1,0:T(8,128)(2,1)S(1)} %get-tuple-element.26), channel_id=1, source_target_pairs={{0,2},{2,0},{4,6},{6,4},{1,3},{3,1},{5,7},{7,5},{8,10},{10,8},{12,... | collective-permute-start | bytes 294920 | tf_op jit(solution)/shard_map/ppermute | solution.py:67
  19.5 2.1 %collective-permute-done.3.refs_0_ = bf16[2,24,1024]{2,1,0:T(8,128)(2,1)S(1)} collective-permute-done((bf16[2,24,1024]{2,1,0:T(8,128)(2,1)S(1)}, bf16[2,24,1024]{2,1,0:T(8,128)(2,1)S(1)}, u32[]{:S(2)}, u32[]{:S(2)}) %collective-permute-start.3) | collective-permute-done | bytes 98336 | tf_op jit(solution)/shard_map/ppermute | solution.py:67
  21.6 4.1 %collective-permute-done.4.refs_1_ = bf16[2,24,1024]{2,1,0:T(8,128)(2,1)S(1)} collective-permute-done((bf16[2,24,1024]{2,1,0:T(8,128)(2,1)S(1)}, bf16[2,24,1024]{2,1,0:T(8,128)(2,1)S(1)}, u32[]{:S(2)}, u32[]{:S(2)}) %collective-permute-start.4) | collective-permute-done | bytes 98336 | tf_op jit(solution)/shard_map/ppermute | solution.py:67
  25.7 0.0 collective-permute-done.5.refs_2_
  25.7 0.0 copy-done.2
  25.7 0.1 residual.1
  25.8 2.5 %collective-permute-start.8 = (bf16[2,24,1024]{2,1,0:T(8,128)(2,1)S(1)}, bf16[2,24,1024]{2,1,0:T(8,128)(2,1)S(1)}, u32[]{:S(2)}, u32[]{:S(2)}) collective-permute-start(bf16[2,24,1024]{2,1,0:T(8,128)(2,1)S(1)} %get-tuple-element.30.refs_0_), channel_id=1, source_target_pairs={{0,6},{2,4},{4,2},{6,0},{1,7},{3,5},{5,3},{7,1},{8,14},{10,12},{12... | collective-permute-start | bytes 294920 | tf_op jit(solution)/shard_map/ppermute | solution.py:67
  28.3 0.0 collective-permute-start.7
  28.3 1.9 %collective-permute-start.6 = (bf16[2,24,1024]{2,1,0:T(8,128)(2,1)S(1)}, bf16[2,24,1024]{2,1,0:T(8,128)(2,1)S(1)}, u32[]{:S(2)}, u32[]{:S(2)}) collective-permute-start(bf16[2,24,1024]{2,1,0:T(8,128)(2,1)S(1)} %get-tuple-element.30.refs_0_), channel_id=1, source_target_pairs={{0,2},{2,0},{4,6},{6,4},{1,3},{3,1},{5,7},{7,5},{8,10},{10,8},{12,... | collective-permute-start | bytes 294920 | tf_op jit(solution)/shard_map/ppermute | solution.py:67
  30.3 3.1 %collective-permute-done.8.refs_3_ = bf16[2,24,1024]{2,1,0:T(8,128)(2,1)S(1)} collective-permute-done((bf16[2,24,1024]{2,1,0:T(8,128)(2,1)S(1)}, bf16[2,24,1024]{2,1,0:T(8,128)(2,1)S(1)}, u32[]{:S(2)}, u32[]{:S(2)}) %collective-permute-start.8) | collective-permute-done | bytes 98336 | tf_op jit(solution)/shard_map/ppermute | solution.py:67
  33.4 2.5 %collective-permute-done.7.refs_2_ = bf16[2,24,1024]{2,1,0:T(8,128)(2,1)S(1)} collective-permute-done((bf16[2,24,1024]{2,1,0:T(8,128)(2,1)S(1)}, bf16[2,24,1024]{2,1,0:T(8,128)(2,1)S(1)}, u32[]{:S(2)}, u32[]{:S(2)}) %collective-permute-start.7) | collective-permute-done | bytes 98336 | tf_op jit(solution)/shard_map/ppermute | solution.py:67
  35.9 0.0 collective-permute-done.6.refs_1_
  35.9 1.2 %back_project.1 = (bf16[4,3,2,16,128]{4,3,2,1,0:T(8,128)(2,1)S(1)}, bf16[4,3,2,16,128]{4,3,2,1,0:T(8,128)(2,1)S(1)}) custom-call(s32[3,4,2,1,128]{4,3,2,1,0:T(1,128)S(1)} %limits.1.limits_ref, bf16[2,3,4,2,48,256]{5,4,3,2,1,0:T(8,128)(2,1)S(1)} %copy-done, bf16[2,3,4,2,48,256]{5,4,3,2,1,0:T(8,128)(2,1)S(1)} %copy-done.1, ...), custom_call_target="tpu_custom_call" | custom-call | flops 150994944 | bytes 2359296 | tf_op jit(solution)/shard_map/back_project/pallas_call | solution.py:399
  37.1 0.1 collective-permute-start.9
  37.2 1.3 %collective-permute-done.9.refs_1_ = bf16[4,3,2,16,128]{4,3,2,1,0:T(8,128)(2,1)S(1)} collective-permute-done((bf16[4,3,2,16,128]{4,3,2,1,0:T(8,128)(2,1)S(1)}, bf16[4,3,2,16,128]{4,3,2,1,0:T(8,128)(2,1)S(1)}, u32[]{:S(2)}, u32[]{:S(2)}) %collective-permute-start.9) | collective-permute-done | bytes 98336 | tf_op jit(solution)/shard_map/ppermute | solution.py:67
  38.5 1.7 %collective-permute-start.11 = (bf16[2,3,2,16,128]{4,3,2,1,0:T(8,128)(2,1)S(1)}, bf16[2,3,2,16,128]{4,3,2,1,0:T(8,128)(2,1)S(1)}, u32[]{:S(2)}, u32[]{:S(2)}) collective-permute-start(bf16[2,3,2,16,128]{4,3,2,1,0:T(8,128)(2,1)S(1)} %get-tuple-element.34), channel_id=1, source_target_pairs={{0,8},{1,17},{8,0},{9,25},{16,24},{17,1},{24,16},{25,9},{2,10},{3,... | collective-permute-start | bytes 147464 | tf_op jit(solution)/shard_map/ppermute | solution.py:460
  40.2 0.7 %collective-permute-start.10 = (bf16[1,3,2,16,128]{4,3,2,1,0:T(8,128)(2,1)S(1)}, bf16[1,3,2,16,128]{4,3,2,1,0:T(8,128)(2,1)S(1)}, u32[]{:S(2)}, u32[]{:S(2)}) collective-permute-start(bf16[1,3,2,16,128]{4,3,2,1,0:T(8,128)(2,1)S(1)} %get-tuple-element.33), channel_id=1, source_target_pairs={{0,24},{1,25},{8,16},{9,17},{16,8},{17,9},{24,0},{25,1},{2,26},{3,... | collective-permute-start | bytes 73736 | tf_op jit(solution)/shard_map/ppermute | solution.py:461
  40.9 2.1 %collective-permute-done.11.pair_ref.refs_2_ = bf16[2,3,2,16,128]{4,3,2,1,0:T(8,128)(2,1)S(1)} collective-permute-done((bf16[2,3,2,16,128]{4,3,2,1,0:T(8,128)(2,1)S(1)}, bf16[2,3,2,16,128]{4,3,2,1,0:T(8,128)(2,1)S(1)}, u32[]{:S(2)}, u32[]{:S(2)}) %collective-permute-start.11) | collective-permute-done | bytes 49184 | tf_op jit(solution)/shard_map/ppermute | solution.py:460
  42.9 0.0 collective-permute-start.12
  42.9 0.7 %pad_maximum_fusion = f32[2,24,1024]{2,1,0:T(8,128)} fusion(f32[1,24,1024]{2,1,0:T(8,128)S(1)} %bitcast.5, f32[1,24,1024]{2,1,0:T(8,128)S(1)} %bitcast.4), kind=kLoop, calls=%fused_computation | loop fusion | flops 49152 | bytes 393216 | tf_op jit(solution)/shard_map/stack | solution.py:546
  43.6 1.3 %collective-permute-done.10.refs_0_ = bf16[1,3,2,16,128]{4,3,2,1,0:T(8,128)(2,1)S(1)} collective-permute-done((bf16[1,3,2,16,128]{4,3,2,1,0:T(8,128)(2,1)S(1)}, bf16[1,3,2,16,128]{4,3,2,1,0:T(8,128)(2,1)S(1)}, u32[]{:S(2)}, u32[]{:S(2)}) %collective-permute-start.10) | collective-permute-done | bytes 24608 | tf_op jit(solution)/shard_map/ppermute | solution.py:461
  44.9 0.0 collective-permute-done.12.refs_1_
  44.9 2.5 %gradient.1 = bf16[4,16,32,1024]{3,2,1,0:T(8,128)(2,1)} custom-call(bf16[24,1024]{1,0:T(8,128)(2,1)S(1)} %get-tuple-element.19.table_ref, bf16[1,3,2,16,128]{4,3,2,1,0:T(8,128)(2,1)S(1)} %collective-permute-done.10.refs_0_, bf16[1,3,2,16,128]{4,3,2,1,0:T(8,128)(2,1)S(1)} %collective-permute-done.12.refs_1_, ...), custom_call_target="tpu_custom_call" | custom-call | tf_op jit(solution)/shard_map/gradient/pallas_call | solution.py:514
  (2 shorter events, 0.0 us)
Async XLA Ops:
  0.6 9.3 %copy-start.3 = (s32[3,4,2]{1,2,0:T(2,128)S(1)}, s32[3,4,2]{1,2,0:T(2,128)}, u32[]{:S(2)}) copy-start(s32[3,4,2]{1,2,0:T(2,128)} %param.8) | copy-start | bytes 292
  0.6 9.9 %copy-start = (bf16[2,3,4,2,48,256]{5,4,3,2,1,0:T(8,128)(2,1)S(1)}, bf16[2,3,4,2,48,256]{5,4,3,2,1,0:T(8,128)(2,1)}, u32[]{:S(2)}) copy-start(bf16[2,3,4,2,48,256]{5,4,3,2,1,0:T(8,128)(2,1)} %right_ref.5) | copy-start | bytes 3538948
  0.7 13.4 %copy-start.1 = (bf16[2,3,4,2,48,256]{5,4,3,2,1,0:T(8,128)(2,1)S(1)}, bf16[2,3,4,2,48,256]{5,4,3,2,1,0:T(8,128)(2,1)}, u32[]{:S(2)}) copy-start(bf16[2,3,4,2,48,256]{5,4,3,2,1,0:T(8,128)(2,1)} %left_ref.3) | copy-start | bytes 3538948
  0.7 25.1 %copy-start.2 = (f32[2,24,1024]{2,1,0:T(8,128)S(1)}, f32[2,24,1024]{2,1,0:T(8,128)}, u32[]{:S(2)}) copy-start(f32[2,24,1024]{2,1,0:T(8,128)} %data_ref.1) | copy-start | bytes 589828
  5.4 5.1 %collective-permute-start = (bf16[3,2,32,128]{3,2,1,0:T(8,128)(2,1)S(1)}, bf16[3,2,32,128]{3,2,1,0:T(8,128)(2,1)S(1)}, u32[]{:S(2)}, u32[]{:S(2)}) collective-permute-start(bf16[3,2,32,128]{3,2,1,0:T(8,128)(2,1)S(1)} %get-tuple-element.21), channel_id=1, source_target_pairs={{0,8},{8,0},{16,24},{24,16},{1,9},{9,1},{17,25},{25,17},{2,10},{10... | collective-permute-start | bytes 147464 | tf_op jit(solution)/shard_map/ppermute | solution.py:67
  8.4 5.0 %collective-permute-start.1 = (bf16[3,2,32,128]{3,2,1,0:T(8,128)(2,1)S(1)}, bf16[3,2,32,128]{3,2,1,0:T(8,128)(2,1)S(1)}, u32[]{:S(2)}, u32[]{:S(2)}) collective-permute-start(bf16[3,2,32,128]{3,2,1,0:T(8,128)(2,1)S(1)} %get-tuple-element.22), channel_id=1, source_target_pairs={{0,24},{8,16},{16,8},{24,0},{1,25},{9,17},{17,9},{25,1},{2,26},{10... | collective-permute-start | bytes 147464 | tf_op jit(solution)/shard_map/ppermute | solution.py:67
  9.9 4.1 %collective-permute-start.2 = (bf16[3,2,32,128]{3,2,1,0:T(8,128)(2,1)S(1)}, bf16[3,2,32,128]{3,2,1,0:T(8,128)(2,1)S(1)}, u32[]{:S(2)}, u32[]{:S(2)}) collective-permute-start(bf16[3,2,32,128]{3,2,1,0:T(8,128)(2,1)S(1)} %get-tuple-element.23), channel_id=1, source_target_pairs={{0,16},{8,24},{16,0},{24,8},{1,17},{9,25},{17,1},{25,9},{2,18},{10... | collective-permute-start | bytes 147464 | tf_op jit(solution)/shard_map/ppermute | solution.py:67
  15.0 6.6 %collective-permute-start.3 = (bf16[2,24,1024]{2,1,0:T(8,128)(2,1)S(1)}, bf16[2,24,1024]{2,1,0:T(8,128)(2,1)S(1)}, u32[]{:S(2)}, u32[]{:S(2)}) collective-permute-start(bf16[2,24,1024]{2,1,0:T(8,128)(2,1)S(1)} %get-tuple-element.24), channel_id=1, source_target_pairs={{0,6},{2,4},{4,2},{6,0},{1,7},{3,5},{5,3},{7,1},{8,14},{10,12},{12... | collective-permute-start | bytes 294920 | tf_op jit(solution)/shard_map/ppermute | solution.py:67
  18.7 7.0 %collective-permute-start.4 = (bf16[2,24,1024]{2,1,0:T(8,128)(2,1)S(1)}, bf16[2,24,1024]{2,1,0:T(8,128)(2,1)S(1)}, u32[]{:S(2)}, u32[]{:S(2)}) collective-permute-start(bf16[2,24,1024]{2,1,0:T(8,128)(2,1)S(1)} %get-tuple-element.25), channel_id=1, source_target_pairs={{0,4},{2,6},{4,0},{6,2},{1,5},{3,7},{5,1},{7,3},{8,12},{10,14},{12... | collective-permute-start | bytes 294920 | tf_op jit(solution)/shard_map/ppermute | solution.py:67
  18.7 7.0 %collective-permute-start.5 = (bf16[2,24,1024]{2,1,0:T(8,128)(2,1)S(1)}, bf16[2,24,1024]{2,1,0:T(8,128)(2,1)S(1)}, u32[]{:S(2)}, u32[]{:S(2)}) collective-permute-start(bf16[2,24,1024]{2,1,0:T(8,128)(2,1)S(1)} %get-tuple-element.26), channel_id=1, source_target_pairs={{0,2},{2,0},{4,6},{6,4},{1,3},{3,1},{5,7},{7,5},{8,10},{10,8},{12,... | collective-permute-start | bytes 294920 | tf_op jit(solution)/shard_map/ppermute | solution.py:67
  25.8 7.6 %collective-permute-start.8 = (bf16[2,24,1024]{2,1,0:T(8,128)(2,1)S(1)}, bf16[2,24,1024]{2,1,0:T(8,128)(2,1)S(1)}, u32[]{:S(2)}, u32[]{:S(2)}) collective-permute-start(bf16[2,24,1024]{2,1,0:T(8,128)(2,1)S(1)} %get-tuple-element.30.refs_0_), channel_id=1, source_target_pairs={{0,6},{2,4},{4,2},{6,0},{1,7},{3,5},{5,3},{7,1},{8,14},{10,12},{12... | collective-permute-start | bytes 294920 | tf_op jit(solution)/shard_map/ppermute | solution.py:67
  28.3 7.6 %collective-permute-start.7 = (bf16[2,24,1024]{2,1,0:T(8,128)(2,1)S(1)}, bf16[2,24,1024]{2,1,0:T(8,128)(2,1)S(1)}, u32[]{:S(2)}, u32[]{:S(2)}) collective-permute-start(bf16[2,24,1024]{2,1,0:T(8,128)(2,1)S(1)} %get-tuple-element.30.refs_0_), channel_id=1, source_target_pairs={{0,4},{2,6},{4,0},{6,2},{1,5},{3,7},{5,1},{7,3},{8,12},{10,14},{12... | collective-permute-start | bytes 294920 | tf_op jit(solution)/shard_map/ppermute | solution.py:67
  28.3 7.6 %collective-permute-start.6 = (bf16[2,24,1024]{2,1,0:T(8,128)(2,1)S(1)}, bf16[2,24,1024]{2,1,0:T(8,128)(2,1)S(1)}, u32[]{:S(2)}, u32[]{:S(2)}) collective-permute-start(bf16[2,24,1024]{2,1,0:T(8,128)(2,1)S(1)} %get-tuple-element.30.refs_0_), channel_id=1, source_target_pairs={{0,2},{2,0},{4,6},{6,4},{1,3},{3,1},{5,7},{7,5},{8,10},{10,8},{12,... | collective-permute-start | bytes 294920 | tf_op jit(solution)/shard_map/ppermute | solution.py:67
  37.1 1.4 %collective-permute-start.9 = (bf16[4,3,2,16,128]{4,3,2,1,0:T(8,128)(2,1)S(1)}, bf16[4,3,2,16,128]{4,3,2,1,0:T(8,128)(2,1)S(1)}, u32[]{:S(2)}, u32[]{:S(2)}) collective-permute-start(bf16[4,3,2,16,128]{4,3,2,1,0:T(8,128)(2,1)S(1)} %get-tuple-element.32), channel_id=1, source_target_pairs={{0,1},{1,0},{2,3},{3,2},{4,5},{5,4},{6,7},{7,6},{8,9},{9,8},{10,11... | collective-permute-start | bytes 294920 | tf_op jit(solution)/shard_map/ppermute | solution.py:67
  38.5 4.4 %collective-permute-start.11 = (bf16[2,3,2,16,128]{4,3,2,1,0:T(8,128)(2,1)S(1)}, bf16[2,3,2,16,128]{4,3,2,1,0:T(8,128)(2,1)S(1)}, u32[]{:S(2)}, u32[]{:S(2)}) collective-permute-start(bf16[2,3,2,16,128]{4,3,2,1,0:T(8,128)(2,1)S(1)} %get-tuple-element.34), channel_id=1, source_target_pairs={{0,8},{1,17},{8,0},{9,25},{16,24},{17,1},{24,16},{25,9},{2,10},{3,... | collective-permute-start | bytes 147464 | tf_op jit(solution)/shard_map/ppermute | solution.py:460
  40.2 4.7 %collective-permute-start.10 = (bf16[1,3,2,16,128]{4,3,2,1,0:T(8,128)(2,1)S(1)}, bf16[1,3,2,16,128]{4,3,2,1,0:T(8,128)(2,1)S(1)}, u32[]{:S(2)}, u32[]{:S(2)}) collective-permute-start(bf16[1,3,2,16,128]{4,3,2,1,0:T(8,128)(2,1)S(1)} %get-tuple-element.33), channel_id=1, source_target_pairs={{0,24},{1,25},{8,16},{9,17},{16,8},{17,9},{24,0},{25,1},{2,26},{3,... | collective-permute-start | bytes 73736 | tf_op jit(solution)/shard_map/ppermute | solution.py:461
  42.9 2.0 %collective-permute-start.12 = (bf16[1,3,2,16,128]{4,3,2,1,0:T(8,128)(2,1)S(1)}, bf16[1,3,2,16,128]{4,3,2,1,0:T(8,128)(2,1)S(1)}, u32[]{:S(2)}, u32[]{:S(2)}) collective-permute-start(bf16[1,3,2,16,128]{4,3,2,1,0:T(8,128)(2,1)S(1)} %other.1), channel_id=1, source_target_pairs={{0,1},{1,0},{2,3},{3,2},{4,5},{5,4},{6,7},{7,6},{8,9},{9,8},{10,11... | collective-permute-start | bytes 73736 | tf_op jit(solution)/shard_map/ppermute | solution.py:462

commit v17 on v13

--- a/solution.py
+++ b/solution.py
@@ -71,6 +71,10 @@
 
 def shared_steps(groups, reps):
     return groups == 4 and reps == 2
+
+
+def middle_first(blocks):
+    return [blocks[step] for step in (2, 3, 1, 0)] if len(blocks) == 4 else blocks[::-1]
 
 
 def spectrum_kernel(model_hbm, table_out_ref, *refs):
@@ -534,7 +538,7 @@
     per_tile = freq_count // green_right.shape[3]
     own = project(limits, spectrum[:per_tile], green_right)
     predicted = predict(limits, own, spectrum[per_tile:], green_right, green_left, tile_count)
-    misfit, *residual = residual_of(exchange(predicted, "rtile")[::-1], data)
+    misfit, *residual = residual_of(middle_first(exchange(predicted, "rtile")), data)
     misfit = exchange([misfit] * tile_count, "rtile")
     partial = back_project(limits, misfit, green_right, green_left, freq_count, rep_count)
     arrived = return_spectra(partial)

time: 47.6 us -> 48 us (level)
  waiting for transfers between devices: 19.8 us -> 20.6 us
where the time goes in v17:
time: 48 us; the launch traced here: 47.8 us
  waiting for transfers between devices  20.6 us (43%)
  starting transfers between devices  15.5 us (32%)
  Pallas kernels  10.2 us (21%)
  between operations  0.73 us (2%)
  other arithmetic  0.7 us (1%)
    ppermute x10, waiting for transfers between devices, exchange(): arrived.append(lax.ppermute(blocks[step], axis, pairs))  16.9 us
    ppermute x10, starting transfers between devices, exchange(): arrived.append(lax.ppermute(blocks[step], axis, pairs))  13.3 us
    pallas_call x1, Pallas kernels, spectrum_of(): pl.pallas_call(spectrum_kernel, in_specs=[pl.BlockSpec(memory_space=pltpu...  4.75 us
    pallas_call x1, Pallas kernels, gradient_of(): pl.pallas_call(functools.partial(gradient_kernel, reps), in_specs=[pl.Blo...  2.5 us
    ppermute x1, waiting for transfers between devices, return_spectra(): pair = lax.ppermute(pair, ('freq', 'rep'), near)  2.18 us
    ppermute x1, starting transfers between devices, return_spectra(): pair = lax.ppermute(pair, ('freq', 'rep'), near)  1.9 us
    ppermute x1, waiting for transfers between devices, return_spectra(): last = lax.ppermute(last, ('freq', 'rep'), far)  1.52 us
    pallas_call x1, Pallas kernels, back_project(): pl.pallas_call(functools.partial(back_kernel, parts, groups, reps), in_sp...  1.19 us
  transfers between devices with their start and end apart: 13, of which 10 were waited for; matrix products, arithmetic and copies ran while one was open for 2% of the time, Pallas kernels for 1%

profile of v17, /device:TPU:0, one launch (start us, length us, event | category | flops | bytes accessed | tf_op | source)
XLA Modules:
  0.0 47.8 jit_solution(15699038336059224615)
XLA Ops:
  0.6 0.0 copy-start.3
  0.6 0.0 copy-start
  0.7 0.0 copy-start.1
  0.7 0.0 copy-start.2
  0.7 4.7 %spectrum.1 = (bf16[24,1024]{1,0:T(8,128)(2,1)S(1)}, bf16[3,2,32,128]{3,2,1,0:T(8,128)(2,1)S(1)}, bf16[3,2,32,128]{3,2,1,0:T(8,128)(2,1)S(1)}, bf16[3,2,32,128]{...) custom-call(bf16[4,32,32,1024]{3,2,1,0:T(8,128)(2,1)} %bitcast.6), custom_call_target="tpu_custom_call" | custom-call | tf_op jit(solution)/shard_map/spectrum/pallas_call | solution.py:125
  5.4 3.0 %collective-permute-start = (bf16[3,2,32,128]{3,2,1,0:T(8,128)(2,1)S(1)}, bf16[3,2,32,128]{3,2,1,0:T(8,128)(2,1)S(1)}, u32[]{:S(2)}, u32[]{:S(2)}) collective-permute-start(bf16[3,2,32,128]{3,2,1,0:T(8,128)(2,1)S(1)} %get-tuple-element.21), channel_id=1, source_target_pairs={{0,8},{8,0},{16,24},{24,16},{1,9},{9,1},{17,25},{25,17},{2,10},{10... | collective-permute-start | bytes 147464 | tf_op jit(solution)/shard_map/ppermute | solution.py:62
  8.4 1.5 %collective-permute-start.1 = (bf16[3,2,32,128]{3,2,1,0:T(8,128)(2,1)S(1)}, bf16[3,2,32,128]{3,2,1,0:T(8,128)(2,1)S(1)}, u32[]{:S(2)}, u32[]{:S(2)}) collective-permute-start(bf16[3,2,32,128]{3,2,1,0:T(8,128)(2,1)S(1)} %get-tuple-element.22), channel_id=1, source_target_pairs={{0,24},{8,16},{16,8},{24,0},{1,25},{9,17},{17,9},{25,1},{2,26},{10... | collective-permute-start | bytes 147464 | tf_op jit(solution)/shard_map/ppermute | solution.py:62
  9.9 0.0 collective-permute-start.2
  10.0 0.0 copy-done.3
  10.0 0.1 copy.7.ranks_ref
  10.1 0.1 limits.1.limits_ref
  10.2 0.3 collective-permute-done.refs_1_
  10.5 0.0 copy-done
  10.5 0.6 %project.1.own_ref = bf16[3,4,48,64]{3,2,1,0:T(8,128)(2,1)S(1)} custom-call(s32[3,4,2,1,128]{4,3,2,1,0:T(1,128)S(1)} %limits.1.limits_ref, bf16[2,3,4,2,48,256]{5,4,3,2,1,0:T(8,128)(2,1)S(1)} %copy-done, bf16[3,2,32,128]{3,2,1,0:T(8,128)(2,1)S(1)} %get-tuple-element.20.refs_0_, bf16[3,2,32,128]{3,2,1,0:T(8,128)(2,1)S(1)} %collective-permute-done.refs_1_), custom_call_target="tpu_custom_call" | custom-call | flops 37748736 | bytes 1179648 | tf_op jit(solution)/shard_map/project/pallas_call | solution.py:231
  11.1 2.3 %collective-permute-done.1.refs_0_ = bf16[3,2,32,128]{3,2,1,0:T(8,128)(2,1)S(1)} collective-permute-done((bf16[3,2,32,128]{3,2,1,0:T(8,128)(2,1)S(1)}, bf16[3,2,32,128]{3,2,1,0:T(8,128)(2,1)S(1)}, u32[]{:S(2)}, u32[]{:S(2)}) %collective-permute-start.1) | collective-permute-done | bytes 49184 | tf_op jit(solution)/shard_map/ppermute | solution.py:62
  13.4 0.6 %collective-permute-done.2.refs_1_ = bf16[3,2,32,128]{3,2,1,0:T(8,128)(2,1)S(1)} collective-permute-done((bf16[3,2,32,128]{3,2,1,0:T(8,128)(2,1)S(1)}, bf16[3,2,32,128]{3,2,1,0:T(8,128)(2,1)S(1)}, u32[]{:S(2)}, u32[]{:S(2)}) %collective-permute-start.2) | collective-permute-done | bytes 49184 | tf_op jit(solution)/shard_map/ppermute | solution.py:62
  14.0 0.0 copy-done.1
  14.0 1.0 %predict.1 = (bf16[2,24,1024]{2,1,0:T(8,128)(2,1)S(1)}, bf16[2,24,1024]{2,1,0:T(8,128)(2,1)S(1)}, bf16[2,24,1024]{2,1,0:T(8,128)(2,1)S(1)}, bf16[2,24,1024]{2,1,0:T(8,128)(2,1)S(1)}) custom-call(s32[3,4,2,1,128]{4,3,2,1,0:T(1,128)S(1)} %limits.1.limits_ref, bf16[2,3,4,2,48,256]{5,4,3,2,1,0:T(8,128)(2,1)S(1)} %copy-done, ...), custom_call_target="tpu_custom_call" | custom-call | flops 150994944 | bytes 2359296 | tf_op jit(solution)/shard_map/predict/pallas_call | solution.py:287
  15.0 2.7 %collective-permute-start.3 = (bf16[2,24,1024]{2,1,0:T(8,128)(2,1)S(1)}, bf16[2,24,1024]{2,1,0:T(8,128)(2,1)S(1)}, u32[]{:S(2)}, u32[]{:S(2)}) collective-permute-start(bf16[2,24,1024]{2,1,0:T(8,128)(2,1)S(1)} %get-tuple-element.24), channel_id=1, source_target_pairs={{0,4},{2,6},{4,0},{6,2},{1,5},{3,7},{5,1},{7,3},{8,12},{10,14},{12... | collective-permute-start | bytes 294920 | tf_op jit(solution)/shard_map/ppermute | solution.py:62
  17.7 1.3 %collective-permute-start.4 = (bf16[2,24,1024]{2,1,0:T(8,128)(2,1)S(1)}, bf16[2,24,1024]{2,1,0:T(8,128)(2,1)S(1)}, u32[]{:S(2)}, u32[]{:S(2)}) collective-permute-start(bf16[2,24,1024]{2,1,0:T(8,128)(2,1)S(1)} %get-tuple-element.25), channel_id=1, source_target_pairs={{0,6},{2,4},{4,2},{6,0},{1,7},{3,5},{5,3},{7,1},{8,14},{10,12},{12... | collective-permute-start | bytes 294920 | tf_op jit(solution)/shard_map/ppermute | solution.py:62
  19.0 0.2 collective-permute-start.5
  19.3 5.5 %collective-permute-done.3.refs_0_ = bf16[2,24,1024]{2,1,0:T(8,128)(2,1)S(1)} collective-permute-done((bf16[2,24,1024]{2,1,0:T(8,128)(2,1)S(1)}, bf16[2,24,1024]{2,1,0:T(8,128)(2,1)S(1)}, u32[]{:S(2)}, u32[]{:S(2)}) %collective-permute-start.3) | collective-permute-done | bytes 98336 | tf_op jit(solution)/shard_map/ppermute | solution.py:62
  24.8 0.0 collective-permute-done.4.refs_1_
  24.8 0.5 collective-permute-done.5.refs_2_
  25.3 0.0 copy-done.2
  25.3 0.1 residual.1
  25.3 2.7 %collective-permute-start.8 = (bf16[2,24,1024]{2,1,0:T(8,128)(2,1)S(1)}, bf16[2,24,1024]{2,1,0:T(8,128)(2,1)S(1)}, u32[]{:S(2)}, u32[]{:S(2)}) collective-permute-start(bf16[2,24,1024]{2,1,0:T(8,128)(2,1)S(1)} %get-tuple-element.30.refs_0_), channel_id=1, source_target_pairs={{0,6},{2,4},{4,2},{6,0},{1,7},{3,5},{5,3},{7,1},{8,14},{10,12},{12... | collective-permute-start | bytes 294920 | tf_op jit(solution)/shard_map/ppermute | solution.py:62
  28.1 0.2 collective-permute-start.7
  28.3 1.5 %collective-permute-start.6 = (bf16[2,24,1024]{2,1,0:T(8,128)(2,1)S(1)}, bf16[2,24,1024]{2,1,0:T(8,128)(2,1)S(1)}, u32[]{:S(2)}, u32[]{:S(2)}) collective-permute-start(bf16[2,24,1024]{2,1,0:T(8,128)(2,1)S(1)} %get-tuple-element.30.refs_0_), channel_id=1, source_target_pairs={{0,2},{2,0},{4,6},{6,4},{1,3},{3,1},{5,7},{7,5},{8,10},{10,8},{12,... | collective-permute-start | bytes 294920 | tf_op jit(solution)/shard_map/ppermute | solution.py:62
  29.8 2.9 %collective-permute-done.8.refs_3_ = bf16[2,24,1024]{2,1,0:T(8,128)(2,1)S(1)} collective-permute-done((bf16[2,24,1024]{2,1,0:T(8,128)(2,1)S(1)}, bf16[2,24,1024]{2,1,0:T(8,128)(2,1)S(1)}, u32[]{:S(2)}, u32[]{:S(2)}) %collective-permute-start.8) | collective-permute-done | bytes 98336 | tf_op jit(solution)/shard_map/ppermute | solution.py:62
  32.7 3.4 %collective-permute-done.7.refs_2_ = bf16[2,24,1024]{2,1,0:T(8,128)(2,1)S(1)} collective-permute-done((bf16[2,24,1024]{2,1,0:T(8,128)(2,1)S(1)}, bf16[2,24,1024]{2,1,0:T(8,128)(2,1)S(1)}, u32[]{:S(2)}, u32[]{:S(2)}) %collective-permute-start.7) | collective-permute-done | bytes 98336 | tf_op jit(solution)/shard_map/ppermute | solution.py:62
  36.1 0.0 collective-permute-done.6.refs_1_
  36.1 1.2 %back_project.1 = (bf16[4,3,2,16,128]{4,3,2,1,0:T(8,128)(2,1)S(1)}, bf16[4,3,2,16,128]{4,3,2,1,0:T(8,128)(2,1)S(1)}) custom-call(s32[3,4,2,1,128]{4,3,2,1,0:T(1,128)S(1)} %limits.1.limits_ref, bf16[2,3,4,2,48,256]{5,4,3,2,1,0:T(8,128)(2,1)S(1)} %copy-done, bf16[2,3,4,2,48,256]{5,4,3,2,1,0:T(8,128)(2,1)S(1)} %copy-done.1, ...), custom_call_target="tpu_custom_call" | custom-call | flops 150994944 | bytes 2359296 | tf_op jit(solution)/shard_map/back_project/pallas_call | solution.py:398
  37.3 0.1 collective-permute-start.9
  37.4 1.3 %collective-permute-done.9.refs_1_ = bf16[4,3,2,16,128]{4,3,2,1,0:T(8,128)(2,1)S(1)} collective-permute-done((bf16[4,3,2,16,128]{4,3,2,1,0:T(8,128)(2,1)S(1)}, bf16[4,3,2,16,128]{4,3,2,1,0:T(8,128)(2,1)S(1)}, u32[]{:S(2)}, u32[]{:S(2)}) %collective-permute-start.9) | collective-permute-done | bytes 98336 | tf_op jit(solution)/shard_map/ppermute | solution.py:62
  38.7 1.9 %collective-permute-start.11 = (bf16[2,3,2,16,128]{4,3,2,1,0:T(8,128)(2,1)S(1)}, bf16[2,3,2,16,128]{4,3,2,1,0:T(8,128)(2,1)S(1)}, u32[]{:S(2)}, u32[]{:S(2)}) collective-permute-start(bf16[2,3,2,16,128]{4,3,2,1,0:T(8,128)(2,1)S(1)} %get-tuple-element.34), channel_id=1, source_target_pairs={{0,8},{1,17},{8,0},{9,25},{16,24},{17,1},{24,16},{25,9},{2,10},{3,... | collective-permute-start | bytes 147464 | tf_op jit(solution)/shard_map/ppermute | solution.py:459
  40.6 0.3 collective-permute-start.10
  40.9 2.2 %collective-permute-done.11.pair_ref.refs_2_ = bf16[2,3,2,16,128]{4,3,2,1,0:T(8,128)(2,1)S(1)} collective-permute-done((bf16[2,3,2,16,128]{4,3,2,1,0:T(8,128)(2,1)S(1)}, bf16[2,3,2,16,128]{4,3,2,1,0:T(8,128)(2,1)S(1)}, u32[]{:S(2)}, u32[]{:S(2)}) %collective-permute-start.11) | collective-permute-done | bytes 49184 | tf_op jit(solution)/shard_map/ppermute | solution.py:459
  43.1 0.0 collective-permute-start.12
  43.1 0.7 %pad_maximum_fusion = f32[2,24,1024]{2,1,0:T(8,128)} fusion(f32[1,24,1024]{2,1,0:T(8,128)S(1)} %bitcast.5, f32[1,24,1024]{2,1,0:T(8,128)S(1)} %bitcast.4), kind=kLoop, calls=%fused_computation | loop fusion | flops 49152 | bytes 393216 | tf_op jit(solution)/shard_map/stack | solution.py:545
  43.8 1.5 %collective-permute-done.10.refs_0_ = bf16[1,3,2,16,128]{4,3,2,1,0:T(8,128)(2,1)S(1)} collective-permute-done((bf16[1,3,2,16,128]{4,3,2,1,0:T(8,128)(2,1)S(1)}, bf16[1,3,2,16,128]{4,3,2,1,0:T(8,128)(2,1)S(1)}, u32[]{:S(2)}, u32[]{:S(2)}) %collective-permute-start.10) | collective-permute-done | bytes 24608 | tf_op jit(solution)/shard_map/ppermute | solution.py:460
  45.3 0.0 collective-permute-done.12.refs_1_
  45.3 2.5 %gradient.1 = bf16[4,16,32,1024]{3,2,1,0:T(8,128)(2,1)} custom-call(bf16[24,1024]{1,0:T(8,128)(2,1)S(1)} %get-tuple-element.19.table_ref, bf16[1,3,2,16,128]{4,3,2,1,0:T(8,128)(2,1)S(1)} %collective-permute-done.10.refs_0_, bf16[1,3,2,16,128]{4,3,2,1,0:T(8,128)(2,1)S(1)} %collective-permute-done.12.refs_1_, ...), custom_call_target="tpu_custom_call" | custom-call | tf_op jit(solution)/shard_map/gradient/pallas_call | solution.py:513
  (2 shorter events, 0.0 us)
Async XLA Ops:
  0.6 9.3 %copy-start.3 = (s32[3,4,2]{1,2,0:T(2,128)S(1)}, s32[3,4,2]{1,2,0:T(2,128)}, u32[]{:S(2)}) copy-start(s32[3,4,2]{1,2,0:T(2,128)} %param.8) | copy-start | bytes 292
  0.6 9.9 %copy-start = (bf16[2,3,4,2,48,256]{5,4,3,2,1,0:T(8,128)(2,1)S(1)}, bf16[2,3,4,2,48,256]{5,4,3,2,1,0:T(8,128)(2,1)}, u32[]{:S(2)}) copy-start(bf16[2,3,4,2,48,256]{5,4,3,2,1,0:T(8,128)(2,1)} %right_ref.5) | copy-start | bytes 3538948
  0.7 13.4 %copy-start.1 = (bf16[2,3,4,2,48,256]{5,4,3,2,1,0:T(8,128)(2,1)S(1)}, bf16[2,3,4,2,48,256]{5,4,3,2,1,0:T(8,128)(2,1)}, u32[]{:S(2)}) copy-start(bf16[2,3,4,2,48,256]{5,4,3,2,1,0:T(8,128)(2,1)} %left_ref.3) | copy-start | bytes 3538948
  0.7 24.6 %copy-start.2 = (f32[2,24,1024]{2,1,0:T(8,128)S(1)}, f32[2,24,1024]{2,1,0:T(8,128)}, u32[]{:S(2)}) copy-start(f32[2,24,1024]{2,1,0:T(8,128)} %data_ref.1) | copy-start | bytes 589828
  5.4 5.1 %collective-permute-start = (bf16[3,2,32,128]{3,2,1,0:T(8,128)(2,1)S(1)}, bf16[3,2,32,128]{3,2,1,0:T(8,128)(2,1)S(1)}, u32[]{:S(2)}, u32[]{:S(2)}) collective-permute-start(bf16[3,2,32,128]{3,2,1,0:T(8,128)(2,1)S(1)} %get-tuple-element.21), channel_id=1, source_target_pairs={{0,8},{8,0},{16,24},{24,16},{1,9},{9,1},{17,25},{25,17},{2,10},{10... | collective-permute-start | bytes 147464 | tf_op jit(solution)/shard_map/ppermute | solution.py:62
  8.4 5.0 %collective-permute-start.1 = (bf16[3,2,32,128]{3,2,1,0:T(8,128)(2,1)S(1)}, bf16[3,2,32,128]{3,2,1,0:T(8,128)(2,1)S(1)}, u32[]{:S(2)}, u32[]{:S(2)}) collective-permute-start(bf16[3,2,32,128]{3,2,1,0:T(8,128)(2,1)S(1)} %get-tuple-element.22), channel_id=1, source_target_pairs={{0,24},{8,16},{16,8},{24,0},{1,25},{9,17},{17,9},{25,1},{2,26},{10... | collective-permute-start | bytes 147464 | tf_op jit(solution)/shard_map/ppermute | solution.py:62
  9.9 4.1 %collective-permute-start.2 = (bf16[3,2,32,128]{3,2,1,0:T(8,128)(2,1)S(1)}, bf16[3,2,32,128]{3,2,1,0:T(8,128)(2,1)S(1)}, u32[]{:S(2)}, u32[]{:S(2)}) collective-permute-start(bf16[3,2,32,128]{3,2,1,0:T(8,128)(2,1)S(1)} %get-tuple-element.23), channel_id=1, source_target_pairs={{0,16},{8,24},{16,0},{24,8},{1,17},{9,25},{17,1},{25,9},{2,18},{10... | collective-permute-start | bytes 147464 | tf_op jit(solution)/shard_map/ppermute | solution.py:62
  15.0 9.8 %collective-permute-start.3 = (bf16[2,24,1024]{2,1,0:T(8,128)(2,1)S(1)}, bf16[2,24,1024]{2,1,0:T(8,128)(2,1)S(1)}, u32[]{:S(2)}, u32[]{:S(2)}) collective-permute-start(bf16[2,24,1024]{2,1,0:T(8,128)(2,1)S(1)} %get-tuple-element.24), channel_id=1, source_target_pairs={{0,4},{2,6},{4,0},{6,2},{1,5},{3,7},{5,1},{7,3},{8,12},{10,14},{12... | collective-permute-start | bytes 294920 | tf_op jit(solution)/shard_map/ppermute | solution.py:62
  17.7 7.1 %collective-permute-start.4 = (bf16[2,24,1024]{2,1,0:T(8,128)(2,1)S(1)}, bf16[2,24,1024]{2,1,0:T(8,128)(2,1)S(1)}, u32[]{:S(2)}, u32[]{:S(2)}) collective-permute-start(bf16[2,24,1024]{2,1,0:T(8,128)(2,1)S(1)} %get-tuple-element.25), channel_id=1, source_target_pairs={{0,6},{2,4},{4,2},{6,0},{1,7},{3,5},{5,3},{7,1},{8,14},{10,12},{12... | collective-permute-start | bytes 294920 | tf_op jit(solution)/shard_map/ppermute | solution.py:62
  19.0 6.2 %collective-permute-start.5 = (bf16[2,24,1024]{2,1,0:T(8,128)(2,1)S(1)}, bf16[2,24,1024]{2,1,0:T(8,128)(2,1)S(1)}, u32[]{:S(2)}, u32[]{:S(2)}) collective-permute-start(bf16[2,24,1024]{2,1,0:T(8,128)(2,1)S(1)} %get-tuple-element.26), channel_id=1, source_target_pairs={{0,2},{2,0},{4,6},{6,4},{1,3},{3,1},{5,7},{7,5},{8,10},{10,8},{12,... | collective-permute-start | bytes 294920 | tf_op jit(solution)/shard_map/ppermute | solution.py:62
  25.3 7.4 %collective-permute-start.8 = (bf16[2,24,1024]{2,1,0:T(8,128)(2,1)S(1)}, bf16[2,24,1024]{2,1,0:T(8,128)(2,1)S(1)}, u32[]{:S(2)}, u32[]{:S(2)}) collective-permute-start(bf16[2,24,1024]{2,1,0:T(8,128)(2,1)S(1)} %get-tuple-element.30.refs_0_), channel_id=1, source_target_pairs={{0,6},{2,4},{4,2},{6,0},{1,7},{3,5},{5,3},{7,1},{8,14},{10,12},{12... | collective-permute-start | bytes 294920 | tf_op jit(solution)/shard_map/ppermute | solution.py:62
  28.1 8.0 %collective-permute-start.7 = (bf16[2,24,1024]{2,1,0:T(8,128)(2,1)S(1)}, bf16[2,24,1024]{2,1,0:T(8,128)(2,1)S(1)}, u32[]{:S(2)}, u32[]{:S(2)}) collective-permute-start(bf16[2,24,1024]{2,1,0:T(8,128)(2,1)S(1)} %get-tuple-element.30.refs_0_), channel_id=1, source_target_pairs={{0,4},{2,6},{4,0},{6,2},{1,5},{3,7},{5,1},{7,3},{8,12},{10,14},{12... | collective-permute-start | bytes 294920 | tf_op jit(solution)/shard_map/ppermute | solution.py:62
  28.3 7.8 %collective-permute-start.6 = (bf16[2,24,1024]{2,1,0:T(8,128)(2,1)S(1)}, bf16[2,24,1024]{2,1,0:T(8,128)(2,1)S(1)}, u32[]{:S(2)}, u32[]{:S(2)}) collective-permute-start(bf16[2,24,1024]{2,1,0:T(8,128)(2,1)S(1)} %get-tuple-element.30.refs_0_), channel_id=1, source_target_pairs={{0,2},{2,0},{4,6},{6,4},{1,3},{3,1},{5,7},{7,5},{8,10},{10,8},{12,... | collective-permute-start | bytes 294920 | tf_op jit(solution)/shard_map/ppermute | solution.py:62
  37.3 1.4 %collective-permute-start.9 = (bf16[4,3,2,16,128]{4,3,2,1,0:T(8,128)(2,1)S(1)}, bf16[4,3,2,16,128]{4,3,2,1,0:T(8,128)(2,1)S(1)}, u32[]{:S(2)}, u32[]{:S(2)}) collective-permute-start(bf16[4,3,2,16,128]{4,3,2,1,0:T(8,128)(2,1)S(1)} %get-tuple-element.32), channel_id=1, source_target_pairs={{0,1},{1,0},{2,3},{3,2},{4,5},{5,4},{6,7},{7,6},{8,9},{9,8},{10,11... | collective-permute-start | bytes 294920 | tf_op jit(solution)/shard_map/ppermute | solution.py:62
  38.7 4.4 %collective-permute-start.11 = (bf16[2,3,2,16,128]{4,3,2,1,0:T(8,128)(2,1)S(1)}, bf16[2,3,2,16,128]{4,3,2,1,0:T(8,128)(2,1)S(1)}, u32[]{:S(2)}, u32[]{:S(2)}) collective-permute-start(bf16[2,3,2,16,128]{4,3,2,1,0:T(8,128)(2,1)S(1)} %get-tuple-element.34), channel_id=1, source_target_pairs={{0,8},{1,17},{8,0},{9,25},{16,24},{17,1},{24,16},{25,9},{2,10},{3,... | collective-permute-start | bytes 147464 | tf_op jit(solution)/shard_map/ppermute | solution.py:459
  40.6 4.7 %collective-permute-start.10 = (bf16[1,3,2,16,128]{4,3,2,1,0:T(8,128)(2,1)S(1)}, bf16[1,3,2,16,128]{4,3,2,1,0:T(8,128)(2,1)S(1)}, u32[]{:S(2)}, u32[]{:S(2)}) collective-permute-start(bf16[1,3,2,16,128]{4,3,2,1,0:T(8,128)(2,1)S(1)} %get-tuple-element.33), channel_id=1, source_target_pairs={{0,24},{1,25},{8,16},{9,17},{16,8},{17,9},{24,0},{25,1},{2,26},{3,... | collective-permute-start | bytes 73736 | tf_op jit(solution)/shard_map/ppermute | solution.py:460
  43.1 2.2 %collective-permute-start.12 = (bf16[1,3,2,16,128]{4,3,2,1,0:T(8,128)(2,1)S(1)}, bf16[1,3,2,16,128]{4,3,2,1,0:T(8,128)(2,1)S(1)}, u32[]{:S(2)}, u32[]{:S(2)}) collective-permute-start(bf16[1,3,2,16,128]{4,3,2,1,0:T(8,128)(2,1)S(1)} %other.1), channel_id=1, source_target_pairs={{0,1},{1,0},{2,3},{3,2},{4,5},{5,4},{6,7},{7,6},{8,9},{9,8},{10,11... | collective-permute-start | bytes 73736 | tf_op jit(solution)/shard_map/ppermute | solution.py:461
